TPU v7x, 512 devices: a whole 4x4x16 slice. The times are simulated.
512 devices in a mesh: dom: 64 (over z_hi, y, x, core), feat: 8 (over z_lo).
Axes of the slice: x: 4, y: 4, z: 16 (z_hi: 2, z_lo: 8; z = z_hi * 8 + z_lo), core: 2. Of those that a mesh axis runs over, the one named last changes fastest.
Arguments:
- features: bfloat16 [256, 851968], P('feat', 'dom'), may hold values from -6 to 6
- block_row: int32 [64, 64], P('dom'), may hold values from 0 to 103, as said below
- block_col: int32 [64, 64], P('dom'), may hold values from 0 to 119, as said below
- block_count: int32 [64], P('dom'), may hold values from 2 to 64, as said below
- block_values: bfloat16 [4096, 128, 128], P('dom'), may hold values from -0.5 to 0.5
- w_self: bfloat16 [256, 256], replicated, may hold values from -0.375 to 0.375
- w_neigh: bfloat16 [256, 256], replicated, may hold values from -0.375 to 0.375
- cotangent: bfloat16 [256, 851968], P(None, ('dom', 'feat')), may hold values from -6 to 6
Outputs:
- feature_grad: bfloat16 [256, 851968], P('feat', 'dom')
- self_grad: bfloat16 [256, 256], replicated
- neigh_grad: bfloat16 [256, 256], replicated
Inputs may be any that keep to these rules, and one draw needn't show every extreme that they name: `block_row`: in every partition slot 0 lies in block row 0 and slot 1 in block row 103. block_col differs from block_row + 8 by at most 8; in every partition slot 0 has the value 0 and slot 1 the value 104 + 2 * 8 - 1. `block_count`: some partition uses all 64 slots in every draw.
All inputs are finite; a program needn't handle non-finite values.
Results may differ from a plain program's by a relative error of at most 0.0061.
Values may be sent and summed in bfloat16 or wider, within the bound.
No kernel may reach another device: no remote copies, remote signals or barrier semaphores. Data moves between devices by JAX's collectives and lax.ppermute only.
A program may use at most 64 MiB of HBM per device.

v0:
```python
import math

import jax
import jax.numpy as jnp
from jax import lax
from jax.sharding import PartitionSpec as P

BLK = 128
REACH = 8


def padded(cells, sides, width):
    for axis, dim in sides:
        count = lax.axis_size(axis)
        head = lax.slice_in_dim(cells, 0, width, axis=dim)
        tail = lax.slice_in_dim(cells, cells.shape[dim] - width, cells.shape[dim], axis=dim)
        cells = jnp.concatenate(
            [
                lax.ppermute(tail, axis, [(i, (i + 1) % count) for i in range(count)]),
                cells,
                lax.ppermute(head, axis, [((i + 1) % count, i) for i in range(count)]),
            ],
            axis=dim,
        )
    return cells


def shifted(shard, axis, by):
    count = lax.axis_size(axis)
    return lax.ppermute(shard, axis, [(i, (i + by) % count) for i in range(count)])


def silu_slope(preact):
    sigma = jax.nn.sigmoid(preact)
    return sigma * (1.0 + preact * (1.0 - sigma))


def on_device(
    features, block_row, block_col, block_count, block_values, w_self, w_neigh, cotangent
):
    shard_width, rows_part = features.shape
    rim = REACH * BLK
    row_blocks = rows_part // BLK
    widened_blocks = row_blocks + 2 * REACH
    slots = block_values.shape[0]
    widened = padded(features, (("dom", 1),), rim)
    block_rows = block_row[0]
    block_cols = block_col[0]
    live = (jnp.arange(slots, dtype=jnp.int32) < block_count[0]).astype(jnp.float32)
    columns = jnp.take(widened.reshape(shard_width, widened_blocks, BLK), block_cols, axis=1)
    products = jnp.einsum("dkj,kij->dki", columns, block_values, preferred_element_type=jnp.float32)
    products = products * live[None, :, None]
    row_onehot = (jnp.arange(row_blocks, dtype=jnp.int32)[:, None] == block_rows[None, :]).astype(
        jnp.float32
    )
    aggregated = jnp.einsum("rk,dki->dri", row_onehot, products, precision=lax.Precision.HIGHEST)
    aggregated = aggregated.reshape(shard_width, rows_part).astype(jnp.bfloat16)
    node_rows, agg_rows = (
        lax.all_to_all(features, "feat", split_axis=1, concat_axis=0, tiled=True),
        lax.all_to_all(aggregated, "feat", split_axis=1, concat_axis=0, tiled=True),
    )
    preact = jnp.einsum("io,in->on", w_self, node_rows, preferred_element_type=jnp.float32)
    preact = preact + jnp.einsum("io,in->on", w_neigh, agg_rows, preferred_element_type=jnp.float32)
    delta = (cotangent.astype(jnp.float32) * silu_slope(preact)).astype(jnp.bfloat16)
    self_term = jnp.einsum("in,on->io", node_rows, delta, preferred_element_type=jnp.float32)
    neigh_term = jnp.einsum("in,on->io", agg_rows, delta, preferred_element_type=jnp.float32)
    direct = jnp.einsum("io,on->in", w_self, delta, preferred_element_type=jnp.float32).astype(
        jnp.bfloat16
    )
    agg_grad = jnp.einsum("io,on->in", w_neigh, delta, preferred_element_type=jnp.float32).astype(
        jnp.bfloat16
    )
    direct_cols, agg_cols = (
        lax.all_to_all(direct, "feat", split_axis=0, concat_axis=1, tiled=True),
        lax.all_to_all(agg_grad, "feat", split_axis=0, concat_axis=1, tiled=True),
    )
    picked = jnp.take(agg_cols.reshape(shard_width, row_blocks, BLK), block_rows, axis=1)
    spread = jnp.einsum("dki,kij->dkj", picked, block_values, preferred_element_type=jnp.float32)
    spread = spread * live[None, :, None]
    col_onehot = (
        jnp.arange(widened_blocks, dtype=jnp.int32)[:, None] == block_cols[None, :]
    ).astype(jnp.float32)
    scattered = jnp.einsum("ek,dkj->dej", col_onehot, spread, precision=lax.Precision.HIGHEST)
    scattered = scattered.reshape(shard_width, widened_blocks * BLK)
    from_next = shifted(scattered[:, :rim].astype(jnp.bfloat16), "dom", -1).astype(jnp.float32)
    from_prev = shifted(scattered[:, rim + rows_part :].astype(jnp.bfloat16), "dom", 1).astype(
        jnp.float32
    )
    total = direct_cols.astype(jnp.float32) + scattered[:, rim : rim + rows_part]
    total = total + jnp.pad(from_prev, ((0, 0), (0, rows_part - rim)))
    total = total + jnp.pad(from_next, ((0, 0), (rows_part - rim, 0)))
    feature_grad = total.astype(jnp.bfloat16)
    self_sum, neigh_sum = lax.psum((self_term, neigh_term), ("dom", "feat"))
    factor = 1.0 / math.sqrt(rows_part * lax.axis_size("dom"))
    self_grad = (self_sum * factor).astype(jnp.bfloat16)
    neigh_grad = (neigh_sum * factor).astype(jnp.bfloat16)
    return (feature_grad, self_grad, neigh_grad)


def solution(mesh):
    return jax.shard_map(
        on_device,
        mesh=mesh,
        in_specs=(
            P("feat", "dom"),
            P("dom", None),
            P("dom", None),
            P("dom"),
            P("dom", None, None),
            P(),
            P(),
            P(None, ("dom", "feat")),
        ),
        out_specs=(P("feat", "dom"), P(), P()),
        check_vma=False,
    )
```

profile of v0, /device:TPU:31, one launch (start us, length us, event | category | flops | bytes accessed | tf_op | source)
XLA Modules:
  0.0 705.8 jit_solution(11143936276071026402)
XLA Ops:
  8.2 15.6 %collective-permute-start = (bf16[32,1024]{1,0:T(8,128)(2,1)S(1)}, bf16[32,1024]{1,0:T(8,128)(2,1)S(1)}, u32[]{:S(2)}, u32[]{:S(2)}) collective-permute-start(bf16[32,1024]{1,0:T(8,128)(2,1)S(1)} %get-tuple-element.19), channel_id=1, source_target_pairs={{0,8},{8,16},{16,24},{24,32},{32,40},{40,48},{48,56},{56,64},{64,7... | collective-permute-start | bytes 196616 | tf_op jit(solution)/shard_map/ppermute | solution.py:19
  23.8 1.9 collective-permute-start.1
  27.7 15.0 %collective-permute-done.1 = bf16[32,1024]{1,0:T(8,128)(2,1)S(1)} collective-permute-done((bf16[32,1024]{1,0:T(8,128)(2,1)S(1)}, bf16[32,1024]{1,0:T(8,128)(2,1)S(1)}, u32[]{:S(2)}, u32[]{:S(2)}) %collective-permute-start.1) | collective-permute-done | bytes 65568 | tf_op jit(solution)/shard_map/ppermute | solution.py:21
  42.7 1.3 copy_bitcast_fusion.1
  44.0 1.4 gather_fusion
  45.5 2.3 fusion.4
  47.7 1.6 fusion.5
  49.3 1.8 convert_element_type.67
  51.1 2.2 copy.39
  53.3 4.4 all-to-all-start.1
  57.7 2.2 copy.64
  59.8 26.3 %all-to-all-done.1 = bf16[32,8,1664]{2,0,1:T(8,128)(2,1)S(1)} async-done(((bf16[32,8,1664]{2,0,1:T(8,128)(2,1)}), bf16[32,8,1664]{2,0,1:T(8,128)(2,1)S(1)}, u32[]{:S(2)}, u32[]{:S(2)}) %all-to-all-start.1) | async-done | bytes 852000 | tf_op jit(solution)/shard_map/all_to_all | solution.py:60
  86.1 4.2 all-to-all-start
  90.4 1.7 convolution_bitcast_fusion
  92.1 38.7 %all-to-all-done = bf16[32,8,1664]{2,0,1:T(8,128)(2,1)} async-done(((bf16[32,8,1664]{2,0,1:T(8,128)(2,1)}), bf16[32,8,1664]{2,0,1:T(8,128)(2,1)}, u32[]{:S(2)}, u32[]{:S(2)}) %all-to-all-start) | async-done | bytes 852000 | tf_op jit(solution)/shard_map/all_to_all | solution.py:59
  130.8 2.8 multiply_convert_fusion
  133.6 1.3 convolution_convert_fusion
  134.9 4.2 all-to-all-start.3
  139.2 1.3 convolution_convert_fusion.1
  140.5 41.7 %all-to-all-done.3 = bf16[8,32,1664]{2,1,0:T(8,128)(2,1)} async-done(((bf16[8,32,1664]{2,1,0:T(8,128)(2,1)}), bf16[8,32,1664]{2,1,0:T(8,128)(2,1)}, u32[]{:S(2)}, u32[]{:S(2)}) %all-to-all-start.3) | async-done | bytes 852000 | tf_op jit(solution)/shard_map/all_to_all | solution.py:75
  182.2 4.2 all-to-all-start.2
  186.4 2.3 fusion.30
  188.7 2.3 convolution_bitcast_fusion.1
  191.1 464.4 %all-reduce.5.cloned.1.call-done = (f32[256,256]{0,1:T(8,128)}, f32[256,256]{0,1:T(8,128)}) async-done(((f32[256,256]{0,1:T(8,128)}, f32[256,256]{0,1:T(8,128)}), (f32[256,256]{0,1:T(8,128)}, f32[256,256]{0,1:T(8,128)})) %all-reduce.5.cloned.1.call-update) | async-done | bytes 524304 | tf_op jit(solution)/shard_map/psum | solution.py:93
  658.9 1.4 copy.42
  660.3 1.9 reshape.107
  662.2 1.3 copy.43
  664.9 1.6 fusion.6
  668.2 9.7 %collective-permute-start.2 = (bf16[32,1024]{1,0:T(8,128)(2,1)S(1)}, bf16[32,1024]{1,0:T(8,128)(2,1)S(1)}, u32[]{:S(2)}, u32[]{:S(2)}) collective-permute-start(bf16[32,1024]{1,0:T(8,128)(2,1)S(1)} %get-tuple-element.17), channel_id=1, source_target_pairs={{0,8},{8,16},{16,24},{24,32},{32,40},{40,48},{48,56},{56,64},{64,7... | collective-permute-start | bytes 196616 | tf_op jit(solution)/shard_map/ppermute | solution.py:30
  677.9 1.9 collective-permute-start.3
  679.9 1.4 convert_bitcast_fusion
  682.1 15.7 %collective-permute-done.3 = bf16[32,1024]{1,0:T(8,128)(2,1)S(1)} collective-permute-done((bf16[32,1024]{1,0:T(8,128)(2,1)S(1)}, bf16[32,1024]{1,0:T(8,128)(2,1)S(1)}, u32[]{:S(2)}, u32[]{:S(2)}) %collective-permute-start.3) | collective-permute-done | bytes 65568 | tf_op jit(solution)/shard_map/ppermute | solution.py:30
  (39 shorter events, 10.9 us)
Async XLA Ops:
  7.2 38.3 %copy-start = (bf16[64,128,128]{2,1,0:T(8,128)(2,1)S(1)}, bf16[64,128,128]{2,1,0:T(8,128)(2,1)}, u32[]{:S(2)}) copy-start(bf16[64,128,128]{2,1,0:T(8,128)(2,1)} %param.12) | copy-start | bytes 6291460
  8.2 19.5 %collective-permute-start = (bf16[32,1024]{1,0:T(8,128)(2,1)S(1)}, bf16[32,1024]{1,0:T(8,128)(2,1)S(1)}, u32[]{:S(2)}, u32[]{:S(2)}) collective-permute-start(bf16[32,1024]{1,0:T(8,128)(2,1)S(1)} %get-tuple-element.19), channel_id=1, source_target_pairs={{0,8},{8,16},{16,24},{24,32},{32,40},{40,48},{48,56},{56,64},{64,7... | collective-permute-start | bytes 196616 | tf_op jit(solution)/shard_map/ppermute | solution.py:19
  23.8 18.9 %collective-permute-start.1 = (bf16[32,1024]{1,0:T(8,128)(2,1)S(1)}, bf16[32,1024]{1,0:T(8,128)(2,1)S(1)}, u32[]{:S(2)}, u32[]{:S(2)}) collective-permute-start(bf16[32,1024]{1,0:T(8,128)(2,1)S(1)} %get-tuple-element.20), channel_id=1, source_target_pairs={{8,0},{16,8},{24,16},{32,24},{40,32},{48,40},{56,48},{64,56},{72,6... | collective-permute-start | bytes 196616 | tf_op jit(solution)/shard_map/ppermute | solution.py:21
  45.5 2.3 copy-start.7
  53.3 32.8 %all-to-all-start.1 = ((bf16[32,8,1664]{2,0,1:T(8,128)(2,1)}), bf16[32,8,1664]{2,0,1:T(8,128)(2,1)S(1)}, u32[]{:S(2)}, u32[]{:S(2)}) async-start(bf16[32,8,1664]{2,0,1:T(8,128)(2,1)} %copy.39), calls=%async_computation.1 | async-start | bytes 1703936 | tf_op jit(solution)/shard_map/all_to_all | solution.py:60
  57.7 32.7 %copy-start.4 = (bf16[256,256]{1,0:T(8,128)(2,1)S(1)}, bf16[256,256]{1,0:T(8,128)(2,1)}, u32[]{:S(2)}) copy-start(bf16[256,256]{1,0:T(8,128)(2,1)} %param.14) | copy-start | bytes 393220
  86.1 6.0 copy-start.3
  86.1 44.7 %all-to-all-start = ((bf16[32,8,1664]{2,0,1:T(8,128)(2,1)}), bf16[32,8,1664]{2,0,1:T(8,128)(2,1)}, u32[]{:S(2)}, u32[]{:S(2)}) async-start(bf16[32,8,1664]{2,0,1:T(8,128)(2,1)} %bitcast.93), calls=%async_computation | async-start | bytes 1703936 | tf_op jit(solution)/shard_map/all_to_all | solution.py:59
  90.4 40.4 %copy-start.5 = (bf16[256,256]{1,0:T(8,128)(2,1)S(1)}, bf16[256,256]{1,0:T(8,128)(2,1)}, u32[]{:S(2)}) copy-start(bf16[256,256]{1,0:T(8,128)(2,1)} %param.13) | copy-start | bytes 393220
  134.9 47.2 %all-to-all-start.3 = ((bf16[8,32,1664]{2,1,0:T(8,128)(2,1)}), bf16[8,32,1664]{2,1,0:T(8,128)(2,1)}, u32[]{:S(2)}, u32[]{:S(2)}) async-start(bf16[8,32,1664]{2,1,0:T(8,128)(2,1)} %bitcast.92), calls=%async_computation.3 | async-start | bytes 1703936 | tf_op jit(solution)/shard_map/all_to_all | solution.py:75
  182.2 497.7 %all-to-all-start.2 = ((bf16[8,32,1664]{2,1,0:T(8,128)(2,1)}), bf16[8,32,1664]{2,1,0:T(8,128)(2,1)}, u32[]{:S(2)}, u32[]{:S(2)}) async-start(bf16[8,32,1664]{2,1,0:T(8,128)(2,1)} %bitcast.91), calls=%async_computation.2 | async-start | bytes 1703936 | tf_op jit(solution)/shard_map/all_to_all | solution.py:74
  186.4 469.1 %all-reduce.5.cloned.1.call-start = ((), (), s32[]{:S(2)}) async-start(), calls=%async_computation.4 | async-start | bytes 1048576 | tf_op jit(solution)/shard_map/psum | solution.py:93
  664.2 0.7 copy-start.6
  666.5 1.3 copy-start.1
  668.2 13.9 %collective-permute-start.2 = (bf16[32,1024]{1,0:T(8,128)(2,1)S(1)}, bf16[32,1024]{1,0:T(8,128)(2,1)S(1)}, u32[]{:S(2)}, u32[]{:S(2)}) collective-permute-start(bf16[32,1024]{1,0:T(8,128)(2,1)S(1)} %get-tuple-element.17), channel_id=1, source_target_pairs={{0,8},{8,16},{16,24},{24,32},{32,40},{40,48},{48,56},{56,64},{64,7... | collective-permute-start | bytes 196616 | tf_op jit(solution)/shard_map/ppermute | solution.py:30
  677.9 19.9 %collective-permute-start.3 = (bf16[32,1024]{1,0:T(8,128)(2,1)S(1)}, bf16[32,1024]{1,0:T(8,128)(2,1)S(1)}, u32[]{:S(2)}, u32[]{:S(2)}) collective-permute-start(bf16[32,1024]{1,0:T(8,128)(2,1)S(1)} %get-tuple-element.18), channel_id=1, source_target_pairs={{0,504},{8,0},{16,8},{24,16},{32,24},{40,32},{48,40},{56,48},{64,5... | collective-permute-start | bytes 196616 | tf_op jit(solution)/shard_map/ppermute | solution.py:30
  679.9 1.8 copy-start.2
Sparse Core Ops, SparseCore 0:
  192.7 462.6 all-reduce.4
where the time goes:
time: 707 us; the launch traced here: 706 us
  waiting for transfers between devices  602 us (85%)
  starting transfers between devices  46.2 us (7%)
  local copies, waits for them, and re-layouts  17.9 us (3%)
  matrix products  17.9 us (3%)
  between operations  14.9 us (2%)
  other arithmetic  7.11 us (1%)
    psum x1, waiting for transfers between devices, on_device(): self_sum, neigh_sum = lax.psum((self_term, neigh_term), ('dom', 'feat'))  464 us
    all_to_all x1, waiting for transfers between devices, on_device(): lax.all_to_all(agg_grad, 'feat', split_axis=0, concat_axis=1, tiled=True)  41.7 us
    all_to_all x1, waiting for transfers between devices, on_device(): lax.all_to_all(features, 'feat', split_axis=1, concat_axis=0, tiled=True)  38.7 us
    all_to_all x1, waiting for transfers between devices, on_device(): lax.all_to_all(aggregated, 'feat', split_axis=1, concat_axis=0, tiled=True)  26.3 us
    ppermute x2, waiting for transfers between devices, shifted(): lax.ppermute(shard, axis, [(i, (i + by) % count) for i in range(count)])  15.7 us
    ppermute x1, starting transfers between devices, padded(): lax.ppermute(tail, axis, [(i, (i + 1) % count) for i in range(count)])  15.6 us
    ppermute x1, waiting for transfers between devices, padded(): lax.ppermute(head, axis, [((i + 1) % count, i) for i in range(count)])  15 us
  transfers between devices with their start and end apart: 9, of which 6 were waited for; matrix products, arithmetic and copies ran while one was open for 3% of the time, Pallas kernels for 0%

commit v1 on v0

v1 whole, which is shorter than its diff:
```python
import functools
import math

import jax
import jax.numpy as jnp
from jax import lax
from jax.experimental import pallas as pl
from jax.experimental.pallas import tpu as pltpu
from jax.sharding import Mesh, PartitionSpec as P

BLK = 128
REACH = 8
DOM = ("zh", "y", "x", "core")
PLANE = ("y", "x", "core")
LINE = ("zh", "feat")
RING = DOM + ("feat",)


def shifted(shard, axis, by):
    count = lax.axis_size(axis)
    return lax.ppermute(shard, axis, [(i, (i + by) % count) for i in range(count)])


def tiles_of(width, tile):
    return [(at, min(tile, width - at)) for at in range(0, width, tile)]


def local_kernel(
    rows_ref,
    cols_ref,
    count_ref,
    pos_ref,
    own_ref,
    before_ref,
    after_ref,
    values_ref,
    w_in_ref,
    w_out_ref,
    cot_ref,
    middle_ref,
    left_ref,
    right_ref,
    terms_ref,
    wide,
    agg,
    stacked,
    delta,
    agg_grad,
    scat,
    sems,
):
    depth, width = own_ref.shape
    rim = before_ref.shape[1]
    chunk = width // BLK
    copies = [
        pltpu.make_async_copy(before_ref, wide.at[:, pl.ds(0, rim)], sems.at[0]),
        pltpu.make_async_copy(own_ref, wide.at[:, pl.ds(rim, width)], sems.at[1]),
        pltpu.make_async_copy(after_ref, wide.at[:, pl.ds(rim + width, rim)], sems.at[2]),
    ]
    for copy in copies:
        copy.start()
    agg[...] = jnp.zeros_like(agg)
    scat[:, :rim] = jnp.zeros((depth, rim), jnp.float32)
    scat[:, rim + width :] = jnp.zeros((depth, rim), jnp.float32)
    first = pos_ref[0] * chunk
    count = count_ref[0]
    for copy in copies:
        copy.wait()

    def gather_slot(slot, carry):
        row = rows_ref[slot] - first

        @pl.when((row >= 0) & (row < chunk))
        def _():
            col = cols_ref[slot] - first
            source = wide[:, pl.ds(pl.multiple_of(col * BLK, BLK), BLK)]
            into = pl.ds(pl.multiple_of(row * BLK, BLK), BLK)
            agg[:, into] += lax.dot_general(
                source,
                values_ref[slot],
                (((1,), (1,)), ((), ())),
                preferred_element_type=jnp.float32,
            )

        return carry

    lax.fori_loop(0, count, gather_slot, 0)

    for at, size in tiles_of(width, 256):
        part = slice(at, at + size)
        stacked[:depth, part] = wide[:, rim + at : rim + at + size]
        stacked[depth:, part] = agg[:, part].astype(jnp.bfloat16)
        preact = jnp.dot(w_in_ref[...], stacked[:, part], preferred_element_type=jnp.float32)
        sigma = 1.0 / (1.0 + jnp.exp(-preact))
        slope = sigma * (1.0 + preact * (1.0 - sigma))
        delta[:, part] = (cot_ref[:, part].astype(jnp.float32) * slope).astype(jnp.bfloat16)
        both = jnp.dot(w_out_ref[...], delta[:, part], preferred_element_type=jnp.float32)
        both = both.astype(jnp.bfloat16)
        scat[:, rim + at : rim + at + size] = both[:depth].astype(jnp.float32)
        agg_grad[:, part] = both[depth:]

    def scatter_slot(slot, carry):
        row = rows_ref[slot] - first

        @pl.when((row >= 0) & (row < chunk))
        def _():
            col = cols_ref[slot] - first
            source = agg_grad[:, pl.ds(pl.multiple_of(row * BLK, BLK), BLK)]
            into = pl.ds(pl.multiple_of(col * BLK, BLK), BLK)
            scat[:, into] += jnp.dot(
                source, values_ref[slot], preferred_element_type=jnp.float32
            )

        return carry

    lax.fori_loop(0, count, scatter_slot, 0)
    left_ref[...] = scat[:, :rim].astype(jnp.bfloat16)
    right_ref[...] = scat[:, rim + width :].astype(jnp.bfloat16)
    middle_ref[...] = scat[:, rim : rim + width]
    terms_ref[...] = lax.dot_general(
        stacked[...], delta[...], (((1,), (1,)), ((), ())), preferred_element_type=jnp.float32
    )


def local_step(rows, cols, count, pos, own, before, after, values, w_in, w_out, cot):
    depth, width = own.shape
    rim = before.shape[1]
    smem = pl.BlockSpec(memory_space=pltpu.SMEM)
    vmem = pl.BlockSpec(memory_space=pltpu.VMEM)
    anywhere = pl.BlockSpec(memory_space=pl.ANY)
    return pl.pallas_call(
        local_kernel,
        out_shape=(
            jax.ShapeDtypeStruct((depth, width), jnp.float32),
            jax.ShapeDtypeStruct((depth, rim), jnp.bfloat16),
            jax.ShapeDtypeStruct((depth, rim), jnp.bfloat16),
            jax.ShapeDtypeStruct((2 * depth, depth), jnp.float32),
        ),
        in_specs=[smem] * 4 + [anywhere] * 3 + [vmem] * 4,
        out_specs=(vmem,) * 4,
        scratch_shapes=[
            pltpu.VMEM((depth, width + 2 * rim), jnp.bfloat16),
            pltpu.VMEM((depth, width), jnp.float32),
            pltpu.VMEM((2 * depth, width), jnp.bfloat16),
            pltpu.VMEM((depth, width), jnp.bfloat16),
            pltpu.VMEM((depth, width), jnp.bfloat16),
            pltpu.VMEM((depth, width + 2 * rim), jnp.float32),
            pltpu.SemaphoreType.DMA((3,)),
        ],
        compiler_params=pltpu.CompilerParams(vmem_limit_bytes=48 * 1024 * 1024),
        cost_estimate=pl.CostEstimate(
            flops=12 * depth * depth * width, bytes_accessed=8 << 20, transcendentals=depth * width
        ),
    )(rows, cols, count, pos, own, before, after, values, w_in, w_out, cot)


def on_device(
    features, block_row, block_col, block_count, block_values, w_self, w_neigh, cotangent
):
    rows_part = features.shape[1]
    depth, width = cotangent.shape
    rim = REACH * BLK
    own = lax.all_to_all(features, "feat", split_axis=1, concat_axis=0, tiled=True)
    before = shifted(own[:, width - rim :], RING, 1)
    after = shifted(own[:, :rim], RING, -1)
    w_in = jnp.concatenate([w_self.T, w_neigh.T], axis=1)
    w_out = jnp.concatenate([w_self, w_neigh], axis=0)
    pos = lax.axis_index("feat").astype(jnp.int32)[None]
    middle, left, right, terms = local_step(
        block_row[0],
        block_col[0],
        block_count,
        pos,
        own,
        before,
        after,
        block_values,
        w_in,
        w_out,
        cotangent,
    )
    from_next = shifted(left, RING, -1).astype(jnp.float32)
    from_prev = shifted(right, RING, 1).astype(jnp.float32)
    total = middle + jnp.pad(from_prev, ((0, 0), (0, width - rim)))
    total = total + jnp.pad(from_next, ((0, 0), (width - rim, 0)))
    total = total.astype(jnp.bfloat16)
    feature_grad = lax.all_to_all(total, "feat", split_axis=0, concat_axis=1, tiled=True)

    plane, line = lax.axis_size(PLANE), lax.axis_size(LINE)
    share = 2 * depth // plane
    pieces = lax.all_to_all(terms, PLANE, split_axis=0, concat_axis=0, tiled=True)
    partial = pieces.reshape(plane, share, depth).sum(0)
    copies = jnp.broadcast_to(partial[None], (line, share, depth))
    copies = lax.all_to_all(copies, LINE, split_axis=0, concat_axis=0, tiled=True)
    factor = 1.0 / math.sqrt(rows_part * lax.axis_size(DOM))
    grads = (copies.sum(0) * factor).astype(jnp.bfloat16)
    grads = jnp.broadcast_to(grads[None], (plane, share, depth))
    grads = lax.all_to_all(grads, PLANE, split_axis=0, concat_axis=0, tiled=True)
    grads = grads.reshape(2 * depth, depth)
    return (feature_grad, grads[:depth], grads[depth:])


def solution(mesh):
    fine = Mesh(mesh.devices.reshape(2, 4, 4, 2, 8), RING)
    return jax.shard_map(
        on_device,
        mesh=fine,
        in_specs=(
            P("feat", DOM),
            P(DOM, None),
            P(DOM, None),
            P(DOM),
            P(DOM, None, None),
            P(),
            P(),
            P(None, RING),
        ),
        out_specs=(P("feat", DOM), P(), P()),
        check_vma=False,
    )
```

time: 707 us -> 217 us (0.31)
  the two profiles are of different devices: /device:TPU:31 before, /device:TPU:6 now
where the time goes in v1:
time: 217 us; the launch traced here: 216 us
  waiting for transfers between devices  79.4 us (37%)
  blocking collectives  75.4 us (35%)
  starting transfers between devices  44.9 us (21%)
  local copies, waits for them, and re-layouts  6.5 us (3%)
  Pallas kernels  6.36 us (3%)
  other arithmetic  2.4 us (1%)
    all_to_all x1, blocking collectives, on_device(): lax.all_to_all(features, 'feat', split_axis=1, concat_axis=0, tiled=True)  55.2 us
    all_to_all x1, waiting for transfers between devices, on_device(): lax.all_to_all(total, 'feat', split_axis=0, concat_axis=1, tiled=True)  42.8 us
    ppermute x4, waiting for transfers between devices, shifted(): lax.ppermute(shard, axis, [(i, (i + by) % count) for i in range(count)])  30.3 us
    all_to_all x1, blocking collectives, on_device(): lax.all_to_all(terms, PLANE, split_axis=0, concat_axis=0, tiled=True)  20.2 us
    ppermute x4, starting transfers between devices, shifted(): lax.ppermute(shard, axis, [(i, (i + by) % count) for i in range(count)])  19.4 us
    all_to_all x1, starting transfers between devices, on_device(): lax.all_to_all(copies, LINE, split_axis=0, concat_axis=0, tiled=True)  9.05 us
    all_to_all x1, starting transfers between devices, on_device(): lax.all_to_all(total, 'feat', split_axis=0, concat_axis=1, tiled=True)  8.54 us
    all_to_all x1, starting transfers between devices, on_device(): lax.all_to_all(grads, PLANE, split_axis=0, concat_axis=0, tiled=True)  7.92 us
  transfers between devices with their start and end apart: 7, of which 6 were waited for; matrix products, arithmetic and copies ran while one was open for 2% of the time, Pallas kernels for 0%

profile of v1, /device:TPU:6, one launch (start us, length us, event | category | flops | bytes accessed | tf_op | source)
XLA Modules:
  0.0 216.4 jit_solution(15905124145226411532)
XLA Ops:
  0.6 1.2 copy.22
  1.9 0.0 copy-start.7
  1.9 0.0 copy-start.6
  1.9 55.2 %all_to_all.57 = bf16[32,8,1664]{2,0,1:T(8,128)(2,1)S(1)} all-to-all(bf16[32,8,1664]{2,0,1:T(8,128)(2,1)S(1)} %bitcast.25), channel_id=1, replica_groups=mesh['zh'=2,'y'=4,'x'=4,'core'=2,'feat'=8] {'feat'}, dimensions={1} | all-to-all | bytes 1703936 | tf_op jit(solution)/shard_map/all_to_all | solution.py:163
  57.1 1.1 fusion
  58.2 4.5 %collective-permute-start.1 = (bf16[256,1024]{1,0:T(8,128)(2,1)}, bf16[256,1024]{1,0:T(8,128)(2,1)S(1)}, u32[]{:S(2)}, u32[]{:S(2)}) collective-permute-start(bf16[256,1024]{1,0:T(8,128)(2,1)} %get-tuple-element.11), channel_id=1, source_target_pairs={{0,511},{1,0},{2,1},{3,2},{4,3},{5,4},{6,5},{7,6},{8,7},{9,8},{10,... | collective-permute-start | bytes 1572872 | tf_op jit(solution)/shard_map/ppermute | solution.py:21
  62.7 1.9 collective-permute-start
  65.3 0.0 copy-done.7
  65.3 0.1 copy.16
  65.4 0.0 copy-done.6
  65.4 0.1 copy.17
  65.5 9.8 %collective-permute-done.1.after_ref = bf16[256,1024]{1,0:T(8,128)(2,1)S(1)} collective-permute-done((bf16[256,1024]{1,0:T(8,128)(2,1)}, bf16[256,1024]{1,0:T(8,128)(2,1)S(1)}, u32[]{:S(2)}, u32[]{:S(2)}) %collective-permute-start.1) | collective-permute-done | bytes 524320 | tf_op jit(solution)/shard_map/ppermute | solution.py:21
  75.3 11.2 %collective-permute-done.before_ref = bf16[256,1024]{1,0:T(8,128)(2,1)S(1)} collective-permute-done((bf16[256,1024]{1,0:T(8,128)(2,1)}, bf16[256,1024]{1,0:T(8,128)(2,1)S(1)}, u32[]{:S(2)}, u32[]{:S(2)}) %collective-permute-start) | collective-permute-done | bytes 524320 | tf_op jit(solution)/shard_map/ppermute | solution.py:21
  86.6 6.4 %shard_map.103 = (f32[256,1664]{1,0:T(8,128)}, bf16[256,1024]{1,0:T(8,128)(2,1)S(1)}, bf16[256,1024]{1,0:T(8,128)(2,1)S(1)}, f32[512,256]{1,0:T(8,128)S(1)}) custom-call(s32[64]{0:T(128)S(1)} %bitcast.22, s32[64]{0:T(128)S(1)} %bitcast.23, s32[1]{0:T(128)S(6)} %copy.23.count_ref, s32[1]{0:T(128)} %bitcast.2.pos_ref, bf16[256,1664]{1,0:T(8,128)(2,1)S(1)} %bitcast.20, ...), custom_call_target="tpu_custom_call" | custom-call | flops 1308622848 | bytes 8388608 | tf_op jit(solution)/shard_map/pallas_call | solution.py:131
  93.0 0.0 copy-start.3
  93.0 0.8 copy-done.3
  93.8 20.2 %all_to_all.58 = f32[32,16,256]{2,1,0:T(8,128)S(1)} all-to-all(f32[32,16,256]{2,1,0:T(8,128)S(1)} %bitcast.21), channel_id=1, replica_groups=mesh['zh'=2,'y'=4,'x'=4,'core'=2,'feat'=8] {'y','x','core'}, dimensions={0} | all-to-all | bytes 1048576 | tf_op jit(solution)/shard_map/all_to_all | solution.py:191
  114.0 0.7 broadcast_in_dim.7
  114.7 9.0 %all-to-all-start.3 = ((f32[16,16,256]{2,1,0:T(8,128)}), f32[16,16,256]{2,1,0:T(8,128)S(1)}, u32[]{:S(2)}, u32[]{:S(2)}) async-start(f32[16,16,256]{2,1,0:T(8,128)} %broadcast_in_dim.7), calls=%async_computation.3 | async-start | bytes 524288 | tf_op jit(solution)/shard_map/all_to_all | solution.py:194
  123.8 3.8 %collective-permute-start.2 = (bf16[256,1024]{1,0:T(8,128)(2,1)S(1)}, bf16[256,1024]{1,0:T(8,128)(2,1)}, u32[]{:S(2)}, u32[]{:S(2)}) collective-permute-start(bf16[256,1024]{1,0:T(8,128)(2,1)S(1)} %copy-done.4), channel_id=1, source_target_pairs={{0,1},{1,2},{2,3},{3,4},{4,5},{5,6},{6,7},{7,8},{8,9},{9,10},{10,1... | collective-permute-start | bytes 1572872 | tf_op jit(solution)/shard_map/ppermute | solution.py:21
  127.6 9.2 %collective-permute-start.3 = (bf16[256,1024]{1,0:T(8,128)(2,1)S(1)}, bf16[256,1024]{1,0:T(8,128)(2,1)}, u32[]{:S(2)}, u32[]{:S(2)}) collective-permute-start(bf16[256,1024]{1,0:T(8,128)(2,1)S(1)} %get-tuple-element.9), channel_id=1, source_target_pairs={{0,511},{1,0},{2,1},{3,2},{4,3},{5,4},{6,5},{7,6},{8,7},{9,8},{10,... | collective-permute-start | bytes 1572872 | tf_op jit(solution)/shard_map/ppermute | solution.py:21
  136.9 6.3 %all-to-all-done.3 = f32[16,16,256]{2,1,0:T(8,128)S(1)} async-done(((f32[16,16,256]{2,1,0:T(8,128)}), f32[16,16,256]{2,1,0:T(8,128)S(1)}, u32[]{:S(2)}, u32[]{:S(2)}) %all-to-all-start.3) | async-done | bytes 262176 | tf_op jit(solution)/shard_map/all_to_all | solution.py:194
  143.2 0.7 broadcast_in_dim.8
  143.9 7.9 %all-to-all-start.4 = ((bf16[32,16,256]{2,1,0:T(8,128)(2,1)}), bf16[32,16,256]{2,1,0:T(8,128)(2,1)S(1)}, u32[]{:S(2)}, u32[]{:S(2)}) async-start(bf16[32,16,256]{2,1,0:T(8,128)(2,1)} %broadcast_in_dim.8), calls=%async_computation.4 | async-start | bytes 524288 | tf_op jit(solution)/shard_map/all_to_all | solution.py:198
  151.9 3.6 %collective-permute-done.2 = bf16[256,1024]{1,0:T(8,128)(2,1)} collective-permute-done((bf16[256,1024]{1,0:T(8,128)(2,1)S(1)}, bf16[256,1024]{1,0:T(8,128)(2,1)}, u32[]{:S(2)}, u32[]{:S(2)}) %collective-permute-start.2) | collective-permute-done | bytes 524320 | tf_op jit(solution)/shard_map/ppermute | solution.py:21
  155.4 5.7 %collective-permute-done.3 = bf16[256,1024]{1,0:T(8,128)(2,1)} collective-permute-done((bf16[256,1024]{1,0:T(8,128)(2,1)S(1)}, bf16[256,1024]{1,0:T(8,128)(2,1)}, u32[]{:S(2)}, u32[]{:S(2)}) %collective-permute-start.3) | collective-permute-done | bytes 524320 | tf_op jit(solution)/shard_map/ppermute | solution.py:21
  161.1 2.3 %add_convert_fusion = bf16[256,1664]{1,0:T(8,128)(2,1)} fusion(f32[256,1664]{1,0:T(8,128)S(1)} %copy-done.5, bf16[256,1024]{1,0:T(8,128)(2,1)} %collective-permute-done.3, bf16[256,1024]{1,0:T(8,128)(2,1)} %collective-permute-done.2), kind=kLoop, calls=%fused_computation | loop fusion | flops 2129920 | bytes 3604480 | tf_op jit(solution)/shard_map/convert_element_type | solution.py:186
  163.4 0.0 all-to-all-done.4
  163.4 8.5 %all-to-all-start.1 = ((bf16[8,32,1664]{2,1,0:T(8,128)(2,1)}), bf16[8,32,1664]{2,1,0:T(8,128)(2,1)S(1)}, u32[]{:S(2)}, u32[]{:S(2)}) async-start(bf16[8,32,1664]{2,1,0:T(8,128)(2,1)} %bitcast.8), calls=%async_computation.1 | async-start | bytes 1703936 | tf_op jit(solution)/shard_map/all_to_all | solution.py:187
  171.9 0.7 fusion.1
  172.6 42.8 %all-to-all-done.1 = bf16[8,32,1664]{2,1,0:T(8,128)(2,1)S(1)} async-done(((bf16[8,32,1664]{2,1,0:T(8,128)(2,1)}), bf16[8,32,1664]{2,1,0:T(8,128)(2,1)S(1)}, u32[]{:S(2)}, u32[]{:S(2)}) %all-to-all-start.1) | async-done | bytes 852000 | tf_op jit(solution)/shard_map/all_to_all | solution.py:187
  215.5 1.0 copy.20
  (15 shorter events, 0.1 us)
Async XLA Ops:
  1.9 63.4 %copy-start.7 = (bf16[256,256]{1,0:T(8,128)(2,1)S(1)}, bf16[256,256]{1,0:T(8,128)(2,1)}, u32[]{:S(2)}) copy-start(bf16[256,256]{1,0:T(8,128)(2,1)} %param.13) | copy-start | bytes 393220
  1.9 63.5 %copy-start.6 = (bf16[256,256]{1,0:T(8,128)(2,1)S(1)}, bf16[256,256]{1,0:T(8,128)(2,1)}, u32[]{:S(2)}) copy-start(bf16[256,256]{1,0:T(8,128)(2,1)} %param.14) | copy-start | bytes 393220
  57.1 29.5 %copy-start = (bf16[256,1664]{1,0:T(8,128)(2,1)S(1)}, bf16[256,1664]{1,0:T(8,128)(2,1)}, u32[]{:S(2)}) copy-start(bf16[256,1664]{1,0:T(8,128)(2,1)} %cot_ref.1) | copy-start | bytes 2555908
  57.1 29.5 %copy-start.1 = (s32[1,64]{1,0:T(1,128)S(1)}, s32[1,64]{1,0:T(1,128)}, u32[]{:S(2)}) copy-start(s32[1,64]{1,0:T(1,128)} %param.9) | copy-start | bytes 772
  57.1 29.5 %copy-start.2 = (s32[1,64]{1,0:T(1,128)S(1)}, s32[1,64]{1,0:T(1,128)}, u32[]{:S(2)}) copy-start(s32[1,64]{1,0:T(1,128)} %param.10) | copy-start | bytes 772
  58.2 17.1 %collective-permute-start.1 = (bf16[256,1024]{1,0:T(8,128)(2,1)}, bf16[256,1024]{1,0:T(8,128)(2,1)S(1)}, u32[]{:S(2)}, u32[]{:S(2)}) collective-permute-start(bf16[256,1024]{1,0:T(8,128)(2,1)} %get-tuple-element.11), channel_id=1, source_target_pairs={{0,511},{1,0},{2,1},{3,2},{4,3},{5,4},{6,5},{7,6},{8,7},{9,8},{10,... | collective-permute-start | bytes 1572872 | tf_op jit(solution)/shard_map/ppermute | solution.py:21
  62.7 23.9 %collective-permute-start = (bf16[256,1024]{1,0:T(8,128)(2,1)}, bf16[256,1024]{1,0:T(8,128)(2,1)S(1)}, u32[]{:S(2)}, u32[]{:S(2)}) collective-permute-start(bf16[256,1024]{1,0:T(8,128)(2,1)} %get-tuple-element.12), channel_id=1, source_target_pairs={{0,1},{1,2},{2,3},{3,4},{4,5},{5,6},{6,7},{7,8},{8,9},{9,10},{10,1... | collective-permute-start | bytes 1572872 | tf_op jit(solution)/shard_map/ppermute | solution.py:21
  93.0 0.8 copy-start.3
  93.8 30.0 %copy-start.4 = (bf16[256,1024]{1,0:T(8,128)(2,1)S(1)}, bf16[256,1024]{1,0:T(8,128)(2,1)}, u32[]{:S(2)}) copy-start(bf16[256,1024]{1,0:T(8,128)(2,1)} %copy-done.3) | copy-start | bytes 1572868
  93.8 67.3 %copy-start.5 = (f32[256,1664]{1,0:T(8,128)S(1)}, f32[256,1664]{1,0:T(8,128)}, u32[]{:S(2)}) copy-start(f32[256,1664]{1,0:T(8,128)} %get-tuple-element.7) | copy-start | bytes 5111812
  114.7 28.4 %all-to-all-start.3 = ((f32[16,16,256]{2,1,0:T(8,128)}), f32[16,16,256]{2,1,0:T(8,128)S(1)}, u32[]{:S(2)}, u32[]{:S(2)}) async-start(f32[16,16,256]{2,1,0:T(8,128)} %broadcast_in_dim.7), calls=%async_computation.3 | async-start | bytes 524288 | tf_op jit(solution)/shard_map/all_to_all | solution.py:194
  123.8 31.6 %collective-permute-start.2 = (bf16[256,1024]{1,0:T(8,128)(2,1)S(1)}, bf16[256,1024]{1,0:T(8,128)(2,1)}, u32[]{:S(2)}, u32[]{:S(2)}) collective-permute-start(bf16[256,1024]{1,0:T(8,128)(2,1)S(1)} %copy-done.4), channel_id=1, source_target_pairs={{0,1},{1,2},{2,3},{3,4},{4,5},{5,6},{6,7},{7,8},{8,9},{9,10},{10,1... | collective-permute-start | bytes 1572872 | tf_op jit(solution)/shard_map/ppermute | solution.py:21
  127.6 33.5 %collective-permute-start.3 = (bf16[256,1024]{1,0:T(8,128)(2,1)S(1)}, bf16[256,1024]{1,0:T(8,128)(2,1)}, u32[]{:S(2)}, u32[]{:S(2)}) collective-permute-start(bf16[256,1024]{1,0:T(8,128)(2,1)S(1)} %get-tuple-element.9), channel_id=1, source_target_pairs={{0,511},{1,0},{2,1},{3,2},{4,3},{5,4},{6,5},{7,6},{8,7},{9,8},{10,... | collective-permute-start | bytes 1572872 | tf_op jit(solution)/shard_map/ppermute | solution.py:21
  143.9 19.5 %all-to-all-start.4 = ((bf16[32,16,256]{2,1,0:T(8,128)(2,1)}), bf16[32,16,256]{2,1,0:T(8,128)(2,1)S(1)}, u32[]{:S(2)}, u32[]{:S(2)}) async-start(bf16[32,16,256]{2,1,0:T(8,128)(2,1)} %broadcast_in_dim.8), calls=%async_computation.4 | async-start | bytes 524288 | tf_op jit(solution)/shard_map/all_to_all | solution.py:198
  163.4 52.1 %all-to-all-start.1 = ((bf16[8,32,1664]{2,1,0:T(8,128)(2,1)}), bf16[8,32,1664]{2,1,0:T(8,128)(2,1)S(1)}, u32[]{:S(2)}, u32[]{:S(2)}) async-start(bf16[8,32,1664]{2,1,0:T(8,128)(2,1)} %bitcast.8), calls=%async_computation.1 | async-start | bytes 1703936 | tf_op jit(solution)/shard_map/all_to_all | solution.py:187

commit v2 on v1

--- a/solution.py
+++ b/solution.py
@@ -14,6 +14,8 @@
 PLANE = ("y", "x", "core")
 LINE = ("zh", "feat")
 RING = DOM + ("feat",)
+EARLY = (4, 2, 6, 1)
+LATE = (3, 5, 7)
 
 
 def shifted(shard, axis, by):
@@ -40,11 +42,10 @@
     middle_ref,
     left_ref,
     right_ref,
-    terms_ref,
+    stacked,
+    delta,
     wide,
     agg,
-    stacked,
-    delta,
     agg_grad,
     scat,
     sems,
@@ -117,9 +118,65 @@
     left_ref[...] = scat[:, :rim].astype(jnp.bfloat16)
     right_ref[...] = scat[:, rim + width :].astype(jnp.bfloat16)
     middle_ref[...] = scat[:, rim : rim + width]
-    terms_ref[...] = lax.dot_general(
-        stacked[...], delta[...], (((1,), (1,)), ((), ())), preferred_element_type=jnp.float32
-    )
+
+
+def send_kernel(pos_ref, middle_ref, prev_ref, next_ref, *piece_refs):
+    pieces = len(piece_refs)
+    height, width = piece_refs[0].shape
+    rim = prev_ref.shape[1]
+    for step, piece_ref in enumerate(piece_refs):
+        dest = lax.rem(pos_ref[0] + step, pieces)
+        rows = pl.ds(pl.multiple_of(dest * height, height), height)
+        for at, size in ((0, width - rim), (width - rim, 2 * rim - width), (rim, width - rim)):
+            part = middle_ref[rows, at : at + size]
+            if at < rim:
+                part = part + prev_ref[rows, at : at + size].astype(jnp.float32)
+            if at >= width - rim:
+                here = at - (width - rim)
+                part = part + next_ref[rows, here : here + size].astype(jnp.float32)
+            piece_ref[:, at : at + size] = part.astype(jnp.bfloat16)
+
+
+def send_step(pos, middle, prev_part, next_part, pieces):
+    depth, width = middle.shape
+    vmem = pl.BlockSpec(memory_space=pltpu.VMEM)
+    return pl.pallas_call(
+        send_kernel,
+        out_shape=(jax.ShapeDtypeStruct((depth // pieces, width), jnp.bfloat16),) * pieces,
+        in_specs=[pl.BlockSpec(memory_space=pltpu.SMEM)] + [vmem] * 3,
+        out_specs=(vmem,) * pieces,
+        compiler_params=pltpu.CompilerParams(vmem_limit_bytes=32 * 1024 * 1024),
+        cost_estimate=pl.CostEstimate(flops=0, bytes_accessed=4 << 20, transcendentals=0),
+    )(pos, middle, prev_part, next_part)
+
+
+def place_kernel(pos_ref, *refs):
+    piece_refs, out_ref, sems = refs[:-2], refs[-2], refs[-1]
+    pieces = len(piece_refs)
+    width = piece_refs[0].shape[1]
+    copies = []
+    for step, piece_ref in enumerate(piece_refs):
+        source = lax.rem(pos_ref[0] + pieces - step, pieces)
+        into = pl.ds(pl.multiple_of(source * width, BLK), width)
+        copies.append(pltpu.make_async_copy(piece_ref, out_ref.at[:, into], sems.at[step]))
+    for copy in copies:
+        copy.start()
+    for copy in copies:
+        copy.wait()
+
+
+def place_step(pos, received):
+    pieces = len(received)
+    height, width = received[0].shape
+    anywhere = pl.BlockSpec(memory_space=pl.ANY)
+    return pl.pallas_call(
+        place_kernel,
+        out_shape=jax.ShapeDtypeStruct((height, pieces * width), jnp.bfloat16),
+        in_specs=[pl.BlockSpec(memory_space=pltpu.SMEM)] + [anywhere] * pieces,
+        out_specs=anywhere,
+        scratch_shapes=[pltpu.SemaphoreType.DMA((pieces,))],
+        cost_estimate=pl.CostEstimate(flops=0, bytes_accessed=2 << 20, transcendentals=0),
+    )(pos, *received)
 
 
 def local_step(rows, cols, count, pos, own, before, after, values, w_in, w_out, cot):
@@ -134,15 +191,14 @@
             jax.ShapeDtypeStruct((depth, width), jnp.float32),
             jax.ShapeDtypeStruct((depth, rim), jnp.bfloat16),
             jax.ShapeDtypeStruct((depth, rim), jnp.bfloat16),
-            jax.ShapeDtypeStruct((2 * depth, depth), jnp.float32),
+            jax.ShapeDtypeStruct((2 * depth, width), jnp.bfloat16),
+            jax.ShapeDtypeStruct((depth, width), jnp.bfloat16),
         ),
         in_specs=[smem] * 4 + [anywhere] * 3 + [vmem] * 4,
-        out_specs=(vmem,) * 4,
+        out_specs=(vmem,) * 5,
         scratch_shapes=[
             pltpu.VMEM((depth, width + 2 * rim), jnp.bfloat16),
             pltpu.VMEM((depth, width), jnp.float32),
-            pltpu.VMEM((2 * depth, width), jnp.bfloat16),
-            pltpu.VMEM((depth, width), jnp.bfloat16),
             pltpu.VMEM((depth, width), jnp.bfloat16),
             pltpu.VMEM((depth, width + 2 * rim), jnp.float32),
             pltpu.SemaphoreType.DMA((3,)),
@@ -166,7 +222,7 @@
     w_in = jnp.concatenate([w_self.T, w_neigh.T], axis=1)
     w_out = jnp.concatenate([w_self, w_neigh], axis=0)
     pos = lax.axis_index("feat").astype(jnp.int32)[None]
-    middle, left, right, terms = local_step(
+    middle, left, right, stacked, delta = local_step(
         block_row[0],
         block_col[0],
         block_count,
@@ -179,24 +235,34 @@
         w_out,
         cotangent,
     )
-    from_next = shifted(left, RING, -1).astype(jnp.float32)
-    from_prev = shifted(right, RING, 1).astype(jnp.float32)
-    total = middle + jnp.pad(from_prev, ((0, 0), (0, width - rim)))
-    total = total + jnp.pad(from_next, ((0, 0), (width - rim, 0)))
-    total = total.astype(jnp.bfloat16)
-    feature_grad = lax.all_to_all(total, "feat", split_axis=0, concat_axis=1, tiled=True)
-
+    from_next = shifted(left, RING, -1)
+    from_prev = shifted(right, RING, 1)
+    pieces = lax.axis_size("feat")
+    to_send = list(send_step(pos, middle, from_prev, from_next, pieces))
+
+    terms = jnp.einsum("in,on->io", stacked, delta, preferred_element_type=jnp.float32)
     plane, line = lax.axis_size(PLANE), lax.axis_size(LINE)
     share = 2 * depth // plane
-    pieces = lax.all_to_all(terms, PLANE, split_axis=0, concat_axis=0, tiled=True)
-    partial = pieces.reshape(plane, share, depth).sum(0)
+    parts = lax.all_to_all(terms, PLANE, split_axis=0, concat_axis=0, tiled=True)
+    partial = parts.reshape(plane, share, depth).sum(0)
+    partial, to_send[0] = lax.optimization_barrier((partial, to_send[0]))
     copies = jnp.broadcast_to(partial[None], (line, share, depth))
     copies = lax.all_to_all(copies, LINE, split_axis=0, concat_axis=0, tiled=True)
     factor = 1.0 / math.sqrt(rows_part * lax.axis_size(DOM))
     grads = (copies.sum(0) * factor).astype(jnp.bfloat16)
+    received = {0: to_send[0]}
+    for step in EARLY:
+        received[step] = shifted(to_send[step], "feat", step)
+    steps = EARLY + LATE
+    held = [received[step] for step in EARLY] + [to_send[step] for step in LATE]
+    grads, *held = lax.optimization_barrier((grads, *held))
+    received.update(zip(steps, held))
+    for step in LATE:
+        received[step] = shifted(received[step], "feat", step)
     grads = jnp.broadcast_to(grads[None], (plane, share, depth))
     grads = lax.all_to_all(grads, PLANE, split_axis=0, concat_axis=0, tiled=True)
     grads = grads.reshape(2 * depth, depth)
+    feature_grad = place_step(pos, [received[step] for step in range(pieces)])
     return (feature_grad, grads[:depth], grads[depth:])
 
 

time: 217 us -> 235 us (1.083)
  waiting for transfers between devices: 79.4 us -> 40.6 us
  starting transfers between devices: 44.9 us -> 74.2 us
  Pallas kernels: 6.36 us -> 35.6 us
  blocking collectives: 75.4 us -> 72 us
    all_to_all x1 -> x0, waiting for transfers between devices: 42.8 us -> none  [on_device(): lax.all_to_all(total, 'feat', split_axis=0, concat_axis=1, tiled=True)]
    ppermute x4 -> x11, starting transfers between devices: 19.4 us -> 56.4 us  [shifted(): lax.ppermute(shard, axis, [(i, (i + by) % count) for i in range(count)])]
    pallas_call x0 -> x2, Pallas kernels: none -> 27.2 us  [the longest x1 27 us: place_step(): pl.pallas_call(place_kernel, out_shape=jax.ShapeDtypeStruct((height, piec...]
    ppermute x4 -> x11, waiting for transfers between devices: 30.3 us -> 40.6 us  [shifted(): lax.ppermute(shard, axis, [(i, (i + by) % count) for i in range(count)])]
    all_to_all x1 -> x0, starting transfers between devices: 8.54 us -> none  [on_device(): lax.all_to_all(total, 'feat', split_axis=0, concat_axis=1, tiled=True)]
    all_to_all x1, waiting for transfers between devices: 6.29 us -> 0.01 us  [on_device(): lax.all_to_all(copies, LINE, split_axis=0, concat_axis=0, tiled=True)]
    all_to_all x1, blocking collectives: 20.2 us -> 16.8 us  [on_device(): lax.all_to_all(terms, PLANE, split_axis=0, concat_axis=0, tiled=True)]
  transfers between devices with their start and end apart: 7 -> 13, of which waited for: 6 -> 5; matrix products, arithmetic and copies ran while one was open for 2% -> 2% of each run, Pallas kernels for 0% -> 12%
where the time goes in v2:
time: 235 us; the launch traced here: 234 us
  starting transfers between devices  74.2 us (32%)
  blocking collectives  72 us (31%)
  waiting for transfers between devices  40.6 us (17%)
  Pallas kernels  35.6 us (15%)
  local copies, waits for them, and re-layouts  6.11 us (3%)
    ppermute x11, starting transfers between devices, shifted(): lax.ppermute(shard, axis, [(i, (i + by) % count) for i in range(count)])  56.4 us
    all_to_all x1, blocking collectives, on_device(): lax.all_to_all(features, 'feat', split_axis=1, concat_axis=0, tiled=True)  55.2 us
    ppermute x11, waiting for transfers between devices, shifted(): lax.ppermute(shard, axis, [(i, (i + by) % count) for i in range(count)])  40.6 us
    pallas_call x1, Pallas kernels, place_step(): pl.pallas_call(place_kernel, out_shape=jax.ShapeDtypeStruct((height, piec...  27 us
    all_to_all x1, blocking collectives, on_device(): lax.all_to_all(terms, PLANE, split_axis=0, concat_axis=0, tiled=True)  16.8 us
    all_to_all x1, starting transfers between devices, on_device(): lax.all_to_all(copies, LINE, split_axis=0, concat_axis=0, tiled=True)  11 us
    pallas_call x1, Pallas kernels, local_step(): pl.pallas_call(local_kernel, out_shape=(jax.ShapeDtypeStruct((depth, widt...  8.4 us
    all_to_all x1, starting transfers between devices, on_device(): lax.all_to_all(grads, PLANE, split_axis=0, concat_axis=0, tiled=True)  6.8 us
  transfers between devices with their start and end apart: 13, of which 5 were waited for; matrix products, arithmetic and copies ran while one was open for 2% of the time, Pallas kernels for 12%

profile of v2, /device:TPU:6, one launch (start us, length us, event | category | flops | bytes accessed | tf_op | source)
XLA Modules:
  0.0 233.5 jit_solution(8490276180610679529)
XLA Ops:
  0.6 1.2 copy.19
  1.9 55.2 %all_to_all.38 = bf16[32,8,1664]{2,0,1:T(8,128)(2,1)S(1)} all-to-all(bf16[32,8,1664]{2,0,1:T(8,128)(2,1)S(1)} %bitcast.21), channel_id=1, replica_groups=mesh['zh'=2,'y'=4,'x'=4,'core'=2,'feat'=8] {'feat'}, dimensions={1} | all-to-all | bytes 1703936 | tf_op jit(solution)/shard_map/all_to_all | solution.py:219
  57.1 1.1 fusion
  58.2 4.5 %collective-permute-start.1 = (bf16[256,1024]{1,0:T(8,128)(2,1)}, bf16[256,1024]{1,0:T(8,128)(2,1)S(1)}, u32[]{:S(2)}, u32[]{:S(2)}) collective-permute-start(bf16[256,1024]{1,0:T(8,128)(2,1)} %get-tuple-element.49), channel_id=1, source_target_pairs={{0,511},{1,0},{2,1},{3,2},{4,3},{5,4},{6,5},{7,6},{8,7},{9,8},{10,... | collective-permute-start | bytes 1572872 | tf_op jit(solution)/shard_map/ppermute | solution.py:23
  62.7 1.9 collective-permute-start
  65.6 9.8 %collective-permute-done.1.after_ref = bf16[256,1024]{1,0:T(8,128)(2,1)S(1)} collective-permute-done((bf16[256,1024]{1,0:T(8,128)(2,1)}, bf16[256,1024]{1,0:T(8,128)(2,1)S(1)}, u32[]{:S(2)}, u32[]{:S(2)}) %collective-permute-start.1) | collective-permute-done | bytes 524320 | tf_op jit(solution)/shard_map/ppermute | solution.py:23
  75.4 11.2 %collective-permute-done.before_ref = bf16[256,1024]{1,0:T(8,128)(2,1)S(1)} collective-permute-done((bf16[256,1024]{1,0:T(8,128)(2,1)}, bf16[256,1024]{1,0:T(8,128)(2,1)S(1)}, u32[]{:S(2)}, u32[]{:S(2)}) %collective-permute-start) | collective-permute-done | bytes 524320 | tf_op jit(solution)/shard_map/ppermute | solution.py:23
  86.6 8.4 %shard_map.103 = (f32[256,1664]{1,0:T(8,128)}, bf16[256,1024]{1,0:T(8,128)(2,1)S(1)}, bf16[256,1024]{1,0:T(8,128)(2,1)}, bf16[512,1664]{1,0:T(8,128)(2,1)}, bf16[256,1664]{1,0:T(8,128)(2,1)S(1)}) custom-call(s32[64]{0:T(128)S(1)} %bitcast.19, s32[64]{0:T(128)S(1)} %bitcast.20, s32[1]{0:T(128)S(6)} %copy.20.count_ref, s32[1]{0:T(128)} %bitcast.pos_ref, ...), custom_call_target="tpu_custom_call" | custom-call | flops 1308622848 | bytes 8388608 | tf_op jit(solution)/shard_map/pallas_call | solution.py:188
  95.0 2.9 %collective-permute-start.2 = (bf16[256,1024]{1,0:T(8,128)(2,1)}, bf16[256,1024]{1,0:T(8,128)(2,1)S(1)}, u32[]{:S(2)}, u32[]{:S(2)}) collective-permute-start(bf16[256,1024]{1,0:T(8,128)(2,1)} %get-tuple-element.29), channel_id=1, source_target_pairs={{0,1},{1,2},{2,3},{3,4},{4,5},{5,6},{6,7},{7,8},{8,9},{9,10},{10,1... | collective-permute-start | bytes 1572872 | tf_op jit(solution)/shard_map/ppermute | solution.py:23
  98.0 10.1 %collective-permute-start.3 = (bf16[256,1024]{1,0:T(8,128)(2,1)S(1)}, bf16[256,1024]{1,0:T(8,128)(2,1)S(1)}, u32[]{:S(2)}, u32[]{:S(2)}) collective-permute-start(bf16[256,1024]{1,0:T(8,128)(2,1)S(1)} %get-tuple-element.30), channel_id=1, source_target_pairs={{0,511},{1,0},{2,1},{3,2},{4,3},{5,4},{6,5},{7,6},{8,7},{9,8},{10,... | collective-permute-start | bytes 1572872 | tf_op jit(solution)/shard_map/ppermute | solution.py:23
  108.1 2.3 fusion.2
  110.4 16.8 %all_to_all.39 = f32[32,16,256]{2,1,0:T(8,128)} all-to-all(f32[32,16,256]{2,1,0:T(8,128)S(1)} %bitcast.23), channel_id=1, replica_groups=mesh['zh'=2,'y'=4,'x'=4,'core'=2,'feat'=8] {'y','x','core'}, dimensions={0} | all-to-all | bytes 1048576 | tf_op jit(solution)/shard_map/all_to_all | solution.py:246
  127.2 1.1 reduce_sum.18
  128.3 0.2 shard_map.104
  128.5 0.6 copy-done.2
  129.1 0.7 broadcast_in_dim.7
  129.9 11.0 %all-to-all-start.2 = ((f32[16,16,256]{2,1,0:T(8,128)}), f32[16,16,256]{2,1,0:T(8,128)S(1)}, u32[]{:S(2)}, u32[]{:S(2)}) async-start(f32[16,16,256]{2,1,0:T(8,128)} %broadcast_in_dim.7), calls=%async_computation.2 | async-start | bytes 524288 | tf_op jit(solution)/shard_map/all_to_all | solution.py:250
  140.9 7.7 %collective-permute-start.4 = (bf16[32,1664]{1,0:T(8,128)(2,1)S(1)}, bf16[32,1664]{1,0:T(8,128)(2,1)S(1)}, u32[]{:S(2)}, u32[]{:S(2)}) collective-permute-start(bf16[32,1664]{1,0:T(8,128)(2,1)S(1)} %get-tuple-element.34), channel_id=1, source_target_pairs={{0,4},{1,5},{2,6},{3,7},{4,0},{5,1},{6,2},{7,3},{8,12},{9,13},{10,... | collective-permute-start | bytes 319496 | tf_op jit(solution)/shard_map/ppermute | solution.py:23
  148.6 4.3 %collective-permute-start.5 = (bf16[32,1664]{1,0:T(8,128)(2,1)S(1)}, bf16[32,1664]{1,0:T(8,128)(2,1)S(1)}, u32[]{:S(2)}, u32[]{:S(2)}) collective-permute-start(bf16[32,1664]{1,0:T(8,128)(2,1)S(1)} %get-tuple-element.35), channel_id=1, source_target_pairs={{0,2},{1,3},{2,4},{3,5},{4,6},{5,7},{6,0},{7,1},{8,10},{9,11},{10,... | collective-permute-start | bytes 319496 | tf_op jit(solution)/shard_map/ppermute | solution.py:23
  152.9 7.3 %collective-permute-start.6 = (bf16[32,1664]{1,0:T(8,128)(2,1)S(1)}, bf16[32,1664]{1,0:T(8,128)(2,1)S(1)}, u32[]{:S(2)}, u32[]{:S(2)}) collective-permute-start(bf16[32,1664]{1,0:T(8,128)(2,1)S(1)} %get-tuple-element.36), channel_id=1, source_target_pairs={{0,6},{1,7},{2,0},{3,1},{4,2},{5,3},{6,4},{7,5},{8,14},{9,15},{10,... | collective-permute-start | bytes 319496 | tf_op jit(solution)/shard_map/ppermute | solution.py:23
  160.2 3.4 %collective-permute-start.7 = (bf16[32,1664]{1,0:T(8,128)(2,1)S(1)}, bf16[32,1664]{1,0:T(8,128)(2,1)S(1)}, u32[]{:S(2)}, u32[]{:S(2)}) collective-permute-start(bf16[32,1664]{1,0:T(8,128)(2,1)S(1)} %get-tuple-element.37), channel_id=1, source_target_pairs={{0,1},{1,2},{2,3},{3,4},{4,5},{5,6},{6,7},{7,0},{8,9},{9,10},{10,1... | collective-permute-start | bytes 319496 | tf_op jit(solution)/shard_map/ppermute | solution.py:23
  163.6 13.1 %collective-permute-done.4.refs_4_ = bf16[32,1664]{1,0:T(8,128)(2,1)S(1)} collective-permute-done((bf16[32,1664]{1,0:T(8,128)(2,1)S(1)}, bf16[32,1664]{1,0:T(8,128)(2,1)S(1)}, u32[]{:S(2)}, u32[]{:S(2)}) %collective-permute-start.4) | collective-permute-done | bytes 106528 | tf_op jit(solution)/shard_map/ppermute | solution.py:23
  176.8 0.8 broadcast_in_dim.8
  177.6 6.8 %all-to-all-start.3 = ((bf16[32,16,256]{2,1,0:T(8,128)(2,1)}), bf16[32,16,256]{2,1,0:T(8,128)(2,1)S(1)}, u32[]{:S(2)}, u32[]{:S(2)}) async-start(bf16[32,16,256]{2,1,0:T(8,128)(2,1)} %broadcast_in_dim.8), calls=%async_computation.3 | async-start | bytes 524288 | tf_op jit(solution)/shard_map/all_to_all | solution.py:263
  184.4 3.0 %collective-permute-start.8 = (bf16[32,1664]{1,0:T(8,128)(2,1)S(1)}, bf16[32,1664]{1,0:T(8,128)(2,1)S(1)}, u32[]{:S(2)}, u32[]{:S(2)}) collective-permute-start(bf16[32,1664]{1,0:T(8,128)(2,1)S(1)} %get-tuple-element.43), channel_id=1, source_target_pairs={{0,3},{1,4},{2,5},{3,6},{4,7},{5,0},{6,1},{7,2},{8,11},{9,12},{10,... | collective-permute-start | bytes 319496 | tf_op jit(solution)/shard_map/ppermute | solution.py:23
  187.3 7.7 %collective-permute-start.9 = (bf16[32,1664]{1,0:T(8,128)(2,1)S(1)}, bf16[32,1664]{1,0:T(8,128)(2,1)S(1)}, u32[]{:S(2)}, u32[]{:S(2)}) collective-permute-start(bf16[32,1664]{1,0:T(8,128)(2,1)S(1)} %get-tuple-element.45), channel_id=1, source_target_pairs={{0,5},{1,6},{2,7},{3,0},{4,1},{5,2},{6,3},{7,4},{8,13},{9,14},{10,... | collective-permute-start | bytes 319496 | tf_op jit(solution)/shard_map/ppermute | solution.py:23
  195.0 3.6 %collective-permute-start.10 = (bf16[32,1664]{1,0:T(8,128)(2,1)S(1)}, bf16[32,1664]{1,0:T(8,128)(2,1)S(1)}, u32[]{:S(2)}, u32[]{:S(2)}) collective-permute-start(bf16[32,1664]{1,0:T(8,128)(2,1)S(1)} %get-tuple-element.47), channel_id=1, source_target_pairs={{0,7},{1,0},{2,1},{3,2},{4,3},{5,4},{6,5},{7,6},{8,15},{9,8},{10,9... | collective-permute-start | bytes 319496 | tf_op jit(solution)/shard_map/ppermute | solution.py:23
  198.7 5.7 %collective-permute-done.8.refs_3_ = bf16[32,1664]{1,0:T(8,128)(2,1)S(1)} collective-permute-done((bf16[32,1664]{1,0:T(8,128)(2,1)S(1)}, bf16[32,1664]{1,0:T(8,128)(2,1)S(1)}, u32[]{:S(2)}, u32[]{:S(2)}) %collective-permute-start.8) | collective-permute-done | bytes 106528 | tf_op jit(solution)/shard_map/ppermute | solution.py:23
  204.4 0.8 collective-permute-done.10.refs_7_
  205.2 0.6 copy-done.13
  205.8 27.0 %shard_map.105 = bf16[32,13312]{1,0:T(8,128)(2,1)} custom-call(s32[1]{0:T(128)} %bitcast.pos_ref, bf16[32,1664]{1,0:T(8,128)(2,1)} %copy-done.2, bf16[32,1664]{1,0:T(8,128)(2,1)} %copy-done.10, bf16[32,1664]{1,0:T(8,128)(2,1)} %copy-done.8, bf16[32,1664]{1,0:T(8,128)(2,1)} %copy-done.11, bf16[32,1664]{1,0:T(8,128)(2,1)} %copy-done.7, ...), custom_call_target="tpu_custom_call" | custom-call | bytes 2097152 | tf_op jit(solution)/shard_map/pallas_call | solution.py:172
  232.8 0.7 fusion.1
  (40 shorter events, 0.3 us)
Async XLA Ops:
  1.9 63.4 %copy-start.6 = (bf16[256,256]{1,0:T(8,128)(2,1)S(1)}, bf16[256,256]{1,0:T(8,128)(2,1)}, u32[]{:S(2)}) copy-start(bf16[256,256]{1,0:T(8,128)(2,1)} %param.13) | copy-start | bytes 393220
  1.9 63.5 %copy-start.5 = (bf16[256,256]{1,0:T(8,128)(2,1)S(1)}, bf16[256,256]{1,0:T(8,128)(2,1)}, u32[]{:S(2)}) copy-start(bf16[256,256]{1,0:T(8,128)(2,1)} %param.14) | copy-start | bytes 393220
  57.1 29.5 %copy-start.1 = (bf16[256,1664]{1,0:T(8,128)(2,1)S(1)}, bf16[256,1664]{1,0:T(8,128)(2,1)}, u32[]{:S(2)}) copy-start(bf16[256,1664]{1,0:T(8,128)(2,1)} %cot_ref.1) | copy-start | bytes 2555908
  57.1 29.5 %copy-start.3 = (s32[1,64]{1,0:T(1,128)S(1)}, s32[1,64]{1,0:T(1,128)}, u32[]{:S(2)}) copy-start(s32[1,64]{1,0:T(1,128)} %param.9) | copy-start | bytes 772
  57.1 29.5 %copy-start.4 = (s32[1,64]{1,0:T(1,128)S(1)}, s32[1,64]{1,0:T(1,128)}, u32[]{:S(2)}) copy-start(s32[1,64]{1,0:T(1,128)} %param.10) | copy-start | bytes 772
  58.2 17.1 %collective-permute-start.1 = (bf16[256,1024]{1,0:T(8,128)(2,1)}, bf16[256,1024]{1,0:T(8,128)(2,1)S(1)}, u32[]{:S(2)}, u32[]{:S(2)}) collective-permute-start(bf16[256,1024]{1,0:T(8,128)(2,1)} %get-tuple-element.49), channel_id=1, source_target_pairs={{0,511},{1,0},{2,1},{3,2},{4,3},{5,4},{6,5},{7,6},{8,7},{9,8},{10,... | collective-permute-start | bytes 1572872 | tf_op jit(solution)/shard_map/ppermute | solution.py:23
  62.7 23.9 %collective-permute-start = (bf16[256,1024]{1,0:T(8,128)(2,1)}, bf16[256,1024]{1,0:T(8,128)(2,1)S(1)}, u32[]{:S(2)}, u32[]{:S(2)}) collective-permute-start(bf16[256,1024]{1,0:T(8,128)(2,1)} %get-tuple-element.50), channel_id=1, source_target_pairs={{0,1},{1,2},{2,3},{3,4},{4,5},{5,6},{6,7},{7,8},{8,9},{9,10},{10,1... | collective-permute-start | bytes 1572872 | tf_op jit(solution)/shard_map/ppermute | solution.py:23
  95.0 33.3 %collective-permute-start.2 = (bf16[256,1024]{1,0:T(8,128)(2,1)}, bf16[256,1024]{1,0:T(8,128)(2,1)S(1)}, u32[]{:S(2)}, u32[]{:S(2)}) collective-permute-start(bf16[256,1024]{1,0:T(8,128)(2,1)} %get-tuple-element.29), channel_id=1, source_target_pairs={{0,1},{1,2},{2,3},{3,4},{4,5},{5,6},{6,7},{7,8},{8,9},{9,10},{10,1... | collective-permute-start | bytes 1572872 | tf_op jit(solution)/shard_map/ppermute | solution.py:23
  98.0 30.3 %collective-permute-start.3 = (bf16[256,1024]{1,0:T(8,128)(2,1)S(1)}, bf16[256,1024]{1,0:T(8,128)(2,1)S(1)}, u32[]{:S(2)}, u32[]{:S(2)}) collective-permute-start(bf16[256,1024]{1,0:T(8,128)(2,1)S(1)} %get-tuple-element.30), channel_id=1, source_target_pairs={{0,511},{1,0},{2,1},{3,2},{4,3},{5,4},{6,5},{7,6},{8,7},{9,8},{10,... | collective-permute-start | bytes 1572872 | tf_op jit(solution)/shard_map/ppermute | solution.py:23
  108.1 20.2 %copy-start = (f32[256,1664]{1,0:T(8,128)S(1)}, f32[256,1664]{1,0:T(8,128)}, u32[]{:S(2)}) copy-start(f32[256,1664]{1,0:T(8,128)} %get-tuple-element.28.middle_ref) | copy-start | bytes 5111812
  128.5 0.6 copy-start.2
  129.9 33.7 %all-to-all-start.2 = ((f32[16,16,256]{2,1,0:T(8,128)}), f32[16,16,256]{2,1,0:T(8,128)S(1)}, u32[]{:S(2)}, u32[]{:S(2)}) async-start(f32[16,16,256]{2,1,0:T(8,128)} %broadcast_in_dim.7), calls=%async_computation.2 | async-start | bytes 524288 | tf_op jit(solution)/shard_map/all_to_all | solution.py:250
  140.9 35.8 %collective-permute-start.4 = (bf16[32,1664]{1,0:T(8,128)(2,1)S(1)}, bf16[32,1664]{1,0:T(8,128)(2,1)S(1)}, u32[]{:S(2)}, u32[]{:S(2)}) collective-permute-start(bf16[32,1664]{1,0:T(8,128)(2,1)S(1)} %get-tuple-element.34), channel_id=1, source_target_pairs={{0,4},{1,5},{2,6},{3,7},{4,0},{5,1},{6,2},{7,3},{8,12},{9,13},{10,... | collective-permute-start | bytes 319496 | tf_op jit(solution)/shard_map/ppermute | solution.py:23
  148.6 28.1 %collective-permute-start.5 = (bf16[32,1664]{1,0:T(8,128)(2,1)S(1)}, bf16[32,1664]{1,0:T(8,128)(2,1)S(1)}, u32[]{:S(2)}, u32[]{:S(2)}) collective-permute-start(bf16[32,1664]{1,0:T(8,128)(2,1)S(1)} %get-tuple-element.35), channel_id=1, source_target_pairs={{0,2},{1,3},{2,4},{3,5},{4,6},{5,7},{6,0},{7,1},{8,10},{9,11},{10,... | collective-permute-start | bytes 319496 | tf_op jit(solution)/shard_map/ppermute | solution.py:23
  152.9 23.8 %collective-permute-start.6 = (bf16[32,1664]{1,0:T(8,128)(2,1)S(1)}, bf16[32,1664]{1,0:T(8,128)(2,1)S(1)}, u32[]{:S(2)}, u32[]{:S(2)}) collective-permute-start(bf16[32,1664]{1,0:T(8,128)(2,1)S(1)} %get-tuple-element.36), channel_id=1, source_target_pairs={{0,6},{1,7},{2,0},{3,1},{4,2},{5,3},{6,4},{7,5},{8,14},{9,15},{10,... | collective-permute-start | bytes 319496 | tf_op jit(solution)/shard_map/ppermute | solution.py:23
  160.2 16.6 %collective-permute-start.7 = (bf16[32,1664]{1,0:T(8,128)(2,1)S(1)}, bf16[32,1664]{1,0:T(8,128)(2,1)S(1)}, u32[]{:S(2)}, u32[]{:S(2)}) collective-permute-start(bf16[32,1664]{1,0:T(8,128)(2,1)S(1)} %get-tuple-element.37), channel_id=1, source_target_pairs={{0,1},{1,2},{2,3},{3,4},{4,5},{5,6},{6,7},{7,0},{8,9},{9,10},{10,1... | collective-permute-start | bytes 319496 | tf_op jit(solution)/shard_map/ppermute | solution.py:23
  176.7 28.4 %copy-start.7 = (bf16[32,1664]{1,0:T(8,128)(2,1)}, bf16[32,1664]{1,0:T(8,128)(2,1)S(1)}, u32[]{:S(2)}) copy-start(bf16[32,1664]{1,0:T(8,128)(2,1)S(1)} %collective-permute-done.4.refs_4_) | copy-start | bytes 319492
  176.7 28.4 %copy-start.8 = (bf16[32,1664]{1,0:T(8,128)(2,1)}, bf16[32,1664]{1,0:T(8,128)(2,1)S(1)}, u32[]{:S(2)}) copy-start(bf16[32,1664]{1,0:T(8,128)(2,1)S(1)} %collective-permute-done.5.refs_2_) | copy-start | bytes 319492
  176.7 28.4 %copy-start.9 = (bf16[32,1664]{1,0:T(8,128)(2,1)}, bf16[32,1664]{1,0:T(8,128)(2,1)S(1)}, u32[]{:S(2)}) copy-start(bf16[32,1664]{1,0:T(8,128)(2,1)S(1)} %collective-permute-done.6.refs_6_) | copy-start | bytes 319492
  176.8 28.4 %copy-start.10 = (bf16[32,1664]{1,0:T(8,128)(2,1)}, bf16[32,1664]{1,0:T(8,128)(2,1)S(1)}, u32[]{:S(2)}) copy-start(bf16[32,1664]{1,0:T(8,128)(2,1)S(1)} %collective-permute-done.7.refs_1_) | copy-start | bytes 319492
  177.6 55.2 %all-to-all-start.3 = ((bf16[32,16,256]{2,1,0:T(8,128)(2,1)}), bf16[32,16,256]{2,1,0:T(8,128)(2,1)S(1)}, u32[]{:S(2)}, u32[]{:S(2)}) async-start(bf16[32,16,256]{2,1,0:T(8,128)(2,1)} %broadcast_in_dim.8), calls=%async_computation.3 | async-start | bytes 524288 | tf_op jit(solution)/shard_map/all_to_all | solution.py:263
  184.4 20.0 %collective-permute-start.8 = (bf16[32,1664]{1,0:T(8,128)(2,1)S(1)}, bf16[32,1664]{1,0:T(8,128)(2,1)S(1)}, u32[]{:S(2)}, u32[]{:S(2)}) collective-permute-start(bf16[32,1664]{1,0:T(8,128)(2,1)S(1)} %get-tuple-element.43), channel_id=1, source_target_pairs={{0,3},{1,4},{2,5},{3,6},{4,7},{5,0},{6,1},{7,2},{8,11},{9,12},{10,... | collective-permute-start | bytes 319496 | tf_op jit(solution)/shard_map/ppermute | solution.py:23
  187.3 17.0 %collective-permute-start.9 = (bf16[32,1664]{1,0:T(8,128)(2,1)S(1)}, bf16[32,1664]{1,0:T(8,128)(2,1)S(1)}, u32[]{:S(2)}, u32[]{:S(2)}) collective-permute-start(bf16[32,1664]{1,0:T(8,128)(2,1)S(1)} %get-tuple-element.45), channel_id=1, source_target_pairs={{0,5},{1,6},{2,7},{3,0},{4,1},{5,2},{6,3},{7,4},{8,13},{9,14},{10,... | collective-permute-start | bytes 319496 | tf_op jit(solution)/shard_map/ppermute | solution.py:23
  195.0 10.1 %collective-permute-start.10 = (bf16[32,1664]{1,0:T(8,128)(2,1)S(1)}, bf16[32,1664]{1,0:T(8,128)(2,1)S(1)}, u32[]{:S(2)}, u32[]{:S(2)}) collective-permute-start(bf16[32,1664]{1,0:T(8,128)(2,1)S(1)} %get-tuple-element.47), channel_id=1, source_target_pairs={{0,7},{1,0},{2,1},{3,2},{4,3},{5,4},{6,5},{7,6},{8,15},{9,8},{10,9... | collective-permute-start | bytes 319496 | tf_op jit(solution)/shard_map/ppermute | solution.py:23
  204.4 0.8 copy-start.11
  204.4 0.8 copy-start.12
  205.2 0.6 copy-start.13

commit v3 on v1

--- a/solution.py
+++ b/solution.py
@@ -19,6 +19,20 @@
 def shifted(shard, axis, by):
     count = lax.axis_size(axis)
     return lax.ppermute(shard, axis, [(i, (i + by) % count) for i in range(count)])
+
+
+def collected(rows):
+    for axis in reversed(PLANE):
+        count = lax.axis_size(axis)
+        apart = 1
+        while apart < count:
+            other = lax.ppermute(rows, axis, [(i, i ^ apart) for i in range(count)])
+            second = (lax.axis_index(axis) & apart) != 0
+            rows = jnp.concatenate(
+                [jnp.where(second, other, rows), jnp.where(second, rows, other)], axis=0
+            )
+            apart *= 2
+    return rows
 
 
 def tiles_of(width, tile):
@@ -40,11 +54,10 @@
     middle_ref,
     left_ref,
     right_ref,
-    terms_ref,
+    stacked,
+    delta,
     wide,
     agg,
-    stacked,
-    delta,
     agg_grad,
     scat,
     sems,
@@ -117,9 +130,6 @@
     left_ref[...] = scat[:, :rim].astype(jnp.bfloat16)
     right_ref[...] = scat[:, rim + width :].astype(jnp.bfloat16)
     middle_ref[...] = scat[:, rim : rim + width]
-    terms_ref[...] = lax.dot_general(
-        stacked[...], delta[...], (((1,), (1,)), ((), ())), preferred_element_type=jnp.float32
-    )
 
 
 def local_step(rows, cols, count, pos, own, before, after, values, w_in, w_out, cot):
@@ -134,15 +144,14 @@
             jax.ShapeDtypeStruct((depth, width), jnp.float32),
             jax.ShapeDtypeStruct((depth, rim), jnp.bfloat16),
             jax.ShapeDtypeStruct((depth, rim), jnp.bfloat16),
-            jax.ShapeDtypeStruct((2 * depth, depth), jnp.float32),
+            jax.ShapeDtypeStruct((2 * depth, width), jnp.bfloat16),
+            jax.ShapeDtypeStruct((depth, width), jnp.bfloat16),
         ),
         in_specs=[smem] * 4 + [anywhere] * 3 + [vmem] * 4,
-        out_specs=(vmem,) * 4,
+        out_specs=(vmem,) * 5,
         scratch_shapes=[
             pltpu.VMEM((depth, width + 2 * rim), jnp.bfloat16),
             pltpu.VMEM((depth, width), jnp.float32),
-            pltpu.VMEM((2 * depth, width), jnp.bfloat16),
-            pltpu.VMEM((depth, width), jnp.bfloat16),
             pltpu.VMEM((depth, width), jnp.bfloat16),
             pltpu.VMEM((depth, width + 2 * rim), jnp.float32),
             pltpu.SemaphoreType.DMA((3,)),
@@ -166,7 +175,7 @@
     w_in = jnp.concatenate([w_self.T, w_neigh.T], axis=1)
     w_out = jnp.concatenate([w_self, w_neigh], axis=0)
     pos = lax.axis_index("feat").astype(jnp.int32)[None]
-    middle, left, right, terms = local_step(
+    middle, left, right, stacked, delta = local_step(
         block_row[0],
         block_col[0],
         block_count,
@@ -179,24 +188,24 @@
         w_out,
         cotangent,
     )
-    from_next = shifted(left, RING, -1).astype(jnp.float32)
-    from_prev = shifted(right, RING, 1).astype(jnp.float32)
-    total = middle + jnp.pad(from_prev, ((0, 0), (0, width - rim)))
-    total = total + jnp.pad(from_next, ((0, 0), (width - rim, 0)))
-    total = total.astype(jnp.bfloat16)
-    feature_grad = lax.all_to_all(total, "feat", split_axis=0, concat_axis=1, tiled=True)
-
+    terms = jnp.einsum("in,on->io", stacked, delta, preferred_element_type=jnp.float32)
     plane, line = lax.axis_size(PLANE), lax.axis_size(LINE)
     share = 2 * depth // plane
-    pieces = lax.all_to_all(terms, PLANE, split_axis=0, concat_axis=0, tiled=True)
-    partial = pieces.reshape(plane, share, depth).sum(0)
+    from_next = shifted(left, RING, -1)
+    parts = lax.all_to_all(terms, PLANE, split_axis=0, concat_axis=0, tiled=True)
+    partial = parts.reshape(plane, share, depth).sum(0)
+    partial, from_next, right = lax.optimization_barrier((partial, from_next, right))
+    from_prev = shifted(right, RING, 1)
     copies = jnp.broadcast_to(partial[None], (line, share, depth))
     copies = lax.all_to_all(copies, LINE, split_axis=0, concat_axis=0, tiled=True)
     factor = 1.0 / math.sqrt(rows_part * lax.axis_size(DOM))
-    grads = (copies.sum(0) * factor).astype(jnp.bfloat16)
-    grads = jnp.broadcast_to(grads[None], (plane, share, depth))
-    grads = lax.all_to_all(grads, PLANE, split_axis=0, concat_axis=0, tiled=True)
-    grads = grads.reshape(2 * depth, depth)
+    grads = (copies.reshape(line, share, depth).sum(0) * factor).astype(jnp.bfloat16)
+    total = middle + jnp.pad(from_prev.astype(jnp.float32), ((0, 0), (0, width - rim)))
+    total = total + jnp.pad(from_next.astype(jnp.float32), ((0, 0), (width - rim, 0)))
+    total = total.astype(jnp.bfloat16)
+    total, grads = lax.optimization_barrier((total, grads))
+    feature_grad = lax.all_to_all(total, "feat", split_axis=0, concat_axis=1, tiled=True)
+    grads = collected(grads)
     return (feature_grad, grads[:depth], grads[depth:])
 
 

time: 217 us -> 206 us (0.949)
  waiting for transfers between devices: 79.4 us -> 62.8 us
  starting transfers between devices: 44.9 us -> 51.2 us
  blocking collectives: 75.4 us -> 73 us
  local copies, waits for them, and re-layouts: 6.5 us -> 4.25 us
    all_to_all x1, waiting for transfers between devices: 42.8 us -> 11.3 us  [on_device(): lax.all_to_all(total, 'feat', split_axis=0, concat_axis=1, tiled=True)]
    ppermute x0 -> x5, waiting for transfers between devices: none -> 18.3 us  [collected(): other = lax.ppermute(rows, axis, [(i, i ^ apart) for i in range(count)])]
    ppermute x0 -> x5, starting transfers between devices: none -> 12.2 us  [collected(): other = lax.ppermute(rows, axis, [(i, i ^ apart) for i in range(count)])]
    all_to_all x1 -> x0, starting transfers between devices: 7.92 us -> none  [on_device(): lax.all_to_all(grads, PLANE, split_axis=0, concat_axis=0, tiled=True)]
    ppermute x4, waiting for transfers between devices: 30.3 us -> 24.2 us  [shifted(): lax.ppermute(shard, axis, [(i, (i + by) % count) for i in range(count)])]
    all_to_all x1, waiting for transfers between devices: 6.29 us -> 8.92 us  [on_device(): lax.all_to_all(copies, LINE, split_axis=0, concat_axis=0, tiled=True)]
    all_to_all x1, blocking collectives: 20.2 us -> 17.8 us  [on_device(): lax.all_to_all(terms, PLANE, split_axis=0, concat_axis=0, tiled=True)]
    ppermute x4, starting transfers between devices: 19.4 us -> 21.7 us  [shifted(): lax.ppermute(shard, axis, [(i, (i + by) % count) for i in range(count)])]
  transfers between devices with their start and end apart: 7 -> 11, of which waited for: 6 -> 10; matrix products, arithmetic and copies ran while one was open for 2% -> 3% of each run, Pallas kernels for 0% -> 0%
where the time goes in v3:
time: 206 us
  blocking collectives  73 us (35%)
  waiting for transfers between devices  62.8 us (30%)
  starting transfers between devices  51.2 us (25%)
  Pallas kernels  7.51 us (4%)
  local copies, waits for them, and re-layouts  4.25 us (2%)
  other arithmetic  3.08 us (1%)
  matrix products  2.13 us (1%)
    all_to_all x1, blocking collectives, on_device(): lax.all_to_all(features, 'feat', split_axis=1, concat_axis=0, tiled=True)  55.2 us
    ppermute x4, waiting for transfers between devices, shifted(): lax.ppermute(shard, axis, [(i, (i + by) % count) for i in range(count)])  24.2 us
    ppermute x4, starting transfers between devices, shifted(): lax.ppermute(shard, axis, [(i, (i + by) % count) for i in range(count)])  21.7 us
    ppermute x5, waiting for transfers between devices, collected(): other = lax.ppermute(rows, axis, [(i, i ^ apart) for i in range(count)])  18.3 us
    all_to_all x1, blocking collectives, on_device(): lax.all_to_all(terms, PLANE, split_axis=0, concat_axis=0, tiled=True)  17.8 us
    ppermute x5, starting transfers between devices, collected(): other = lax.ppermute(rows, axis, [(i, i ^ apart) for i in range(count)])  12.2 us
    all_to_all x1, waiting for transfers between devices, on_device(): lax.all_to_all(total, 'feat', split_axis=0, concat_axis=1, tiled=True)  11.3 us
    all_to_all x1, starting transfers between devices, on_device(): lax.all_to_all(copies, LINE, split_axis=0, concat_axis=0, tiled=True)  10.6 us
  transfers between devices with their start and end apart: 11, of which 10 were waited for; matrix products, arithmetic and copies ran while one was open for 3% of the time, Pallas kernels for 0%

profile of v3, /device:TPU:6, one launch (start us, length us, event | category | flops | bytes accessed | tf_op | source)
XLA Modules:
  0.0 205.5 jit_solution(2206008623230965857)
XLA Ops:
  0.6 1.2 copy.22
  1.9 55.2 %all_to_all.52 = bf16[32,8,1664]{2,0,1:T(8,128)(2,1)S(1)} all-to-all(bf16[32,8,1664]{2,0,1:T(8,128)(2,1)S(1)} %bitcast.24), channel_id=1, replica_groups=mesh['zh'=2,'y'=4,'x'=4,'core'=2,'feat'=8] {'feat'}, dimensions={1} | all-to-all | bytes 1703936 | tf_op jit(solution)/shard_map/all_to_all | solution.py:172
  57.1 1.1 fusion
  58.2 2.4 %collective-permute-start = (bf16[256,1024]{1,0:T(8,128)(2,1)}, bf16[256,1024]{1,0:T(8,128)(2,1)S(1)}, u32[]{:S(2)}, u32[]{:S(2)}) collective-permute-start(bf16[256,1024]{1,0:T(8,128)(2,1)} %get-tuple-element.24), channel_id=1, source_target_pairs={{0,1},{1,2},{2,3},{3,4},{4,5},{5,6},{6,7},{7,8},{8,9},{9,10},{10,1... | collective-permute-start | bytes 1572872 | tf_op jit(solution)/shard_map/ppermute | solution.py:21
  60.6 10.7 %collective-permute-start.1 = (bf16[256,1024]{1,0:T(8,128)(2,1)}, bf16[256,1024]{1,0:T(8,128)(2,1)S(1)}, u32[]{:S(2)}, u32[]{:S(2)}) collective-permute-start(bf16[256,1024]{1,0:T(8,128)(2,1)} %get-tuple-element.23), channel_id=1, source_target_pairs={{0,511},{1,0},{2,1},{3,2},{4,3},{5,4},{6,5},{7,6},{8,7},{9,8},{10,... | collective-permute-start | bytes 1572872 | tf_op jit(solution)/shard_map/ppermute | solution.py:21
  71.3 0.1 copy.16
  72.2 9.9 %collective-permute-done.before_ref = bf16[256,1024]{1,0:T(8,128)(2,1)S(1)} collective-permute-done((bf16[256,1024]{1,0:T(8,128)(2,1)}, bf16[256,1024]{1,0:T(8,128)(2,1)S(1)}, u32[]{:S(2)}, u32[]{:S(2)}) %collective-permute-start) | collective-permute-done | bytes 524320 | tf_op jit(solution)/shard_map/ppermute | solution.py:21
  82.1 3.5 %collective-permute-done.1.after_ref = bf16[256,1024]{1,0:T(8,128)(2,1)S(1)} collective-permute-done((bf16[256,1024]{1,0:T(8,128)(2,1)}, bf16[256,1024]{1,0:T(8,128)(2,1)S(1)}, u32[]{:S(2)}, u32[]{:S(2)}) %collective-permute-start.1) | collective-permute-done | bytes 524320 | tf_op jit(solution)/shard_map/ppermute | solution.py:21
  85.7 7.5 %shard_map.103 = (f32[256,1664]{1,0:T(8,128)}, bf16[256,1024]{1,0:T(8,128)(2,1)}, bf16[256,1024]{1,0:T(8,128)(2,1)S(1)}, bf16[512,1664]{1,0:T(8,128)(2,1)}, bf16[256,1664]{1,0:T(8,128)(2,1)S(1)}) custom-call(s32[64]{0:T(128)S(1)} %bitcast.21, s32[64]{0:T(128)S(1)} %bitcast.22, s32[1]{0:T(128)S(6)} %copy.23.count_ref, s32[1]{0:T(128)} %bitcast.2.pos_ref, ...), custom_call_target="tpu_custom_call" | custom-call | flops 1308622848 | bytes 8388608 | tf_op jit(solution)/shard_map/pallas_call | solution.py:141
  93.2 6.7 %collective-permute-start.2 = (bf16[256,1024]{1,0:T(8,128)(2,1)}, bf16[256,1024]{1,0:T(8,128)(2,1)S(1)}, u32[]{:S(2)}, u32[]{:S(2)}) collective-permute-start(bf16[256,1024]{1,0:T(8,128)(2,1)} %get-tuple-element.16), channel_id=1, source_target_pairs={{0,511},{1,0},{2,1},{3,2},{4,3},{5,4},{6,5},{7,6},{8,7},{9,8},{10,... | collective-permute-start | bytes 1572872 | tf_op jit(solution)/shard_map/ppermute | solution.py:21
  99.9 2.1 %fusion.1 = f32[512,256]{1,0:T(8,128)S(1)} fusion(bf16[512,1664]{1,0:T(8,128)(2,1)} %get-tuple-element.14, bf16[256,1664]{1,0:T(8,128)(2,1)S(1)} %get-tuple-element.15), kind=kOutput, calls=%fused_computation.20 | convolution fusion | flops 436207616 | bytes 3080192 | tf_op jit(solution)/shard_map/in,on->io/dot_general | solution.py:191
  102.1 17.8 %all_to_all.53 = f32[32,16,256]{2,1,0:T(8,128)S(1)} all-to-all(f32[32,16,256]{2,1,0:T(8,128)S(1)} %bitcast.27), channel_id=1, replica_groups=mesh['zh'=2,'y'=4,'x'=4,'core'=2,'feat'=8] {'y','x','core'}, dimensions={0} | all-to-all | bytes 1048576 | tf_op jit(solution)/shard_map/all_to_all | solution.py:195
  119.9 1.9 collective-permute-start.3
  121.9 0.7 broadcast_in_dim.10
  122.6 10.6 %all-to-all-start.2 = ((f32[16,16,256]{2,1,0:T(8,128)}), f32[16,16,256]{2,1,0:T(8,128)S(1)}, u32[]{:S(2)}, u32[]{:S(2)}) async-start(f32[16,16,256]{2,1,0:T(8,128)} %broadcast_in_dim.10), calls=%async_computation.2 | async-start | bytes 524288 | tf_op jit(solution)/shard_map/all_to_all | solution.py:200
  133.3 10.8 %collective-permute-done.3 = bf16[256,1024]{1,0:T(8,128)(2,1)} collective-permute-done((bf16[256,1024]{1,0:T(8,128)(2,1)S(1)}, bf16[256,1024]{1,0:T(8,128)(2,1)}, u32[]{:S(2)}, u32[]{:S(2)}) %collective-permute-start.3) | collective-permute-done | bytes 524320 | tf_op jit(solution)/shard_map/ppermute | solution.py:21
  144.1 2.1 %add_convert_fusion = bf16[256,1664]{1,0:T(8,128)(2,1)} fusion(f32[256,1664]{1,0:T(8,128)S(1)} %copy-done.3, bf16[256,1024]{1,0:T(8,128)(2,1)S(1)} %collective-permute-done.2, bf16[256,1024]{1,0:T(8,128)(2,1)} %collective-permute-done.3), kind=kLoop, calls=%fused_computation | loop fusion | flops 2129920 | bytes 3604480 | tf_op jit(solution)/shard_map/convert_element_type | solution.py:205
  146.2 8.9 %all-to-all-done.2 = f32[16,16,256]{2,1,0:T(8,128)S(1)} async-done(((f32[16,16,256]{2,1,0:T(8,128)}), f32[16,16,256]{2,1,0:T(8,128)S(1)}, u32[]{:S(2)}, u32[]{:S(2)}) %all-to-all-start.2) | async-done | bytes 262176 | tf_op jit(solution)/shard_map/all_to_all | solution.py:200
  155.2 6.7 %all-to-all-start.3 = ((bf16[8,32,1664]{2,1,0:T(8,128)(2,1)}), bf16[8,32,1664]{2,1,0:T(8,128)(2,1)S(1)}, u32[]{:S(2)}, u32[]{:S(2)}) async-start(bf16[8,32,1664]{2,1,0:T(8,128)(2,1)} %bitcast.9), calls=%async_computation.3 | async-start | bytes 1703936 | tf_op jit(solution)/shard_map/all_to_all | solution.py:207
  161.9 1.9 collective-permute-start.4
  163.8 1.1 collective-permute-done.4
  164.9 1.9 collective-permute-start.5
  166.9 3.7 %collective-permute-done.5 = bf16[32,256]{1,0:T(8,128)(2,1)S(1)} collective-permute-done((bf16[32,256]{1,0:T(8,128)(2,1)S(1)}, bf16[32,256]{1,0:T(8,128)(2,1)S(1)}, u32[]{:S(2)}, u32[]{:S(2)}) %collective-permute-start.5) | collective-permute-done | bytes 16416 | tf_op jit(solution)/shard_map/ppermute | solution.py:29
  170.6 3.4 %collective-permute-start.6 = (bf16[64,256]{1,0:T(8,128)(2,1)S(1)}, bf16[64,256]{1,0:T(8,128)(2,1)S(1)}, u32[]{:S(2)}, u32[]{:S(2)}) collective-permute-start(bf16[64,256]{1,0:T(8,128)(2,1)S(1)} %pad_maximum_fusion.4), channel_id=1, source_target_pairs={{0,32},{16,48},{32,0},{48,16},{1,33},{17,49},{33,1},{49,17},{2,34}... | collective-permute-start | bytes 98312 | tf_op jit(solution)/shard_map/ppermute | solution.py:29
  174.0 3.9 %collective-permute-done.6 = bf16[64,256]{1,0:T(8,128)(2,1)S(1)} collective-permute-done((bf16[64,256]{1,0:T(8,128)(2,1)S(1)}, bf16[64,256]{1,0:T(8,128)(2,1)S(1)}, u32[]{:S(2)}, u32[]{:S(2)}) %collective-permute-start.6) | collective-permute-done | bytes 32800 | tf_op jit(solution)/shard_map/ppermute | solution.py:29
  177.9 2.5 %collective-permute-start.7 = (bf16[128,256]{1,0:T(8,128)(2,1)S(1)}, bf16[128,256]{1,0:T(8,128)(2,1)S(1)}, u32[]{:S(2)}, u32[]{:S(2)}) collective-permute-start(bf16[128,256]{1,0:T(8,128)(2,1)S(1)} %pad_maximum_fusion.3), channel_id=1, source_target_pairs={{0,64},{64,0},{128,192},{192,128},{1,65},{65,1},{129,193},{193,129... | collective-permute-start | bytes 196616 | tf_op jit(solution)/shard_map/ppermute | solution.py:29
  180.5 3.6 %collective-permute-done.7 = bf16[128,256]{1,0:T(8,128)(2,1)S(1)} collective-permute-done((bf16[128,256]{1,0:T(8,128)(2,1)S(1)}, bf16[128,256]{1,0:T(8,128)(2,1)S(1)}, u32[]{:S(2)}, u32[]{:S(2)}) %collective-permute-start.7) | collective-permute-done | bytes 65568 | tf_op jit(solution)/shard_map/ppermute | solution.py:29
  184.1 2.4 %collective-permute-start.8 = (bf16[256,256]{1,0:T(8,128)(2,1)S(1)}, bf16[256,256]{1,0:T(8,128)(2,1)S(1)}, u32[]{:S(2)}, u32[]{:S(2)}) collective-permute-start(bf16[256,256]{1,0:T(8,128)(2,1)S(1)} %pad_maximum_fusion.2), channel_id=1, source_target_pairs={{0,128},{64,192},{128,0},{192,64},{1,129},{65,193},{129,1},{193,65... | collective-permute-start | bytes 393224 | tf_op jit(solution)/shard_map/ppermute | solution.py:29
  186.6 5.9 %collective-permute-done.8 = bf16[256,256]{1,0:T(8,128)(2,1)S(1)} collective-permute-done((bf16[256,256]{1,0:T(8,128)(2,1)S(1)}, bf16[256,256]{1,0:T(8,128)(2,1)S(1)}, u32[]{:S(2)}, u32[]{:S(2)}) %collective-permute-start.8) | collective-permute-done | bytes 131104 | tf_op jit(solution)/shard_map/ppermute | solution.py:29
  192.5 0.7 broadcast_select_fusion
  193.3 11.3 %all-to-all-done.3 = bf16[8,32,1664]{2,1,0:T(8,128)(2,1)S(1)} async-done(((bf16[8,32,1664]{2,1,0:T(8,128)(2,1)}), bf16[8,32,1664]{2,1,0:T(8,128)(2,1)S(1)}, u32[]{:S(2)}, u32[]{:S(2)}) %all-to-all-start.3) | async-done | bytes 852000 | tf_op jit(solution)/shard_map/all_to_all | solution.py:207
  204.6 1.0 copy.20
  (27 shorter events, 0.3 us)
Async XLA Ops:
  1.9 69.4 %copy-start.5 = (bf16[256,256]{1,0:T(8,128)(2,1)S(1)}, bf16[256,256]{1,0:T(8,128)(2,1)}, u32[]{:S(2)}) copy-start(bf16[256,256]{1,0:T(8,128)(2,1)} %param.13) | copy-start | bytes 393220
  1.9 69.5 %copy-start.4 = (bf16[256,256]{1,0:T(8,128)(2,1)S(1)}, bf16[256,256]{1,0:T(8,128)(2,1)}, u32[]{:S(2)}) copy-start(bf16[256,256]{1,0:T(8,128)(2,1)} %param.14) | copy-start | bytes 393220
  57.1 28.6 %copy-start = (bf16[256,1664]{1,0:T(8,128)(2,1)S(1)}, bf16[256,1664]{1,0:T(8,128)(2,1)}, u32[]{:S(2)}) copy-start(bf16[256,1664]{1,0:T(8,128)(2,1)} %cot_ref.1) | copy-start | bytes 2555908
  57.1 28.6 %copy-start.1 = (s32[1,64]{1,0:T(1,128)S(1)}, s32[1,64]{1,0:T(1,128)}, u32[]{:S(2)}) copy-start(s32[1,64]{1,0:T(1,128)} %param.9) | copy-start | bytes 772
  57.1 28.6 %copy-start.2 = (s32[1,64]{1,0:T(1,128)S(1)}, s32[1,64]{1,0:T(1,128)}, u32[]{:S(2)}) copy-start(s32[1,64]{1,0:T(1,128)} %param.10) | copy-start | bytes 772
  58.2 23.9 %collective-permute-start = (bf16[256,1024]{1,0:T(8,128)(2,1)}, bf16[256,1024]{1,0:T(8,128)(2,1)S(1)}, u32[]{:S(2)}, u32[]{:S(2)}) collective-permute-start(bf16[256,1024]{1,0:T(8,128)(2,1)} %get-tuple-element.24), channel_id=1, source_target_pairs={{0,1},{1,2},{2,3},{3,4},{4,5},{5,6},{6,7},{7,8},{8,9},{9,10},{10,1... | collective-permute-start | bytes 1572872 | tf_op jit(solution)/shard_map/ppermute | solution.py:21
  60.6 25.1 %collective-permute-start.1 = (bf16[256,1024]{1,0:T(8,128)(2,1)}, bf16[256,1024]{1,0:T(8,128)(2,1)S(1)}, u32[]{:S(2)}, u32[]{:S(2)}) collective-permute-start(bf16[256,1024]{1,0:T(8,128)(2,1)} %get-tuple-element.23), channel_id=1, source_target_pairs={{0,511},{1,0},{2,1},{3,2},{4,3},{5,4},{6,5},{7,6},{8,7},{9,8},{10,... | collective-permute-start | bytes 1572872 | tf_op jit(solution)/shard_map/ppermute | solution.py:21
  93.2 26.7 %collective-permute-start.2 = (bf16[256,1024]{1,0:T(8,128)(2,1)}, bf16[256,1024]{1,0:T(8,128)(2,1)S(1)}, u32[]{:S(2)}, u32[]{:S(2)}) collective-permute-start(bf16[256,1024]{1,0:T(8,128)(2,1)} %get-tuple-element.16), channel_id=1, source_target_pairs={{0,511},{1,0},{2,1},{3,2},{4,3},{5,4},{6,5},{7,6},{8,7},{9,8},{10,... | collective-permute-start | bytes 1572872 | tf_op jit(solution)/shard_map/ppermute | solution.py:21
  102.1 42.0 %copy-start.3 = (f32[256,1664]{1,0:T(8,128)S(1)}, f32[256,1664]{1,0:T(8,128)}, u32[]{:S(2)}) copy-start(f32[256,1664]{1,0:T(8,128)} %get-tuple-element.13) | copy-start | bytes 5111812
  119.9 24.1 %collective-permute-start.3 = (bf16[256,1024]{1,0:T(8,128)(2,1)S(1)}, bf16[256,1024]{1,0:T(8,128)(2,1)}, u32[]{:S(2)}, u32[]{:S(2)}) collective-permute-start(bf16[256,1024]{1,0:T(8,128)(2,1)S(1)} %get-tuple-element.18), channel_id=1, source_target_pairs={{0,1},{1,2},{2,3},{3,4},{4,5},{5,6},{6,7},{7,8},{8,9},{9,10},{10,1... | collective-permute-start | bytes 1572872 | tf_op jit(solution)/shard_map/ppermute | solution.py:21
  122.6 32.5 %all-to-all-start.2 = ((f32[16,16,256]{2,1,0:T(8,128)}), f32[16,16,256]{2,1,0:T(8,128)S(1)}, u32[]{:S(2)}, u32[]{:S(2)}) async-start(f32[16,16,256]{2,1,0:T(8,128)} %broadcast_in_dim.10), calls=%async_computation.2 | async-start | bytes 524288 | tf_op jit(solution)/shard_map/all_to_all | solution.py:200
  155.2 49.4 %all-to-all-start.3 = ((bf16[8,32,1664]{2,1,0:T(8,128)(2,1)}), bf16[8,32,1664]{2,1,0:T(8,128)(2,1)S(1)}, u32[]{:S(2)}, u32[]{:S(2)}) async-start(bf16[8,32,1664]{2,1,0:T(8,128)(2,1)} %bitcast.9), calls=%async_computation.3 | async-start | bytes 1703936 | tf_op jit(solution)/shard_map/all_to_all | solution.py:207
  161.9 3.1 %collective-permute-start.4 = (bf16[16,256]{1,0:T(8,128)(2,1)S(1)}, bf16[16,256]{1,0:T(8,128)(2,1)S(1)}, u32[]{:S(2)}, u32[]{:S(2)}) collective-permute-start(bf16[16,256]{1,0:T(8,128)(2,1)S(1)} %multiply_convert_fusion), channel_id=1, source_target_pairs={{0,8},{8,0},{1,9},{9,1},{2,10},{10,2},{3,11},{11,3},{4,12},{12,4},... | collective-permute-start | bytes 24584 | tf_op jit(solution)/shard_map/ppermute | solution.py:29
  164.9 5.6 %collective-permute-start.5 = (bf16[32,256]{1,0:T(8,128)(2,1)S(1)}, bf16[32,256]{1,0:T(8,128)(2,1)S(1)}, u32[]{:S(2)}, u32[]{:S(2)}) collective-permute-start(bf16[32,256]{1,0:T(8,128)(2,1)S(1)} %pad_maximum_fusion.5), channel_id=1, source_target_pairs={{0,16},{16,0},{32,48},{48,32},{1,17},{17,1},{33,49},{49,33},{2,18}... | collective-permute-start | bytes 49160 | tf_op jit(solution)/shard_map/ppermute | solution.py:29
  170.6 7.3 %collective-permute-start.6 = (bf16[64,256]{1,0:T(8,128)(2,1)S(1)}, bf16[64,256]{1,0:T(8,128)(2,1)S(1)}, u32[]{:S(2)}, u32[]{:S(2)}) collective-permute-start(bf16[64,256]{1,0:T(8,128)(2,1)S(1)} %pad_maximum_fusion.4), channel_id=1, source_target_pairs={{0,32},{16,48},{32,0},{48,16},{1,33},{17,49},{33,1},{49,17},{2,34}... | collective-permute-start | bytes 98312 | tf_op jit(solution)/shard_map/ppermute | solution.py:29
  177.9 6.2 %collective-permute-start.7 = (bf16[128,256]{1,0:T(8,128)(2,1)S(1)}, bf16[128,256]{1,0:T(8,128)(2,1)S(1)}, u32[]{:S(2)}, u32[]{:S(2)}) collective-permute-start(bf16[128,256]{1,0:T(8,128)(2,1)S(1)} %pad_maximum_fusion.3), channel_id=1, source_target_pairs={{0,64},{64,0},{128,192},{192,128},{1,65},{65,1},{129,193},{193,129... | collective-permute-start | bytes 196616 | tf_op jit(solution)/shard_map/ppermute | solution.py:29
  184.1 8.4 %collective-permute-start.8 = (bf16[256,256]{1,0:T(8,128)(2,1)S(1)}, bf16[256,256]{1,0:T(8,128)(2,1)S(1)}, u32[]{:S(2)}, u32[]{:S(2)}) collective-permute-start(bf16[256,256]{1,0:T(8,128)(2,1)S(1)} %pad_maximum_fusion.2), channel_id=1, source_target_pairs={{0,128},{64,192},{128,0},{192,64},{1,129},{65,193},{129,1},{193,65... | collective-permute-start | bytes 393224 | tf_op jit(solution)/shard_map/ppermute | solution.py:29

commit v4 on v3

v4 whole, which is shorter than its diff:
```python
import functools
import math

import jax
import jax.numpy as jnp
from jax import lax
from jax.experimental import pallas as pl
from jax.experimental.pallas import tpu as pltpu
from jax.sharding import Mesh, PartitionSpec as P

BLK = 128
REACH = 8
DOM = ("zh", "y", "x", "core")
PLANE = ("y", "x", "core")
RING = DOM + ("feat",)


def shifted(shard, axis, by):
    count = lax.axis_size(axis)
    return lax.ppermute(shard, axis, [(i, (i + by) % count) for i in range(count)])


def collected(rows):
    for axis in reversed(PLANE):
        count = lax.axis_size(axis)
        apart = 1
        while apart < count:
            other = lax.ppermute(rows, axis, [(i, i ^ apart) for i in range(count)])
            second = (lax.axis_index(axis) & apart) != 0
            rows = jnp.concatenate(
                [jnp.where(second, other, rows), jnp.where(second, rows, other)], axis=0
            )
            apart *= 2
    return rows


def tiles_of(width, tile):
    return [(at, min(tile, width - at)) for at in range(0, width, tile)]


SMEM = pl.BlockSpec(memory_space=pltpu.SMEM)
VMEM = pl.BlockSpec(memory_space=pltpu.VMEM)
LEFT, OWN, RIGHT = range(3)


def list_kernel(chunk, rows_ref, cols_ref, count_ref, pos_ref, used_ref, slot_ref, row_ref, col_ref):
    slots = rows_ref.shape[0]
    first = pos_ref[0] * chunk
    for kind in range(3):
        used_ref[kind] = 0

    def step(slot, carry):
        row = rows_ref[slot] - first

        @pl.when((row >= 0) & (row < chunk))
        def _():
            col = cols_ref[slot] - first - REACH
            kind = jnp.where(col < 0, LEFT, jnp.where(col < chunk, OWN, RIGHT))
            base = jnp.where(col < 0, REACH, jnp.where(col < chunk, 0, -chunk))
            at = kind * slots + used_ref[kind]
            slot_ref[at] = slot
            row_ref[at] = row
            col_ref[at] = col + base
            used_ref[kind] = used_ref[kind] + 1

        return carry

    lax.fori_loop(0, jnp.minimum(count_ref[0], slots), step, 0)


def list_step(rows, cols, count, pos, chunk):
    table = jax.ShapeDtypeStruct((3 * rows.shape[0],), jnp.int32)
    return pl.pallas_call(
        functools.partial(list_kernel, chunk),
        out_shape=(jax.ShapeDtypeStruct((3,), jnp.int32), table, table, table),
        in_specs=[SMEM] * 4,
        out_specs=(SMEM,) * 4,
        cost_estimate=pl.CostEstimate(flops=0, bytes_accessed=4096, transcendentals=0),
    )(rows, cols, count, pos)


def block(index):
    return pl.ds(pl.multiple_of(index * BLK, BLK), BLK)


def add_slots(lists, kind, source, into, values, forward):
    used_ref, slot_ref, row_ref, col_ref = lists
    base = kind * (slot_ref.shape[0] // 3)
    count = used_ref[kind]

    def some(indices):
        products = []
        for at in indices:
            read = col_ref[at] if forward else row_ref[at]
            products.append(
                lax.dot_general(
                    source[:, block(read)],
                    values[slot_ref[at]],
                    (((1,), (1 if forward else 0,)), ((), ())),
                    preferred_element_type=jnp.float32,
                )
            )
        for at, product in zip(indices, products):
            write = row_ref[at] if forward else col_ref[at]
            into[:, block(write)] += product

    def pair(step, carry):
        some([base + 2 * step, base + 2 * step + 1])
        return carry

    lax.fori_loop(0, lax.div(count, 2), pair, 0)

    @pl.when(lax.rem(count, 2) == 1)
    def _():
        some([base + count - 1])


def before_kernel(*refs):
    lists, (own_ref, values_ref, agg_ref) = refs[:4], refs[4:]
    agg_ref[...] = jnp.zeros_like(agg_ref)
    add_slots(lists, OWN, own_ref, agg_ref, values_ref, True)


def before_step(lists, own, values):
    return pl.pallas_call(
        before_kernel,
        out_shape=jax.ShapeDtypeStruct(own.shape, jnp.float32),
        in_specs=[SMEM] * 4 + [VMEM] * 2,
        out_specs=VMEM,
        compiler_params=pltpu.CompilerParams(vmem_limit_bytes=24 * 1024 * 1024),
        cost_estimate=pl.CostEstimate(flops=1 << 28, bytes_accessed=4 << 20, transcendentals=0),
    )(*lists, own, values)


def local_kernel(*refs):
    lists = refs[:4]
    (agg_ref, own_ref, before_ref, after_ref, values_ref, w_in_ref, w_out_ref, cot_ref) = refs[4:12]
    left_ref, right_ref, stacked, delta, both_ref, agg, scat = refs[12:]
    depth, width = own_ref.shape
    agg[...] = agg_ref[...]
    add_slots(lists, LEFT, before_ref, agg, values_ref, True)
    add_slots(lists, RIGHT, after_ref, agg, values_ref, True)
    for at, size in tiles_of(width, 256):
        part = slice(at, at + size)
        stacked[:depth, part] = own_ref[:, part]
        stacked[depth:, part] = agg[:, part].astype(jnp.bfloat16)
        preact = jnp.dot(w_in_ref[...], stacked[:, part], preferred_element_type=jnp.float32)
        sigma = 1.0 / (1.0 + jnp.exp(-preact))
        slope = sigma * (1.0 + preact * (1.0 - sigma))
        delta[:, part] = (cot_ref[:, part].astype(jnp.float32) * slope).astype(jnp.bfloat16)
        both = jnp.dot(w_out_ref[...], delta[:, part], preferred_element_type=jnp.float32)
        both_ref[:, part] = both.astype(jnp.bfloat16)
    agg_grad = both_ref.at[pl.ds(depth, depth)]
    for kind, out_ref in ((LEFT, left_ref), (RIGHT, right_ref)):
        scat[...] = jnp.zeros_like(scat)
        add_slots(lists, kind, agg_grad, scat, values_ref, False)
        out_ref[...] = scat[...].astype(jnp.bfloat16)


def local_step(lists, agg, own, before, after, values, w_in, w_out, cot):
    depth, width = own.shape
    rim = before.shape[1]
    return pl.pallas_call(
        local_kernel,
        out_shape=(
            jax.ShapeDtypeStruct((depth, rim), jnp.bfloat16),
            jax.ShapeDtypeStruct((depth, rim), jnp.bfloat16),
            jax.ShapeDtypeStruct((2 * depth, width), jnp.bfloat16),
            jax.ShapeDtypeStruct((depth, width), jnp.bfloat16),
            jax.ShapeDtypeStruct((2 * depth, width), jnp.bfloat16),
        ),
        in_specs=[SMEM] * 4 + [VMEM] * 8,
        out_specs=(VMEM,) * 5,
        scratch_shapes=[
            pltpu.VMEM((depth, width), jnp.float32),
            pltpu.VMEM((depth, rim), jnp.float32),
        ],
        compiler_params=pltpu.CompilerParams(vmem_limit_bytes=40 * 1024 * 1024),
        cost_estimate=pl.CostEstimate(
            flops=12 * depth * depth * width, bytes_accessed=8 << 20, transcendentals=depth * width
        ),
    )(*lists, agg, own, before, after, values, w_in, w_out, cot)


def after_kernel(*refs):
    lists, (both_ref, values_ref, middle_ref) = refs[:4], refs[4:]
    depth = middle_ref.shape[0]
    middle_ref[...] = both_ref[:depth].astype(jnp.float32)
    add_slots(lists, OWN, both_ref.at[pl.ds(depth, depth)], middle_ref, values_ref, False)


def after_step(lists, both, values):
    return pl.pallas_call(
        after_kernel,
        out_shape=jax.ShapeDtypeStruct((both.shape[0] // 2, both.shape[1]), jnp.float32),
        in_specs=[SMEM] * 4 + [VMEM] * 2,
        out_specs=VMEM,
        compiler_params=pltpu.CompilerParams(vmem_limit_bytes=24 * 1024 * 1024),
        cost_estimate=pl.CostEstimate(flops=1 << 28, bytes_accessed=6 << 20, transcendentals=0),
    )(*lists, both, values)


def on_device(
    features, block_row, block_col, block_count, block_values, w_self, w_neigh, cotangent
):
    rows_part = features.shape[1]
    depth, width = cotangent.shape
    rim = REACH * BLK
    chunk = width // BLK
    pos = lax.axis_index("feat").astype(jnp.int32)[None]
    lists = list_step(block_row[0], block_col[0], block_count, pos, chunk)
    w_in = jnp.concatenate([w_self.T, w_neigh.T], axis=1)
    w_out = jnp.concatenate([w_self, w_neigh], axis=0)
    own = lax.all_to_all(features, "feat", split_axis=1, concat_axis=0, tiled=True)
    before = shifted(own[:, width - rim :], RING, 1)
    after = shifted(own[:, :rim], RING, -1)
    agg = before_step(lists, own, block_values)
    left, right, stacked, delta, both = local_step(
        lists, agg, own, before, after, block_values, w_in, w_out, cotangent
    )
    terms = jnp.einsum("in,on->io", stacked, delta, preferred_element_type=jnp.float32)
    plane, line = lax.axis_size(PLANE), lax.axis_size("feat")
    share = 2 * depth // plane
    from_next = shifted(left, RING, -1)
    parts = lax.all_to_all(terms, PLANE, split_axis=0, concat_axis=0, tiled=True)
    partial = parts.reshape(plane, share, depth).sum(0)
    partial, from_next, right, both = lax.optimization_barrier((partial, from_next, right, both))
    from_prev = shifted(right, RING, 1)
    middle = after_step(lists, both, block_values)
    copies = jnp.broadcast_to(partial[None], (line, share, depth))
    copies = lax.all_to_all(copies, "feat", split_axis=0, concat_axis=0, tiled=True)
    grads = copies.sum(0)
    total = middle + jnp.pad(from_prev.astype(jnp.float32), ((0, 0), (0, width - rim)))
    total = total + jnp.pad(from_next.astype(jnp.float32), ((0, 0), (width - rim, 0)))
    total = total.astype(jnp.bfloat16)
    total, grads = lax.optimization_barrier((total, grads))
    feature_grad = lax.all_to_all(total, "feat", split_axis=0, concat_axis=1, tiled=True)
    grads = grads + shifted(grads, "zh", 1)
    factor = 1.0 / math.sqrt(rows_part * lax.axis_size(DOM))
    grads = collected((grads * factor).astype(jnp.bfloat16))
    return (feature_grad, grads[:depth], grads[depth:])


def solution(mesh):
    fine = Mesh(mesh.devices.reshape(2, 4, 4, 2, 8), RING)
    return jax.shard_map(
        on_device,
        mesh=fine,
        in_specs=(
            P("feat", DOM),
            P(DOM, None),
            P(DOM, None),
            P(DOM),
            P(DOM, None, None),
            P(),
            P(),
            P(None, RING),
        ),
        out_specs=(P("feat", DOM), P(), P()),
        check_vma=False,
    )
```

time: 206 us -> 229 us (1.11)
  the two profiles are of different devices: /device:TPU:6 before, /device:TPU:64 now
where the time goes in v4:
time: 229 us; the launch traced here: 228 us
  waiting for transfers between devices  73.6 us (32%)
  blocking collectives  71.1 us (31%)
  starting transfers between devices  55.2 us (24%)
  local copies, waits for them, and re-layouts  13.8 us (6%)
  Pallas kernels  6.72 us (3%)
  other arithmetic  5.42 us (2%)
    all_to_all x1, blocking collectives, on_device(): lax.all_to_all(features, 'feat', split_axis=1, concat_axis=0, tiled=True)  52.2 us
    ppermute x5, waiting for transfers between devices, shifted(): lax.ppermute(shard, axis, [(i, (i + by) % count) for i in range(count)])  45.3 us
    ppermute x5, starting transfers between devices, shifted(): lax.ppermute(shard, axis, [(i, (i + by) % count) for i in range(count)])  21.4 us
    all_to_all x1, blocking collectives, on_device(): lax.all_to_all(terms, PLANE, split_axis=0, concat_axis=0, tiled=True)  18.9 us
    ppermute x5, waiting for transfers between devices, collected(): other = lax.ppermute(rows, axis, [(i, i ^ apart) for i in range(count)])  18.3 us
    all_to_all x1, starting transfers between devices, on_device(): lax.all_to_all(copies, 'feat', split_axis=0, concat_axis=0, tiled=True)  15.1 us
    ppermute x5, starting transfers between devices, collected(): other = lax.ppermute(rows, axis, [(i, i ^ apart) for i in range(count)])  12.2 us
    all_to_all x1, waiting for transfers between devices, on_device(): lax.all_to_all(copies, 'feat', split_axis=0, concat_axis=0, tiled=True)  9.96 us
  transfers between devices with their start and end apart: 12, of which 8 were waited for; matrix products, arithmetic and copies ran while one was open for 3% of the time, Pallas kernels for 1%

profile of v4, /device:TPU:64, one launch (start us, length us, event | category | flops | bytes accessed | tf_op | source)
XLA Modules:
  0.0 228.1 jit_solution(13248225641832372014)
XLA Ops:
  0.6 1.2 copy.22
  1.9 52.2 %all_to_all.52 = bf16[32,8,1664]{2,0,1:T(8,128)(2,1)S(1)} all-to-all(bf16[32,8,1664]{2,0,1:T(8,128)(2,1)S(1)} %bitcast.23), channel_id=1, replica_groups=mesh['zh'=2,'y'=4,'x'=4,'core'=2,'feat'=8] {'feat'}, dimensions={1} | all-to-all | bytes 1703936 | tf_op jit(solution)/shard_map/all_to_all | solution.py:214
  54.1 1.1 fusion
  55.2 2.4 %collective-permute-start = (bf16[256,1024]{1,0:T(8,128)(2,1)}, bf16[256,1024]{1,0:T(8,128)(2,1)S(1)}, u32[]{:S(2)}, u32[]{:S(2)}) collective-permute-start(bf16[256,1024]{1,0:T(8,128)(2,1)} %get-tuple-element.34), channel_id=1, source_target_pairs={{0,1},{1,2},{2,3},{3,4},{4,5},{5,6},{6,7},{7,8},{8,9},{9,10},{10,1... | collective-permute-start | bytes 1572872 | tf_op jit(solution)/shard_map/ppermute | solution.py:20
  57.6 3.5 %collective-permute-start.1 = (bf16[256,1024]{1,0:T(8,128)(2,1)}, bf16[256,1024]{1,0:T(8,128)(2,1)}, u32[]{:S(2)}, u32[]{:S(2)}) collective-permute-start(bf16[256,1024]{1,0:T(8,128)(2,1)} %get-tuple-element.33), channel_id=1, source_target_pairs={{0,511},{1,0},{2,1},{3,2},{4,3},{5,4},{6,5},{7,6},{8,7},{9,8},{10,... | collective-permute-start | bytes 1572872 | tf_op jit(solution)/shard_map/ppermute | solution.py:20
  61.7 1.7 copy.16
  63.4 1.7 copy.17
  65.0 1.4 shard_map.103
  71.8 10.8 %collective-permute-done.1.refs_7_ = bf16[256,1024]{1,0:T(8,128)(2,1)} collective-permute-done((bf16[256,1024]{1,0:T(8,128)(2,1)}, bf16[256,1024]{1,0:T(8,128)(2,1)}, u32[]{:S(2)}, u32[]{:S(2)}) %collective-permute-start.1) | collective-permute-done | bytes 524320 | tf_op jit(solution)/shard_map/ppermute | solution.py:20
  82.6 3.9 %shard_map.105 = (bf16[256,1024]{1,0:T(8,128)(2,1)}, bf16[256,1024]{1,0:T(8,128)(2,1)S(1)}, bf16[512,1664]{1,0:T(8,128)(2,1)S(1)}, bf16[256,1664]{1,0:T(8,128)(2,1)S(1)}, bf16[512,1664]{1,0:T(8,128)(2,1)S(1)}) custom-call(s32[3]{0:T(128)S(1)} %copy-done.12, s32[192]{0:T(256)S(1)} %copy-done.6, s32[192]{0:T(256)S(1)} %copy-done.8, s32[192]{0:T(256)S(1)} %copy-done.10, ...), custom_call_target="tpu_custom_call" | custom-call | flops 1308622848 | bytes 8388608 | tf_op jit(solution)/shard_map/pallas_call | solution.py:163
  86.6 1.2 copy-done.2
  87.8 2.6 %collective-permute-start.2 = (bf16[256,1024]{1,0:T(8,128)(2,1)}, bf16[256,1024]{1,0:T(8,128)(2,1)S(1)}, u32[]{:S(2)}, u32[]{:S(2)}) collective-permute-start(bf16[256,1024]{1,0:T(8,128)(2,1)} %get-tuple-element.24), channel_id=1, source_target_pairs={{0,511},{1,0},{2,1},{3,2},{4,3},{5,4},{6,5},{7,6},{8,7},{9,8},{10,... | collective-permute-start | bytes 1572872 | tf_op jit(solution)/shard_map/ppermute | solution.py:20
  91.1 18.9 %all_to_all.53 = f32[32,16,256]{2,1,0:T(8,128)S(1)} all-to-all(f32[32,16,256]{2,1,0:T(8,128)S(1)} %bitcast.26), channel_id=1, replica_groups=mesh['zh'=2,'y'=4,'x'=4,'core'=2,'feat'=8] {'y','x','core'}, dimensions={0} | all-to-all | bytes 1048576 | tf_op jit(solution)/shard_map/all_to_all | solution.py:225
  110.1 4.1 %collective-permute-start.3 = (bf16[256,1024]{1,0:T(8,128)(2,1)}, bf16[256,1024]{1,0:T(8,128)(2,1)S(1)}, u32[]{:S(2)}, u32[]{:S(2)}) collective-permute-start(bf16[256,1024]{1,0:T(8,128)(2,1)} %copy-done.13), channel_id=1, source_target_pairs={{0,1},{1,2},{2,3},{3,4},{4,5},{5,6},{6,7},{7,8},{8,9},{9,10},{10,1... | collective-permute-start | bytes 1572872 | tf_op jit(solution)/shard_map/ppermute | solution.py:20
  114.9 15.1 %all-to-all-start.2 = ((f32[8,16,256]{2,1,0:T(8,128)}), f32[8,16,256]{2,1,0:T(8,128)S(1)}, u32[]{:S(2)}, u32[]{:S(2)}) async-start(f32[8,16,256]{2,1,0:T(8,128)} %broadcast_in_dim.10), calls=%async_computation.2 | async-start | bytes 262144 | tf_op jit(solution)/shard_map/all_to_all | solution.py:231
  130.0 1.5 copy-done.3
  132.1 1.2 copy-done.1
  133.4 10.0 %all-to-all-done.2 = f32[8,16,256]{2,1,0:T(8,128)S(1)} async-done(((f32[8,16,256]{2,1,0:T(8,128)}), f32[8,16,256]{2,1,0:T(8,128)S(1)}, u32[]{:S(2)}, u32[]{:S(2)}) %all-to-all-start.2) | async-done | bytes 131104 | tf_op jit(solution)/shard_map/all_to_all | solution.py:231
  143.4 2.6 %add_convert_fusion = bf16[256,1664]{1,0:T(8,128)(2,1)} fusion(f32[256,1664]{1,0:T(8,128)} %copy-done.1, bf16[256,1024]{1,0:T(8,128)(2,1)S(1)} %collective-permute-done.2, bf16[256,1024]{1,0:T(8,128)(2,1)S(1)} %collective-permute-done.3), kind=kLoop, calls=%fused_computation | loop fusion | flops 2129920 | bytes 3604480 | tf_op jit(solution)/shard_map/convert_element_type | solution.py:235
  145.9 6.5 %all-to-all-start.3 = ((bf16[8,32,1664]{2,1,0:T(8,128)(2,1)}), bf16[8,32,1664]{2,1,0:T(8,128)(2,1)S(1)}, u32[]{:S(2)}, u32[]{:S(2)}) async-start(bf16[8,32,1664]{2,1,0:T(8,128)(2,1)} %bitcast.9), calls=%async_computation.3 | async-start | bytes 1703936 | tf_op jit(solution)/shard_map/all_to_all | solution.py:237
  152.4 8.8 %collective-permute-start.4 = (f32[16,256]{1,0:T(8,128)S(1)}, f32[16,256]{1,0:T(8,128)S(1)}, u32[]{:S(2)}, u32[]{:S(2)}) collective-permute-start(f32[16,256]{1,0:T(8,128)S(1)} %reduce_sum.19), channel_id=1, source_target_pairs={{0,256},{256,0},{1,257},{257,1},{2,258},{258,2},{3,259},{259,3},{4... | collective-permute-start | bytes 49160 | tf_op jit(solution)/shard_map/ppermute | solution.py:20
  161.2 34.5 %collective-permute-done.4 = f32[16,256]{1,0:T(8,128)S(1)} collective-permute-done((f32[16,256]{1,0:T(8,128)S(1)}, f32[16,256]{1,0:T(8,128)S(1)}, u32[]{:S(2)}, u32[]{:S(2)}) %collective-permute-start.4) | collective-permute-done | bytes 16416 | tf_op jit(solution)/shard_map/ppermute | solution.py:20
  195.7 1.9 collective-permute-start.5
  197.7 1.1 collective-permute-done.5
  198.8 2.5 %collective-permute-start.6 = (bf16[32,256]{1,0:T(8,128)(2,1)S(1)}, bf16[32,256]{1,0:T(8,128)(2,1)S(1)}, u32[]{:S(2)}, u32[]{:S(2)}) collective-permute-start(bf16[32,256]{1,0:T(8,128)(2,1)S(1)} %pad_maximum_fusion.5), channel_id=1, source_target_pairs={{0,16},{16,0},{32,48},{48,32},{1,17},{17,1},{33,49},{49,33},{2,18}... | collective-permute-start | bytes 49160 | tf_op jit(solution)/shard_map/ppermute | solution.py:28
  201.3 3.1 %collective-permute-done.6 = bf16[32,256]{1,0:T(8,128)(2,1)S(1)} collective-permute-done((bf16[32,256]{1,0:T(8,128)(2,1)S(1)}, bf16[32,256]{1,0:T(8,128)(2,1)S(1)}, u32[]{:S(2)}, u32[]{:S(2)}) %collective-permute-start.6) | collective-permute-done | bytes 16416 | tf_op jit(solution)/shard_map/ppermute | solution.py:28
  204.5 3.3 %collective-permute-start.7 = (bf16[64,256]{1,0:T(8,128)(2,1)S(1)}, bf16[64,256]{1,0:T(8,128)(2,1)S(1)}, u32[]{:S(2)}, u32[]{:S(2)}) collective-permute-start(bf16[64,256]{1,0:T(8,128)(2,1)S(1)} %pad_maximum_fusion.4), channel_id=1, source_target_pairs={{0,32},{16,48},{32,0},{48,16},{1,33},{17,49},{33,1},{49,17},{2,34}... | collective-permute-start | bytes 98312 | tf_op jit(solution)/shard_map/ppermute | solution.py:28
  207.7 4.0 %collective-permute-done.7 = bf16[64,256]{1,0:T(8,128)(2,1)S(1)} collective-permute-done((bf16[64,256]{1,0:T(8,128)(2,1)S(1)}, bf16[64,256]{1,0:T(8,128)(2,1)S(1)}, u32[]{:S(2)}, u32[]{:S(2)}) %collective-permute-start.7) | collective-permute-done | bytes 32800 | tf_op jit(solution)/shard_map/ppermute | solution.py:28
  211.8 1.9 collective-permute-start.8
  213.7 4.2 %collective-permute-done.8 = bf16[128,256]{1,0:T(8,128)(2,1)S(1)} collective-permute-done((bf16[128,256]{1,0:T(8,128)(2,1)S(1)}, bf16[128,256]{1,0:T(8,128)(2,1)S(1)}, u32[]{:S(2)}, u32[]{:S(2)}) %collective-permute-start.8) | collective-permute-done | bytes 65568 | tf_op jit(solution)/shard_map/ppermute | solution.py:28
  218.0 2.6 %collective-permute-start.9 = (bf16[256,256]{1,0:T(8,128)(2,1)S(1)}, bf16[256,256]{1,0:T(8,128)(2,1)S(1)}, u32[]{:S(2)}, u32[]{:S(2)}) collective-permute-start(bf16[256,256]{1,0:T(8,128)(2,1)S(1)} %pad_maximum_fusion.2), channel_id=1, source_target_pairs={{0,128},{64,192},{128,0},{192,64},{1,129},{65,193},{129,1},{193,65... | collective-permute-start | bytes 393224 | tf_op jit(solution)/shard_map/ppermute | solution.py:28
  220.6 5.7 %collective-permute-done.9 = bf16[256,256]{1,0:T(8,128)(2,1)S(1)} collective-permute-done((bf16[256,256]{1,0:T(8,128)(2,1)S(1)}, bf16[256,256]{1,0:T(8,128)(2,1)S(1)}, u32[]{:S(2)}, u32[]{:S(2)}) %collective-permute-start.9) | collective-permute-done | bytes 131104 | tf_op jit(solution)/shard_map/ppermute | solution.py:28
  (48 shorter events, 9.2 us)
Async XLA Ops:
  54.1 14.4 %copy-start = (bf16[64,128,128]{2,1,0:T(8,128)(2,1)S(1)}, bf16[64,128,128]{2,1,0:T(8,128)(2,1)}, u32[]{:S(2)}) copy-start(bf16[64,128,128]{2,1,0:T(8,128)(2,1)} %refs_5_.3) | copy-start | bytes 6291460
  55.2 16.6 %collective-permute-start = (bf16[256,1024]{1,0:T(8,128)(2,1)}, bf16[256,1024]{1,0:T(8,128)(2,1)S(1)}, u32[]{:S(2)}, u32[]{:S(2)}) collective-permute-start(bf16[256,1024]{1,0:T(8,128)(2,1)} %get-tuple-element.34), channel_id=1, source_target_pairs={{0,1},{1,2},{2,3},{3,4},{4,5},{5,6},{6,7},{7,8},{8,9},{9,10},{10,1... | collective-permute-start | bytes 1572872 | tf_op jit(solution)/shard_map/ppermute | solution.py:20
  57.6 25.0 %collective-permute-start.1 = (bf16[256,1024]{1,0:T(8,128)(2,1)}, bf16[256,1024]{1,0:T(8,128)(2,1)}, u32[]{:S(2)}, u32[]{:S(2)}) collective-permute-start(bf16[256,1024]{1,0:T(8,128)(2,1)} %get-tuple-element.33), channel_id=1, source_target_pairs={{0,511},{1,0},{2,1},{3,2},{4,3},{5,4},{6,5},{7,6},{8,7},{9,8},{10,... | collective-permute-start | bytes 1572872 | tf_op jit(solution)/shard_map/ppermute | solution.py:20
  68.4 0.7 copy-start.5
  69.1 0.7 copy-start.7
  69.8 0.7 copy-start.9
  70.4 0.6 copy-start.11
  71.0 11.6 %copy-start.4 = (bf16[256,1664]{1,0:T(8,128)(2,1)S(1)}, bf16[256,1664]{1,0:T(8,128)(2,1)}, u32[]{:S(2)}) copy-start(bf16[256,1664]{1,0:T(8,128)(2,1)} %refs_11_.1) | copy-start | bytes 2555908
  71.0 11.6 %copy-start.6 = (s32[192]{0:T(256)S(1)}, s32[192]{0:T(256)}, u32[]{:S(2)}) copy-start(s32[192]{0:T(256)} %get-tuple-element.19.refs_1_) | copy-start | bytes 2308
  71.1 11.6 %copy-start.8 = (s32[192]{0:T(256)S(1)}, s32[192]{0:T(256)}, u32[]{:S(2)}) copy-start(s32[192]{0:T(256)} %get-tuple-element.20.refs_2_) | copy-start | bytes 2308
  71.1 11.6 %copy-start.10 = (s32[192]{0:T(256)S(1)}, s32[192]{0:T(256)}, u32[]{:S(2)}) copy-start(s32[192]{0:T(256)} %get-tuple-element.21.refs_3_) | copy-start | bytes 2308
  71.1 11.6 %copy-start.12 = (s32[3]{0:T(128)S(1)}, s32[3]{0:T(128)}, u32[]{:S(2)}) copy-start(s32[3]{0:T(128)} %get-tuple-element.18.refs_0_) | copy-start | bytes 40
  86.6 1.2 copy-start.2
  87.8 3.3 %copy-start.13 = (bf16[256,1024]{1,0:T(8,128)(2,1)}, bf16[256,1024]{1,0:T(8,128)(2,1)S(1)}, u32[]{:S(2)}) copy-start(bf16[256,1024]{1,0:T(8,128)(2,1)S(1)} %get-tuple-element.28) | copy-start | bytes 1572868
  87.8 22.3 %collective-permute-start.2 = (bf16[256,1024]{1,0:T(8,128)(2,1)}, bf16[256,1024]{1,0:T(8,128)(2,1)S(1)}, u32[]{:S(2)}, u32[]{:S(2)}) collective-permute-start(bf16[256,1024]{1,0:T(8,128)(2,1)} %get-tuple-element.24), channel_id=1, source_target_pairs={{0,511},{1,0},{2,1},{3,2},{4,3},{5,4},{6,5},{7,6},{8,7},{9,8},{10,... | collective-permute-start | bytes 1572872 | tf_op jit(solution)/shard_map/ppermute | solution.py:20
  110.1 33.3 %collective-permute-start.3 = (bf16[256,1024]{1,0:T(8,128)(2,1)}, bf16[256,1024]{1,0:T(8,128)(2,1)S(1)}, u32[]{:S(2)}, u32[]{:S(2)}) collective-permute-start(bf16[256,1024]{1,0:T(8,128)(2,1)} %copy-done.13), channel_id=1, source_target_pairs={{0,1},{1,2},{2,3},{3,4},{4,5},{5,6},{6,7},{7,8},{8,9},{9,10},{10,1... | collective-permute-start | bytes 1572872 | tf_op jit(solution)/shard_map/ppermute | solution.py:20
  114.9 28.5 %all-to-all-start.2 = ((f32[8,16,256]{2,1,0:T(8,128)}), f32[8,16,256]{2,1,0:T(8,128)S(1)}, u32[]{:S(2)}, u32[]{:S(2)}) async-start(f32[8,16,256]{2,1,0:T(8,128)} %broadcast_in_dim.10), calls=%async_computation.2 | async-start | bytes 262144 | tf_op jit(solution)/shard_map/all_to_all | solution.py:231
  130.0 1.5 copy-start.3
  132.1 1.2 copy-start.1
  145.9 81.2 %all-to-all-start.3 = ((bf16[8,32,1664]{2,1,0:T(8,128)(2,1)}), bf16[8,32,1664]{2,1,0:T(8,128)(2,1)S(1)}, u32[]{:S(2)}, u32[]{:S(2)}) async-start(bf16[8,32,1664]{2,1,0:T(8,128)(2,1)} %bitcast.9), calls=%async_computation.3 | async-start | bytes 1703936 | tf_op jit(solution)/shard_map/all_to_all | solution.py:237
  152.4 43.4 %collective-permute-start.4 = (f32[16,256]{1,0:T(8,128)S(1)}, f32[16,256]{1,0:T(8,128)S(1)}, u32[]{:S(2)}, u32[]{:S(2)}) collective-permute-start(f32[16,256]{1,0:T(8,128)S(1)} %reduce_sum.19), channel_id=1, source_target_pairs={{0,256},{256,0},{1,257},{257,1},{2,258},{258,2},{3,259},{259,3},{4... | collective-permute-start | bytes 49160 | tf_op jit(solution)/shard_map/ppermute | solution.py:20
  195.7 3.1 %collective-permute-start.5 = (bf16[16,256]{1,0:T(8,128)(2,1)S(1)}, bf16[16,256]{1,0:T(8,128)(2,1)S(1)}, u32[]{:S(2)}, u32[]{:S(2)}) collective-permute-start(bf16[16,256]{1,0:T(8,128)(2,1)S(1)} %multiply_convert_fusion), channel_id=1, source_target_pairs={{0,8},{8,0},{1,9},{9,1},{2,10},{10,2},{3,11},{11,3},{4,12},{12,4},... | collective-permute-start | bytes 24584 | tf_op jit(solution)/shard_map/ppermute | solution.py:28
  198.8 5.6 %collective-permute-start.6 = (bf16[32,256]{1,0:T(8,128)(2,1)S(1)}, bf16[32,256]{1,0:T(8,128)(2,1)S(1)}, u32[]{:S(2)}, u32[]{:S(2)}) collective-permute-start(bf16[32,256]{1,0:T(8,128)(2,1)S(1)} %pad_maximum_fusion.5), channel_id=1, source_target_pairs={{0,16},{16,0},{32,48},{48,32},{1,17},{17,1},{33,49},{49,33},{2,18}... | collective-permute-start | bytes 49160 | tf_op jit(solution)/shard_map/ppermute | solution.py:28
  204.5 7.3 %collective-permute-start.7 = (bf16[64,256]{1,0:T(8,128)(2,1)S(1)}, bf16[64,256]{1,0:T(8,128)(2,1)S(1)}, u32[]{:S(2)}, u32[]{:S(2)}) collective-permute-start(bf16[64,256]{1,0:T(8,128)(2,1)S(1)} %pad_maximum_fusion.4), channel_id=1, source_target_pairs={{0,32},{16,48},{32,0},{48,16},{1,33},{17,49},{33,1},{49,17},{2,34}... | collective-permute-start | bytes 98312 | tf_op jit(solution)/shard_map/ppermute | solution.py:28
  211.8 6.2 %collective-permute-start.8 = (bf16[128,256]{1,0:T(8,128)(2,1)S(1)}, bf16[128,256]{1,0:T(8,128)(2,1)S(1)}, u32[]{:S(2)}, u32[]{:S(2)}) collective-permute-start(bf16[128,256]{1,0:T(8,128)(2,1)S(1)} %pad_maximum_fusion.3), channel_id=1, source_target_pairs={{0,64},{64,0},{128,192},{192,128},{1,65},{65,1},{129,193},{193,129... | collective-permute-start | bytes 196616 | tf_op jit(solution)/shard_map/ppermute | solution.py:28
  218.0 8.4 %collective-permute-start.9 = (bf16[256,256]{1,0:T(8,128)(2,1)S(1)}, bf16[256,256]{1,0:T(8,128)(2,1)S(1)}, u32[]{:S(2)}, u32[]{:S(2)}) collective-permute-start(bf16[256,256]{1,0:T(8,128)(2,1)S(1)} %pad_maximum_fusion.2), channel_id=1, source_target_pairs={{0,128},{64,192},{128,0},{192,64},{1,129},{65,193},{129,1},{193,65... | collective-permute-start | bytes 393224 | tf_op jit(solution)/shard_map/ppermute | solution.py:28

commit v5 on v4

--- a/solution.py
+++ b/solution.py
@@ -12,6 +12,7 @@
 REACH = 8
 DOM = ("zh", "y", "x", "core")
 PLANE = ("y", "x", "core")
+LINE = ("zh", "feat")
 RING = DOM + ("feat",)
 
 
@@ -200,6 +201,30 @@
     )(*lists, both, values)
 
 
+def total_kernel(middle_ref, prev_ref, next_ref, out_ref):
+    width, rim = middle_ref.shape[1], prev_ref.shape[1]
+    edges = sorted({0, min(rim, width - rim), max(rim, width - rim), width})
+    for at, end in zip(edges, edges[1:]):
+        part = middle_ref[:, at:end]
+        if at < rim:
+            part = part + prev_ref[:, at:end].astype(jnp.float32)
+        if at >= width - rim:
+            here = at - (width - rim)
+            part = part + next_ref[:, here : here + end - at].astype(jnp.float32)
+        out_ref[:, at:end] = part.astype(jnp.bfloat16)
+
+
+def total_step(middle, from_prev, from_next):
+    return pl.pallas_call(
+        total_kernel,
+        out_shape=jax.ShapeDtypeStruct(middle.shape, jnp.bfloat16),
+        in_specs=[VMEM] * 3,
+        out_specs=VMEM,
+        compiler_params=pltpu.CompilerParams(vmem_limit_bytes=24 * 1024 * 1024),
+        cost_estimate=pl.CostEstimate(flops=0, bytes_accessed=4 << 20, transcendentals=0),
+    )(middle, from_prev, from_next)
+
+
 def on_device(
     features, block_row, block_col, block_count, block_values, w_self, w_neigh, cotangent
 ):
@@ -219,25 +244,24 @@
         lists, agg, own, before, after, block_values, w_in, w_out, cotangent
     )
     terms = jnp.einsum("in,on->io", stacked, delta, preferred_element_type=jnp.float32)
-    plane, line = lax.axis_size(PLANE), lax.axis_size("feat")
+    plane, line = lax.axis_size(PLANE), lax.axis_size(LINE)
     share = 2 * depth // plane
     from_next = shifted(left, RING, -1)
+    from_prev = shifted(right, RING, 1)
     parts = lax.all_to_all(terms, PLANE, split_axis=0, concat_axis=0, tiled=True)
-    partial = parts.reshape(plane, share, depth).sum(0)
-    partial, from_next, right, both = lax.optimization_barrier((partial, from_next, right, both))
-    from_prev = shifted(right, RING, 1)
-    middle = after_step(lists, both, block_values)
+    partial = parts.reshape(plane, share, depth).sum(0).astype(jnp.bfloat16)
+    partial, from_next, from_prev, used = lax.optimization_barrier(
+        (partial, from_next, from_prev, lists[0])
+    )
+    middle = after_step([used, *lists[1:]], both, block_values)
     copies = jnp.broadcast_to(partial[None], (line, share, depth))
-    copies = lax.all_to_all(copies, "feat", split_axis=0, concat_axis=0, tiled=True)
-    grads = copies.sum(0)
-    total = middle + jnp.pad(from_prev.astype(jnp.float32), ((0, 0), (0, width - rim)))
-    total = total + jnp.pad(from_next.astype(jnp.float32), ((0, 0), (width - rim, 0)))
-    total = total.astype(jnp.bfloat16)
-    total, grads = lax.optimization_barrier((total, grads))
+    copies = lax.all_to_all(copies, LINE, split_axis=0, concat_axis=0, tiled=True)
+    factor = 1.0 / math.sqrt(rows_part * lax.axis_size(DOM))
+    grads = copies.reshape(line, share, depth).astype(jnp.float32).sum(0) * factor
+    total = total_step(middle, from_prev, from_next)
+    total, grads = lax.optimization_barrier((total, grads.astype(jnp.bfloat16)))
     feature_grad = lax.all_to_all(total, "feat", split_axis=0, concat_axis=1, tiled=True)
-    grads = grads + shifted(grads, "zh", 1)
-    factor = 1.0 / math.sqrt(rows_part * lax.axis_size(DOM))
-    grads = collected((grads * factor).astype(jnp.bfloat16))
+    grads = collected(grads)
     return (feature_grad, grads[:depth], grads[depth:])
 
 

time: 229 us -> 197 us (0.86)
  the two profiles are of different devices: /device:TPU:64 before, /device:TPU:6 now
where the time goes in v5:
time: 197 us; the launch traced here: 195 us
  blocking collectives  74.3 us (38%)
  starting transfers between devices  49.4 us (25%)
  waiting for transfers between devices  43.3 us (22%)
  local copies, waits for them, and re-layouts  12.5 us (6%)
  Pallas kernels  9.72 us (5%)
  other arithmetic  3.92 us (2%)
    all_to_all x1, blocking collectives, on_device(): lax.all_to_all(features, 'feat', split_axis=1, concat_axis=0, tiled=True)  55.1 us
    ppermute x4, starting transfers between devices, shifted(): lax.ppermute(shard, axis, [(i, (i + by) % count) for i in range(count)])  22.2 us
    all_to_all x1, blocking collectives, on_device(): lax.all_to_all(terms, PLANE, split_axis=0, concat_axis=0, tiled=True)  19.2 us
    ppermute x5, waiting for transfers between devices, collected(): other = lax.ppermute(rows, axis, [(i, i ^ apart) for i in range(count)])  17.7 us
    ppermute x5, starting transfers between devices, collected(): other = lax.ppermute(rows, axis, [(i, i ^ apart) for i in range(count)])  12.8 us
    all_to_all x1, waiting for transfers between devices, on_device(): lax.all_to_all(total, 'feat', split_axis=0, concat_axis=1, tiled=True)  11.5 us
    all_to_all x1, waiting for transfers between devices, on_device(): lax.all_to_all(copies, LINE, split_axis=0, concat_axis=0, tiled=True)  10.3 us
    all_to_all x1, starting transfers between devices, on_device(): lax.all_to_all(copies, LINE, split_axis=0, concat_axis=0, tiled=True)  8.99 us
  transfers between devices with their start and end apart: 11, of which 9 were waited for; matrix products, arithmetic and copies ran while one was open for 4% of the time, Pallas kernels for 3%

profile of v5, /device:TPU:6, one launch (start us, length us, event | category | flops | bytes accessed | tf_op | source)
XLA Modules:
  0.0 195.4 jit_solution(3931242584701051819)
XLA Ops:
  0.6 1.2 copy.22
  1.9 55.1 %all_to_all.52 = bf16[32,8,1664]{2,0,1:T(8,128)(2,1)S(1)} all-to-all(bf16[32,8,1664]{2,0,1:T(8,128)(2,1)S(1)} %bitcast.23), channel_id=1, replica_groups=mesh['zh'=2,'y'=4,'x'=4,'core'=2,'feat'=8] {'feat'}, dimensions={1} | all-to-all | bytes 1703936 | tf_op jit(solution)/shard_map/all_to_all | solution.py:239
  57.0 1.1 fusion
  58.1 2.4 %collective-permute-start = (bf16[256,1024]{1,0:T(8,128)(2,1)}, bf16[256,1024]{1,0:T(8,128)(2,1)S(1)}, u32[]{:S(2)}, u32[]{:S(2)}) collective-permute-start(bf16[256,1024]{1,0:T(8,128)(2,1)} %get-tuple-element.34), channel_id=1, source_target_pairs={{0,1},{1,2},{2,3},{3,4},{4,5},{5,6},{6,7},{7,8},{8,9},{9,10},{10,1... | collective-permute-start | bytes 1572872 | tf_op jit(solution)/shard_map/ppermute | solution.py:21
  60.5 10.7 %collective-permute-start.1 = (bf16[256,1024]{1,0:T(8,128)(2,1)}, bf16[256,1024]{1,0:T(8,128)(2,1)}, u32[]{:S(2)}, u32[]{:S(2)}) collective-permute-start(bf16[256,1024]{1,0:T(8,128)(2,1)} %get-tuple-element.33), channel_id=1, source_target_pairs={{0,511},{1,0},{2,1},{3,2},{4,3},{5,4},{6,5},{7,6},{8,7},{9,8},{10,... | collective-permute-start | bytes 1572872 | tf_op jit(solution)/shard_map/ppermute | solution.py:21
  71.8 1.7 copy.16
  73.5 1.7 copy.17
  75.1 2.1 %shard_map.103 = (s32[3]{0:T(128)}, s32[192]{0:T(256)}, s32[192]{0:T(256)}, s32[192]{0:T(256)}) custom-call(s32[64]{0:T(128)} %bitcast.29, s32[64]{0:T(128)} %bitcast.30, s32[1]{0:T(128)S(6)} %copy.23.count_ref, s32[1]{0:T(128)} %bitcast.2.pos_ref), custom_call_target="tpu_custom_call" | custom-call | bytes 4096 | tf_op jit(solution)/shard_map/pallas_call | solution.py:74
  81.7 1.1 shard_map.104.refs_4_
  82.9 2.7 %collective-permute-done.1.refs_7_ = bf16[256,1024]{1,0:T(8,128)(2,1)} collective-permute-done((bf16[256,1024]{1,0:T(8,128)(2,1)}, bf16[256,1024]{1,0:T(8,128)(2,1)}, u32[]{:S(2)}, u32[]{:S(2)}) %collective-permute-start.1) | collective-permute-done | bytes 524320 | tf_op jit(solution)/shard_map/ppermute | solution.py:21
  85.7 4.4 %shard_map.105 = (bf16[256,1024]{1,0:T(8,128)(2,1)}, bf16[256,1024]{1,0:T(8,128)(2,1)}, bf16[512,1664]{1,0:T(8,128)(2,1)S(1)}, bf16[256,1664]{1,0:T(8,128)(2,1)S(1)}, bf16[512,1664]{1,0:T(8,128)(2,1)S(1)}) custom-call(s32[3]{0:T(128)S(1)} %copy-done.11, s32[192]{0:T(256)S(1)} %copy-done.5, s32[192]{0:T(256)S(1)} %copy-done.7, s32[192]{0:T(256)S(1)} %copy-done.9, ...), custom_call_target="tpu_custom_call" | custom-call | flops 1308622848 | bytes 8388608 | tf_op jit(solution)/shard_map/pallas_call | solution.py:164
  90.0 1.2 copy-done.1
  91.3 7.2 %collective-permute-start.2 = (bf16[256,1024]{1,0:T(8,128)(2,1)}, bf16[256,1024]{1,0:T(8,128)(2,1)S(1)}, u32[]{:S(2)}, u32[]{:S(2)}) collective-permute-start(bf16[256,1024]{1,0:T(8,128)(2,1)} %get-tuple-element.24), channel_id=1, source_target_pairs={{0,511},{1,0},{2,1},{3,2},{4,3},{5,4},{6,5},{7,6},{8,7},{9,8},{10,... | collective-permute-start | bytes 1572872 | tf_op jit(solution)/shard_map/ppermute | solution.py:21
  98.5 1.9 collective-permute-start.3
  101.1 19.2 %all_to_all.53 = f32[32,16,256]{2,1,0:T(8,128)} all-to-all(f32[32,16,256]{2,1,0:T(8,128)S(1)} %bitcast.26), channel_id=1, replica_groups=mesh['zh'=2,'y'=4,'x'=4,'core'=2,'feat'=8] {'y','x','core'}, dimensions={0} | all-to-all | bytes 1048576 | tf_op jit(solution)/shard_map/all_to_all | solution.py:251
  120.3 1.1 reduce_sum.18
  121.4 1.2 collective-permute-done.3.prev_ref
  123.2 9.0 %all-to-all-start.2 = ((bf16[16,16,256]{2,1,0:T(8,128)(2,1)}), bf16[16,16,256]{2,1,0:T(8,128)(2,1)S(1)}, u32[]{:S(2)}, u32[]{:S(2)}) async-start(bf16[16,16,256]{2,1,0:T(8,128)(2,1)} %broadcast_in_dim.10), calls=%async_computation.2 | async-start | bytes 262144 | tf_op jit(solution)/shard_map/all_to_all | solution.py:258
  132.2 1.4 copy-done.2
  135.8 10.3 %all-to-all-done.2 = bf16[16,16,256]{2,1,0:T(8,128)(2,1)S(1)} async-done(((bf16[16,16,256]{2,1,0:T(8,128)(2,1)}), bf16[16,16,256]{2,1,0:T(8,128)(2,1)S(1)}, u32[]{:S(2)}, u32[]{:S(2)}) %all-to-all-start.2) | async-done | bytes 131104 | tf_op jit(solution)/shard_map/all_to_all | solution.py:258
  146.1 5.5 %all-to-all-start.3 = ((bf16[8,32,1664]{2,1,0:T(8,128)(2,1)}), bf16[8,32,1664]{2,1,0:T(8,128)(2,1)S(1)}, u32[]{:S(2)}, u32[]{:S(2)}) async-start(bf16[8,32,1664]{2,1,0:T(8,128)(2,1)} %bitcast.9), calls=%async_computation.3 | async-start | bytes 1703936 | tf_op jit(solution)/shard_map/all_to_all | solution.py:263
  151.6 1.9 collective-permute-start.4
  153.5 1.1 collective-permute-done.4
  154.6 1.9 collective-permute-start.5
  156.6 3.7 %collective-permute-done.5 = bf16[32,256]{1,0:T(8,128)(2,1)S(1)} collective-permute-done((bf16[32,256]{1,0:T(8,128)(2,1)S(1)}, bf16[32,256]{1,0:T(8,128)(2,1)S(1)}, u32[]{:S(2)}, u32[]{:S(2)}) %collective-permute-start.5) | collective-permute-done | bytes 16416 | tf_op jit(solution)/shard_map/ppermute | solution.py:29
  160.3 3.8 %collective-permute-start.6 = (bf16[64,256]{1,0:T(8,128)(2,1)S(1)}, bf16[64,256]{1,0:T(8,128)(2,1)S(1)}, u32[]{:S(2)}, u32[]{:S(2)}) collective-permute-start(bf16[64,256]{1,0:T(8,128)(2,1)S(1)} %pad_maximum_fusion.4), channel_id=1, source_target_pairs={{0,32},{16,48},{32,0},{48,16},{1,33},{17,49},{33,1},{49,17},{2,34}... | collective-permute-start | bytes 98312 | tf_op jit(solution)/shard_map/ppermute | solution.py:29
  164.1 3.5 %collective-permute-done.6 = bf16[64,256]{1,0:T(8,128)(2,1)S(1)} collective-permute-done((bf16[64,256]{1,0:T(8,128)(2,1)S(1)}, bf16[64,256]{1,0:T(8,128)(2,1)S(1)}, u32[]{:S(2)}, u32[]{:S(2)}) %collective-permute-start.6) | collective-permute-done | bytes 32800 | tf_op jit(solution)/shard_map/ppermute | solution.py:29
  167.6 2.5 %collective-permute-start.7 = (bf16[128,256]{1,0:T(8,128)(2,1)S(1)}, bf16[128,256]{1,0:T(8,128)(2,1)S(1)}, u32[]{:S(2)}, u32[]{:S(2)}) collective-permute-start(bf16[128,256]{1,0:T(8,128)(2,1)S(1)} %pad_maximum_fusion.3), channel_id=1, source_target_pairs={{0,64},{64,0},{128,192},{192,128},{1,65},{65,1},{129,193},{193,129... | collective-permute-start | bytes 196616 | tf_op jit(solution)/shard_map/ppermute | solution.py:29
  170.2 3.6 %collective-permute-done.7 = bf16[128,256]{1,0:T(8,128)(2,1)S(1)} collective-permute-done((bf16[128,256]{1,0:T(8,128)(2,1)S(1)}, bf16[128,256]{1,0:T(8,128)(2,1)S(1)}, u32[]{:S(2)}, u32[]{:S(2)}) %collective-permute-start.7) | collective-permute-done | bytes 65568 | tf_op jit(solution)/shard_map/ppermute | solution.py:29
  173.9 2.6 %collective-permute-start.8 = (bf16[256,256]{1,0:T(8,128)(2,1)S(1)}, bf16[256,256]{1,0:T(8,128)(2,1)S(1)}, u32[]{:S(2)}, u32[]{:S(2)}) collective-permute-start(bf16[256,256]{1,0:T(8,128)(2,1)S(1)} %pad_maximum_fusion.2), channel_id=1, source_target_pairs={{0,128},{64,192},{128,0},{192,64},{1,129},{65,193},{129,1},{193,65... | collective-permute-start | bytes 393224 | tf_op jit(solution)/shard_map/ppermute | solution.py:29
  176.5 5.7 %collective-permute-done.8 = bf16[256,256]{1,0:T(8,128)(2,1)S(1)} collective-permute-done((bf16[256,256]{1,0:T(8,128)(2,1)S(1)}, bf16[256,256]{1,0:T(8,128)(2,1)S(1)}, u32[]{:S(2)}, u32[]{:S(2)}) %collective-permute-start.8) | collective-permute-done | bytes 131104 | tf_op jit(solution)/shard_map/ppermute | solution.py:29
  183.0 11.5 %all-to-all-done.3 = bf16[8,32,1664]{2,1,0:T(8,128)(2,1)S(1)} async-done(((bf16[8,32,1664]{2,1,0:T(8,128)(2,1)}), bf16[8,32,1664]{2,1,0:T(8,128)(2,1)S(1)}, u32[]{:S(2)}, u32[]{:S(2)}) %all-to-all-start.3) | async-done | bytes 852000 | tf_op jit(solution)/shard_map/all_to_all | solution.py:263
  (42 shorter events, 9.8 us)
Async XLA Ops:
  56.9 22.2 %copy-start = (bf16[64,128,128]{2,1,0:T(8,128)(2,1)S(1)}, bf16[64,128,128]{2,1,0:T(8,128)(2,1)}, u32[]{:S(2)}) copy-start(bf16[64,128,128]{2,1,0:T(8,128)(2,1)} %refs_5_.3) | copy-start | bytes 6291460
  58.1 24.8 %collective-permute-start = (bf16[256,1024]{1,0:T(8,128)(2,1)}, bf16[256,1024]{1,0:T(8,128)(2,1)S(1)}, u32[]{:S(2)}, u32[]{:S(2)}) collective-permute-start(bf16[256,1024]{1,0:T(8,128)(2,1)} %get-tuple-element.34), channel_id=1, source_target_pairs={{0,1},{1,2},{2,3},{3,4},{4,5},{5,6},{6,7},{7,8},{8,9},{9,10},{10,1... | collective-permute-start | bytes 1572872 | tf_op jit(solution)/shard_map/ppermute | solution.py:21
  60.5 25.2 %collective-permute-start.1 = (bf16[256,1024]{1,0:T(8,128)(2,1)}, bf16[256,1024]{1,0:T(8,128)(2,1)}, u32[]{:S(2)}, u32[]{:S(2)}) collective-permute-start(bf16[256,1024]{1,0:T(8,128)(2,1)} %get-tuple-element.33), channel_id=1, source_target_pairs={{0,511},{1,0},{2,1},{3,2},{4,3},{5,4},{6,5},{7,6},{8,7},{9,8},{10,... | collective-permute-start | bytes 1572872 | tf_op jit(solution)/shard_map/ppermute | solution.py:21
  79.2 0.7 copy-start.4
  79.9 0.7 copy-start.6
  80.5 0.6 copy-start.8
  81.1 0.6 copy-start.10
  81.7 3.9 %copy-start.3 = (bf16[256,1664]{1,0:T(8,128)(2,1)S(1)}, bf16[256,1664]{1,0:T(8,128)(2,1)}, u32[]{:S(2)}) copy-start(bf16[256,1664]{1,0:T(8,128)(2,1)} %refs_11_.1) | copy-start | bytes 2555908
  81.7 3.9 %copy-start.5 = (s32[192]{0:T(256)S(1)}, s32[192]{0:T(256)}, u32[]{:S(2)}) copy-start(s32[192]{0:T(256)} %get-tuple-element.19.refs_1_) | copy-start | bytes 2308
  81.7 3.9 %copy-start.7 = (s32[192]{0:T(256)S(1)}, s32[192]{0:T(256)}, u32[]{:S(2)}) copy-start(s32[192]{0:T(256)} %get-tuple-element.20.refs_2_) | copy-start | bytes 2308
  81.7 3.9 %copy-start.9 = (s32[192]{0:T(256)S(1)}, s32[192]{0:T(256)}, u32[]{:S(2)}) copy-start(s32[192]{0:T(256)} %get-tuple-element.21.refs_3_) | copy-start | bytes 2308
  81.7 3.9 %copy-start.11 = (s32[3]{0:T(128)S(1)}, s32[3]{0:T(128)}, u32[]{:S(2)}) copy-start(s32[3]{0:T(128)} %get-tuple-element.26.refs_0_) | copy-start | bytes 40
  90.0 1.2 copy-start.1
  91.3 30.1 %collective-permute-start.2 = (bf16[256,1024]{1,0:T(8,128)(2,1)}, bf16[256,1024]{1,0:T(8,128)(2,1)S(1)}, u32[]{:S(2)}, u32[]{:S(2)}) collective-permute-start(bf16[256,1024]{1,0:T(8,128)(2,1)} %get-tuple-element.24), channel_id=1, source_target_pairs={{0,511},{1,0},{2,1},{3,2},{4,3},{5,4},{6,5},{7,6},{8,7},{9,8},{10,... | collective-permute-start | bytes 1572872 | tf_op jit(solution)/shard_map/ppermute | solution.py:21
  98.5 24.1 %collective-permute-start.3 = (bf16[256,1024]{1,0:T(8,128)(2,1)}, bf16[256,1024]{1,0:T(8,128)(2,1)S(1)}, u32[]{:S(2)}, u32[]{:S(2)}) collective-permute-start(bf16[256,1024]{1,0:T(8,128)(2,1)} %get-tuple-element.25), channel_id=1, source_target_pairs={{0,1},{1,2},{2,3},{3,4},{4,5},{5,6},{6,7},{7,8},{8,9},{9,10},{10,1... | collective-permute-start | bytes 1572872 | tf_op jit(solution)/shard_map/ppermute | solution.py:21
  123.2 22.9 %all-to-all-start.2 = ((bf16[16,16,256]{2,1,0:T(8,128)(2,1)}), bf16[16,16,256]{2,1,0:T(8,128)(2,1)S(1)}, u32[]{:S(2)}, u32[]{:S(2)}) async-start(bf16[16,16,256]{2,1,0:T(8,128)(2,1)} %broadcast_in_dim.10), calls=%async_computation.2 | async-start | bytes 262144 | tf_op jit(solution)/shard_map/all_to_all | solution.py:258
  132.2 1.5 copy-start.2
  146.1 48.3 %all-to-all-start.3 = ((bf16[8,32,1664]{2,1,0:T(8,128)(2,1)}), bf16[8,32,1664]{2,1,0:T(8,128)(2,1)S(1)}, u32[]{:S(2)}, u32[]{:S(2)}) async-start(bf16[8,32,1664]{2,1,0:T(8,128)(2,1)} %bitcast.9), calls=%async_computation.3 | async-start | bytes 1703936 | tf_op jit(solution)/shard_map/all_to_all | solution.py:263
  151.6 3.1 %collective-permute-start.4 = (bf16[16,256]{1,0:T(8,128)(2,1)S(1)}, bf16[16,256]{1,0:T(8,128)(2,1)S(1)}, u32[]{:S(2)}, u32[]{:S(2)}) collective-permute-start(bf16[16,256]{1,0:T(8,128)(2,1)S(1)} %multiply_convert_fusion), channel_id=1, source_target_pairs={{0,8},{8,0},{1,9},{9,1},{2,10},{10,2},{3,11},{11,3},{4,12},{12,4},... | collective-permute-start | bytes 24584 | tf_op jit(solution)/shard_map/ppermute | solution.py:29
  154.6 5.6 %collective-permute-start.5 = (bf16[32,256]{1,0:T(8,128)(2,1)S(1)}, bf16[32,256]{1,0:T(8,128)(2,1)S(1)}, u32[]{:S(2)}, u32[]{:S(2)}) collective-permute-start(bf16[32,256]{1,0:T(8,128)(2,1)S(1)} %pad_maximum_fusion.5), channel_id=1, source_target_pairs={{0,16},{16,0},{32,48},{48,32},{1,17},{17,1},{33,49},{49,33},{2,18}... | collective-permute-start | bytes 49160 | tf_op jit(solution)/shard_map/ppermute | solution.py:29
  160.3 7.3 %collective-permute-start.6 = (bf16[64,256]{1,0:T(8,128)(2,1)S(1)}, bf16[64,256]{1,0:T(8,128)(2,1)S(1)}, u32[]{:S(2)}, u32[]{:S(2)}) collective-permute-start(bf16[64,256]{1,0:T(8,128)(2,1)S(1)} %pad_maximum_fusion.4), channel_id=1, source_target_pairs={{0,32},{16,48},{32,0},{48,16},{1,33},{17,49},{33,1},{49,17},{2,34}... | collective-permute-start | bytes 98312 | tf_op jit(solution)/shard_map/ppermute | solution.py:29
  167.6 6.2 %collective-permute-start.7 = (bf16[128,256]{1,0:T(8,128)(2,1)S(1)}, bf16[128,256]{1,0:T(8,128)(2,1)S(1)}, u32[]{:S(2)}, u32[]{:S(2)}) collective-permute-start(bf16[128,256]{1,0:T(8,128)(2,1)S(1)} %pad_maximum_fusion.3), channel_id=1, source_target_pairs={{0,64},{64,0},{128,192},{192,128},{1,65},{65,1},{129,193},{193,129... | collective-permute-start | bytes 196616 | tf_op jit(solution)/shard_map/ppermute | solution.py:29
  173.9 8.4 %collective-permute-start.8 = (bf16[256,256]{1,0:T(8,128)(2,1)S(1)}, bf16[256,256]{1,0:T(8,128)(2,1)S(1)}, u32[]{:S(2)}, u32[]{:S(2)}) collective-permute-start(bf16[256,256]{1,0:T(8,128)(2,1)S(1)} %pad_maximum_fusion.2), channel_id=1, source_target_pairs={{0,128},{64,192},{128,0},{192,64},{1,129},{65,193},{129,1},{193,65... | collective-permute-start | bytes 393224 | tf_op jit(solution)/shard_map/ppermute | solution.py:29

commit v6 on v5

--- a/solution.py
+++ b/solution.py
@@ -41,6 +41,7 @@
 
 SMEM = pl.BlockSpec(memory_space=pltpu.SMEM)
 VMEM = pl.BlockSpec(memory_space=pltpu.VMEM)
+HBM = pl.BlockSpec(memory_space=pltpu.HBM)
 LEFT, OWN, RIGHT = range(3)
 
 
@@ -136,7 +137,7 @@
 def local_kernel(*refs):
     lists = refs[:4]
     (agg_ref, own_ref, before_ref, after_ref, values_ref, w_in_ref, w_out_ref, cot_ref) = refs[4:12]
-    left_ref, right_ref, stacked, delta, both_ref, agg, scat = refs[12:]
+    terms_ref, both_ref, stacked, delta, agg, held, terms, sems = refs[12:]
     depth, width = own_ref.shape
     agg[...] = agg_ref[...]
     add_slots(lists, LEFT, before_ref, agg, values_ref, True)
@@ -150,31 +151,62 @@
         slope = sigma * (1.0 + preact * (1.0 - sigma))
         delta[:, part] = (cot_ref[:, part].astype(jnp.float32) * slope).astype(jnp.bfloat16)
         both = jnp.dot(w_out_ref[...], delta[:, part], preferred_element_type=jnp.float32)
-        both_ref[:, part] = both.astype(jnp.bfloat16)
-    agg_grad = both_ref.at[pl.ds(depth, depth)]
+        held[:, part] = both.astype(jnp.bfloat16)
+    first = pltpu.make_async_copy(held, both_ref, sems.at[0])
+    first.start()
+    terms[...] = lax.dot_general(
+        stacked[...], delta[...], (((1,), (1,)), ((), ())), preferred_element_type=jnp.float32
+    )
+    second = pltpu.make_async_copy(terms, terms_ref, sems.at[1])
+    second.start()
+    first.wait()
+    second.wait()
+
+
+def edge_kernel(*refs):
+    lists, (both_ref, values_ref, left_ref, right_ref, agg_grad, scat, sem) = refs[:4], refs[4:]
+    depth = left_ref.shape[0]
+    fetch = pltpu.make_async_copy(both_ref.at[pl.ds(depth, depth)], agg_grad, sem)
+    fetch.start()
+    fetch.wait()
     for kind, out_ref in ((LEFT, left_ref), (RIGHT, right_ref)):
         scat[...] = jnp.zeros_like(scat)
         add_slots(lists, kind, agg_grad, scat, values_ref, False)
         out_ref[...] = scat[...].astype(jnp.bfloat16)
 
 
+def edge_step(lists, both, values, rim):
+    depth, width = both.shape[0] // 2, both.shape[1]
+    return pl.pallas_call(
+        edge_kernel,
+        out_shape=(jax.ShapeDtypeStruct((depth, rim), jnp.bfloat16),) * 2,
+        in_specs=[SMEM] * 4 + [HBM, VMEM],
+        out_specs=(VMEM,) * 2,
+        scratch_shapes=[
+            pltpu.VMEM((depth, width), jnp.bfloat16),
+            pltpu.VMEM((depth, rim), jnp.float32),
+            pltpu.SemaphoreType.DMA,
+        ],
+        compiler_params=pltpu.CompilerParams(vmem_limit_bytes=24 * 1024 * 1024),
+        cost_estimate=pl.CostEstimate(flops=1 << 28, bytes_accessed=4 << 20, transcendentals=0),
+    )(*lists, both, values)
+
+
 def local_step(lists, agg, own, before, after, values, w_in, w_out, cot):
     depth, width = own.shape
-    rim = before.shape[1]
+    both = jax.ShapeDtypeStruct((2 * depth, width), jnp.bfloat16)
     return pl.pallas_call(
         local_kernel,
-        out_shape=(
-            jax.ShapeDtypeStruct((depth, rim), jnp.bfloat16),
-            jax.ShapeDtypeStruct((depth, rim), jnp.bfloat16),
-            jax.ShapeDtypeStruct((2 * depth, width), jnp.bfloat16),
-            jax.ShapeDtypeStruct((depth, width), jnp.bfloat16),
-            jax.ShapeDtypeStruct((2 * depth, width), jnp.bfloat16),
-        ),
+        out_shape=(jax.ShapeDtypeStruct((2 * depth, depth), jnp.float32), both),
         in_specs=[SMEM] * 4 + [VMEM] * 8,
-        out_specs=(VMEM,) * 5,
+        out_specs=(HBM, HBM),
         scratch_shapes=[
+            pltpu.VMEM((2 * depth, width), jnp.bfloat16),
+            pltpu.VMEM((depth, width), jnp.bfloat16),
             pltpu.VMEM((depth, width), jnp.float32),
-            pltpu.VMEM((depth, rim), jnp.float32),
+            pltpu.VMEM((2 * depth, width), jnp.bfloat16),
+            pltpu.VMEM((2 * depth, depth), jnp.float32),
+            pltpu.SemaphoreType.DMA((2,)),
         ],
         compiler_params=pltpu.CompilerParams(vmem_limit_bytes=40 * 1024 * 1024),
         cost_estimate=pl.CostEstimate(
@@ -240,19 +272,18 @@
     before = shifted(own[:, width - rim :], RING, 1)
     after = shifted(own[:, :rim], RING, -1)
     agg = before_step(lists, own, block_values)
-    left, right, stacked, delta, both = local_step(
+    terms, both = local_step(
         lists, agg, own, before, after, block_values, w_in, w_out, cotangent
     )
-    terms = jnp.einsum("in,on->io", stacked, delta, preferred_element_type=jnp.float32)
     plane, line = lax.axis_size(PLANE), lax.axis_size(LINE)
     share = 2 * depth // plane
+    used, terms = lax.optimization_barrier((lists[0], terms))
+    left, right = edge_step([used, *lists[1:]], both, block_values, rim)
     from_next = shifted(left, RING, -1)
     from_prev = shifted(right, RING, 1)
     parts = lax.all_to_all(terms, PLANE, split_axis=0, concat_axis=0, tiled=True)
     partial = parts.reshape(plane, share, depth).sum(0).astype(jnp.bfloat16)
-    partial, from_next, from_prev, used = lax.optimization_barrier(
-        (partial, from_next, from_prev, lists[0])
-    )
+    partial, used = lax.optimization_barrier((partial, used))
     middle = after_step([used, *lists[1:]], both, block_values)
     copies = jnp.broadcast_to(partial[None], (line, share, depth))
     copies = lax.all_to_all(copies, LINE, split_axis=0, concat_axis=0, tiled=True)

time: 197 us -> 197 us (level)
  blocking collectives: 74.3 us -> 55.1 us
  starting transfers between devices: 49.4 us -> 65.7 us
  Pallas kernels: 9.72 us -> 12.3 us
  local copies, waits for them, and re-layouts: 12.5 us -> 14.8 us
    all_to_all x1 -> x0, blocking collectives: 19.2 us -> none  [on_device(): lax.all_to_all(terms, PLANE, split_axis=0, concat_axis=0, tiled=True)]
    all_to_all x0 -> x1, starting transfers between devices: none -> 7.81 us  [on_device(): lax.all_to_all(terms, PLANE, split_axis=0, concat_axis=0, tiled=True)]
    ppermute x4, waiting for transfers between devices: 3.93 us -> 8.95 us  [shifted(): lax.ppermute(shard, axis, [(i, (i + by) % count) for i in range(count)])]
    all_to_all x1, waiting for transfers between devices: 10.3 us -> 5.78 us  [on_device(): lax.all_to_all(copies, LINE, split_axis=0, concat_axis=0, tiled=True)]
    ppermute x4, starting transfers between devices: 22.2 us -> 26.1 us  [shifted(): lax.ppermute(shard, axis, [(i, (i + by) % count) for i in range(count)])]
    all_to_all x1, starting transfers between devices: 5.46 us -> 8.8 us  [on_device(): lax.all_to_all(total, 'feat', split_axis=0, concat_axis=1, tiled=True)]
    pallas_call x1 -> x2, Pallas kernels: 4.38 us -> 7.52 us  [the longest x1 5.47 us: local_step(): pl.pallas_call(local_kernel, out_shape=(jax.ShapeDtypeStruct((2 * depth,...]
    ppermute x5, starting transfers between devices: 12.8 us -> 15.3 us  [collected(): other = lax.ppermute(rows, axis, [(i, i ^ apart) for i in range(count)])]
  transfers between devices with their start and end apart: 11 -> 12, of which waited for: 9 -> 9; matrix products, arithmetic and copies ran while one was open for 4% -> 4% of each run, Pallas kernels for 3% -> 4%
where the time goes in v6:
time: 197 us; the launch traced here: 195 us
  starting transfers between devices  65.7 us (33%)
  blocking collectives  55.1 us (28%)
  waiting for transfers between devices  41.9 us (21%)
  local copies, waits for them, and re-layouts  14.8 us (8%)
  Pallas kernels  12.3 us (6%)
  other arithmetic  3.92 us (2%)
    all_to_all x1, blocking collectives, on_device(): lax.all_to_all(features, 'feat', split_axis=1, concat_axis=0, tiled=True)  55.1 us
    ppermute x4, starting transfers between devices, shifted(): lax.ppermute(shard, axis, [(i, (i + by) % count) for i in range(count)])  26.1 us
    ppermute x5, starting transfers between devices, collected(): other = lax.ppermute(rows, axis, [(i, i ^ apart) for i in range(count)])  15.3 us
    ppermute x5, waiting for transfers between devices, collected(): other = lax.ppermute(rows, axis, [(i, i ^ apart) for i in range(count)])  15.1 us
    all_to_all x1, waiting for transfers between devices, on_device(): lax.all_to_all(total, 'feat', split_axis=0, concat_axis=1, tiled=True)  12.1 us
    unnamed x30, local copies, waits for them, and re-layouts  10.8 us
    ppermute x4, waiting for transfers between devices, shifted(): lax.ppermute(shard, axis, [(i, (i + by) % count) for i in range(count)])  8.95 us
    all_to_all x1, starting transfers between devices, on_device(): lax.all_to_all(total, 'feat', split_axis=0, concat_axis=1, tiled=True)  8.8 us
  transfers between devices with their start and end apart: 12, of which 9 were waited for; matrix products, arithmetic and copies ran while one was open for 4% of the time, Pallas kernels for 4%

profile of v6, /device:TPU:6, one launch (start us, length us, event | category | flops | bytes accessed | tf_op | source)
XLA Modules:
  0.0 195.4 jit_solution(413707355698046577)
XLA Ops:
  0.6 1.2 copy.22
  1.9 55.1 %all_to_all.52 = bf16[32,8,1664]{2,0,1:T(8,128)(2,1)S(1)} all-to-all(bf16[32,8,1664]{2,0,1:T(8,128)(2,1)S(1)} %bitcast.22), channel_id=1, replica_groups=mesh['zh'=2,'y'=4,'x'=4,'core'=2,'feat'=8] {'feat'}, dimensions={1} | all-to-all | bytes 1703936 | tf_op jit(solution)/shard_map/all_to_all | solution.py:271
  57.0 1.1 fusion
  58.1 2.4 %collective-permute-start = (bf16[256,1024]{1,0:T(8,128)(2,1)}, bf16[256,1024]{1,0:T(8,128)(2,1)S(1)}, u32[]{:S(2)}, u32[]{:S(2)}) collective-permute-start(bf16[256,1024]{1,0:T(8,128)(2,1)} %get-tuple-element.32), channel_id=1, source_target_pairs={{0,1},{1,2},{2,3},{3,4},{4,5},{5,6},{6,7},{7,8},{8,9},{9,10},{10,1... | collective-permute-start | bytes 1572872 | tf_op jit(solution)/shard_map/ppermute | solution.py:21
  60.5 10.7 %collective-permute-start.1 = (bf16[256,1024]{1,0:T(8,128)(2,1)}, bf16[256,1024]{1,0:T(8,128)(2,1)}, u32[]{:S(2)}, u32[]{:S(2)}) collective-permute-start(bf16[256,1024]{1,0:T(8,128)(2,1)} %get-tuple-element.31), channel_id=1, source_target_pairs={{0,511},{1,0},{2,1},{3,2},{4,3},{5,4},{6,5},{7,6},{8,7},{9,8},{10,... | collective-permute-start | bytes 1572872 | tf_op jit(solution)/shard_map/ppermute | solution.py:21
  71.8 1.7 copy.16
  73.5 1.7 copy.17
  75.1 1.9 shard_map.103
  82.6 3.0 %collective-permute-done.1.refs_7_ = bf16[256,1024]{1,0:T(8,128)(2,1)} collective-permute-done((bf16[256,1024]{1,0:T(8,128)(2,1)}, bf16[256,1024]{1,0:T(8,128)(2,1)}, u32[]{:S(2)}, u32[]{:S(2)}) %collective-permute-start.1) | collective-permute-done | bytes 524320 | tf_op jit(solution)/shard_map/ppermute | solution.py:21
  85.7 5.5 %shard_map.105 = (f32[512,256]{1,0:T(8,128)S(1)}, bf16[512,1664]{1,0:T(8,128)(2,1)S(1)}) custom-call(s32[3]{0:T(128)S(1)} %copy-done.13, s32[192]{0:T(256)S(1)} %copy-done.7, s32[192]{0:T(256)S(1)} %copy-done.9, s32[192]{0:T(256)S(1)} %copy-done.11, f32[256,1664]{1,0:T(8,128)S(1)} %shard_map.104.refs_4_, bf16[256,1664]{1,0:T(8,128)(2,1)S(1)} %bitcast.19, ...), custom_call_target="tpu_custom_call" | custom-call | flops 1308622848 | bytes 8388608 | tf_op jit(solution)/shard_map/pallas_call | solution.py:198
  91.2 1.2 copy-done.1
  93.2 7.8 %all-to-all-start.1 = ((f32[32,16,256]{2,1,0:T(8,128)}), f32[32,16,256]{2,1,0:T(8,128)}, u32[]{:S(2)}, u32[]{:S(2)}) async-start(f32[32,16,256]{2,1,0:T(8,128)} %bitcast.20), calls=%async_computation.1 | async-start | bytes 1048576 | tf_op jit(solution)/shard_map/all_to_all | solution.py:284
  101.0 1.4 copy-done.2
  102.4 2.1 %shard_map.107 = (bf16[256,1024]{1,0:T(8,128)(2,1)}, bf16[256,1024]{1,0:T(8,128)(2,1)}) custom-call(s32[3]{0:T(128)S(1)} %copy-done.13, s32[192]{0:T(256)S(1)} %copy-done.7, s32[192]{0:T(256)S(1)} %copy-done.9, s32[192]{0:T(256)S(1)} %copy-done.11, bf16[512,1664]{1,0:T(8,128)(2,1)S(1)} %copy-done.2, bf16[64,128,128]{2,1,0:T(8,128)(2,1)S(1)} %copy-done), custom_call_target="tpu_custom_call" | custom-call | flops 268435456 | bytes 4194304 | tf_op jit(solution)/shard_map/pallas_call | solution.py:180
  104.5 1.9 collective-permute-start.2
  106.4 11.1 %collective-permute-start.3 = (bf16[256,1024]{1,0:T(8,128)(2,1)}, bf16[256,1024]{1,0:T(8,128)(2,1)S(1)}, u32[]{:S(2)}, u32[]{:S(2)}) collective-permute-start(bf16[256,1024]{1,0:T(8,128)(2,1)} %get-tuple-element.27), channel_id=1, source_target_pairs={{0,511},{1,0},{2,1},{3,2},{4,3},{5,4},{6,5},{7,6},{8,7},{9,8},{10,... | collective-permute-start | bytes 1572872 | tf_op jit(solution)/shard_map/ppermute | solution.py:21
  117.6 1.1 reduce_sum.18
  119.4 7.7 %all-to-all-start.2 = ((bf16[16,16,256]{2,1,0:T(8,128)(2,1)}), bf16[16,16,256]{2,1,0:T(8,128)(2,1)S(1)}, u32[]{:S(2)}, u32[]{:S(2)}) async-start(bf16[16,16,256]{2,1,0:T(8,128)(2,1)} %broadcast_in_dim.10), calls=%async_computation.2 | async-start | bytes 262144 | tf_op jit(solution)/shard_map/all_to_all | solution.py:289
  127.0 1.4 copy-done.3
  129.4 5.9 %collective-permute-done.3.next_ref = bf16[256,1024]{1,0:T(8,128)(2,1)S(1)} collective-permute-done((bf16[256,1024]{1,0:T(8,128)(2,1)}, bf16[256,1024]{1,0:T(8,128)(2,1)S(1)}, u32[]{:S(2)}, u32[]{:S(2)}) %collective-permute-start.3) | collective-permute-done | bytes 524320 | tf_op jit(solution)/shard_map/ppermute | solution.py:21
  136.4 5.8 %all-to-all-done.2 = bf16[16,16,256]{2,1,0:T(8,128)(2,1)S(1)} async-done(((bf16[16,16,256]{2,1,0:T(8,128)(2,1)}), bf16[16,16,256]{2,1,0:T(8,128)(2,1)S(1)}, u32[]{:S(2)}, u32[]{:S(2)}) %all-to-all-start.2) | async-done | bytes 131104 | tf_op jit(solution)/shard_map/all_to_all | solution.py:289
  142.2 8.8 %all-to-all-start.3 = ((bf16[8,32,1664]{2,1,0:T(8,128)(2,1)}), bf16[8,32,1664]{2,1,0:T(8,128)(2,1)S(1)}, u32[]{:S(2)}, u32[]{:S(2)}) async-start(bf16[8,32,1664]{2,1,0:T(8,128)(2,1)} %bitcast.9), calls=%async_computation.3 | async-start | bytes 1703936 | tf_op jit(solution)/shard_map/all_to_all | solution.py:294
  151.0 2.2 %collective-permute-start.4 = (bf16[16,256]{1,0:T(8,128)(2,1)S(1)}, bf16[16,256]{1,0:T(8,128)(2,1)S(1)}, u32[]{:S(2)}, u32[]{:S(2)}) collective-permute-start(bf16[16,256]{1,0:T(8,128)(2,1)S(1)} %multiply_convert_fusion), channel_id=1, source_target_pairs={{0,8},{8,0},{1,9},{9,1},{2,10},{10,2},{3,11},{11,3},{4,12},{12,4},... | collective-permute-start | bytes 24584 | tf_op jit(solution)/shard_map/ppermute | solution.py:29
  154.1 2.4 %collective-permute-start.5 = (bf16[32,256]{1,0:T(8,128)(2,1)S(1)}, bf16[32,256]{1,0:T(8,128)(2,1)S(1)}, u32[]{:S(2)}, u32[]{:S(2)}) collective-permute-start(bf16[32,256]{1,0:T(8,128)(2,1)S(1)} %pad_maximum_fusion.5), channel_id=1, source_target_pairs={{0,16},{16,0},{32,48},{48,32},{1,17},{17,1},{33,49},{49,33},{2,18}... | collective-permute-start | bytes 49160 | tf_op jit(solution)/shard_map/ppermute | solution.py:29
  156.5 3.2 %collective-permute-done.5 = bf16[32,256]{1,0:T(8,128)(2,1)S(1)} collective-permute-done((bf16[32,256]{1,0:T(8,128)(2,1)S(1)}, bf16[32,256]{1,0:T(8,128)(2,1)S(1)}, u32[]{:S(2)}, u32[]{:S(2)}) %collective-permute-start.5) | collective-permute-done | bytes 16416 | tf_op jit(solution)/shard_map/ppermute | solution.py:29
  159.7 3.1 %collective-permute-start.6 = (bf16[64,256]{1,0:T(8,128)(2,1)S(1)}, bf16[64,256]{1,0:T(8,128)(2,1)S(1)}, u32[]{:S(2)}, u32[]{:S(2)}) collective-permute-start(bf16[64,256]{1,0:T(8,128)(2,1)S(1)} %pad_maximum_fusion.4), channel_id=1, source_target_pairs={{0,32},{16,48},{32,0},{48,16},{1,33},{17,49},{33,1},{49,17},{2,34}... | collective-permute-start | bytes 98312 | tf_op jit(solution)/shard_map/ppermute | solution.py:29
  162.8 4.2 %collective-permute-done.6 = bf16[64,256]{1,0:T(8,128)(2,1)S(1)} collective-permute-done((bf16[64,256]{1,0:T(8,128)(2,1)S(1)}, bf16[64,256]{1,0:T(8,128)(2,1)S(1)}, u32[]{:S(2)}, u32[]{:S(2)}) %collective-permute-start.6) | collective-permute-done | bytes 32800 | tf_op jit(solution)/shard_map/ppermute | solution.py:29
  167.1 3.1 %collective-permute-start.7 = (bf16[128,256]{1,0:T(8,128)(2,1)S(1)}, bf16[128,256]{1,0:T(8,128)(2,1)S(1)}, u32[]{:S(2)}, u32[]{:S(2)}) collective-permute-start(bf16[128,256]{1,0:T(8,128)(2,1)S(1)} %pad_maximum_fusion.3), channel_id=1, source_target_pairs={{0,64},{64,0},{128,192},{192,128},{1,65},{65,1},{129,193},{193,129... | collective-permute-start | bytes 196616 | tf_op jit(solution)/shard_map/ppermute | solution.py:29
  170.2 3.0 %collective-permute-done.7 = bf16[128,256]{1,0:T(8,128)(2,1)S(1)} collective-permute-done((bf16[128,256]{1,0:T(8,128)(2,1)S(1)}, bf16[128,256]{1,0:T(8,128)(2,1)S(1)}, u32[]{:S(2)}, u32[]{:S(2)}) %collective-permute-start.7) | collective-permute-done | bytes 65568 | tf_op jit(solution)/shard_map/ppermute | solution.py:29
  173.3 4.5 %collective-permute-start.8 = (bf16[256,256]{1,0:T(8,128)(2,1)S(1)}, bf16[256,256]{1,0:T(8,128)(2,1)S(1)}, u32[]{:S(2)}, u32[]{:S(2)}) collective-permute-start(bf16[256,256]{1,0:T(8,128)(2,1)S(1)} %pad_maximum_fusion.2), channel_id=1, source_target_pairs={{0,128},{64,192},{128,0},{192,64},{1,129},{65,193},{129,1},{193,65... | collective-permute-start | bytes 393224 | tf_op jit(solution)/shard_map/ppermute | solution.py:29
  177.8 3.8 %collective-permute-done.8 = bf16[256,256]{1,0:T(8,128)(2,1)S(1)} collective-permute-done((bf16[256,256]{1,0:T(8,128)(2,1)S(1)}, bf16[256,256]{1,0:T(8,128)(2,1)S(1)}, u32[]{:S(2)}, u32[]{:S(2)}) %collective-permute-start.8) | collective-permute-done | bytes 131104 | tf_op jit(solution)/shard_map/ppermute | solution.py:29
  182.4 12.1 %all-to-all-done.3 = bf16[8,32,1664]{2,1,0:T(8,128)(2,1)S(1)} async-done(((bf16[8,32,1664]{2,1,0:T(8,128)(2,1)}), bf16[8,32,1664]{2,1,0:T(8,128)(2,1)S(1)}, u32[]{:S(2)}, u32[]{:S(2)}) %all-to-all-start.3) | async-done | bytes 852000 | tf_op jit(solution)/shard_map/all_to_all | solution.py:294
  (47 shorter events, 11.6 us)
Async XLA Ops:
  56.9 22.1 %copy-start = (bf16[64,128,128]{2,1,0:T(8,128)(2,1)S(1)}, bf16[64,128,128]{2,1,0:T(8,128)(2,1)}, u32[]{:S(2)}) copy-start(bf16[64,128,128]{2,1,0:T(8,128)(2,1)} %refs_5_.5) | copy-start | bytes 6291460
  58.1 24.5 %collective-permute-start = (bf16[256,1024]{1,0:T(8,128)(2,1)}, bf16[256,1024]{1,0:T(8,128)(2,1)S(1)}, u32[]{:S(2)}, u32[]{:S(2)}) collective-permute-start(bf16[256,1024]{1,0:T(8,128)(2,1)} %get-tuple-element.32), channel_id=1, source_target_pairs={{0,1},{1,2},{2,3},{3,4},{4,5},{5,6},{6,7},{7,8},{8,9},{9,10},{10,1... | collective-permute-start | bytes 1572872 | tf_op jit(solution)/shard_map/ppermute | solution.py:21
  60.5 25.2 %collective-permute-start.1 = (bf16[256,1024]{1,0:T(8,128)(2,1)}, bf16[256,1024]{1,0:T(8,128)(2,1)}, u32[]{:S(2)}, u32[]{:S(2)}) collective-permute-start(bf16[256,1024]{1,0:T(8,128)(2,1)} %get-tuple-element.31), channel_id=1, source_target_pairs={{0,511},{1,0},{2,1},{3,2},{4,3},{5,4},{6,5},{7,6},{8,7},{9,8},{10,... | collective-permute-start | bytes 1572872 | tf_op jit(solution)/shard_map/ppermute | solution.py:21
  79.1 0.7 copy-start.6
  79.8 0.7 copy-start.8
  80.4 0.7 copy-start.10
  81.1 0.6 copy-start.12
  81.6 4.0 %copy-start.4 = (bf16[256,1664]{1,0:T(8,128)(2,1)S(1)}, bf16[256,1664]{1,0:T(8,128)(2,1)}, u32[]{:S(2)}) copy-start(bf16[256,1664]{1,0:T(8,128)(2,1)} %refs_11_.1) | copy-start | bytes 2555908
  81.6 4.0 %copy-start.7 = (s32[192]{0:T(256)S(1)}, s32[192]{0:T(256)}, u32[]{:S(2)}) copy-start(s32[192]{0:T(256)} %get-tuple-element.18.refs_1_) | copy-start | bytes 2308
  81.6 4.0 %copy-start.9 = (s32[192]{0:T(256)S(1)}, s32[192]{0:T(256)}, u32[]{:S(2)}) copy-start(s32[192]{0:T(256)} %get-tuple-element.19.refs_2_) | copy-start | bytes 2308
  81.7 4.0 %copy-start.11 = (s32[192]{0:T(256)S(1)}, s32[192]{0:T(256)}, u32[]{:S(2)}) copy-start(s32[192]{0:T(256)} %get-tuple-element.20.refs_3_) | copy-start | bytes 2308
  81.7 4.0 %copy-start.13 = (s32[3]{0:T(128)S(1)}, s32[3]{0:T(128)}, u32[]{:S(2)}) copy-start(s32[3]{0:T(128)} %get-tuple-element.24.refs_0_) | copy-start | bytes 40
  91.1 1.2 copy-start.1
  92.4 0.8 copy-start.5
  93.2 24.4 %all-to-all-start.1 = ((f32[32,16,256]{2,1,0:T(8,128)}), f32[32,16,256]{2,1,0:T(8,128)}, u32[]{:S(2)}, u32[]{:S(2)}) async-start(f32[32,16,256]{2,1,0:T(8,128)} %bitcast.20), calls=%async_computation.1 | async-start | bytes 1048576 | tf_op jit(solution)/shard_map/all_to_all | solution.py:284
  101.0 1.5 copy-start.2
  104.5 24.9 %collective-permute-start.2 = (bf16[256,1024]{1,0:T(8,128)(2,1)}, bf16[256,1024]{1,0:T(8,128)(2,1)S(1)}, u32[]{:S(2)}, u32[]{:S(2)}) collective-permute-start(bf16[256,1024]{1,0:T(8,128)(2,1)} %get-tuple-element.26), channel_id=1, source_target_pairs={{0,1},{1,2},{2,3},{3,4},{4,5},{5,6},{6,7},{7,8},{8,9},{9,10},{10,1... | collective-permute-start | bytes 1572872 | tf_op jit(solution)/shard_map/ppermute | solution.py:21
  106.4 28.9 %collective-permute-start.3 = (bf16[256,1024]{1,0:T(8,128)(2,1)}, bf16[256,1024]{1,0:T(8,128)(2,1)S(1)}, u32[]{:S(2)}, u32[]{:S(2)}) collective-permute-start(bf16[256,1024]{1,0:T(8,128)(2,1)} %get-tuple-element.27), channel_id=1, source_target_pairs={{0,511},{1,0},{2,1},{3,2},{4,3},{5,4},{6,5},{7,6},{8,7},{9,8},{10,... | collective-permute-start | bytes 1572872 | tf_op jit(solution)/shard_map/ppermute | solution.py:21
  119.4 22.8 %all-to-all-start.2 = ((bf16[16,16,256]{2,1,0:T(8,128)(2,1)}), bf16[16,16,256]{2,1,0:T(8,128)(2,1)S(1)}, u32[]{:S(2)}, u32[]{:S(2)}) async-start(bf16[16,16,256]{2,1,0:T(8,128)(2,1)} %broadcast_in_dim.10), calls=%async_computation.2 | async-start | bytes 262144 | tf_op jit(solution)/shard_map/all_to_all | solution.py:289
  127.0 1.5 copy-start.3
  142.2 52.3 %all-to-all-start.3 = ((bf16[8,32,1664]{2,1,0:T(8,128)(2,1)}), bf16[8,32,1664]{2,1,0:T(8,128)(2,1)S(1)}, u32[]{:S(2)}, u32[]{:S(2)}) async-start(bf16[8,32,1664]{2,1,0:T(8,128)(2,1)} %bitcast.9), calls=%async_computation.3 | async-start | bytes 1703936 | tf_op jit(solution)/shard_map/all_to_all | solution.py:294
  151.0 3.1 %collective-permute-start.4 = (bf16[16,256]{1,0:T(8,128)(2,1)S(1)}, bf16[16,256]{1,0:T(8,128)(2,1)S(1)}, u32[]{:S(2)}, u32[]{:S(2)}) collective-permute-start(bf16[16,256]{1,0:T(8,128)(2,1)S(1)} %multiply_convert_fusion), channel_id=1, source_target_pairs={{0,8},{8,0},{1,9},{9,1},{2,10},{10,2},{3,11},{11,3},{4,12},{12,4},... | collective-permute-start | bytes 24584 | tf_op jit(solution)/shard_map/ppermute | solution.py:29
  154.1 5.6 %collective-permute-start.5 = (bf16[32,256]{1,0:T(8,128)(2,1)S(1)}, bf16[32,256]{1,0:T(8,128)(2,1)S(1)}, u32[]{:S(2)}, u32[]{:S(2)}) collective-permute-start(bf16[32,256]{1,0:T(8,128)(2,1)S(1)} %pad_maximum_fusion.5), channel_id=1, source_target_pairs={{0,16},{16,0},{32,48},{48,32},{1,17},{17,1},{33,49},{49,33},{2,18}... | collective-permute-start | bytes 49160 | tf_op jit(solution)/shard_map/ppermute | solution.py:29
  159.7 7.3 %collective-permute-start.6 = (bf16[64,256]{1,0:T(8,128)(2,1)S(1)}, bf16[64,256]{1,0:T(8,128)(2,1)S(1)}, u32[]{:S(2)}, u32[]{:S(2)}) collective-permute-start(bf16[64,256]{1,0:T(8,128)(2,1)S(1)} %pad_maximum_fusion.4), channel_id=1, source_target_pairs={{0,32},{16,48},{32,0},{48,16},{1,33},{17,49},{33,1},{49,17},{2,34}... | collective-permute-start | bytes 98312 | tf_op jit(solution)/shard_map/ppermute | solution.py:29
  167.1 6.2 %collective-permute-start.7 = (bf16[128,256]{1,0:T(8,128)(2,1)S(1)}, bf16[128,256]{1,0:T(8,128)(2,1)S(1)}, u32[]{:S(2)}, u32[]{:S(2)}) collective-permute-start(bf16[128,256]{1,0:T(8,128)(2,1)S(1)} %pad_maximum_fusion.3), channel_id=1, source_target_pairs={{0,64},{64,0},{128,192},{192,128},{1,65},{65,1},{129,193},{193,129... | collective-permute-start | bytes 196616 | tf_op jit(solution)/shard_map/ppermute | solution.py:29
  173.3 8.4 %collective-permute-start.8 = (bf16[256,256]{1,0:T(8,128)(2,1)S(1)}, bf16[256,256]{1,0:T(8,128)(2,1)S(1)}, u32[]{:S(2)}, u32[]{:S(2)}) collective-permute-start(bf16[256,256]{1,0:T(8,128)(2,1)S(1)} %pad_maximum_fusion.2), channel_id=1, source_target_pairs={{0,128},{64,192},{128,0},{192,64},{1,129},{65,193},{129,1},{193,65... | collective-permute-start | bytes 393224 | tf_op jit(solution)/shard_map/ppermute | solution.py:29

commit v7 on v6

--- a/solution.py
+++ b/solution.py
@@ -257,6 +257,61 @@
     )(middle, from_prev, from_next)
 
 
+def cut_kernel(pos_ref, features_ref, *refs):
+    piece_refs, sems = refs[:-1], refs[-1]
+    pieces, width = len(piece_refs), piece_refs[0].shape[1]
+    copies = []
+    for step, piece_ref in enumerate(piece_refs):
+        dest = lax.rem(pos_ref[0] + step, pieces)
+        part = pl.ds(pl.multiple_of(dest * width, BLK), width)
+        copies.append(pltpu.make_async_copy(features_ref.at[:, part], piece_ref, sems.at[step]))
+    for copy in copies:
+        copy.start()
+    for copy in copies:
+        copy.wait()
+
+
+def cut_step(pos, features, pieces):
+    height, width = features.shape[0], features.shape[1] // pieces
+    return pl.pallas_call(
+        cut_kernel,
+        out_shape=(jax.ShapeDtypeStruct((height, width), features.dtype),) * pieces,
+        in_specs=[SMEM, pl.BlockSpec(memory_space=pl.ANY)],
+        out_specs=(VMEM,) * pieces,
+        scratch_shapes=[pltpu.SemaphoreType.DMA((pieces,))],
+        compiler_params=pltpu.CompilerParams(vmem_limit_bytes=16 * 1024 * 1024),
+        cost_estimate=pl.CostEstimate(flops=0, bytes_accessed=2 << 20, transcendentals=0),
+    )(pos, features)
+
+
+def join_kernel(pos_ref, *refs):
+    piece_refs, (own_ref, head_ref, tail_ref) = refs[:-3], refs[-3:]
+    pieces = len(piece_refs)
+    height, width = piece_refs[0].shape
+    rim = head_ref.shape[1]
+    for step, piece_ref in enumerate(piece_refs):
+        source = lax.rem(pos_ref[0] + pieces - step, pieces)
+        rows = pl.ds(pl.multiple_of(source * height, height), height)
+        own_ref[rows, :] = piece_ref[...]
+        head_ref[rows, :] = piece_ref[:, :rim]
+        tail_ref[rows, :] = piece_ref[:, width - rim :]
+
+
+def join_step(pos, received, rim):
+    pieces = len(received)
+    height, width = received[0].shape
+    depth, kind = pieces * height, received[0].dtype
+    edge = jax.ShapeDtypeStruct((depth, rim), kind)
+    return pl.pallas_call(
+        join_kernel,
+        out_shape=(jax.ShapeDtypeStruct((depth, width), kind), edge, edge),
+        in_specs=[SMEM] + [VMEM] * pieces,
+        out_specs=(VMEM,) * 3,
+        compiler_params=pltpu.CompilerParams(vmem_limit_bytes=16 * 1024 * 1024),
+        cost_estimate=pl.CostEstimate(flops=0, bytes_accessed=4 << 20, transcendentals=0),
+    )(pos, *received)
+
+
 def on_device(
     features, block_row, block_col, block_count, block_values, w_self, w_neigh, cotangent
 ):
@@ -268,9 +323,13 @@
     lists = list_step(block_row[0], block_col[0], block_count, pos, chunk)
     w_in = jnp.concatenate([w_self.T, w_neigh.T], axis=1)
     w_out = jnp.concatenate([w_self, w_neigh], axis=0)
-    own = lax.all_to_all(features, "feat", split_axis=1, concat_axis=0, tiled=True)
-    before = shifted(own[:, width - rim :], RING, 1)
-    after = shifted(own[:, :rim], RING, -1)
+    pieces = lax.axis_size("feat")
+    received = list(cut_step(pos, features, pieces))
+    for step in sorted(range(1, pieces), key=lambda step: (abs(2 * step - pieces), step)):
+        received[step] = shifted(received[step], "feat", step)
+    own, head, tail = join_step(pos, received, rim)
+    before = shifted(tail, RING, 1)
+    after = shifted(head, RING, -1)
     agg = before_step(lists, own, block_values)
     terms, both = local_step(
         lists, agg, own, before, after, block_values, w_in, w_out, cotangent

time: 197 us -> 192 us (0.975)
  blocking collectives: 55.1 us -> 0 us
  starting transfers between devices: 65.7 us -> 96.1 us
  waiting for transfers between devices: 41.9 us -> 61.6 us
    all_to_all x1 -> x0, blocking collectives: 55.1 us -> none  [on_device(): lax.all_to_all(features, 'feat', split_axis=1, concat_axis=0, tiled=True)]
    ppermute x4 -> x11, starting transfers between devices: 26.1 us -> 58.4 us  [shifted(): lax.ppermute(shard, axis, [(i, (i + by) % count) for i in range(count)])]
    ppermute x4 -> x11, waiting for transfers between devices: 8.95 us -> 24 us  [shifted(): lax.ppermute(shard, axis, [(i, (i + by) % count) for i in range(count)])]
    all_to_all x1, waiting for transfers between devices: 5.78 us -> 11.9 us  [on_device(): lax.all_to_all(copies, LINE, split_axis=0, concat_axis=0, tiled=True)]
    all_to_all x1, starting transfers between devices: 8.8 us -> 3.75 us  [on_device(): lax.all_to_all(total, 'feat', split_axis=0, concat_axis=1, tiled=True)]
    all_to_all x1, starting transfers between devices: 7.67 us -> 10.5 us  [on_device(): lax.all_to_all(copies, LINE, split_axis=0, concat_axis=0, tiled=True)]
    unnamed x30 -> x32, local copies, waits for them, and re-layouts: 10.8 us -> 12.2 us
  transfers between devices with their start and end apart: 12 -> 19, of which waited for: 9 -> 11; matrix products, arithmetic and copies ran while one was open for 4% -> 4% of each run, Pallas kernels for 4% -> 4%
where the time goes in v7:
time: 192 us; the launch traced here: 191 us
  starting transfers between devices  96.1 us (50%)
  waiting for transfers between devices  61.6 us (32%)
  local copies, waits for them, and re-layouts  13.9 us (7%)
  Pallas kernels  13.7 us (7%)
  other arithmetic  3.92 us (2%)
    ppermute x11, starting transfers between devices, shifted(): lax.ppermute(shard, axis, [(i, (i + by) % count) for i in range(count)])  58.4 us
    ppermute x11, waiting for transfers between devices, shifted(): lax.ppermute(shard, axis, [(i, (i + by) % count) for i in range(count)])  24 us
    ppermute x5, starting transfers between devices, collected(): other = lax.ppermute(rows, axis, [(i, i ^ apart) for i in range(count)])  15.9 us
    ppermute x5, waiting for transfers between devices, collected(): other = lax.ppermute(rows, axis, [(i, i ^ apart) for i in range(count)])  14.6 us
    unnamed x32, local copies, waits for them, and re-layouts  12.2 us
    all_to_all x1, waiting for transfers between devices, on_device(): lax.all_to_all(copies, LINE, split_axis=0, concat_axis=0, tiled=True)  11.9 us
    all_to_all x1, waiting for transfers between devices, on_device(): lax.all_to_all(total, 'feat', split_axis=0, concat_axis=1, tiled=True)  11.2 us
    all_to_all x1, starting transfers between devices, on_device(): lax.all_to_all(copies, LINE, split_axis=0, concat_axis=0, tiled=True)  10.5 us
  transfers between devices with their start and end apart: 19, of which 11 were waited for; matrix products, arithmetic and copies ran while one was open for 4% of the time, Pallas kernels for 4%

profile of v7, /device:TPU:6, one launch (start us, length us, event | category | flops | bytes accessed | tf_op | source)
XLA Modules:
  0.0 190.9 jit_solution(14229900856614461946)
XLA Ops:
  2.3 3.8 %collective-permute-start = (bf16[32,1664]{1,0:T(8,128)(2,1)S(1)}, bf16[32,1664]{1,0:T(8,128)(2,1)S(1)}, u32[]{:S(2)}, u32[]{:S(2)}) collective-permute-start(bf16[32,1664]{1,0:T(8,128)(2,1)S(1)} %get-tuple-element.33), channel_id=1, source_target_pairs={{0,1},{1,2},{2,3},{3,4},{4,5},{5,6},{6,7},{7,0},{8,9},{9,10},{10,1... | collective-permute-start | bytes 319496 | tf_op jit(solution)/shard_map/ppermute | solution.py:21
  6.2 5.2 %collective-permute-start.1 = (bf16[32,1664]{1,0:T(8,128)(2,1)S(1)}, bf16[32,1664]{1,0:T(8,128)(2,1)S(1)}, u32[]{:S(2)}, u32[]{:S(2)}) collective-permute-start(bf16[32,1664]{1,0:T(8,128)(2,1)S(1)} %get-tuple-element.34), channel_id=1, source_target_pairs={{0,2},{1,3},{2,4},{3,5},{4,6},{5,7},{6,0},{7,1},{8,10},{9,11},{10,... | collective-permute-start | bytes 319496 | tf_op jit(solution)/shard_map/ppermute | solution.py:21
  11.3 7.7 %collective-permute-start.2 = (bf16[32,1664]{1,0:T(8,128)(2,1)S(1)}, bf16[32,1664]{1,0:T(8,128)(2,1)S(1)}, u32[]{:S(2)}, u32[]{:S(2)}) collective-permute-start(bf16[32,1664]{1,0:T(8,128)(2,1)S(1)} %get-tuple-element.35), channel_id=1, source_target_pairs={{0,3},{1,4},{2,5},{3,6},{4,7},{5,0},{6,1},{7,2},{8,11},{9,12},{10,... | collective-permute-start | bytes 319496 | tf_op jit(solution)/shard_map/ppermute | solution.py:21
  19.1 3.3 %collective-permute-start.3 = (bf16[32,1664]{1,0:T(8,128)(2,1)S(1)}, bf16[32,1664]{1,0:T(8,128)(2,1)S(1)}, u32[]{:S(2)}, u32[]{:S(2)}) collective-permute-start(bf16[32,1664]{1,0:T(8,128)(2,1)S(1)} %get-tuple-element.36), channel_id=1, source_target_pairs={{0,4},{1,5},{2,6},{3,7},{4,0},{5,1},{6,2},{7,3},{8,12},{9,13},{10,... | collective-permute-start | bytes 319496 | tf_op jit(solution)/shard_map/ppermute | solution.py:21
  22.4 7.8 %collective-permute-start.4 = (bf16[32,1664]{1,0:T(8,128)(2,1)S(1)}, bf16[32,1664]{1,0:T(8,128)(2,1)S(1)}, u32[]{:S(2)}, u32[]{:S(2)}) collective-permute-start(bf16[32,1664]{1,0:T(8,128)(2,1)S(1)} %get-tuple-element.37), channel_id=1, source_target_pairs={{0,5},{1,6},{2,7},{3,0},{4,1},{5,2},{6,3},{7,4},{8,13},{9,14},{10,... | collective-permute-start | bytes 319496 | tf_op jit(solution)/shard_map/ppermute | solution.py:21
  30.2 4.6 %collective-permute-start.5 = (bf16[32,1664]{1,0:T(8,128)(2,1)S(1)}, bf16[32,1664]{1,0:T(8,128)(2,1)S(1)}, u32[]{:S(2)}, u32[]{:S(2)}) collective-permute-start(bf16[32,1664]{1,0:T(8,128)(2,1)S(1)} %get-tuple-element.38), channel_id=1, source_target_pairs={{0,6},{1,7},{2,0},{3,1},{4,2},{5,3},{6,4},{7,5},{8,14},{9,15},{10,... | collective-permute-start | bytes 319496 | tf_op jit(solution)/shard_map/ppermute | solution.py:21
  34.8 2.9 %collective-permute-start.6 = (bf16[32,1664]{1,0:T(8,128)(2,1)S(1)}, bf16[32,1664]{1,0:T(8,128)(2,1)S(1)}, u32[]{:S(2)}, u32[]{:S(2)}) collective-permute-start(bf16[32,1664]{1,0:T(8,128)(2,1)S(1)} %get-tuple-element.39), channel_id=1, source_target_pairs={{0,7},{1,0},{2,1},{3,2},{4,3},{5,4},{6,5},{7,6},{8,15},{9,8},{10,9... | collective-permute-start | bytes 319496 | tf_op jit(solution)/shard_map/ppermute | solution.py:21
  37.7 3.3 %collective-permute-done.2.refs_3_ = bf16[32,1664]{1,0:T(8,128)(2,1)S(1)} collective-permute-done((bf16[32,1664]{1,0:T(8,128)(2,1)S(1)}, bf16[32,1664]{1,0:T(8,128)(2,1)S(1)}, u32[]{:S(2)}, u32[]{:S(2)}) %collective-permute-start.2) | collective-permute-done | bytes 106528 | tf_op jit(solution)/shard_map/ppermute | solution.py:21
  41.1 4.8 %collective-permute-done.5.refs_6_ = bf16[32,1664]{1,0:T(8,128)(2,1)S(1)} collective-permute-done((bf16[32,1664]{1,0:T(8,128)(2,1)S(1)}, bf16[32,1664]{1,0:T(8,128)(2,1)S(1)}, u32[]{:S(2)}, u32[]{:S(2)}) %collective-permute-start.5) | collective-permute-done | bytes 106528 | tf_op jit(solution)/shard_map/ppermute | solution.py:21
  47.0 5.1 %collective-permute-start.7 = (bf16[256,1024]{1,0:T(8,128)(2,1)}, bf16[256,1024]{1,0:T(8,128)(2,1)S(1)}, u32[]{:S(2)}, u32[]{:S(2)}) collective-permute-start(bf16[256,1024]{1,0:T(8,128)(2,1)} %get-tuple-element.41), channel_id=1, source_target_pairs={{0,1},{1,2},{2,3},{3,4},{4,5},{5,6},{6,7},{7,8},{8,9},{9,10},{10,1... | collective-permute-start | bytes 1572872 | tf_op jit(solution)/shard_map/ppermute | solution.py:21
  52.1 9.4 %collective-permute-start.8 = (bf16[256,1024]{1,0:T(8,128)(2,1)}, bf16[256,1024]{1,0:T(8,128)(2,1)}, u32[]{:S(2)}, u32[]{:S(2)}) collective-permute-start(bf16[256,1024]{1,0:T(8,128)(2,1)} %get-tuple-element.42), channel_id=1, source_target_pairs={{0,511},{1,0},{2,1},{3,2},{4,3},{5,4},{6,5},{7,6},{8,7},{9,8},{10,... | collective-permute-start | bytes 1572872 | tf_op jit(solution)/shard_map/ppermute | solution.py:21
  65.5 1.8 shard_map.103
  72.9 7.5 %collective-permute-done.8.refs_7_ = bf16[256,1024]{1,0:T(8,128)(2,1)} collective-permute-done((bf16[256,1024]{1,0:T(8,128)(2,1)}, bf16[256,1024]{1,0:T(8,128)(2,1)}, u32[]{:S(2)}, u32[]{:S(2)}) %collective-permute-start.8) | collective-permute-done | bytes 524320 | tf_op jit(solution)/shard_map/ppermute | solution.py:21
  80.4 5.5 %shard_map.107 = (f32[512,256]{1,0:T(8,128)S(1)}, bf16[512,1664]{1,0:T(8,128)(2,1)S(1)}) custom-call(s32[3]{0:T(128)S(1)} %copy-done.14, s32[192]{0:T(256)S(1)} %copy-done.8, s32[192]{0:T(256)S(1)} %copy-done.10, s32[192]{0:T(256)S(1)} %copy-done.12, f32[256,1664]{1,0:T(8,128)S(1)} %shard_map.106.refs_4_, ...), custom_call_target="tpu_custom_call" | custom-call | flops 1308622848 | bytes 8388608 | tf_op jit(solution)/shard_map/pallas_call | solution.py:198
  87.9 7.6 %all-to-all-start = ((f32[32,16,256]{2,1,0:T(8,128)}), f32[32,16,256]{2,1,0:T(8,128)}, u32[]{:S(2)}, u32[]{:S(2)}) async-start(f32[32,16,256]{2,1,0:T(8,128)} %bitcast.10), calls=%async_computation | async-start | bytes 1048576 | tf_op jit(solution)/shard_map/all_to_all | solution.py:343
  97.0 2.1 %shard_map.109 = (bf16[256,1024]{1,0:T(8,128)(2,1)}, bf16[256,1024]{1,0:T(8,128)(2,1)}) custom-call(s32[3]{0:T(128)S(1)} %copy-done.14, s32[192]{0:T(256)S(1)} %copy-done.8, s32[192]{0:T(256)S(1)} %copy-done.10, s32[192]{0:T(256)S(1)} %copy-done.12, bf16[512,1664]{1,0:T(8,128)(2,1)S(1)} %copy-done.2, bf16[64,128,128]{2,1,0:T(8,128)(2,1)S(1)} %copy-done), custom_call_target="tpu_custom_call" | custom-call | flops 268435456 | bytes 4194304 | tf_op jit(solution)/shard_map/pallas_call | solution.py:180
  99.0 6.6 %collective-permute-start.10 = (bf16[256,1024]{1,0:T(8,128)(2,1)}, bf16[256,1024]{1,0:T(8,128)(2,1)S(1)}, u32[]{:S(2)}, u32[]{:S(2)}) collective-permute-start(bf16[256,1024]{1,0:T(8,128)(2,1)} %get-tuple-element.49), channel_id=1, source_target_pairs={{0,511},{1,0},{2,1},{3,2},{4,3},{5,4},{6,5},{7,6},{8,7},{9,8},{10,... | collective-permute-start | bytes 1572872 | tf_op jit(solution)/shard_map/ppermute | solution.py:21
  105.7 1.9 %collective-permute-start.9 = (bf16[256,1024]{1,0:T(8,128)(2,1)}, bf16[256,1024]{1,0:T(8,128)(2,1)S(1)}, u32[]{:S(2)}, u32[]{:S(2)}) collective-permute-start(bf16[256,1024]{1,0:T(8,128)(2,1)} %get-tuple-element.48), channel_id=1, source_target_pairs={{0,1},{1,2},{2,3},{3,4},{4,5},{5,6},{6,7},{7,8},{8,9},{9,10},{10,1... | collective-permute-start | bytes 1572872 | tf_op jit(solution)/shard_map/ppermute | solution.py:21
  109.4 10.5 %all-to-all-start.1 = ((bf16[16,16,256]{2,1,0:T(8,128)(2,1)}), bf16[16,16,256]{2,1,0:T(8,128)(2,1)S(1)}, u32[]{:S(2)}, u32[]{:S(2)}) async-start(bf16[16,16,256]{2,1,0:T(8,128)(2,1)} %broadcast_in_dim.10), calls=%async_computation.1 | async-start | bytes 262144 | tf_op jit(solution)/shard_map/all_to_all | solution.py:348
  122.2 8.4 %collective-permute-done.9.prev_ref = bf16[256,1024]{1,0:T(8,128)(2,1)S(1)} collective-permute-done((bf16[256,1024]{1,0:T(8,128)(2,1)}, bf16[256,1024]{1,0:T(8,128)(2,1)S(1)}, u32[]{:S(2)}, u32[]{:S(2)}) %collective-permute-start.9) | collective-permute-done | bytes 524320 | tf_op jit(solution)/shard_map/ppermute | solution.py:21
  131.7 11.9 %all-to-all-done.1 = bf16[16,16,256]{2,1,0:T(8,128)(2,1)S(1)} async-done(((bf16[16,16,256]{2,1,0:T(8,128)(2,1)}), bf16[16,16,256]{2,1,0:T(8,128)(2,1)S(1)}, u32[]{:S(2)}, u32[]{:S(2)}) %all-to-all-start.1) | async-done | bytes 131104 | tf_op jit(solution)/shard_map/all_to_all | solution.py:348
  143.6 3.7 %all-to-all-start.2 = ((bf16[8,32,1664]{2,1,0:T(8,128)(2,1)}), bf16[8,32,1664]{2,1,0:T(8,128)(2,1)S(1)}, u32[]{:S(2)}, u32[]{:S(2)}) async-start(bf16[8,32,1664]{2,1,0:T(8,128)(2,1)} %bitcast.6), calls=%async_computation.2 | async-start | bytes 1703936 | tf_op jit(solution)/shard_map/all_to_all | solution.py:353
  147.4 1.9 collective-permute-start.11
  150.4 2.7 %collective-permute-start.12 = (bf16[32,256]{1,0:T(8,128)(2,1)S(1)}, bf16[32,256]{1,0:T(8,128)(2,1)S(1)}, u32[]{:S(2)}, u32[]{:S(2)}) collective-permute-start(bf16[32,256]{1,0:T(8,128)(2,1)S(1)} %pad_maximum_fusion.5), channel_id=1, source_target_pairs={{0,16},{16,0},{32,48},{48,32},{1,17},{17,1},{33,49},{49,33},{2,18}... | collective-permute-start | bytes 49160 | tf_op jit(solution)/shard_map/ppermute | solution.py:29
  153.1 2.9 %collective-permute-done.12 = bf16[32,256]{1,0:T(8,128)(2,1)S(1)} collective-permute-done((bf16[32,256]{1,0:T(8,128)(2,1)S(1)}, bf16[32,256]{1,0:T(8,128)(2,1)S(1)}, u32[]{:S(2)}, u32[]{:S(2)}) %collective-permute-start.12) | collective-permute-done | bytes 16416 | tf_op jit(solution)/shard_map/ppermute | solution.py:29
  156.1 3.2 %collective-permute-start.13 = (bf16[64,256]{1,0:T(8,128)(2,1)S(1)}, bf16[64,256]{1,0:T(8,128)(2,1)S(1)}, u32[]{:S(2)}, u32[]{:S(2)}) collective-permute-start(bf16[64,256]{1,0:T(8,128)(2,1)S(1)} %pad_maximum_fusion.4), channel_id=1, source_target_pairs={{0,32},{16,48},{32,0},{48,16},{1,33},{17,49},{33,1},{49,17},{2,34}... | collective-permute-start | bytes 98312 | tf_op jit(solution)/shard_map/ppermute | solution.py:29
  159.3 4.1 %collective-permute-done.13 = bf16[64,256]{1,0:T(8,128)(2,1)S(1)} collective-permute-done((bf16[64,256]{1,0:T(8,128)(2,1)S(1)}, bf16[64,256]{1,0:T(8,128)(2,1)S(1)}, u32[]{:S(2)}, u32[]{:S(2)}) %collective-permute-start.13) | collective-permute-done | bytes 32800 | tf_op jit(solution)/shard_map/ppermute | solution.py:29
  163.4 3.2 %collective-permute-start.14 = (bf16[128,256]{1,0:T(8,128)(2,1)S(1)}, bf16[128,256]{1,0:T(8,128)(2,1)S(1)}, u32[]{:S(2)}, u32[]{:S(2)}) collective-permute-start(bf16[128,256]{1,0:T(8,128)(2,1)S(1)} %pad_maximum_fusion.3), channel_id=1, source_target_pairs={{0,64},{64,0},{128,192},{192,128},{1,65},{65,1},{129,193},{193,129... | collective-permute-start | bytes 196616 | tf_op jit(solution)/shard_map/ppermute | solution.py:29
  166.7 2.9 %collective-permute-done.14 = bf16[128,256]{1,0:T(8,128)(2,1)S(1)} collective-permute-done((bf16[128,256]{1,0:T(8,128)(2,1)S(1)}, bf16[128,256]{1,0:T(8,128)(2,1)S(1)}, u32[]{:S(2)}, u32[]{:S(2)}) %collective-permute-start.14) | collective-permute-done | bytes 65568 | tf_op jit(solution)/shard_map/ppermute | solution.py:29
  169.6 4.8 %collective-permute-start.15 = (bf16[256,256]{1,0:T(8,128)(2,1)S(1)}, bf16[256,256]{1,0:T(8,128)(2,1)S(1)}, u32[]{:S(2)}, u32[]{:S(2)}) collective-permute-start(bf16[256,256]{1,0:T(8,128)(2,1)S(1)} %pad_maximum_fusion.2), channel_id=1, source_target_pairs={{0,128},{64,192},{128,0},{192,64},{1,129},{65,193},{129,1},{193,65... | collective-permute-start | bytes 393224 | tf_op jit(solution)/shard_map/ppermute | solution.py:29
  174.5 3.5 %collective-permute-done.15 = bf16[256,256]{1,0:T(8,128)(2,1)S(1)} collective-permute-done((bf16[256,256]{1,0:T(8,128)(2,1)S(1)}, bf16[256,256]{1,0:T(8,128)(2,1)S(1)}, u32[]{:S(2)}, u32[]{:S(2)}) %collective-permute-start.15) | collective-permute-done | bytes 131104 | tf_op jit(solution)/shard_map/ppermute | solution.py:29
  178.7 11.2 %all-to-all-done.2 = bf16[8,32,1664]{2,1,0:T(8,128)(2,1)S(1)} async-done(((bf16[8,32,1664]{2,1,0:T(8,128)(2,1)}), bf16[8,32,1664]{2,1,0:T(8,128)(2,1)S(1)}, u32[]{:S(2)}, u32[]{:S(2)}) %all-to-all-start.2) | async-done | bytes 852000 | tf_op jit(solution)/shard_map/all_to_all | solution.py:353
  (62 shorter events, 23.3 us)
Async XLA Ops:
  0.6 68.6 %copy-start = (bf16[64,128,128]{2,1,0:T(8,128)(2,1)S(1)}, bf16[64,128,128]{2,1,0:T(8,128)(2,1)}, u32[]{:S(2)}) copy-start(bf16[64,128,128]{2,1,0:T(8,128)(2,1)} %refs_5_.5) | copy-start | bytes 6291460
  0.6 1.3 copy-start.4
  2.3 27.9 %collective-permute-start = (bf16[32,1664]{1,0:T(8,128)(2,1)S(1)}, bf16[32,1664]{1,0:T(8,128)(2,1)S(1)}, u32[]{:S(2)}, u32[]{:S(2)}) collective-permute-start(bf16[32,1664]{1,0:T(8,128)(2,1)S(1)} %get-tuple-element.33), channel_id=1, source_target_pairs={{0,1},{1,2},{2,3},{3,4},{4,5},{5,6},{6,7},{7,0},{8,9},{9,10},{10,1... | collective-permute-start | bytes 319496 | tf_op jit(solution)/shard_map/ppermute | solution.py:21
  6.2 28.6 %collective-permute-start.1 = (bf16[32,1664]{1,0:T(8,128)(2,1)S(1)}, bf16[32,1664]{1,0:T(8,128)(2,1)S(1)}, u32[]{:S(2)}, u32[]{:S(2)}) collective-permute-start(bf16[32,1664]{1,0:T(8,128)(2,1)S(1)} %get-tuple-element.34), channel_id=1, source_target_pairs={{0,2},{1,3},{2,4},{3,5},{4,6},{5,7},{6,0},{7,1},{8,10},{9,11},{10,... | collective-permute-start | bytes 319496 | tf_op jit(solution)/shard_map/ppermute | solution.py:21
  11.3 29.7 %collective-permute-start.2 = (bf16[32,1664]{1,0:T(8,128)(2,1)S(1)}, bf16[32,1664]{1,0:T(8,128)(2,1)S(1)}, u32[]{:S(2)}, u32[]{:S(2)}) collective-permute-start(bf16[32,1664]{1,0:T(8,128)(2,1)S(1)} %get-tuple-element.35), channel_id=1, source_target_pairs={{0,3},{1,4},{2,5},{3,6},{4,7},{5,0},{6,1},{7,2},{8,11},{9,12},{10,... | collective-permute-start | bytes 319496 | tf_op jit(solution)/shard_map/ppermute | solution.py:21
  19.1 22.0 %collective-permute-start.3 = (bf16[32,1664]{1,0:T(8,128)(2,1)S(1)}, bf16[32,1664]{1,0:T(8,128)(2,1)S(1)}, u32[]{:S(2)}, u32[]{:S(2)}) collective-permute-start(bf16[32,1664]{1,0:T(8,128)(2,1)S(1)} %get-tuple-element.36), channel_id=1, source_target_pairs={{0,4},{1,5},{2,6},{3,7},{4,0},{5,1},{6,2},{7,3},{8,12},{9,13},{10,... | collective-permute-start | bytes 319496 | tf_op jit(solution)/shard_map/ppermute | solution.py:21
  22.4 18.7 %collective-permute-start.4 = (bf16[32,1664]{1,0:T(8,128)(2,1)S(1)}, bf16[32,1664]{1,0:T(8,128)(2,1)S(1)}, u32[]{:S(2)}, u32[]{:S(2)}) collective-permute-start(bf16[32,1664]{1,0:T(8,128)(2,1)S(1)} %get-tuple-element.37), channel_id=1, source_target_pairs={{0,5},{1,6},{2,7},{3,0},{4,1},{5,2},{6,3},{7,4},{8,13},{9,14},{10,... | collective-permute-start | bytes 319496 | tf_op jit(solution)/shard_map/ppermute | solution.py:21
  30.2 15.6 %collective-permute-start.5 = (bf16[32,1664]{1,0:T(8,128)(2,1)S(1)}, bf16[32,1664]{1,0:T(8,128)(2,1)S(1)}, u32[]{:S(2)}, u32[]{:S(2)}) collective-permute-start(bf16[32,1664]{1,0:T(8,128)(2,1)S(1)} %get-tuple-element.38), channel_id=1, source_target_pairs={{0,6},{1,7},{2,0},{3,1},{4,2},{5,3},{6,4},{7,5},{8,14},{9,15},{10,... | collective-permute-start | bytes 319496 | tf_op jit(solution)/shard_map/ppermute | solution.py:21
  34.8 11.1 %collective-permute-start.6 = (bf16[32,1664]{1,0:T(8,128)(2,1)S(1)}, bf16[32,1664]{1,0:T(8,128)(2,1)S(1)}, u32[]{:S(2)}, u32[]{:S(2)}) collective-permute-start(bf16[32,1664]{1,0:T(8,128)(2,1)S(1)} %get-tuple-element.39), channel_id=1, source_target_pairs={{0,7},{1,0},{2,1},{3,2},{4,3},{5,4},{6,5},{7,6},{8,15},{9,8},{10,9... | collective-permute-start | bytes 319496 | tf_op jit(solution)/shard_map/ppermute | solution.py:21
  47.0 25.9 %collective-permute-start.7 = (bf16[256,1024]{1,0:T(8,128)(2,1)}, bf16[256,1024]{1,0:T(8,128)(2,1)S(1)}, u32[]{:S(2)}, u32[]{:S(2)}) collective-permute-start(bf16[256,1024]{1,0:T(8,128)(2,1)} %get-tuple-element.41), channel_id=1, source_target_pairs={{0,1},{1,2},{2,3},{3,4},{4,5},{5,6},{6,7},{7,8},{8,9},{9,10},{10,1... | collective-permute-start | bytes 1572872 | tf_op jit(solution)/shard_map/ppermute | solution.py:21
  52.1 28.3 %collective-permute-start.8 = (bf16[256,1024]{1,0:T(8,128)(2,1)}, bf16[256,1024]{1,0:T(8,128)(2,1)}, u32[]{:S(2)}, u32[]{:S(2)}) collective-permute-start(bf16[256,1024]{1,0:T(8,128)(2,1)} %get-tuple-element.42), channel_id=1, source_target_pairs={{0,511},{1,0},{2,1},{3,2},{4,3},{5,4},{6,5},{7,6},{8,7},{9,8},{10,... | collective-permute-start | bytes 1572872 | tf_op jit(solution)/shard_map/ppermute | solution.py:21
  69.2 0.7 copy-start.7
  71.3 0.7 copy-start.13
  72.0 8.4 %copy-start.5 = (bf16[256,1664]{1,0:T(8,128)(2,1)S(1)}, bf16[256,1664]{1,0:T(8,128)(2,1)}, u32[]{:S(2)}) copy-start(bf16[256,1664]{1,0:T(8,128)(2,1)} %refs_11_.1) | copy-start | bytes 2555908
  72.0 8.4 %copy-start.8 = (s32[192]{0:T(256)S(1)}, s32[192]{0:T(256)}, u32[]{:S(2)}) copy-start(s32[192]{0:T(256)} %get-tuple-element.29.refs_1_) | copy-start | bytes 2308
  72.0 8.4 %copy-start.10 = (s32[192]{0:T(256)S(1)}, s32[192]{0:T(256)}, u32[]{:S(2)}) copy-start(s32[192]{0:T(256)} %get-tuple-element.30.refs_2_) | copy-start | bytes 2308
  72.0 8.4 %copy-start.12 = (s32[192]{0:T(256)S(1)}, s32[192]{0:T(256)}, u32[]{:S(2)}) copy-start(s32[192]{0:T(256)} %get-tuple-element.31.refs_3_) | copy-start | bytes 2308
  72.0 8.4 %copy-start.14 = (s32[3]{0:T(128)S(1)}, s32[3]{0:T(128)}, u32[]{:S(2)}) copy-start(s32[3]{0:T(128)} %get-tuple-element.46.refs_0_) | copy-start | bytes 40
  85.9 1.2 copy-start.1
  87.1 0.8 copy-start.6
  87.9 19.7 %all-to-all-start = ((f32[32,16,256]{2,1,0:T(8,128)}), f32[32,16,256]{2,1,0:T(8,128)}, u32[]{:S(2)}, u32[]{:S(2)}) async-start(f32[32,16,256]{2,1,0:T(8,128)} %bitcast.10), calls=%async_computation | async-start | bytes 1048576 | tf_op jit(solution)/shard_map/all_to_all | solution.py:343
  95.5 1.5 copy-start.2
  99.0 23.2 %collective-permute-start.10 = (bf16[256,1024]{1,0:T(8,128)(2,1)}, bf16[256,1024]{1,0:T(8,128)(2,1)S(1)}, u32[]{:S(2)}, u32[]{:S(2)}) collective-permute-start(bf16[256,1024]{1,0:T(8,128)(2,1)} %get-tuple-element.49), channel_id=1, source_target_pairs={{0,511},{1,0},{2,1},{3,2},{4,3},{5,4},{6,5},{7,6},{8,7},{9,8},{10,... | collective-permute-start | bytes 1572872 | tf_op jit(solution)/shard_map/ppermute | solution.py:21
  105.7 24.9 %collective-permute-start.9 = (bf16[256,1024]{1,0:T(8,128)(2,1)}, bf16[256,1024]{1,0:T(8,128)(2,1)S(1)}, u32[]{:S(2)}, u32[]{:S(2)}) collective-permute-start(bf16[256,1024]{1,0:T(8,128)(2,1)} %get-tuple-element.48), channel_id=1, source_target_pairs={{0,1},{1,2},{2,3},{3,4},{4,5},{5,6},{6,7},{7,8},{8,9},{9,10},{10,1... | collective-permute-start | bytes 1572872 | tf_op jit(solution)/shard_map/ppermute | solution.py:21
  109.4 34.2 %all-to-all-start.1 = ((bf16[16,16,256]{2,1,0:T(8,128)(2,1)}), bf16[16,16,256]{2,1,0:T(8,128)(2,1)S(1)}, u32[]{:S(2)}, u32[]{:S(2)}) async-start(bf16[16,16,256]{2,1,0:T(8,128)(2,1)} %broadcast_in_dim.10), calls=%async_computation.1 | async-start | bytes 262144 | tf_op jit(solution)/shard_map/all_to_all | solution.py:348
  119.8 1.5 copy-start.3
  143.6 46.3 %all-to-all-start.2 = ((bf16[8,32,1664]{2,1,0:T(8,128)(2,1)}), bf16[8,32,1664]{2,1,0:T(8,128)(2,1)S(1)}, u32[]{:S(2)}, u32[]{:S(2)}) async-start(bf16[8,32,1664]{2,1,0:T(8,128)(2,1)} %bitcast.6), calls=%async_computation.2 | async-start | bytes 1703936 | tf_op jit(solution)/shard_map/all_to_all | solution.py:353
  147.4 3.1 %collective-permute-start.11 = (bf16[16,256]{1,0:T(8,128)(2,1)S(1)}, bf16[16,256]{1,0:T(8,128)(2,1)S(1)}, u32[]{:S(2)}, u32[]{:S(2)}) collective-permute-start(bf16[16,256]{1,0:T(8,128)(2,1)S(1)} %multiply_convert_fusion), channel_id=1, source_target_pairs={{0,8},{8,0},{1,9},{9,1},{2,10},{10,2},{3,11},{11,3},{4,12},{12,4},... | collective-permute-start | bytes 24584 | tf_op jit(solution)/shard_map/ppermute | solution.py:29
  150.4 5.6 %collective-permute-start.12 = (bf16[32,256]{1,0:T(8,128)(2,1)S(1)}, bf16[32,256]{1,0:T(8,128)(2,1)S(1)}, u32[]{:S(2)}, u32[]{:S(2)}) collective-permute-start(bf16[32,256]{1,0:T(8,128)(2,1)S(1)} %pad_maximum_fusion.5), channel_id=1, source_target_pairs={{0,16},{16,0},{32,48},{48,32},{1,17},{17,1},{33,49},{49,33},{2,18}... | collective-permute-start | bytes 49160 | tf_op jit(solution)/shard_map/ppermute | solution.py:29
  156.1 7.3 %collective-permute-start.13 = (bf16[64,256]{1,0:T(8,128)(2,1)S(1)}, bf16[64,256]{1,0:T(8,128)(2,1)S(1)}, u32[]{:S(2)}, u32[]{:S(2)}) collective-permute-start(bf16[64,256]{1,0:T(8,128)(2,1)S(1)} %pad_maximum_fusion.4), channel_id=1, source_target_pairs={{0,32},{16,48},{32,0},{48,16},{1,33},{17,49},{33,1},{49,17},{2,34}... | collective-permute-start | bytes 98312 | tf_op jit(solution)/shard_map/ppermute | solution.py:29
  163.4 6.2 %collective-permute-start.14 = (bf16[128,256]{1,0:T(8,128)(2,1)S(1)}, bf16[128,256]{1,0:T(8,128)(2,1)S(1)}, u32[]{:S(2)}, u32[]{:S(2)}) collective-permute-start(bf16[128,256]{1,0:T(8,128)(2,1)S(1)} %pad_maximum_fusion.3), channel_id=1, source_target_pairs={{0,64},{64,0},{128,192},{192,128},{1,65},{65,1},{129,193},{193,129... | collective-permute-start | bytes 196616 | tf_op jit(solution)/shard_map/ppermute | solution.py:29
  169.6 8.4 %collective-permute-start.15 = (bf16[256,256]{1,0:T(8,128)(2,1)S(1)}, bf16[256,256]{1,0:T(8,128)(2,1)S(1)}, u32[]{:S(2)}, u32[]{:S(2)}) collective-permute-start(bf16[256,256]{1,0:T(8,128)(2,1)S(1)} %pad_maximum_fusion.2), channel_id=1, source_target_pairs={{0,128},{64,192},{128,0},{192,64},{1,129},{65,193},{129,1},{193,65... | collective-permute-start | bytes 393224 | tf_op jit(solution)/shard_map/ppermute | solution.py:29
  (2 other events, 1.3 us)

commit v8 on v7

--- a/solution.py
+++ b/solution.py
@@ -117,31 +117,54 @@
         some([base + count - 1])
 
 
-def before_kernel(*refs):
-    lists, (own_ref, values_ref, agg_ref) = refs[:4], refs[4:]
+def before_kernel(pos_ref, *refs):
+    lists, (own_ref, values_ref, prev_ref, next_ref) = refs[:4], refs[4:8]
+    piece_refs, (agg_ref, rim_ref) = refs[8:-2], refs[-2:]
     agg_ref[...] = jnp.zeros_like(agg_ref)
     add_slots(lists, OWN, own_ref, agg_ref, values_ref, True)
-
-
-def before_step(lists, own, values):
+    last = len(piece_refs)
+    height = prev_ref.shape[0]
+
+    @pl.when(pos_ref[0] == 0)
+    def _():
+        for group, ref in enumerate((prev_ref, *piece_refs)):
+            rim_ref[group * height : (group + 1) * height] = ref[...]
+
+    @pl.when(pos_ref[0] != 0)
+    def _():
+        for group, ref in enumerate((next_ref, *piece_refs)):
+            rim_ref[(last - group) * height : (last - group + 1) * height] = ref[...]
+
+
+def before_step(pos, lists, own, values, prev_part, next_part, gathered):
+    depth, rim = own.shape[0], prev_part.shape[1]
     return pl.pallas_call(
         before_kernel,
-        out_shape=jax.ShapeDtypeStruct(own.shape, jnp.float32),
-        in_specs=[SMEM] * 4 + [VMEM] * 2,
-        out_specs=VMEM,
+        out_shape=(
+            jax.ShapeDtypeStruct(own.shape, jnp.float32),
+            jax.ShapeDtypeStruct((depth, rim), own.dtype),
+        ),
+        in_specs=[SMEM] * 5 + [VMEM] * (4 + len(gathered)),
+        out_specs=(VMEM,) * 2,
         compiler_params=pltpu.CompilerParams(vmem_limit_bytes=24 * 1024 * 1024),
         cost_estimate=pl.CostEstimate(flops=1 << 28, bytes_accessed=4 << 20, transcendentals=0),
-    )(*lists, own, values)
-
-
-def local_kernel(*refs):
+    )(pos, *lists, own, values, prev_part, next_part, *gathered)
+
+
+def local_kernel(last, pos_ref, *refs):
     lists = refs[:4]
-    (agg_ref, own_ref, before_ref, after_ref, values_ref, w_in_ref, w_out_ref, cot_ref) = refs[4:12]
-    terms_ref, both_ref, stacked, delta, agg, held, terms, sems = refs[12:]
+    agg_ref, own_ref, before_ref, after_ref, rim_ref, values_ref = refs[4:10]
+    w_in_ref, w_out_ref, cot_ref = refs[10:13]
+    terms_ref, both_ref, stacked, delta, agg, held, terms, sems = refs[13:]
     depth, width = own_ref.shape
     agg[...] = agg_ref[...]
-    add_slots(lists, LEFT, before_ref, agg, values_ref, True)
-    add_slots(lists, RIGHT, after_ref, agg, values_ref, True)
+    for kind, ref, edge in ((LEFT, before_ref, 0), (RIGHT, after_ref, last)):
+        pl.when(pos_ref[0] == edge)(
+            functools.partial(add_slots, lists, kind, rim_ref, agg, values_ref, True)
+        )
+        pl.when(pos_ref[0] != edge)(
+            functools.partial(add_slots, lists, kind, ref, agg, values_ref, True)
+        )
     for at, size in tiles_of(width, 256):
         part = slice(at, at + size)
         stacked[:depth, part] = own_ref[:, part]
@@ -192,13 +215,13 @@
     )(*lists, both, values)
 
 
-def local_step(lists, agg, own, before, after, values, w_in, w_out, cot):
+def local_step(pos, lists, agg, own, before, after, rim_part, values, w_in, w_out, cot):
     depth, width = own.shape
     both = jax.ShapeDtypeStruct((2 * depth, width), jnp.bfloat16)
     return pl.pallas_call(
-        local_kernel,
+        functools.partial(local_kernel, lax.axis_size("feat") - 1),
         out_shape=(jax.ShapeDtypeStruct((2 * depth, depth), jnp.float32), both),
-        in_specs=[SMEM] * 4 + [VMEM] * 8,
+        in_specs=[SMEM] * 5 + [VMEM] * 9,
         out_specs=(HBM, HBM),
         scratch_shapes=[
             pltpu.VMEM((2 * depth, width), jnp.bfloat16),
@@ -212,7 +235,7 @@
         cost_estimate=pl.CostEstimate(
             flops=12 * depth * depth * width, bytes_accessed=8 << 20, transcendentals=depth * width
         ),
-    )(*lists, agg, own, before, after, values, w_in, w_out, cot)
+    )(pos, *lists, agg, own, before, after, rim_part, values, w_in, w_out, cot)
 
 
 def after_kernel(*refs):
@@ -327,12 +350,21 @@
     received = list(cut_step(pos, features, pieces))
     for step in sorted(range(1, pieces), key=lambda step: (abs(2 * step - pieces), step)):
         received[step] = shifted(received[step], "feat", step)
+    prev_part = shifted(features[:, rows_part - rim :], DOM, 1)
+    next_part = shifted(features[:, :rim], DOM, -1)
+    gathered = []
+    for step in range(1, pieces):
+        part = jnp.where(pos[0] == step, prev_part, next_part)
+        gathered.append(
+            lax.ppermute(part, "feat", [(step, 0), (pieces - 1 - step, pieces - 1)])
+        )
+    *received, gathered = lax.optimization_barrier((*received, gathered))
     own, head, tail = join_step(pos, received, rim)
-    before = shifted(tail, RING, 1)
-    after = shifted(head, RING, -1)
-    agg = before_step(lists, own, block_values)
+    before = lax.ppermute(tail, "feat", [(i, i + 1) for i in range(pieces - 1)])
+    after = lax.ppermute(head, "feat", [(i + 1, i) for i in range(pieces - 1)])
+    agg, rim_part = before_step(pos, lists, own, block_values, prev_part, next_part, gathered)
     terms, both = local_step(
-        lists, agg, own, before, after, block_values, w_in, w_out, cotangent
+        pos, lists, agg, own, before, after, rim_part, block_values, w_in, w_out, cotangent
     )
     plane, line = lax.axis_size(PLANE), lax.axis_size(LINE)
     share = 2 * depth // plane

time: 192 us -> 219 us (1.14); the launches traced: 191 us -> 216 us
  starting transfers between devices: 96.1 us -> 127 us
  waiting for transfers between devices: 61.6 us -> 44.3 us
  local copies, waits for them, and re-layouts: 13.9 us -> 24.3 us
    ppermute x0 -> x9, starting transfers between devices: none -> 27.4 us  [the longest x7 23.9 us: on_device(): lax.ppermute(part, 'feat', [(step, 0), (pieces - 1 - step, pieces - 1)])]
    ppermute x11, waiting for transfers between devices: 24 us -> 12.1 us  [shifted(): lax.ppermute(shard, axis, [(i, (i + by) % count) for i in range(count)])]
    unnamed x32 -> x64, local copies, waits for them, and re-layouts: 12.2 us -> 22.7 us
    all_to_all x1, waiting for transfers between devices: 11.9 us -> 3.88 us  [on_device(): lax.all_to_all(copies, LINE, split_axis=0, concat_axis=0, tiled=True)]
    all_to_all x1, starting transfers between devices: 7.62 us -> 13 us  [on_device(): lax.all_to_all(terms, PLANE, split_axis=0, concat_axis=0, tiled=True)]
    ppermute x11, starting transfers between devices: 58.4 us -> 54.1 us  [shifted(): lax.ppermute(shard, axis, [(i, (i + by) % count) for i in range(count)])]
    ppermute x0 -> x9, waiting for transfers between devices: none -> 3.97 us  [the longest x7 3.96 us: on_device(): lax.ppermute(part, 'feat', [(step, 0), (pieces - 1 - step, pieces - 1)])]
    all_to_all x1, starting transfers between devices: 3.75 us -> 7.33 us  [on_device(): lax.all_to_all(total, 'feat', split_axis=0, concat_axis=1, tiled=True)]
  transfers between devices with their start and end apart: 19 -> 28, of which waited for: 11 -> 11; matrix products, arithmetic and copies ran while one was open for 4% -> 4% of each run, Pallas kernels for 4% -> 3%
where the time goes in v8:
time: 219 us; the launch traced here: 216 us
  starting transfers between devices  127 us (58%)
  waiting for transfers between devices  44.3 us (20%)
  local copies, waits for them, and re-layouts  24.3 us (11%)
  Pallas kernels  14.1 us (6%)
  other arithmetic  3.96 us (2%)
    ppermute x11, starting transfers between devices, shifted(): lax.ppermute(shard, axis, [(i, (i + by) % count) for i in range(count)])  54.1 us
    ppermute x7, starting transfers between devices, on_device(): lax.ppermute(part, 'feat', [(step, 0), (pieces - 1 - step, pieces - 1)])  23.9 us
    unnamed x64, local copies, waits for them, and re-layouts  22.7 us
    ppermute x5, starting transfers between devices, collected(): other = lax.ppermute(rows, axis, [(i, i ^ apart) for i in range(count)])  16.4 us
    ppermute x5, waiting for transfers between devices, collected(): other = lax.ppermute(rows, axis, [(i, i ^ apart) for i in range(count)])  14 us
    all_to_all x1, starting transfers between devices, on_device(): lax.all_to_all(terms, PLANE, split_axis=0, concat_axis=0, tiled=True)  13 us
    ppermute x11, waiting for transfers between devices, shifted(): lax.ppermute(shard, axis, [(i, (i + by) % count) for i in range(count)])  12.1 us
    all_to_all x1, waiting for transfers between devices, on_device(): lax.all_to_all(total, 'feat', split_axis=0, concat_axis=1, tiled=True)  10.4 us
  transfers between devices with their start and end apart: 28, of which 11 were waited for; matrix products, arithmetic and copies ran while one was open for 4% of the time, Pallas kernels for 3%

profile of v8, /device:TPU:6, one launch (start us, length us, event | category | flops | bytes accessed | tf_op | source)
XLA Modules:
  0.0 215.6 jit_solution(4249489225817333708)
XLA Ops:
  2.8 4.0 %collective-permute-start = (bf16[32,1664]{1,0:T(8,128)(2,1)}, bf16[32,1664]{1,0:T(8,128)(2,1)S(1)}, u32[]{:S(2)}, u32[]{:S(2)}) collective-permute-start(bf16[32,1664]{1,0:T(8,128)(2,1)} %get-tuple-element.50), channel_id=1, source_target_pairs={{0,1},{1,2},{2,3},{3,4},{4,5},{5,6},{6,7},{7,0},{8,9},{9,10},{10,1... | collective-permute-start | bytes 319496 | tf_op jit(solution)/shard_map/ppermute | solution.py:21
  6.8 5.2 %collective-permute-start.1 = (bf16[32,1664]{1,0:T(8,128)(2,1)S(1)}, bf16[32,1664]{1,0:T(8,128)(2,1)S(1)}, u32[]{:S(2)}, u32[]{:S(2)}) collective-permute-start(bf16[32,1664]{1,0:T(8,128)(2,1)S(1)} %get-tuple-element.51), channel_id=1, source_target_pairs={{0,2},{1,3},{2,4},{3,5},{4,6},{5,7},{6,0},{7,1},{8,10},{9,11},{10,... | collective-permute-start | bytes 319496 | tf_op jit(solution)/shard_map/ppermute | solution.py:21
  12.0 1.9 collective-permute-start.7
  13.9 3.6 %collective-permute-start.8 = (bf16[32,1024]{1,0:T(8,128)(2,1)S(1)}, bf16[32,1024]{1,0:T(8,128)(2,1)S(1)}, u32[]{:S(2)}, u32[]{:S(2)}) collective-permute-start(bf16[32,1024]{1,0:T(8,128)(2,1)S(1)} %get-tuple-element.87), channel_id=1, source_target_pairs={{0,504},{8,0},{16,8},{24,16},{32,24},{40,32},{48,40},{56,48},{64,5... | collective-permute-start | bytes 196616 | tf_op jit(solution)/shard_map/ppermute | solution.py:21
  17.6 7.7 %collective-permute-start.2 = (bf16[32,1664]{1,0:T(8,128)(2,1)S(1)}, bf16[32,1664]{1,0:T(8,128)(2,1)S(1)}, u32[]{:S(2)}, u32[]{:S(2)}) collective-permute-start(bf16[32,1664]{1,0:T(8,128)(2,1)S(1)} %get-tuple-element.52), channel_id=1, source_target_pairs={{0,3},{1,4},{2,5},{3,6},{4,7},{5,0},{6,1},{7,2},{8,11},{9,12},{10,... | collective-permute-start | bytes 319496 | tf_op jit(solution)/shard_map/ppermute | solution.py:21
  25.3 3.3 %collective-permute-start.3 = (bf16[32,1664]{1,0:T(8,128)(2,1)S(1)}, bf16[32,1664]{1,0:T(8,128)(2,1)S(1)}, u32[]{:S(2)}, u32[]{:S(2)}) collective-permute-start(bf16[32,1664]{1,0:T(8,128)(2,1)S(1)} %get-tuple-element.53), channel_id=1, source_target_pairs={{0,4},{1,5},{2,6},{3,7},{4,0},{5,1},{6,2},{7,3},{8,12},{9,13},{10,... | collective-permute-start | bytes 319496 | tf_op jit(solution)/shard_map/ppermute | solution.py:21
  28.6 7.8 %collective-permute-start.4 = (bf16[32,1664]{1,0:T(8,128)(2,1)S(1)}, bf16[32,1664]{1,0:T(8,128)(2,1)S(1)}, u32[]{:S(2)}, u32[]{:S(2)}) collective-permute-start(bf16[32,1664]{1,0:T(8,128)(2,1)S(1)} %get-tuple-element.54), channel_id=1, source_target_pairs={{0,5},{1,6},{2,7},{3,0},{4,1},{5,2},{6,3},{7,4},{8,13},{9,14},{10,... | collective-permute-start | bytes 319496 | tf_op jit(solution)/shard_map/ppermute | solution.py:21
  36.5 4.6 %collective-permute-start.5 = (bf16[32,1664]{1,0:T(8,128)(2,1)S(1)}, bf16[32,1664]{1,0:T(8,128)(2,1)S(1)}, u32[]{:S(2)}, u32[]{:S(2)}) collective-permute-start(bf16[32,1664]{1,0:T(8,128)(2,1)S(1)} %get-tuple-element.55), channel_id=1, source_target_pairs={{0,6},{1,7},{2,0},{3,1},{4,2},{5,3},{6,4},{7,5},{8,14},{9,15},{10,... | collective-permute-start | bytes 319496 | tf_op jit(solution)/shard_map/ppermute | solution.py:21
  41.1 2.9 %collective-permute-start.6 = (bf16[32,1664]{1,0:T(8,128)(2,1)S(1)}, bf16[32,1664]{1,0:T(8,128)(2,1)S(1)}, u32[]{:S(2)}, u32[]{:S(2)}) collective-permute-start(bf16[32,1664]{1,0:T(8,128)(2,1)S(1)} %get-tuple-element.56), channel_id=1, source_target_pairs={{0,7},{1,0},{2,1},{3,2},{4,3},{5,4},{6,5},{7,6},{8,15},{9,8},{10,9... | collective-permute-start | bytes 319496 | tf_op jit(solution)/shard_map/ppermute | solution.py:21
  48.0 1.9 collective-permute-done.5.refs_6_
  54.1 16.2 %collective-permute-start.15 = (bf16[32,1024]{1,0:T(8,128)(2,1)S(1)}, bf16[32,1024]{1,0:T(8,128)(2,1)S(1)}, u32[]{:S(2)}, u32[]{:S(2)}) collective-permute-start(bf16[32,1024]{1,0:T(8,128)(2,1)S(1)} %get-tuple-element.93), channel_id=1, source_target_pairs={{7,0},{0,7},{15,8},{8,15},{23,16},{16,23},{31,24},{24,31},{39,32},... | collective-permute-start | bytes 196616 | tf_op jit(solution)/shard_map/ppermute | solution.py:359
  74.7 2.4 %collective-permute-done.9.refs_8_ = bf16[32,1024]{1,0:T(8,128)(2,1)S(1)} collective-permute-done((bf16[32,1024]{1,0:T(8,128)(2,1)S(1)}, bf16[32,1024]{1,0:T(8,128)(2,1)S(1)}, u32[]{:S(2)}, u32[]{:S(2)}) %collective-permute-start.9) | collective-permute-done | bytes 65568 | tf_op jit(solution)/shard_map/ppermute | solution.py:359
  78.8 2.2 %collective-permute-start.16 = (bf16[256,1024]{1,0:T(8,128)(2,1)}, bf16[256,1024]{1,0:T(8,128)(2,1)S(1)}, u32[]{:S(2)}, u32[]{:S(2)}) collective-permute-start(bf16[256,1024]{1,0:T(8,128)(2,1)} %get-tuple-element.74), channel_id=1, source_target_pairs={{0,1},{1,2},{2,3},{3,4},{4,5},{5,6},{6,7},{8,9},{9,10},{10,11},{11... | collective-permute-start | bytes 1572872 | tf_op jit(solution)/shard_map/ppermute | solution.py:363
  100.5 5.5 %shard_map.107 = (f32[512,256]{1,0:T(8,128)S(1)}, bf16[512,1664]{1,0:T(8,128)(2,1)S(1)}) custom-call(s32[1]{0:T(128)} %bitcast.2.pos_ref, s32[3]{0:T(128)S(1)} %copy-done.30, s32[192]{0:T(256)S(1)} %copy-done.24, s32[192]{0:T(256)S(1)} %copy-done.26, s32[192]{0:T(256)S(1)} %copy-done.28, f32[256,1664]{1,0:T(8,128)S(1)} %get-tuple-element.73.refs_4_, ...), custom_call_target="tpu_custom_call" | custom-call | flops 1308622848 | bytes 8388608 | tf_op jit(solution)/shard_map/pallas_call | solution.py:221
  108.0 13.0 %all-to-all-start = ((f32[32,16,256]{2,1,0:T(8,128)}), f32[32,16,256]{2,1,0:T(8,128)}, u32[]{:S(2)}, u32[]{:S(2)}) async-start(f32[32,16,256]{2,1,0:T(8,128)} %bitcast.10), calls=%async_computation | async-start | bytes 1048576 | tf_op jit(solution)/shard_map/all_to_all | solution.py:375
  122.5 2.0 shard_map.109
  124.5 4.3 %collective-permute-start.18 = (bf16[256,1024]{1,0:T(8,128)(2,1)}, bf16[256,1024]{1,0:T(8,128)(2,1)S(1)}, u32[]{:S(2)}, u32[]{:S(2)}) collective-permute-start(bf16[256,1024]{1,0:T(8,128)(2,1)} %get-tuple-element.82), channel_id=1, source_target_pairs={{0,1},{1,2},{2,3},{3,4},{4,5},{5,6},{6,7},{7,8},{8,9},{9,10},{10,1... | collective-permute-start | bytes 1572872 | tf_op jit(solution)/shard_map/ppermute | solution.py:21
  128.9 8.7 %collective-permute-start.19 = (bf16[256,1024]{1,0:T(8,128)(2,1)}, bf16[256,1024]{1,0:T(8,128)(2,1)S(1)}, u32[]{:S(2)}, u32[]{:S(2)}) collective-permute-start(bf16[256,1024]{1,0:T(8,128)(2,1)} %get-tuple-element.83), channel_id=1, source_target_pairs={{0,511},{1,0},{2,1},{3,2},{4,3},{5,4},{6,5},{7,6},{8,7},{9,8},{10,... | collective-permute-start | bytes 1572872 | tf_op jit(solution)/shard_map/ppermute | solution.py:21
  139.4 8.7 %all-to-all-start.1 = ((bf16[16,16,256]{2,1,0:T(8,128)(2,1)}), bf16[16,16,256]{2,1,0:T(8,128)(2,1)S(1)}, u32[]{:S(2)}, u32[]{:S(2)}) async-start(bf16[16,16,256]{2,1,0:T(8,128)(2,1)} %broadcast_in_dim.10), calls=%async_computation.1 | async-start | bytes 262144 | tf_op jit(solution)/shard_map/all_to_all | solution.py:380
  150.4 10.1 %collective-permute-done.19.next_ref = bf16[256,1024]{1,0:T(8,128)(2,1)S(1)} collective-permute-done((bf16[256,1024]{1,0:T(8,128)(2,1)}, bf16[256,1024]{1,0:T(8,128)(2,1)S(1)}, u32[]{:S(2)}, u32[]{:S(2)}) %collective-permute-start.19) | collective-permute-done | bytes 524320 | tf_op jit(solution)/shard_map/ppermute | solution.py:21
  161.6 3.9 %all-to-all-done.1 = bf16[16,16,256]{2,1,0:T(8,128)(2,1)S(1)} async-done(((bf16[16,16,256]{2,1,0:T(8,128)(2,1)}), bf16[16,16,256]{2,1,0:T(8,128)(2,1)S(1)}, u32[]{:S(2)}, u32[]{:S(2)}) %all-to-all-start.1) | async-done | bytes 131104 | tf_op jit(solution)/shard_map/all_to_all | solution.py:380
  165.5 7.3 %all-to-all-start.2 = ((bf16[8,32,1664]{2,1,0:T(8,128)(2,1)}), bf16[8,32,1664]{2,1,0:T(8,128)(2,1)S(1)}, u32[]{:S(2)}, u32[]{:S(2)}) async-start(bf16[8,32,1664]{2,1,0:T(8,128)(2,1)} %bitcast.6), calls=%async_computation.2 | async-start | bytes 1703936 | tf_op jit(solution)/shard_map/all_to_all | solution.py:385
  172.8 1.9 collective-permute-start.20
  175.9 2.6 %collective-permute-start.21 = (bf16[32,256]{1,0:T(8,128)(2,1)S(1)}, bf16[32,256]{1,0:T(8,128)(2,1)S(1)}, u32[]{:S(2)}, u32[]{:S(2)}) collective-permute-start(bf16[32,256]{1,0:T(8,128)(2,1)S(1)} %pad_maximum_fusion.5), channel_id=1, source_target_pairs={{0,16},{16,0},{32,48},{48,32},{1,17},{17,1},{33,49},{49,33},{2,18}... | collective-permute-start | bytes 49160 | tf_op jit(solution)/shard_map/ppermute | solution.py:29
  178.6 3.0 %collective-permute-done.21 = bf16[32,256]{1,0:T(8,128)(2,1)S(1)} collective-permute-done((bf16[32,256]{1,0:T(8,128)(2,1)S(1)}, bf16[32,256]{1,0:T(8,128)(2,1)S(1)}, u32[]{:S(2)}, u32[]{:S(2)}) %collective-permute-start.21) | collective-permute-done | bytes 16416 | tf_op jit(solution)/shard_map/ppermute | solution.py:29
  181.6 3.4 %collective-permute-start.22 = (bf16[64,256]{1,0:T(8,128)(2,1)S(1)}, bf16[64,256]{1,0:T(8,128)(2,1)S(1)}, u32[]{:S(2)}, u32[]{:S(2)}) collective-permute-start(bf16[64,256]{1,0:T(8,128)(2,1)S(1)} %pad_maximum_fusion.4), channel_id=1, source_target_pairs={{0,32},{16,48},{32,0},{48,16},{1,33},{17,49},{33,1},{49,17},{2,34}... | collective-permute-start | bytes 98312 | tf_op jit(solution)/shard_map/ppermute | solution.py:29
  185.0 3.9 %collective-permute-done.22 = bf16[64,256]{1,0:T(8,128)(2,1)S(1)} collective-permute-done((bf16[64,256]{1,0:T(8,128)(2,1)S(1)}, bf16[64,256]{1,0:T(8,128)(2,1)S(1)}, u32[]{:S(2)}, u32[]{:S(2)}) %collective-permute-start.22) | collective-permute-done | bytes 32800 | tf_op jit(solution)/shard_map/ppermute | solution.py:29
  188.9 3.5 %collective-permute-start.23 = (bf16[128,256]{1,0:T(8,128)(2,1)S(1)}, bf16[128,256]{1,0:T(8,128)(2,1)S(1)}, u32[]{:S(2)}, u32[]{:S(2)}) collective-permute-start(bf16[128,256]{1,0:T(8,128)(2,1)S(1)} %pad_maximum_fusion.3), channel_id=1, source_target_pairs={{0,64},{64,0},{128,192},{192,128},{1,65},{65,1},{129,193},{193,129... | collective-permute-start | bytes 196616 | tf_op jit(solution)/shard_map/ppermute | solution.py:29
  192.4 2.7 %collective-permute-done.23 = bf16[128,256]{1,0:T(8,128)(2,1)S(1)} collective-permute-done((bf16[128,256]{1,0:T(8,128)(2,1)S(1)}, bf16[128,256]{1,0:T(8,128)(2,1)S(1)}, u32[]{:S(2)}, u32[]{:S(2)}) %collective-permute-start.23) | collective-permute-done | bytes 65568 | tf_op jit(solution)/shard_map/ppermute | solution.py:29
  195.1 5.0 %collective-permute-start.24 = (bf16[256,256]{1,0:T(8,128)(2,1)S(1)}, bf16[256,256]{1,0:T(8,128)(2,1)S(1)}, u32[]{:S(2)}, u32[]{:S(2)}) collective-permute-start(bf16[256,256]{1,0:T(8,128)(2,1)S(1)} %pad_maximum_fusion.2), channel_id=1, source_target_pairs={{0,128},{64,192},{128,0},{192,64},{1,129},{65,193},{129,1},{193,65... | collective-permute-start | bytes 393224 | tf_op jit(solution)/shard_map/ppermute | solution.py:29
  200.2 3.3 %collective-permute-done.24 = bf16[256,256]{1,0:T(8,128)(2,1)S(1)} collective-permute-done((bf16[256,256]{1,0:T(8,128)(2,1)S(1)}, bf16[256,256]{1,0:T(8,128)(2,1)S(1)}, u32[]{:S(2)}, u32[]{:S(2)}) %collective-permute-start.24) | collective-permute-done | bytes 131104 | tf_op jit(solution)/shard_map/ppermute | solution.py:29
  204.2 10.4 %all-to-all-done.2 = bf16[8,32,1664]{2,1,0:T(8,128)(2,1)S(1)} async-done(((bf16[8,32,1664]{2,1,0:T(8,128)(2,1)}), bf16[8,32,1664]{2,1,0:T(8,128)(2,1)S(1)}, u32[]{:S(2)}, u32[]{:S(2)}) %all-to-all-start.2) | async-done | bytes 852000 | tf_op jit(solution)/shard_map/all_to_all | solution.py:385
  (114 shorter events, 46.7 us)
Async XLA Ops:
  2.8 87.1 %copy-start = (bf16[64,128,128]{2,1,0:T(8,128)(2,1)S(1)}, bf16[64,128,128]{2,1,0:T(8,128)(2,1)}, u32[]{:S(2)}) copy-start(bf16[64,128,128]{2,1,0:T(8,128)(2,1)} %refs_5_.5) | copy-start | bytes 6291460
  2.8 33.7 %collective-permute-start = (bf16[32,1664]{1,0:T(8,128)(2,1)}, bf16[32,1664]{1,0:T(8,128)(2,1)S(1)}, u32[]{:S(2)}, u32[]{:S(2)}) collective-permute-start(bf16[32,1664]{1,0:T(8,128)(2,1)} %get-tuple-element.50), channel_id=1, source_target_pairs={{0,1},{1,2},{2,3},{3,4},{4,5},{5,6},{6,7},{7,0},{8,9},{9,10},{10,1... | collective-permute-start | bytes 319496 | tf_op jit(solution)/shard_map/ppermute | solution.py:21
  6.8 34.3 %collective-permute-start.1 = (bf16[32,1664]{1,0:T(8,128)(2,1)S(1)}, bf16[32,1664]{1,0:T(8,128)(2,1)S(1)}, u32[]{:S(2)}, u32[]{:S(2)}) collective-permute-start(bf16[32,1664]{1,0:T(8,128)(2,1)S(1)} %get-tuple-element.51), channel_id=1, source_target_pairs={{0,2},{1,3},{2,4},{3,5},{4,6},{5,7},{6,0},{7,1},{8,10},{9,11},{10,... | collective-permute-start | bytes 319496 | tf_op jit(solution)/shard_map/ppermute | solution.py:21
  12.0 13.3 %collective-permute-start.7 = (bf16[32,1024]{1,0:T(8,128)(2,1)S(1)}, bf16[32,1024]{1,0:T(8,128)(2,1)S(1)}, u32[]{:S(2)}, u32[]{:S(2)}) collective-permute-start(bf16[32,1024]{1,0:T(8,128)(2,1)S(1)} %get-tuple-element.88), channel_id=1, source_target_pairs={{0,8},{8,16},{16,24},{24,32},{32,40},{40,48},{48,56},{56,64},{64,7... | collective-permute-start | bytes 196616 | tf_op jit(solution)/shard_map/ppermute | solution.py:21
  13.9 14.7 %collective-permute-start.8 = (bf16[32,1024]{1,0:T(8,128)(2,1)S(1)}, bf16[32,1024]{1,0:T(8,128)(2,1)S(1)}, u32[]{:S(2)}, u32[]{:S(2)}) collective-permute-start(bf16[32,1024]{1,0:T(8,128)(2,1)S(1)} %get-tuple-element.87), channel_id=1, source_target_pairs={{0,504},{8,0},{16,8},{24,16},{32,24},{40,32},{48,40},{56,48},{64,5... | collective-permute-start | bytes 196616 | tf_op jit(solution)/shard_map/ppermute | solution.py:21
  17.6 26.5 %collective-permute-start.2 = (bf16[32,1664]{1,0:T(8,128)(2,1)S(1)}, bf16[32,1664]{1,0:T(8,128)(2,1)S(1)}, u32[]{:S(2)}, u32[]{:S(2)}) collective-permute-start(bf16[32,1664]{1,0:T(8,128)(2,1)S(1)} %get-tuple-element.52), channel_id=1, source_target_pairs={{0,3},{1,4},{2,5},{3,6},{4,7},{5,0},{6,1},{7,2},{8,11},{9,12},{10,... | collective-permute-start | bytes 319496 | tf_op jit(solution)/shard_map/ppermute | solution.py:21
  25.3 20.1 %collective-permute-start.3 = (bf16[32,1664]{1,0:T(8,128)(2,1)S(1)}, bf16[32,1664]{1,0:T(8,128)(2,1)S(1)}, u32[]{:S(2)}, u32[]{:S(2)}) collective-permute-start(bf16[32,1664]{1,0:T(8,128)(2,1)S(1)} %get-tuple-element.53), channel_id=1, source_target_pairs={{0,4},{1,5},{2,6},{3,7},{4,0},{5,1},{6,2},{7,3},{8,12},{9,13},{10,... | collective-permute-start | bytes 319496 | tf_op jit(solution)/shard_map/ppermute | solution.py:21
  28.6 48.4 %copy-start.7 = (bf16[32,1024]{1,0:T(8,128)(2,1)}, bf16[32,1024]{1,0:T(8,128)(2,1)S(1)}, u32[]{:S(2)}) copy-start(bf16[32,1024]{1,0:T(8,128)(2,1)S(1)} %collective-permute-done.8.refs_7_) | copy-start | bytes 196612
  28.6 18.0 %collective-permute-start.4 = (bf16[32,1664]{1,0:T(8,128)(2,1)S(1)}, bf16[32,1664]{1,0:T(8,128)(2,1)S(1)}, u32[]{:S(2)}, u32[]{:S(2)}) collective-permute-start(bf16[32,1664]{1,0:T(8,128)(2,1)S(1)} %get-tuple-element.54), channel_id=1, source_target_pairs={{0,5},{1,6},{2,7},{3,0},{4,1},{5,2},{6,3},{7,4},{8,13},{9,14},{10,... | collective-permute-start | bytes 319496 | tf_op jit(solution)/shard_map/ppermute | solution.py:21
  36.5 13.4 %collective-permute-start.5 = (bf16[32,1664]{1,0:T(8,128)(2,1)S(1)}, bf16[32,1664]{1,0:T(8,128)(2,1)S(1)}, u32[]{:S(2)}, u32[]{:S(2)}) collective-permute-start(bf16[32,1664]{1,0:T(8,128)(2,1)S(1)} %get-tuple-element.55), channel_id=1, source_target_pairs={{0,6},{1,7},{2,0},{3,1},{4,2},{5,3},{6,4},{7,5},{8,14},{9,15},{10,... | collective-permute-start | bytes 319496 | tf_op jit(solution)/shard_map/ppermute | solution.py:21
  41.1 10.1 %collective-permute-start.6 = (bf16[32,1664]{1,0:T(8,128)(2,1)S(1)}, bf16[32,1664]{1,0:T(8,128)(2,1)S(1)}, u32[]{:S(2)}, u32[]{:S(2)}) collective-permute-start(bf16[32,1664]{1,0:T(8,128)(2,1)S(1)} %get-tuple-element.56), channel_id=1, source_target_pairs={{0,7},{1,0},{2,1},{3,2},{4,3},{5,4},{6,5},{7,6},{8,15},{9,8},{10,9... | collective-permute-start | bytes 319496 | tf_op jit(solution)/shard_map/ppermute | solution.py:21
  44.1 10.0 %collective-permute-start.10 = (bf16[32,1024]{1,0:T(8,128)(2,1)S(1)}, bf16[32,1024]{1,0:T(8,128)(2,1)S(1)}, u32[]{:S(2)}, u32[]{:S(2)}) collective-permute-start(bf16[32,1024]{1,0:T(8,128)(2,1)S(1)} %get-tuple-element.98), channel_id=1, source_target_pairs={{2,0},{5,7},{10,8},{13,15},{18,16},{21,23},{26,24},{29,31},{34,32}... | collective-permute-start | bytes 196616 | tf_op jit(solution)/shard_map/ppermute | solution.py:359
  45.4 24.9 %collective-permute-start.11 = (bf16[32,1024]{1,0:T(8,128)(2,1)S(1)}, bf16[32,1024]{1,0:T(8,128)(2,1)S(1)}, u32[]{:S(2)}, u32[]{:S(2)}) collective-permute-start(bf16[32,1024]{1,0:T(8,128)(2,1)S(1)} %get-tuple-element.97), channel_id=1, source_target_pairs={{3,0},{4,7},{11,8},{12,15},{19,16},{20,23},{27,24},{28,31},{35,32}... | collective-permute-start | bytes 196616 | tf_op jit(solution)/shard_map/ppermute | solution.py:359
  46.7 25.5 %collective-permute-start.12 = (bf16[32,1024]{1,0:T(8,128)(2,1)S(1)}, bf16[32,1024]{1,0:T(8,128)(2,1)S(1)}, u32[]{:S(2)}, u32[]{:S(2)}) collective-permute-start(bf16[32,1024]{1,0:T(8,128)(2,1)S(1)} %get-tuple-element.96), channel_id=1, source_target_pairs={{4,0},{3,7},{12,8},{11,15},{20,16},{19,23},{28,24},{27,31},{36,32}... | collective-permute-start | bytes 196616 | tf_op jit(solution)/shard_map/ppermute | solution.py:359
  49.9 22.9 %collective-permute-start.13 = (bf16[32,1024]{1,0:T(8,128)(2,1)S(1)}, bf16[32,1024]{1,0:T(8,128)(2,1)S(1)}, u32[]{:S(2)}, u32[]{:S(2)}) collective-permute-start(bf16[32,1024]{1,0:T(8,128)(2,1)S(1)} %get-tuple-element.95), channel_id=1, source_target_pairs={{5,0},{2,7},{13,8},{10,15},{21,16},{18,23},{29,24},{26,31},{37,32}... | collective-permute-start | bytes 196616 | tf_op jit(solution)/shard_map/ppermute | solution.py:359
  51.2 22.3 %collective-permute-start.14 = (bf16[32,1024]{1,0:T(8,128)(2,1)S(1)}, bf16[32,1024]{1,0:T(8,128)(2,1)S(1)}, u32[]{:S(2)}, u32[]{:S(2)}) collective-permute-start(bf16[32,1024]{1,0:T(8,128)(2,1)S(1)} %get-tuple-element.94), channel_id=1, source_target_pairs={{6,0},{1,7},{14,8},{9,15},{22,16},{17,23},{30,24},{25,31},{38,32},... | collective-permute-start | bytes 196616 | tf_op jit(solution)/shard_map/ppermute | solution.py:359
  54.1 24.7 %copy-start.9 = (bf16[32,1024]{1,0:T(8,128)(2,1)}, bf16[32,1024]{1,0:T(8,128)(2,1)S(1)}, u32[]{:S(2)}) copy-start(bf16[32,1024]{1,0:T(8,128)(2,1)S(1)} %collective-permute-done.10.refs_9_) | copy-start | bytes 196612
  54.1 20.0 %collective-permute-start.15 = (bf16[32,1024]{1,0:T(8,128)(2,1)S(1)}, bf16[32,1024]{1,0:T(8,128)(2,1)S(1)}, u32[]{:S(2)}, u32[]{:S(2)}) collective-permute-start(bf16[32,1024]{1,0:T(8,128)(2,1)S(1)} %get-tuple-element.93), channel_id=1, source_target_pairs={{7,0},{0,7},{15,8},{8,15},{23,16},{16,23},{31,24},{24,31},{39,32},... | collective-permute-start | bytes 196616 | tf_op jit(solution)/shard_map/ppermute | solution.py:359
  70.9 6.1 %collective-permute-start.9 = (bf16[32,1024]{1,0:T(8,128)(2,1)S(1)}, bf16[32,1024]{1,0:T(8,128)(2,1)S(1)}, u32[]{:S(2)}, u32[]{:S(2)}) collective-permute-start(bf16[32,1024]{1,0:T(8,128)(2,1)S(1)} %get-tuple-element.99), channel_id=1, source_target_pairs={{1,0},{6,7},{9,8},{14,15},{17,16},{22,23},{25,24},{30,31},{33,32},... | collective-permute-start | bytes 196616 | tf_op jit(solution)/shard_map/ppermute | solution.py:359
  78.8 21.5 %collective-permute-start.16 = (bf16[256,1024]{1,0:T(8,128)(2,1)}, bf16[256,1024]{1,0:T(8,128)(2,1)S(1)}, u32[]{:S(2)}, u32[]{:S(2)}) collective-permute-start(bf16[256,1024]{1,0:T(8,128)(2,1)} %get-tuple-element.74), channel_id=1, source_target_pairs={{0,1},{1,2},{2,3},{3,4},{4,5},{5,6},{6,7},{8,9},{9,10},{10,11},{11... | collective-permute-start | bytes 1572872 | tf_op jit(solution)/shard_map/ppermute | solution.py:363
  81.0 19.3 %collective-permute-start.17 = (bf16[256,1024]{1,0:T(8,128)(2,1)}, bf16[256,1024]{1,0:T(8,128)(2,1)}, u32[]{:S(2)}, u32[]{:S(2)}) collective-permute-start(bf16[256,1024]{1,0:T(8,128)(2,1)} %get-tuple-element.75), channel_id=1, source_target_pairs={{1,0},{2,1},{3,2},{4,3},{5,4},{6,5},{7,6},{9,8},{10,9},{11,10},{12... | collective-permute-start | bytes 1572872 | tf_op jit(solution)/shard_map/ppermute | solution.py:364
  108.0 29.6 %all-to-all-start = ((f32[32,16,256]{2,1,0:T(8,128)}), f32[32,16,256]{2,1,0:T(8,128)}, u32[]{:S(2)}, u32[]{:S(2)}) async-start(f32[32,16,256]{2,1,0:T(8,128)} %bitcast.10), calls=%async_computation | async-start | bytes 1048576 | tf_op jit(solution)/shard_map/all_to_all | solution.py:375
  121.0 1.5 copy-start.2
  124.5 25.8 %collective-permute-start.18 = (bf16[256,1024]{1,0:T(8,128)(2,1)}, bf16[256,1024]{1,0:T(8,128)(2,1)S(1)}, u32[]{:S(2)}, u32[]{:S(2)}) collective-permute-start(bf16[256,1024]{1,0:T(8,128)(2,1)} %get-tuple-element.82), channel_id=1, source_target_pairs={{0,1},{1,2},{2,3},{3,4},{4,5},{5,6},{6,7},{7,8},{8,9},{9,10},{10,1... | collective-permute-start | bytes 1572872 | tf_op jit(solution)/shard_map/ppermute | solution.py:21
  128.9 31.7 %collective-permute-start.19 = (bf16[256,1024]{1,0:T(8,128)(2,1)}, bf16[256,1024]{1,0:T(8,128)(2,1)S(1)}, u32[]{:S(2)}, u32[]{:S(2)}) collective-permute-start(bf16[256,1024]{1,0:T(8,128)(2,1)} %get-tuple-element.83), channel_id=1, source_target_pairs={{0,511},{1,0},{2,1},{3,2},{4,3},{5,4},{6,5},{7,6},{8,7},{9,8},{10,... | collective-permute-start | bytes 1572872 | tf_op jit(solution)/shard_map/ppermute | solution.py:21
  139.4 26.1 %all-to-all-start.1 = ((bf16[16,16,256]{2,1,0:T(8,128)(2,1)}), bf16[16,16,256]{2,1,0:T(8,128)(2,1)S(1)}, u32[]{:S(2)}, u32[]{:S(2)}) async-start(bf16[16,16,256]{2,1,0:T(8,128)(2,1)} %broadcast_in_dim.10), calls=%async_computation.1 | async-start | bytes 262144 | tf_op jit(solution)/shard_map/all_to_all | solution.py:380
  165.5 49.1 %all-to-all-start.2 = ((bf16[8,32,1664]{2,1,0:T(8,128)(2,1)}), bf16[8,32,1664]{2,1,0:T(8,128)(2,1)S(1)}, u32[]{:S(2)}, u32[]{:S(2)}) async-start(bf16[8,32,1664]{2,1,0:T(8,128)(2,1)} %bitcast.6), calls=%async_computation.2 | async-start | bytes 1703936 | tf_op jit(solution)/shard_map/all_to_all | solution.py:385
  172.8 3.1 %collective-permute-start.20 = (bf16[16,256]{1,0:T(8,128)(2,1)S(1)}, bf16[16,256]{1,0:T(8,128)(2,1)S(1)}, u32[]{:S(2)}, u32[]{:S(2)}) collective-permute-start(bf16[16,256]{1,0:T(8,128)(2,1)S(1)} %multiply_convert_fusion), channel_id=1, source_target_pairs={{0,8},{8,0},{1,9},{9,1},{2,10},{10,2},{3,11},{11,3},{4,12},{12,4},... | collective-permute-start | bytes 24584 | tf_op jit(solution)/shard_map/ppermute | solution.py:29
  175.9 5.6 %collective-permute-start.21 = (bf16[32,256]{1,0:T(8,128)(2,1)S(1)}, bf16[32,256]{1,0:T(8,128)(2,1)S(1)}, u32[]{:S(2)}, u32[]{:S(2)}) collective-permute-start(bf16[32,256]{1,0:T(8,128)(2,1)S(1)} %pad_maximum_fusion.5), channel_id=1, source_target_pairs={{0,16},{16,0},{32,48},{48,32},{1,17},{17,1},{33,49},{49,33},{2,18}... | collective-permute-start | bytes 49160 | tf_op jit(solution)/shard_map/ppermute | solution.py:29
  181.6 7.3 %collective-permute-start.22 = (bf16[64,256]{1,0:T(8,128)(2,1)S(1)}, bf16[64,256]{1,0:T(8,128)(2,1)S(1)}, u32[]{:S(2)}, u32[]{:S(2)}) collective-permute-start(bf16[64,256]{1,0:T(8,128)(2,1)S(1)} %pad_maximum_fusion.4), channel_id=1, source_target_pairs={{0,32},{16,48},{32,0},{48,16},{1,33},{17,49},{33,1},{49,17},{2,34}... | collective-permute-start | bytes 98312 | tf_op jit(solution)/shard_map/ppermute | solution.py:29
  188.9 6.2 %collective-permute-start.23 = (bf16[128,256]{1,0:T(8,128)(2,1)S(1)}, bf16[128,256]{1,0:T(8,128)(2,1)S(1)}, u32[]{:S(2)}, u32[]{:S(2)}) collective-permute-start(bf16[128,256]{1,0:T(8,128)(2,1)S(1)} %pad_maximum_fusion.3), channel_id=1, source_target_pairs={{0,64},{64,0},{128,192},{192,128},{1,65},{65,1},{129,193},{193,129... | collective-permute-start | bytes 196616 | tf_op jit(solution)/shard_map/ppermute | solution.py:29
  195.1 8.4 %collective-permute-start.24 = (bf16[256,256]{1,0:T(8,128)(2,1)S(1)}, bf16[256,256]{1,0:T(8,128)(2,1)S(1)}, u32[]{:S(2)}, u32[]{:S(2)}) collective-permute-start(bf16[256,256]{1,0:T(8,128)(2,1)S(1)} %pad_maximum_fusion.2), channel_id=1, source_target_pairs={{0,128},{64,192},{128,0},{192,64},{1,129},{65,193},{129,1},{193,65... | collective-permute-start | bytes 393224 | tf_op jit(solution)/shard_map/ppermute | solution.py:29
  (27 other events, 23.5 us)

commit v9 on v7

--- a/solution.py
+++ b/solution.py
@@ -41,7 +41,6 @@
 
 SMEM = pl.BlockSpec(memory_space=pltpu.SMEM)
 VMEM = pl.BlockSpec(memory_space=pltpu.VMEM)
-HBM = pl.BlockSpec(memory_space=pltpu.HBM)
 LEFT, OWN, RIGHT = range(3)
 
 
@@ -137,7 +136,7 @@
 def local_kernel(*refs):
     lists = refs[:4]
     (agg_ref, own_ref, before_ref, after_ref, values_ref, w_in_ref, w_out_ref, cot_ref) = refs[4:12]
-    terms_ref, both_ref, stacked, delta, agg, held, terms, sems = refs[12:]
+    left_ref, right_ref, terms_ref, both_ref, stacked, delta, agg, scat = refs[12:]
     depth, width = own_ref.shape
     agg[...] = agg_ref[...]
     add_slots(lists, LEFT, before_ref, agg, values_ref, True)
@@ -151,62 +150,35 @@
         slope = sigma * (1.0 + preact * (1.0 - sigma))
         delta[:, part] = (cot_ref[:, part].astype(jnp.float32) * slope).astype(jnp.bfloat16)
         both = jnp.dot(w_out_ref[...], delta[:, part], preferred_element_type=jnp.float32)
-        held[:, part] = both.astype(jnp.bfloat16)
-    first = pltpu.make_async_copy(held, both_ref, sems.at[0])
-    first.start()
-    terms[...] = lax.dot_general(
-        stacked[...], delta[...], (((1,), (1,)), ((), ())), preferred_element_type=jnp.float32
-    )
-    second = pltpu.make_async_copy(terms, terms_ref, sems.at[1])
-    second.start()
-    first.wait()
-    second.wait()
-
-
-def edge_kernel(*refs):
-    lists, (both_ref, values_ref, left_ref, right_ref, agg_grad, scat, sem) = refs[:4], refs[4:]
-    depth = left_ref.shape[0]
-    fetch = pltpu.make_async_copy(both_ref.at[pl.ds(depth, depth)], agg_grad, sem)
-    fetch.start()
-    fetch.wait()
+        both_ref[:, part] = both.astype(jnp.bfloat16)
+    agg_grad = both_ref.at[pl.ds(depth, depth)]
     for kind, out_ref in ((LEFT, left_ref), (RIGHT, right_ref)):
         scat[...] = jnp.zeros_like(scat)
         add_slots(lists, kind, agg_grad, scat, values_ref, False)
         out_ref[...] = scat[...].astype(jnp.bfloat16)
-
-
-def edge_step(lists, both, values, rim):
-    depth, width = both.shape[0] // 2, both.shape[1]
-    return pl.pallas_call(
-        edge_kernel,
-        out_shape=(jax.ShapeDtypeStruct((depth, rim), jnp.bfloat16),) * 2,
-        in_specs=[SMEM] * 4 + [HBM, VMEM],
-        out_specs=(VMEM,) * 2,
-        scratch_shapes=[
-            pltpu.VMEM((depth, width), jnp.bfloat16),
-            pltpu.VMEM((depth, rim), jnp.float32),
-            pltpu.SemaphoreType.DMA,
-        ],
-        compiler_params=pltpu.CompilerParams(vmem_limit_bytes=24 * 1024 * 1024),
-        cost_estimate=pl.CostEstimate(flops=1 << 28, bytes_accessed=4 << 20, transcendentals=0),
-    )(*lists, both, values)
+    terms_ref[...] = lax.dot_general(
+        stacked[...], delta[...], (((1,), (1,)), ((), ())), preferred_element_type=jnp.float32
+    )
 
 
 def local_step(lists, agg, own, before, after, values, w_in, w_out, cot):
     depth, width = own.shape
-    both = jax.ShapeDtypeStruct((2 * depth, width), jnp.bfloat16)
+    rim = before.shape[1]
     return pl.pallas_call(
         local_kernel,
-        out_shape=(jax.ShapeDtypeStruct((2 * depth, depth), jnp.float32), both),
+        out_shape=(
+            jax.ShapeDtypeStruct((depth, rim), jnp.bfloat16),
+            jax.ShapeDtypeStruct((depth, rim), jnp.bfloat16),
+            jax.ShapeDtypeStruct((2 * depth, depth), jnp.float32),
+            jax.ShapeDtypeStruct((2 * depth, width), jnp.bfloat16),
+        ),
         in_specs=[SMEM] * 4 + [VMEM] * 8,
-        out_specs=(HBM, HBM),
+        out_specs=(VMEM,) * 4,
         scratch_shapes=[
             pltpu.VMEM((2 * depth, width), jnp.bfloat16),
             pltpu.VMEM((depth, width), jnp.bfloat16),
             pltpu.VMEM((depth, width), jnp.float32),
-            pltpu.VMEM((2 * depth, width), jnp.bfloat16),
-            pltpu.VMEM((2 * depth, depth), jnp.float32),
-            pltpu.SemaphoreType.DMA((2,)),
+            pltpu.VMEM((depth, rim), jnp.float32),
         ],
         compiler_params=pltpu.CompilerParams(vmem_limit_bytes=40 * 1024 * 1024),
         cost_estimate=pl.CostEstimate(
@@ -331,19 +303,19 @@
     before = shifted(tail, RING, 1)
     after = shifted(head, RING, -1)
     agg = before_step(lists, own, block_values)
-    terms, both = local_step(
+    left, right, terms, both = local_step(
         lists, agg, own, before, after, block_values, w_in, w_out, cotangent
     )
     plane, line = lax.axis_size(PLANE), lax.axis_size(LINE)
     share = 2 * depth // plane
-    used, terms = lax.optimization_barrier((lists[0], terms))
-    left, right = edge_step([used, *lists[1:]], both, block_values, rim)
     from_next = shifted(left, RING, -1)
     from_prev = shifted(right, RING, 1)
     parts = lax.all_to_all(terms, PLANE, split_axis=0, concat_axis=0, tiled=True)
     partial = parts.reshape(plane, share, depth).sum(0).astype(jnp.bfloat16)
-    partial, used = lax.optimization_barrier((partial, used))
-    middle = after_step([used, *lists[1:]], both, block_values)
+    middle = after_step(lists, both, block_values)
+    partial, from_next, from_prev, middle = lax.optimization_barrier(
+        (partial, from_next, from_prev, middle)
+    )
     copies = jnp.broadcast_to(partial[None], (line, share, depth))
     copies = lax.all_to_all(copies, LINE, split_axis=0, concat_axis=0, tiled=True)
     factor = 1.0 / math.sqrt(rows_part * lax.axis_size(DOM))

time: 192 us -> 197 us (1.026)
  starting transfers between devices: 96.1 us -> 101 us
  Pallas kernels: 13.7 us -> 11.4 us
    ppermute x11, waiting for transfers between devices: 24 us -> 15.8 us  [shifted(): lax.ppermute(shard, axis, [(i, (i + by) % count) for i in range(count)])]
    all_to_all x1, waiting for transfers between devices: 0.01 us -> 6.36 us  [on_device(): lax.all_to_all(terms, PLANE, split_axis=0, concat_axis=0, tiled=True)]
    ppermute x11, starting transfers between devices: 58.4 us -> 62.9 us  [shifted(): lax.ppermute(shard, axis, [(i, (i + by) % count) for i in range(count)])]
    ppermute x5, waiting for transfers between devices: 14.6 us -> 16.9 us  [collected(): other = lax.ppermute(rows, axis, [(i, i ^ apart) for i in range(count)])]
    ppermute x5, starting transfers between devices: 15.9 us -> 13.6 us  [collected(): other = lax.ppermute(rows, axis, [(i, i ^ apart) for i in range(count)])]
    all_to_all x1, starting transfers between devices: 3.75 us -> 5.77 us  [on_device(): lax.all_to_all(total, 'feat', split_axis=0, concat_axis=1, tiled=True)]
    pallas_call x2 -> x1, Pallas kernels: 7.52 us -> 5.61 us  [local_step(): pl.pallas_call(local_kernel, out_shape=(jax.ShapeDtypeStruct((depth, rim)...]
    unnamed x32 -> x34, local copies, waits for them, and re-layouts: 12.2 us -> 13.5 us
  transfers between devices with their start and end apart: 19 -> 19, of which waited for: 11 -> 11; matrix products, arithmetic and copies ran while one was open for 4% -> 4% of each run, Pallas kernels for 4% -> 2%
where the time goes in v9:
time: 197 us; the launch traced here: 195 us
  starting transfers between devices  101 us (51%)
  waiting for transfers between devices  61.9 us (31%)
  local copies, waits for them, and re-layouts  15.1 us (8%)
  Pallas kernels  11.4 us (6%)
  other arithmetic  3.92 us (2%)
    ppermute x11, starting transfers between devices, shifted(): lax.ppermute(shard, axis, [(i, (i + by) % count) for i in range(count)])  62.9 us
    ppermute x5, waiting for transfers between devices, collected(): other = lax.ppermute(rows, axis, [(i, i ^ apart) for i in range(count)])  16.9 us
    ppermute x11, waiting for transfers between devices, shifted(): lax.ppermute(shard, axis, [(i, (i + by) % count) for i in range(count)])  15.8 us
    ppermute x5, starting transfers between devices, collected(): other = lax.ppermute(rows, axis, [(i, i ^ apart) for i in range(count)])  13.6 us
    unnamed x34, local copies, waits for them, and re-layouts  13.5 us
    all_to_all x1, waiting for transfers between devices, on_device(): lax.all_to_all(total, 'feat', split_axis=0, concat_axis=1, tiled=True)  11.6 us
    all_to_all x1, starting transfers between devices, on_device(): lax.all_to_all(copies, LINE, split_axis=0, concat_axis=0, tiled=True)  11.6 us
    all_to_all x1, waiting for transfers between devices, on_device(): lax.all_to_all(copies, LINE, split_axis=0, concat_axis=0, tiled=True)  11.2 us
  transfers between devices with their start and end apart: 19, of which 11 were waited for; matrix products, arithmetic and copies ran while one was open for 4% of the time, Pallas kernels for 2%

profile of v9, /device:TPU:6, one launch (start us, length us, event | category | flops | bytes accessed | tf_op | source)
XLA Modules:
  0.0 195.0 jit_solution(5296311465710821445)
XLA Ops:
  2.3 3.8 %collective-permute-start = (bf16[32,1664]{1,0:T(8,128)(2,1)S(1)}, bf16[32,1664]{1,0:T(8,128)(2,1)S(1)}, u32[]{:S(2)}, u32[]{:S(2)}) collective-permute-start(bf16[32,1664]{1,0:T(8,128)(2,1)S(1)} %get-tuple-element.33), channel_id=1, source_target_pairs={{0,1},{1,2},{2,3},{3,4},{4,5},{5,6},{6,7},{7,0},{8,9},{9,10},{10,1... | collective-permute-start | bytes 319496 | tf_op jit(solution)/shard_map/ppermute | solution.py:21
  6.2 5.2 %collective-permute-start.1 = (bf16[32,1664]{1,0:T(8,128)(2,1)S(1)}, bf16[32,1664]{1,0:T(8,128)(2,1)S(1)}, u32[]{:S(2)}, u32[]{:S(2)}) collective-permute-start(bf16[32,1664]{1,0:T(8,128)(2,1)S(1)} %get-tuple-element.34), channel_id=1, source_target_pairs={{0,2},{1,3},{2,4},{3,5},{4,6},{5,7},{6,0},{7,1},{8,10},{9,11},{10,... | collective-permute-start | bytes 319496 | tf_op jit(solution)/shard_map/ppermute | solution.py:21
  11.3 7.7 %collective-permute-start.2 = (bf16[32,1664]{1,0:T(8,128)(2,1)S(1)}, bf16[32,1664]{1,0:T(8,128)(2,1)S(1)}, u32[]{:S(2)}, u32[]{:S(2)}) collective-permute-start(bf16[32,1664]{1,0:T(8,128)(2,1)S(1)} %get-tuple-element.35), channel_id=1, source_target_pairs={{0,3},{1,4},{2,5},{3,6},{4,7},{5,0},{6,1},{7,2},{8,11},{9,12},{10,... | collective-permute-start | bytes 319496 | tf_op jit(solution)/shard_map/ppermute | solution.py:21
  19.1 3.3 %collective-permute-start.3 = (bf16[32,1664]{1,0:T(8,128)(2,1)S(1)}, bf16[32,1664]{1,0:T(8,128)(2,1)S(1)}, u32[]{:S(2)}, u32[]{:S(2)}) collective-permute-start(bf16[32,1664]{1,0:T(8,128)(2,1)S(1)} %get-tuple-element.36), channel_id=1, source_target_pairs={{0,4},{1,5},{2,6},{3,7},{4,0},{5,1},{6,2},{7,3},{8,12},{9,13},{10,... | collective-permute-start | bytes 319496 | tf_op jit(solution)/shard_map/ppermute | solution.py:21
  22.4 7.8 %collective-permute-start.4 = (bf16[32,1664]{1,0:T(8,128)(2,1)S(1)}, bf16[32,1664]{1,0:T(8,128)(2,1)S(1)}, u32[]{:S(2)}, u32[]{:S(2)}) collective-permute-start(bf16[32,1664]{1,0:T(8,128)(2,1)S(1)} %get-tuple-element.37), channel_id=1, source_target_pairs={{0,5},{1,6},{2,7},{3,0},{4,1},{5,2},{6,3},{7,4},{8,13},{9,14},{10,... | collective-permute-start | bytes 319496 | tf_op jit(solution)/shard_map/ppermute | solution.py:21
  30.2 4.6 %collective-permute-start.5 = (bf16[32,1664]{1,0:T(8,128)(2,1)S(1)}, bf16[32,1664]{1,0:T(8,128)(2,1)S(1)}, u32[]{:S(2)}, u32[]{:S(2)}) collective-permute-start(bf16[32,1664]{1,0:T(8,128)(2,1)S(1)} %get-tuple-element.38), channel_id=1, source_target_pairs={{0,6},{1,7},{2,0},{3,1},{4,2},{5,3},{6,4},{7,5},{8,14},{9,15},{10,... | collective-permute-start | bytes 319496 | tf_op jit(solution)/shard_map/ppermute | solution.py:21
  34.8 2.9 %collective-permute-start.6 = (bf16[32,1664]{1,0:T(8,128)(2,1)S(1)}, bf16[32,1664]{1,0:T(8,128)(2,1)S(1)}, u32[]{:S(2)}, u32[]{:S(2)}) collective-permute-start(bf16[32,1664]{1,0:T(8,128)(2,1)S(1)} %get-tuple-element.39), channel_id=1, source_target_pairs={{0,7},{1,0},{2,1},{3,2},{4,3},{5,4},{6,5},{7,6},{8,15},{9,8},{10,9... | collective-permute-start | bytes 319496 | tf_op jit(solution)/shard_map/ppermute | solution.py:21
  37.7 3.3 %collective-permute-done.2.refs_3_ = bf16[32,1664]{1,0:T(8,128)(2,1)S(1)} collective-permute-done((bf16[32,1664]{1,0:T(8,128)(2,1)S(1)}, bf16[32,1664]{1,0:T(8,128)(2,1)S(1)}, u32[]{:S(2)}, u32[]{:S(2)}) %collective-permute-start.2) | collective-permute-done | bytes 106528 | tf_op jit(solution)/shard_map/ppermute | solution.py:21
  41.1 4.8 %collective-permute-done.5.refs_6_ = bf16[32,1664]{1,0:T(8,128)(2,1)S(1)} collective-permute-done((bf16[32,1664]{1,0:T(8,128)(2,1)S(1)}, bf16[32,1664]{1,0:T(8,128)(2,1)S(1)}, u32[]{:S(2)}, u32[]{:S(2)}) %collective-permute-start.5) | collective-permute-done | bytes 106528 | tf_op jit(solution)/shard_map/ppermute | solution.py:21
  47.0 5.1 %collective-permute-start.7 = (bf16[256,1024]{1,0:T(8,128)(2,1)}, bf16[256,1024]{1,0:T(8,128)(2,1)S(1)}, u32[]{:S(2)}, u32[]{:S(2)}) collective-permute-start(bf16[256,1024]{1,0:T(8,128)(2,1)} %get-tuple-element.41), channel_id=1, source_target_pairs={{0,1},{1,2},{2,3},{3,4},{4,5},{5,6},{6,7},{7,8},{8,9},{9,10},{10,1... | collective-permute-start | bytes 1572872 | tf_op jit(solution)/shard_map/ppermute | solution.py:21
  52.1 9.4 %collective-permute-start.8 = (bf16[256,1024]{1,0:T(8,128)(2,1)}, bf16[256,1024]{1,0:T(8,128)(2,1)}, u32[]{:S(2)}, u32[]{:S(2)}) collective-permute-start(bf16[256,1024]{1,0:T(8,128)(2,1)} %get-tuple-element.42), channel_id=1, source_target_pairs={{0,511},{1,0},{2,1},{3,2},{4,3},{5,4},{6,5},{7,6},{8,7},{9,8},{10,... | collective-permute-start | bytes 1572872 | tf_op jit(solution)/shard_map/ppermute | solution.py:21
  62.2 1.7 copy.14
  65.5 1.8 shard_map.103
  72.7 7.7 %collective-permute-done.8.refs_7_ = bf16[256,1024]{1,0:T(8,128)(2,1)} collective-permute-done((bf16[256,1024]{1,0:T(8,128)(2,1)}, bf16[256,1024]{1,0:T(8,128)(2,1)}, u32[]{:S(2)}, u32[]{:S(2)}) %collective-permute-start.8) | collective-permute-done | bytes 524320 | tf_op jit(solution)/shard_map/ppermute | solution.py:21
  80.4 5.6 %shard_map.107 = (bf16[256,1024]{1,0:T(8,128)(2,1)}, bf16[256,1024]{1,0:T(8,128)(2,1)}, f32[512,256]{1,0:T(8,128)S(1)}, bf16[512,1664]{1,0:T(8,128)(2,1)S(1)}) custom-call(s32[3]{0:T(128)S(1)} %copy-done.15, s32[192]{0:T(256)S(1)} %copy-done.9, s32[192]{0:T(256)S(1)} %copy-done.11, s32[192]{0:T(256)S(1)} %copy-done.13, f32[256,1664]{1,0:T(8,128)S(1)} %shard_map.106.refs_4_, ...), custom_call_target="tpu_custom_call" | custom-call | flops 1308622848 | bytes 8388608 | tf_op jit(solution)/shard_map/pallas_call | solution.py:167
  88.0 3.5 %collective-permute-start.10 = (bf16[256,1024]{1,0:T(8,128)(2,1)}, bf16[256,1024]{1,0:T(8,128)(2,1)S(1)}, u32[]{:S(2)}, u32[]{:S(2)}) collective-permute-start(bf16[256,1024]{1,0:T(8,128)(2,1)} %get-tuple-element.45), channel_id=1, source_target_pairs={{0,1},{1,2},{2,3},{3,4},{4,5},{5,6},{6,7},{7,8},{8,9},{9,10},{10,1... | collective-permute-start | bytes 1572872 | tf_op jit(solution)/shard_map/ppermute | solution.py:21
  91.6 9.5 %collective-permute-start.9 = (bf16[256,1024]{1,0:T(8,128)(2,1)}, bf16[256,1024]{1,0:T(8,128)(2,1)S(1)}, u32[]{:S(2)}, u32[]{:S(2)}) collective-permute-start(bf16[256,1024]{1,0:T(8,128)(2,1)} %get-tuple-element.44), channel_id=1, source_target_pairs={{0,511},{1,0},{2,1},{3,2},{4,3},{5,4},{6,5},{7,6},{8,7},{9,8},{10,... | collective-permute-start | bytes 1572872 | tf_op jit(solution)/shard_map/ppermute | solution.py:21
  101.1 7.2 %all-to-all-start = ((f32[32,16,256]{2,1,0:T(8,128)}), f32[32,16,256]{2,1,0:T(8,128)}, u32[]{:S(2)}, u32[]{:S(2)}) async-start(f32[32,16,256]{2,1,0:T(8,128)} %bitcast.10), calls=%async_computation | async-start | bytes 1048576 | tf_op jit(solution)/shard_map/all_to_all | solution.py:313
  111.7 6.4 %all-to-all-done = f32[32,16,256]{2,1,0:T(8,128)} async-done(((f32[32,16,256]{2,1,0:T(8,128)}), f32[32,16,256]{2,1,0:T(8,128)}, u32[]{:S(2)}, u32[]{:S(2)}) %all-to-all-start) | async-done | bytes 524320 | tf_op jit(solution)/shard_map/all_to_all | solution.py:313
  119.9 11.6 %all-to-all-start.1 = ((bf16[16,16,256]{2,1,0:T(8,128)(2,1)}), bf16[16,16,256]{2,1,0:T(8,128)(2,1)S(1)}, u32[]{:S(2)}, u32[]{:S(2)}) async-start(bf16[16,16,256]{2,1,0:T(8,128)(2,1)} %broadcast_in_dim.10), calls=%async_computation.1 | async-start | bytes 262144 | tf_op jit(solution)/shard_map/all_to_all | solution.py:320
  134.0 11.2 %all-to-all-done.1 = bf16[16,16,256]{2,1,0:T(8,128)(2,1)S(1)} async-done(((bf16[16,16,256]{2,1,0:T(8,128)(2,1)}), bf16[16,16,256]{2,1,0:T(8,128)(2,1)S(1)}, u32[]{:S(2)}, u32[]{:S(2)}) %all-to-all-start.1) | async-done | bytes 131104 | tf_op jit(solution)/shard_map/all_to_all | solution.py:320
  145.2 5.8 %all-to-all-start.2 = ((bf16[8,32,1664]{2,1,0:T(8,128)(2,1)}), bf16[8,32,1664]{2,1,0:T(8,128)(2,1)S(1)}, u32[]{:S(2)}, u32[]{:S(2)}) async-start(bf16[8,32,1664]{2,1,0:T(8,128)(2,1)} %bitcast.6), calls=%async_computation.2 | async-start | bytes 1703936 | tf_op jit(solution)/shard_map/all_to_all | solution.py:325
  151.0 1.9 collective-permute-start.11
  154.1 2.6 %collective-permute-start.12 = (bf16[32,256]{1,0:T(8,128)(2,1)S(1)}, bf16[32,256]{1,0:T(8,128)(2,1)S(1)}, u32[]{:S(2)}, u32[]{:S(2)}) collective-permute-start(bf16[32,256]{1,0:T(8,128)(2,1)S(1)} %pad_maximum_fusion.5), channel_id=1, source_target_pairs={{0,16},{16,0},{32,48},{48,32},{1,17},{17,1},{33,49},{49,33},{2,18}... | collective-permute-start | bytes 49160 | tf_op jit(solution)/shard_map/ppermute | solution.py:29
  156.7 3.0 %collective-permute-done.12 = bf16[32,256]{1,0:T(8,128)(2,1)S(1)} collective-permute-done((bf16[32,256]{1,0:T(8,128)(2,1)S(1)}, bf16[32,256]{1,0:T(8,128)(2,1)S(1)}, u32[]{:S(2)}, u32[]{:S(2)}) %collective-permute-start.12) | collective-permute-done | bytes 16416 | tf_op jit(solution)/shard_map/ppermute | solution.py:29
  159.7 3.8 %collective-permute-start.13 = (bf16[64,256]{1,0:T(8,128)(2,1)S(1)}, bf16[64,256]{1,0:T(8,128)(2,1)S(1)}, u32[]{:S(2)}, u32[]{:S(2)}) collective-permute-start(bf16[64,256]{1,0:T(8,128)(2,1)S(1)} %pad_maximum_fusion.4), channel_id=1, source_target_pairs={{0,32},{16,48},{32,0},{48,16},{1,33},{17,49},{33,1},{49,17},{2,34}... | collective-permute-start | bytes 98312 | tf_op jit(solution)/shard_map/ppermute | solution.py:29
  163.6 3.5 %collective-permute-done.13 = bf16[64,256]{1,0:T(8,128)(2,1)S(1)} collective-permute-done((bf16[64,256]{1,0:T(8,128)(2,1)S(1)}, bf16[64,256]{1,0:T(8,128)(2,1)S(1)}, u32[]{:S(2)}, u32[]{:S(2)}) %collective-permute-start.13) | collective-permute-done | bytes 32800 | tf_op jit(solution)/shard_map/ppermute | solution.py:29
  167.1 2.5 %collective-permute-start.14 = (bf16[128,256]{1,0:T(8,128)(2,1)S(1)}, bf16[128,256]{1,0:T(8,128)(2,1)S(1)}, u32[]{:S(2)}, u32[]{:S(2)}) collective-permute-start(bf16[128,256]{1,0:T(8,128)(2,1)S(1)} %pad_maximum_fusion.3), channel_id=1, source_target_pairs={{0,64},{64,0},{128,192},{192,128},{1,65},{65,1},{129,193},{193,129... | collective-permute-start | bytes 196616 | tf_op jit(solution)/shard_map/ppermute | solution.py:29
  169.6 3.6 %collective-permute-done.14 = bf16[128,256]{1,0:T(8,128)(2,1)S(1)} collective-permute-done((bf16[128,256]{1,0:T(8,128)(2,1)S(1)}, bf16[128,256]{1,0:T(8,128)(2,1)S(1)}, u32[]{:S(2)}, u32[]{:S(2)}) %collective-permute-start.14) | collective-permute-done | bytes 65568 | tf_op jit(solution)/shard_map/ppermute | solution.py:29
  173.3 2.7 %collective-permute-start.15 = (bf16[256,256]{1,0:T(8,128)(2,1)S(1)}, bf16[256,256]{1,0:T(8,128)(2,1)S(1)}, u32[]{:S(2)}, u32[]{:S(2)}) collective-permute-start(bf16[256,256]{1,0:T(8,128)(2,1)S(1)} %pad_maximum_fusion.2), channel_id=1, source_target_pairs={{0,128},{64,192},{128,0},{192,64},{1,129},{65,193},{129,1},{193,65... | collective-permute-start | bytes 393224 | tf_op jit(solution)/shard_map/ppermute | solution.py:29
  176.0 5.7 %collective-permute-done.15 = bf16[256,256]{1,0:T(8,128)(2,1)S(1)} collective-permute-done((bf16[256,256]{1,0:T(8,128)(2,1)S(1)}, bf16[256,256]{1,0:T(8,128)(2,1)S(1)}, u32[]{:S(2)}, u32[]{:S(2)}) %collective-permute-start.15) | collective-permute-done | bytes 131104 | tf_op jit(solution)/shard_map/ppermute | solution.py:29
  182.4 11.6 %all-to-all-done.2 = bf16[8,32,1664]{2,1,0:T(8,128)(2,1)S(1)} async-done(((bf16[8,32,1664]{2,1,0:T(8,128)(2,1)}), bf16[8,32,1664]{2,1,0:T(8,128)(2,1)S(1)}, u32[]{:S(2)}, u32[]{:S(2)}) %all-to-all-start.2) | async-done | bytes 852000 | tf_op jit(solution)/shard_map/all_to_all | solution.py:325
  (63 shorter events, 22.5 us)
Async XLA Ops:
  0.6 68.6 %copy-start = (bf16[64,128,128]{2,1,0:T(8,128)(2,1)S(1)}, bf16[64,128,128]{2,1,0:T(8,128)(2,1)}, u32[]{:S(2)}) copy-start(bf16[64,128,128]{2,1,0:T(8,128)(2,1)} %refs_5_.3) | copy-start | bytes 6291460
  0.6 1.3 copy-start.5
  2.3 27.9 %collective-permute-start = (bf16[32,1664]{1,0:T(8,128)(2,1)S(1)}, bf16[32,1664]{1,0:T(8,128)(2,1)S(1)}, u32[]{:S(2)}, u32[]{:S(2)}) collective-permute-start(bf16[32,1664]{1,0:T(8,128)(2,1)S(1)} %get-tuple-element.33), channel_id=1, source_target_pairs={{0,1},{1,2},{2,3},{3,4},{4,5},{5,6},{6,7},{7,0},{8,9},{9,10},{10,1... | collective-permute-start | bytes 319496 | tf_op jit(solution)/shard_map/ppermute | solution.py:21
  6.2 28.6 %collective-permute-start.1 = (bf16[32,1664]{1,0:T(8,128)(2,1)S(1)}, bf16[32,1664]{1,0:T(8,128)(2,1)S(1)}, u32[]{:S(2)}, u32[]{:S(2)}) collective-permute-start(bf16[32,1664]{1,0:T(8,128)(2,1)S(1)} %get-tuple-element.34), channel_id=1, source_target_pairs={{0,2},{1,3},{2,4},{3,5},{4,6},{5,7},{6,0},{7,1},{8,10},{9,11},{10,... | collective-permute-start | bytes 319496 | tf_op jit(solution)/shard_map/ppermute | solution.py:21
  11.3 29.7 %collective-permute-start.2 = (bf16[32,1664]{1,0:T(8,128)(2,1)S(1)}, bf16[32,1664]{1,0:T(8,128)(2,1)S(1)}, u32[]{:S(2)}, u32[]{:S(2)}) collective-permute-start(bf16[32,1664]{1,0:T(8,128)(2,1)S(1)} %get-tuple-element.35), channel_id=1, source_target_pairs={{0,3},{1,4},{2,5},{3,6},{4,7},{5,0},{6,1},{7,2},{8,11},{9,12},{10,... | collective-permute-start | bytes 319496 | tf_op jit(solution)/shard_map/ppermute | solution.py:21
  19.1 22.0 %collective-permute-start.3 = (bf16[32,1664]{1,0:T(8,128)(2,1)S(1)}, bf16[32,1664]{1,0:T(8,128)(2,1)S(1)}, u32[]{:S(2)}, u32[]{:S(2)}) collective-permute-start(bf16[32,1664]{1,0:T(8,128)(2,1)S(1)} %get-tuple-element.36), channel_id=1, source_target_pairs={{0,4},{1,5},{2,6},{3,7},{4,0},{5,1},{6,2},{7,3},{8,12},{9,13},{10,... | collective-permute-start | bytes 319496 | tf_op jit(solution)/shard_map/ppermute | solution.py:21
  22.4 18.7 %collective-permute-start.4 = (bf16[32,1664]{1,0:T(8,128)(2,1)S(1)}, bf16[32,1664]{1,0:T(8,128)(2,1)S(1)}, u32[]{:S(2)}, u32[]{:S(2)}) collective-permute-start(bf16[32,1664]{1,0:T(8,128)(2,1)S(1)} %get-tuple-element.37), channel_id=1, source_target_pairs={{0,5},{1,6},{2,7},{3,0},{4,1},{5,2},{6,3},{7,4},{8,13},{9,14},{10,... | collective-permute-start | bytes 319496 | tf_op jit(solution)/shard_map/ppermute | solution.py:21
  30.2 15.6 %collective-permute-start.5 = (bf16[32,1664]{1,0:T(8,128)(2,1)S(1)}, bf16[32,1664]{1,0:T(8,128)(2,1)S(1)}, u32[]{:S(2)}, u32[]{:S(2)}) collective-permute-start(bf16[32,1664]{1,0:T(8,128)(2,1)S(1)} %get-tuple-element.38), channel_id=1, source_target_pairs={{0,6},{1,7},{2,0},{3,1},{4,2},{5,3},{6,4},{7,5},{8,14},{9,15},{10,... | collective-permute-start | bytes 319496 | tf_op jit(solution)/shard_map/ppermute | solution.py:21
  34.8 11.1 %collective-permute-start.6 = (bf16[32,1664]{1,0:T(8,128)(2,1)S(1)}, bf16[32,1664]{1,0:T(8,128)(2,1)S(1)}, u32[]{:S(2)}, u32[]{:S(2)}) collective-permute-start(bf16[32,1664]{1,0:T(8,128)(2,1)S(1)} %get-tuple-element.39), channel_id=1, source_target_pairs={{0,7},{1,0},{2,1},{3,2},{4,3},{5,4},{6,5},{7,6},{8,15},{9,8},{10,9... | collective-permute-start | bytes 319496 | tf_op jit(solution)/shard_map/ppermute | solution.py:21
  47.0 25.7 %collective-permute-start.7 = (bf16[256,1024]{1,0:T(8,128)(2,1)}, bf16[256,1024]{1,0:T(8,128)(2,1)S(1)}, u32[]{:S(2)}, u32[]{:S(2)}) collective-permute-start(bf16[256,1024]{1,0:T(8,128)(2,1)} %get-tuple-element.41), channel_id=1, source_target_pairs={{0,1},{1,2},{2,3},{3,4},{4,5},{5,6},{6,7},{7,8},{8,9},{9,10},{10,1... | collective-permute-start | bytes 1572872 | tf_op jit(solution)/shard_map/ppermute | solution.py:21
  52.1 28.3 %collective-permute-start.8 = (bf16[256,1024]{1,0:T(8,128)(2,1)}, bf16[256,1024]{1,0:T(8,128)(2,1)}, u32[]{:S(2)}, u32[]{:S(2)}) collective-permute-start(bf16[256,1024]{1,0:T(8,128)(2,1)} %get-tuple-element.42), channel_id=1, source_target_pairs={{0,511},{1,0},{2,1},{3,2},{4,3},{5,4},{6,5},{7,6},{8,7},{9,8},{10,... | collective-permute-start | bytes 1572872 | tf_op jit(solution)/shard_map/ppermute | solution.py:21
  71.3 0.7 copy-start.14
  72.0 8.4 %copy-start.6 = (bf16[256,1664]{1,0:T(8,128)(2,1)S(1)}, bf16[256,1664]{1,0:T(8,128)(2,1)}, u32[]{:S(2)}) copy-start(bf16[256,1664]{1,0:T(8,128)(2,1)} %refs_11_.1) | copy-start | bytes 2555908
  72.0 8.4 %copy-start.9 = (s32[192]{0:T(256)S(1)}, s32[192]{0:T(256)}, u32[]{:S(2)}) copy-start(s32[192]{0:T(256)} %get-tuple-element.29.refs_1_) | copy-start | bytes 2308
  72.0 8.4 %copy-start.11 = (s32[192]{0:T(256)S(1)}, s32[192]{0:T(256)}, u32[]{:S(2)}) copy-start(s32[192]{0:T(256)} %get-tuple-element.30.refs_2_) | copy-start | bytes 2308
  72.0 8.4 %copy-start.13 = (s32[192]{0:T(256)S(1)}, s32[192]{0:T(256)}, u32[]{:S(2)}) copy-start(s32[192]{0:T(256)} %get-tuple-element.31.refs_3_) | copy-start | bytes 2308
  72.0 8.4 %copy-start.15 = (s32[3]{0:T(128)S(1)}, s32[3]{0:T(128)}, u32[]{:S(2)}) copy-start(s32[3]{0:T(128)} %get-tuple-element.28.refs_0_) | copy-start | bytes 40
  86.0 1.2 copy-start.3
  87.2 0.8 copy-start.7
  88.0 31.2 %collective-permute-start.10 = (bf16[256,1024]{1,0:T(8,128)(2,1)}, bf16[256,1024]{1,0:T(8,128)(2,1)S(1)}, u32[]{:S(2)}, u32[]{:S(2)}) collective-permute-start(bf16[256,1024]{1,0:T(8,128)(2,1)} %get-tuple-element.45), channel_id=1, source_target_pairs={{0,1},{1,2},{2,3},{3,4},{4,5},{5,6},{6,7},{7,8},{8,9},{9,10},{10,1... | collective-permute-start | bytes 1572872 | tf_op jit(solution)/shard_map/ppermute | solution.py:21
  91.6 27.6 %collective-permute-start.9 = (bf16[256,1024]{1,0:T(8,128)(2,1)}, bf16[256,1024]{1,0:T(8,128)(2,1)S(1)}, u32[]{:S(2)}, u32[]{:S(2)}) collective-permute-start(bf16[256,1024]{1,0:T(8,128)(2,1)} %get-tuple-element.44), channel_id=1, source_target_pairs={{0,511},{1,0},{2,1},{3,2},{4,3},{5,4},{6,5},{7,6},{8,7},{9,8},{10,... | collective-permute-start | bytes 1572872 | tf_op jit(solution)/shard_map/ppermute | solution.py:21
  101.1 17.0 %all-to-all-start = ((f32[32,16,256]{2,1,0:T(8,128)}), f32[32,16,256]{2,1,0:T(8,128)}, u32[]{:S(2)}, u32[]{:S(2)}) async-start(f32[32,16,256]{2,1,0:T(8,128)} %bitcast.10), calls=%async_computation | async-start | bytes 1048576 | tf_op jit(solution)/shard_map/all_to_all | solution.py:313
  108.3 1.5 copy-start.4
  110.5 1.2 copy-start.1
  119.9 25.3 %all-to-all-start.1 = ((bf16[16,16,256]{2,1,0:T(8,128)(2,1)}), bf16[16,16,256]{2,1,0:T(8,128)(2,1)S(1)}, u32[]{:S(2)}, u32[]{:S(2)}) async-start(bf16[16,16,256]{2,1,0:T(8,128)(2,1)} %broadcast_in_dim.10), calls=%async_computation.1 | async-start | bytes 262144 | tf_op jit(solution)/shard_map/all_to_all | solution.py:320
  131.4 1.5 copy-start.2
  145.2 48.8 %all-to-all-start.2 = ((bf16[8,32,1664]{2,1,0:T(8,128)(2,1)}), bf16[8,32,1664]{2,1,0:T(8,128)(2,1)S(1)}, u32[]{:S(2)}, u32[]{:S(2)}) async-start(bf16[8,32,1664]{2,1,0:T(8,128)(2,1)} %bitcast.6), calls=%async_computation.2 | async-start | bytes 1703936 | tf_op jit(solution)/shard_map/all_to_all | solution.py:325
  151.0 3.1 %collective-permute-start.11 = (bf16[16,256]{1,0:T(8,128)(2,1)S(1)}, bf16[16,256]{1,0:T(8,128)(2,1)S(1)}, u32[]{:S(2)}, u32[]{:S(2)}) collective-permute-start(bf16[16,256]{1,0:T(8,128)(2,1)S(1)} %multiply_convert_fusion), channel_id=1, source_target_pairs={{0,8},{8,0},{1,9},{9,1},{2,10},{10,2},{3,11},{11,3},{4,12},{12,4},... | collective-permute-start | bytes 24584 | tf_op jit(solution)/shard_map/ppermute | solution.py:29
  154.1 5.6 %collective-permute-start.12 = (bf16[32,256]{1,0:T(8,128)(2,1)S(1)}, bf16[32,256]{1,0:T(8,128)(2,1)S(1)}, u32[]{:S(2)}, u32[]{:S(2)}) collective-permute-start(bf16[32,256]{1,0:T(8,128)(2,1)S(1)} %pad_maximum_fusion.5), channel_id=1, source_target_pairs={{0,16},{16,0},{32,48},{48,32},{1,17},{17,1},{33,49},{49,33},{2,18}... | collective-permute-start | bytes 49160 | tf_op jit(solution)/shard_map/ppermute | solution.py:29
  159.7 7.3 %collective-permute-start.13 = (bf16[64,256]{1,0:T(8,128)(2,1)S(1)}, bf16[64,256]{1,0:T(8,128)(2,1)S(1)}, u32[]{:S(2)}, u32[]{:S(2)}) collective-permute-start(bf16[64,256]{1,0:T(8,128)(2,1)S(1)} %pad_maximum_fusion.4), channel_id=1, source_target_pairs={{0,32},{16,48},{32,0},{48,16},{1,33},{17,49},{33,1},{49,17},{2,34}... | collective-permute-start | bytes 98312 | tf_op jit(solution)/shard_map/ppermute | solution.py:29
  167.1 6.2 %collective-permute-start.14 = (bf16[128,256]{1,0:T(8,128)(2,1)S(1)}, bf16[128,256]{1,0:T(8,128)(2,1)S(1)}, u32[]{:S(2)}, u32[]{:S(2)}) collective-permute-start(bf16[128,256]{1,0:T(8,128)(2,1)S(1)} %pad_maximum_fusion.3), channel_id=1, source_target_pairs={{0,64},{64,0},{128,192},{192,128},{1,65},{65,1},{129,193},{193,129... | collective-permute-start | bytes 196616 | tf_op jit(solution)/shard_map/ppermute | solution.py:29
  173.3 8.4 %collective-permute-start.15 = (bf16[256,256]{1,0:T(8,128)(2,1)S(1)}, bf16[256,256]{1,0:T(8,128)(2,1)S(1)}, u32[]{:S(2)}, u32[]{:S(2)}) collective-permute-start(bf16[256,256]{1,0:T(8,128)(2,1)S(1)} %pad_maximum_fusion.2), channel_id=1, source_target_pairs={{0,128},{64,192},{128,0},{192,64},{1,129},{65,193},{129,1},{193,65... | collective-permute-start | bytes 393224 | tf_op jit(solution)/shard_map/ppermute | solution.py:29
  (3 other events, 2.0 us)

commit v10 on v9

--- a/solution.py
+++ b/solution.py
@@ -313,9 +313,7 @@
     parts = lax.all_to_all(terms, PLANE, split_axis=0, concat_axis=0, tiled=True)
     partial = parts.reshape(plane, share, depth).sum(0).astype(jnp.bfloat16)
     middle = after_step(lists, both, block_values)
-    partial, from_next, from_prev, middle = lax.optimization_barrier(
-        (partial, from_next, from_prev, middle)
-    )
+    partial, middle = lax.optimization_barrier((partial, middle))
     copies = jnp.broadcast_to(partial[None], (line, share, depth))
     copies = lax.all_to_all(copies, LINE, split_axis=0, concat_axis=0, tiled=True)
     factor = 1.0 / math.sqrt(rows_part * lax.axis_size(DOM))

time: 197 us -> 189 us (0.959)
  starting transfers between devices: 101 us -> 96.6 us
  waiting for transfers between devices: 61.9 us -> 59.2 us
    ppermute x11, waiting for transfers between devices: 15.8 us -> 23.3 us  [shifted(): lax.ppermute(shard, axis, [(i, (i + by) % count) for i in range(count)])]
    all_to_all x1, waiting for transfers between devices: 6.36 us -> 0.01 us  [on_device(): lax.all_to_all(terms, PLANE, split_axis=0, concat_axis=0, tiled=True)]
    ppermute x11, starting transfers between devices: 62.9 us -> 58.2 us  [shifted(): lax.ppermute(shard, axis, [(i, (i + by) % count) for i in range(count)])]
    ppermute x5, waiting for transfers between devices: 16.9 us -> 14.1 us  [collected(): other = lax.ppermute(rows, axis, [(i, i ^ apart) for i in range(count)])]
    ppermute x5, starting transfers between devices: 13.6 us -> 16.3 us  [collected(): other = lax.ppermute(rows, axis, [(i, i ^ apart) for i in range(count)])]
    unnamed x34 -> x38, local copies, waits for them, and re-layouts: 13.5 us -> 14.9 us
where the time goes in v10:
time: 189 us; the launch traced here: 188 us
  starting transfers between devices  96.6 us (51%)
  waiting for transfers between devices  59.2 us (31%)
  local copies, waits for them, and re-layouts  16.6 us (9%)
  Pallas kernels  9.95 us (5%)
  other arithmetic  3.92 us (2%)
    ppermute x11, starting transfers between devices, shifted(): lax.ppermute(shard, axis, [(i, (i + by) % count) for i in range(count)])  58.2 us
    ppermute x11, waiting for transfers between devices, shifted(): lax.ppermute(shard, axis, [(i, (i + by) % count) for i in range(count)])  23.3 us
    ppermute x5, starting transfers between devices, collected(): other = lax.ppermute(rows, axis, [(i, i ^ apart) for i in range(count)])  16.3 us
    unnamed x38, local copies, waits for them, and re-layouts  14.9 us
    ppermute x5, waiting for transfers between devices, collected(): other = lax.ppermute(rows, axis, [(i, i ^ apart) for i in range(count)])  14.1 us
    all_to_all x1, waiting for transfers between devices, on_device(): lax.all_to_all(total, 'feat', split_axis=0, concat_axis=1, tiled=True)  11.4 us
    all_to_all x1, starting transfers between devices, on_device(): lax.all_to_all(copies, LINE, split_axis=0, concat_axis=0, tiled=True)  10.4 us
    all_to_all x1, waiting for transfers between devices, on_device(): lax.all_to_all(copies, LINE, split_axis=0, concat_axis=0, tiled=True)  10.3 us
  transfers between devices with their start and end apart: 19, of which 11 were waited for; matrix products, arithmetic and copies ran while one was open for 4% of the time, Pallas kernels for 2%

profile of v10, /device:TPU:6, one launch (start us, length us, event | category | flops | bytes accessed | tf_op | source)
XLA Modules:
  0.0 187.9 jit_solution(11669395720945816133)
XLA Ops:
  2.3 3.8 %collective-permute-start = (bf16[32,1664]{1,0:T(8,128)(2,1)S(1)}, bf16[32,1664]{1,0:T(8,128)(2,1)S(1)}, u32[]{:S(2)}, u32[]{:S(2)}) collective-permute-start(bf16[32,1664]{1,0:T(8,128)(2,1)S(1)} %get-tuple-element.31), channel_id=1, source_target_pairs={{0,1},{1,2},{2,3},{3,4},{4,5},{5,6},{6,7},{7,0},{8,9},{9,10},{10,1... | collective-permute-start | bytes 319496 | tf_op jit(solution)/shard_map/ppermute | solution.py:21
  6.2 5.2 %collective-permute-start.1 = (bf16[32,1664]{1,0:T(8,128)(2,1)S(1)}, bf16[32,1664]{1,0:T(8,128)(2,1)S(1)}, u32[]{:S(2)}, u32[]{:S(2)}) collective-permute-start(bf16[32,1664]{1,0:T(8,128)(2,1)S(1)} %get-tuple-element.32), channel_id=1, source_target_pairs={{0,2},{1,3},{2,4},{3,5},{4,6},{5,7},{6,0},{7,1},{8,10},{9,11},{10,... | collective-permute-start | bytes 319496 | tf_op jit(solution)/shard_map/ppermute | solution.py:21
  11.3 7.7 %collective-permute-start.2 = (bf16[32,1664]{1,0:T(8,128)(2,1)S(1)}, bf16[32,1664]{1,0:T(8,128)(2,1)S(1)}, u32[]{:S(2)}, u32[]{:S(2)}) collective-permute-start(bf16[32,1664]{1,0:T(8,128)(2,1)S(1)} %get-tuple-element.33), channel_id=1, source_target_pairs={{0,3},{1,4},{2,5},{3,6},{4,7},{5,0},{6,1},{7,2},{8,11},{9,12},{10,... | collective-permute-start | bytes 319496 | tf_op jit(solution)/shard_map/ppermute | solution.py:21
  19.1 3.3 %collective-permute-start.3 = (bf16[32,1664]{1,0:T(8,128)(2,1)S(1)}, bf16[32,1664]{1,0:T(8,128)(2,1)S(1)}, u32[]{:S(2)}, u32[]{:S(2)}) collective-permute-start(bf16[32,1664]{1,0:T(8,128)(2,1)S(1)} %get-tuple-element.34), channel_id=1, source_target_pairs={{0,4},{1,5},{2,6},{3,7},{4,0},{5,1},{6,2},{7,3},{8,12},{9,13},{10,... | collective-permute-start | bytes 319496 | tf_op jit(solution)/shard_map/ppermute | solution.py:21
  22.4 7.8 %collective-permute-start.4 = (bf16[32,1664]{1,0:T(8,128)(2,1)S(1)}, bf16[32,1664]{1,0:T(8,128)(2,1)S(1)}, u32[]{:S(2)}, u32[]{:S(2)}) collective-permute-start(bf16[32,1664]{1,0:T(8,128)(2,1)S(1)} %get-tuple-element.35), channel_id=1, source_target_pairs={{0,5},{1,6},{2,7},{3,0},{4,1},{5,2},{6,3},{7,4},{8,13},{9,14},{10,... | collective-permute-start | bytes 319496 | tf_op jit(solution)/shard_map/ppermute | solution.py:21
  30.2 4.6 %collective-permute-start.5 = (bf16[32,1664]{1,0:T(8,128)(2,1)S(1)}, bf16[32,1664]{1,0:T(8,128)(2,1)S(1)}, u32[]{:S(2)}, u32[]{:S(2)}) collective-permute-start(bf16[32,1664]{1,0:T(8,128)(2,1)S(1)} %get-tuple-element.36), channel_id=1, source_target_pairs={{0,6},{1,7},{2,0},{3,1},{4,2},{5,3},{6,4},{7,5},{8,14},{9,15},{10,... | collective-permute-start | bytes 319496 | tf_op jit(solution)/shard_map/ppermute | solution.py:21
  34.8 2.9 %collective-permute-start.6 = (bf16[32,1664]{1,0:T(8,128)(2,1)S(1)}, bf16[32,1664]{1,0:T(8,128)(2,1)S(1)}, u32[]{:S(2)}, u32[]{:S(2)}) collective-permute-start(bf16[32,1664]{1,0:T(8,128)(2,1)S(1)} %get-tuple-element.37), channel_id=1, source_target_pairs={{0,7},{1,0},{2,1},{3,2},{4,3},{5,4},{6,5},{7,6},{8,15},{9,8},{10,9... | collective-permute-start | bytes 319496 | tf_op jit(solution)/shard_map/ppermute | solution.py:21
  37.7 3.3 %collective-permute-done.2.refs_3_ = bf16[32,1664]{1,0:T(8,128)(2,1)S(1)} collective-permute-done((bf16[32,1664]{1,0:T(8,128)(2,1)S(1)}, bf16[32,1664]{1,0:T(8,128)(2,1)S(1)}, u32[]{:S(2)}, u32[]{:S(2)}) %collective-permute-start.2) | collective-permute-done | bytes 106528 | tf_op jit(solution)/shard_map/ppermute | solution.py:21
  41.1 4.8 %collective-permute-done.5.refs_6_ = bf16[32,1664]{1,0:T(8,128)(2,1)S(1)} collective-permute-done((bf16[32,1664]{1,0:T(8,128)(2,1)S(1)}, bf16[32,1664]{1,0:T(8,128)(2,1)S(1)}, u32[]{:S(2)}, u32[]{:S(2)}) %collective-permute-start.5) | collective-permute-done | bytes 106528 | tf_op jit(solution)/shard_map/ppermute | solution.py:21
  47.0 5.1 %collective-permute-start.7 = (bf16[256,1024]{1,0:T(8,128)(2,1)}, bf16[256,1024]{1,0:T(8,128)(2,1)S(1)}, u32[]{:S(2)}, u32[]{:S(2)}) collective-permute-start(bf16[256,1024]{1,0:T(8,128)(2,1)} %get-tuple-element.39), channel_id=1, source_target_pairs={{0,1},{1,2},{2,3},{3,4},{4,5},{5,6},{6,7},{7,8},{8,9},{9,10},{10,1... | collective-permute-start | bytes 1572872 | tf_op jit(solution)/shard_map/ppermute | solution.py:21
  52.1 9.4 %collective-permute-start.8 = (bf16[256,1024]{1,0:T(8,128)(2,1)}, bf16[256,1024]{1,0:T(8,128)(2,1)}, u32[]{:S(2)}, u32[]{:S(2)}) collective-permute-start(bf16[256,1024]{1,0:T(8,128)(2,1)} %get-tuple-element.40), channel_id=1, source_target_pairs={{0,511},{1,0},{2,1},{3,2},{4,3},{5,4},{6,5},{7,6},{8,7},{9,8},{10,... | collective-permute-start | bytes 1572872 | tf_op jit(solution)/shard_map/ppermute | solution.py:21
  62.2 1.7 copy.14
  63.8 1.7 copy.15
  72.5 7.8 %collective-permute-done.8.refs_7_ = bf16[256,1024]{1,0:T(8,128)(2,1)} collective-permute-done((bf16[256,1024]{1,0:T(8,128)(2,1)}, bf16[256,1024]{1,0:T(8,128)(2,1)}, u32[]{:S(2)}, u32[]{:S(2)}) %collective-permute-start.8) | collective-permute-done | bytes 524320 | tf_op jit(solution)/shard_map/ppermute | solution.py:21
  80.4 4.1 %shard_map.107 = (bf16[256,1024]{1,0:T(8,128)(2,1)S(1)}, bf16[256,1024]{1,0:T(8,128)(2,1)S(1)}, f32[512,256]{1,0:T(8,128)S(1)}, bf16[512,1664]{1,0:T(8,128)(2,1)S(1)}) custom-call(s32[3]{0:T(128)S(1)} %copy-done.15, s32[192]{0:T(256)S(1)} %copy-done.9, s32[192]{0:T(256)S(1)} %copy-done.11, s32[192]{0:T(256)S(1)} %copy-done.13, ...), custom_call_target="tpu_custom_call" | custom-call | flops 1308622848 | bytes 8388608 | tf_op jit(solution)/shard_map/pallas_call | solution.py:167
  88.2 7.8 %all-to-all-start = ((f32[32,16,256]{2,1,0:T(8,128)}), f32[32,16,256]{2,1,0:T(8,128)}, u32[]{:S(2)}, u32[]{:S(2)}) async-start(f32[32,16,256]{2,1,0:T(8,128)} %bitcast.10), calls=%async_computation | async-start | bytes 1048576 | tf_op jit(solution)/shard_map/all_to_all | solution.py:313
  96.0 6.5 %collective-permute-start.10 = (bf16[256,1024]{1,0:T(8,128)(2,1)}, bf16[256,1024]{1,0:T(8,128)(2,1)S(1)}, u32[]{:S(2)}, u32[]{:S(2)}) collective-permute-start(bf16[256,1024]{1,0:T(8,128)(2,1)} %copy-done.17), channel_id=1, source_target_pairs={{0,511},{1,0},{2,1},{3,2},{4,3},{5,4},{6,5},{7,6},{8,7},{9,8},{10,... | collective-permute-start | bytes 1572872 | tf_op jit(solution)/shard_map/ppermute | solution.py:21
  102.5 1.9 %collective-permute-start.9 = (bf16[256,1024]{1,0:T(8,128)(2,1)}, bf16[256,1024]{1,0:T(8,128)(2,1)S(1)}, u32[]{:S(2)}, u32[]{:S(2)}) collective-permute-start(bf16[256,1024]{1,0:T(8,128)(2,1)} %copy-done.16), channel_id=1, source_target_pairs={{0,1},{1,2},{2,3},{3,4},{4,5},{5,6},{6,7},{7,8},{8,9},{9,10},{10,1... | collective-permute-start | bytes 1572872 | tf_op jit(solution)/shard_map/ppermute | solution.py:21
  109.7 10.4 %all-to-all-start.1 = ((bf16[16,16,256]{2,1,0:T(8,128)(2,1)}), bf16[16,16,256]{2,1,0:T(8,128)(2,1)S(1)}, u32[]{:S(2)}, u32[]{:S(2)}) async-start(bf16[16,16,256]{2,1,0:T(8,128)(2,1)} %broadcast_in_dim.10), calls=%async_computation.1 | async-start | bytes 262144 | tf_op jit(solution)/shard_map/all_to_all | solution.py:318
  120.1 7.3 %collective-permute-done.9.prev_ref = bf16[256,1024]{1,0:T(8,128)(2,1)S(1)} collective-permute-done((bf16[256,1024]{1,0:T(8,128)(2,1)}, bf16[256,1024]{1,0:T(8,128)(2,1)S(1)}, u32[]{:S(2)}, u32[]{:S(2)}) %collective-permute-start.9) | collective-permute-done | bytes 524320 | tf_op jit(solution)/shard_map/ppermute | solution.py:21
  129.9 10.3 %all-to-all-done.1 = bf16[16,16,256]{2,1,0:T(8,128)(2,1)S(1)} async-done(((bf16[16,16,256]{2,1,0:T(8,128)(2,1)}), bf16[16,16,256]{2,1,0:T(8,128)(2,1)S(1)}, u32[]{:S(2)}, u32[]{:S(2)}) %all-to-all-start.1) | async-done | bytes 131104 | tf_op jit(solution)/shard_map/all_to_all | solution.py:318
  140.3 3.8 %all-to-all-start.2 = ((bf16[8,32,1664]{2,1,0:T(8,128)(2,1)}), bf16[8,32,1664]{2,1,0:T(8,128)(2,1)S(1)}, u32[]{:S(2)}, u32[]{:S(2)}) async-start(bf16[8,32,1664]{2,1,0:T(8,128)(2,1)} %bitcast.6), calls=%async_computation.2 | async-start | bytes 1703936 | tf_op jit(solution)/shard_map/all_to_all | solution.py:323
  144.1 1.9 %collective-permute-start.11 = (bf16[16,256]{1,0:T(8,128)(2,1)S(1)}, bf16[16,256]{1,0:T(8,128)(2,1)S(1)}, u32[]{:S(2)}, u32[]{:S(2)}) collective-permute-start(bf16[16,256]{1,0:T(8,128)(2,1)S(1)} %multiply_convert_fusion), channel_id=1, source_target_pairs={{0,8},{8,0},{1,9},{9,1},{2,10},{10,2},{3,11},{11,3},{4,12},{12,4},... | collective-permute-start | bytes 24584 | tf_op jit(solution)/shard_map/ppermute | solution.py:29
  147.2 2.8 %collective-permute-start.12 = (bf16[32,256]{1,0:T(8,128)(2,1)S(1)}, bf16[32,256]{1,0:T(8,128)(2,1)S(1)}, u32[]{:S(2)}, u32[]{:S(2)}) collective-permute-start(bf16[32,256]{1,0:T(8,128)(2,1)S(1)} %pad_maximum_fusion.5), channel_id=1, source_target_pairs={{0,16},{16,0},{32,48},{48,32},{1,17},{17,1},{33,49},{49,33},{2,18}... | collective-permute-start | bytes 49160 | tf_op jit(solution)/shard_map/ppermute | solution.py:29
  150.0 2.9 %collective-permute-done.12 = bf16[32,256]{1,0:T(8,128)(2,1)S(1)} collective-permute-done((bf16[32,256]{1,0:T(8,128)(2,1)S(1)}, bf16[32,256]{1,0:T(8,128)(2,1)S(1)}, u32[]{:S(2)}, u32[]{:S(2)}) %collective-permute-start.12) | collective-permute-done | bytes 16416 | tf_op jit(solution)/shard_map/ppermute | solution.py:29
  152.9 3.4 %collective-permute-start.13 = (bf16[64,256]{1,0:T(8,128)(2,1)S(1)}, bf16[64,256]{1,0:T(8,128)(2,1)S(1)}, u32[]{:S(2)}, u32[]{:S(2)}) collective-permute-start(bf16[64,256]{1,0:T(8,128)(2,1)S(1)} %pad_maximum_fusion.4), channel_id=1, source_target_pairs={{0,32},{16,48},{32,0},{48,16},{1,33},{17,49},{33,1},{49,17},{2,34}... | collective-permute-start | bytes 98312 | tf_op jit(solution)/shard_map/ppermute | solution.py:29
  156.2 3.9 %collective-permute-done.13 = bf16[64,256]{1,0:T(8,128)(2,1)S(1)} collective-permute-done((bf16[64,256]{1,0:T(8,128)(2,1)S(1)}, bf16[64,256]{1,0:T(8,128)(2,1)S(1)}, u32[]{:S(2)}, u32[]{:S(2)}) %collective-permute-start.13) | collective-permute-done | bytes 32800 | tf_op jit(solution)/shard_map/ppermute | solution.py:29
  160.2 3.4 %collective-permute-start.14 = (bf16[128,256]{1,0:T(8,128)(2,1)S(1)}, bf16[128,256]{1,0:T(8,128)(2,1)S(1)}, u32[]{:S(2)}, u32[]{:S(2)}) collective-permute-start(bf16[128,256]{1,0:T(8,128)(2,1)S(1)} %pad_maximum_fusion.3), channel_id=1, source_target_pairs={{0,64},{64,0},{128,192},{192,128},{1,65},{65,1},{129,193},{193,129... | collective-permute-start | bytes 196616 | tf_op jit(solution)/shard_map/ppermute | solution.py:29
  163.6 2.8 %collective-permute-done.14 = bf16[128,256]{1,0:T(8,128)(2,1)S(1)} collective-permute-done((bf16[128,256]{1,0:T(8,128)(2,1)S(1)}, bf16[128,256]{1,0:T(8,128)(2,1)S(1)}, u32[]{:S(2)}, u32[]{:S(2)}) %collective-permute-start.14) | collective-permute-done | bytes 65568 | tf_op jit(solution)/shard_map/ppermute | solution.py:29
  166.4 4.9 %collective-permute-start.15 = (bf16[256,256]{1,0:T(8,128)(2,1)S(1)}, bf16[256,256]{1,0:T(8,128)(2,1)S(1)}, u32[]{:S(2)}, u32[]{:S(2)}) collective-permute-start(bf16[256,256]{1,0:T(8,128)(2,1)S(1)} %pad_maximum_fusion.2), channel_id=1, source_target_pairs={{0,128},{64,192},{128,0},{192,64},{1,129},{65,193},{129,1},{193,65... | collective-permute-start | bytes 393224 | tf_op jit(solution)/shard_map/ppermute | solution.py:29
  171.3 3.4 %collective-permute-done.15 = bf16[256,256]{1,0:T(8,128)(2,1)S(1)} collective-permute-done((bf16[256,256]{1,0:T(8,128)(2,1)S(1)}, bf16[256,256]{1,0:T(8,128)(2,1)S(1)}, u32[]{:S(2)}, u32[]{:S(2)}) %collective-permute-start.15) | collective-permute-done | bytes 131104 | tf_op jit(solution)/shard_map/ppermute | solution.py:29
  175.5 11.4 %all-to-all-done.2 = bf16[8,32,1664]{2,1,0:T(8,128)(2,1)S(1)} async-done(((bf16[8,32,1664]{2,1,0:T(8,128)(2,1)}), bf16[8,32,1664]{2,1,0:T(8,128)(2,1)S(1)}, u32[]{:S(2)}, u32[]{:S(2)}) %all-to-all-start.2) | async-done | bytes 852000 | tf_op jit(solution)/shard_map/all_to_all | solution.py:323
  (67 shorter events, 24.1 us)
Async XLA Ops:
  0.6 68.4 %copy-start = (bf16[64,128,128]{2,1,0:T(8,128)(2,1)S(1)}, bf16[64,128,128]{2,1,0:T(8,128)(2,1)}, u32[]{:S(2)}) copy-start(bf16[64,128,128]{2,1,0:T(8,128)(2,1)} %refs_5_.3) | copy-start | bytes 6291460
  0.6 1.3 copy-start.5
  2.3 27.9 %collective-permute-start = (bf16[32,1664]{1,0:T(8,128)(2,1)S(1)}, bf16[32,1664]{1,0:T(8,128)(2,1)S(1)}, u32[]{:S(2)}, u32[]{:S(2)}) collective-permute-start(bf16[32,1664]{1,0:T(8,128)(2,1)S(1)} %get-tuple-element.31), channel_id=1, source_target_pairs={{0,1},{1,2},{2,3},{3,4},{4,5},{5,6},{6,7},{7,0},{8,9},{9,10},{10,1... | collective-permute-start | bytes 319496 | tf_op jit(solution)/shard_map/ppermute | solution.py:21
  6.2 28.6 %collective-permute-start.1 = (bf16[32,1664]{1,0:T(8,128)(2,1)S(1)}, bf16[32,1664]{1,0:T(8,128)(2,1)S(1)}, u32[]{:S(2)}, u32[]{:S(2)}) collective-permute-start(bf16[32,1664]{1,0:T(8,128)(2,1)S(1)} %get-tuple-element.32), channel_id=1, source_target_pairs={{0,2},{1,3},{2,4},{3,5},{4,6},{5,7},{6,0},{7,1},{8,10},{9,11},{10,... | collective-permute-start | bytes 319496 | tf_op jit(solution)/shard_map/ppermute | solution.py:21
  11.3 29.7 %collective-permute-start.2 = (bf16[32,1664]{1,0:T(8,128)(2,1)S(1)}, bf16[32,1664]{1,0:T(8,128)(2,1)S(1)}, u32[]{:S(2)}, u32[]{:S(2)}) collective-permute-start(bf16[32,1664]{1,0:T(8,128)(2,1)S(1)} %get-tuple-element.33), channel_id=1, source_target_pairs={{0,3},{1,4},{2,5},{3,6},{4,7},{5,0},{6,1},{7,2},{8,11},{9,12},{10,... | collective-permute-start | bytes 319496 | tf_op jit(solution)/shard_map/ppermute | solution.py:21
  19.1 22.0 %collective-permute-start.3 = (bf16[32,1664]{1,0:T(8,128)(2,1)S(1)}, bf16[32,1664]{1,0:T(8,128)(2,1)S(1)}, u32[]{:S(2)}, u32[]{:S(2)}) collective-permute-start(bf16[32,1664]{1,0:T(8,128)(2,1)S(1)} %get-tuple-element.34), channel_id=1, source_target_pairs={{0,4},{1,5},{2,6},{3,7},{4,0},{5,1},{6,2},{7,3},{8,12},{9,13},{10,... | collective-permute-start | bytes 319496 | tf_op jit(solution)/shard_map/ppermute | solution.py:21
  22.4 18.7 %collective-permute-start.4 = (bf16[32,1664]{1,0:T(8,128)(2,1)S(1)}, bf16[32,1664]{1,0:T(8,128)(2,1)S(1)}, u32[]{:S(2)}, u32[]{:S(2)}) collective-permute-start(bf16[32,1664]{1,0:T(8,128)(2,1)S(1)} %get-tuple-element.35), channel_id=1, source_target_pairs={{0,5},{1,6},{2,7},{3,0},{4,1},{5,2},{6,3},{7,4},{8,13},{9,14},{10,... | collective-permute-start | bytes 319496 | tf_op jit(solution)/shard_map/ppermute | solution.py:21
  30.2 15.6 %collective-permute-start.5 = (bf16[32,1664]{1,0:T(8,128)(2,1)S(1)}, bf16[32,1664]{1,0:T(8,128)(2,1)S(1)}, u32[]{:S(2)}, u32[]{:S(2)}) collective-permute-start(bf16[32,1664]{1,0:T(8,128)(2,1)S(1)} %get-tuple-element.36), channel_id=1, source_target_pairs={{0,6},{1,7},{2,0},{3,1},{4,2},{5,3},{6,4},{7,5},{8,14},{9,15},{10,... | collective-permute-start | bytes 319496 | tf_op jit(solution)/shard_map/ppermute | solution.py:21
  34.8 11.1 %collective-permute-start.6 = (bf16[32,1664]{1,0:T(8,128)(2,1)S(1)}, bf16[32,1664]{1,0:T(8,128)(2,1)S(1)}, u32[]{:S(2)}, u32[]{:S(2)}) collective-permute-start(bf16[32,1664]{1,0:T(8,128)(2,1)S(1)} %get-tuple-element.37), channel_id=1, source_target_pairs={{0,7},{1,0},{2,1},{3,2},{4,3},{5,4},{6,5},{7,6},{8,15},{9,8},{10,9... | collective-permute-start | bytes 319496 | tf_op jit(solution)/shard_map/ppermute | solution.py:21
  47.0 25.5 %collective-permute-start.7 = (bf16[256,1024]{1,0:T(8,128)(2,1)}, bf16[256,1024]{1,0:T(8,128)(2,1)S(1)}, u32[]{:S(2)}, u32[]{:S(2)}) collective-permute-start(bf16[256,1024]{1,0:T(8,128)(2,1)} %get-tuple-element.39), channel_id=1, source_target_pairs={{0,1},{1,2},{2,3},{3,4},{4,5},{5,6},{6,7},{7,8},{8,9},{9,10},{10,1... | collective-permute-start | bytes 1572872 | tf_op jit(solution)/shard_map/ppermute | solution.py:21
  52.1 28.3 %collective-permute-start.8 = (bf16[256,1024]{1,0:T(8,128)(2,1)}, bf16[256,1024]{1,0:T(8,128)(2,1)}, u32[]{:S(2)}, u32[]{:S(2)}) collective-permute-start(bf16[256,1024]{1,0:T(8,128)(2,1)} %get-tuple-element.40), channel_id=1, source_target_pairs={{0,511},{1,0},{2,1},{3,2},{4,3},{5,4},{6,5},{7,6},{8,7},{9,8},{10,... | collective-permute-start | bytes 1572872 | tf_op jit(solution)/shard_map/ppermute | solution.py:21
  71.6 8.8 %copy-start.6 = (bf16[256,1664]{1,0:T(8,128)(2,1)S(1)}, bf16[256,1664]{1,0:T(8,128)(2,1)}, u32[]{:S(2)}) copy-start(bf16[256,1664]{1,0:T(8,128)(2,1)} %refs_11_.1) | copy-start | bytes 2555908
  71.6 8.8 %copy-start.9 = (s32[192]{0:T(256)S(1)}, s32[192]{0:T(256)}, u32[]{:S(2)}) copy-start(s32[192]{0:T(256)} %get-tuple-element.27.refs_1_) | copy-start | bytes 2308
  71.6 8.8 %copy-start.11 = (s32[192]{0:T(256)S(1)}, s32[192]{0:T(256)}, u32[]{:S(2)}) copy-start(s32[192]{0:T(256)} %get-tuple-element.28.refs_2_) | copy-start | bytes 2308
  71.6 8.8 %copy-start.13 = (s32[192]{0:T(256)S(1)}, s32[192]{0:T(256)}, u32[]{:S(2)}) copy-start(s32[192]{0:T(256)} %get-tuple-element.29.refs_3_) | copy-start | bytes 2308
  71.6 8.8 %copy-start.15 = (s32[3]{0:T(128)S(1)}, s32[3]{0:T(128)}, u32[]{:S(2)}) copy-start(s32[3]{0:T(128)} %get-tuple-element.26.refs_0_) | copy-start | bytes 40
  84.5 1.2 copy-start.3
  85.8 0.8 copy-start.7
  87.4 0.8 copy-start.17
  88.2 19.8 %all-to-all-start = ((f32[32,16,256]{2,1,0:T(8,128)}), f32[32,16,256]{2,1,0:T(8,128)}, u32[]{:S(2)}, u32[]{:S(2)}) async-start(f32[32,16,256]{2,1,0:T(8,128)} %bitcast.10), calls=%async_computation | async-start | bytes 1048576 | tf_op jit(solution)/shard_map/all_to_all | solution.py:313
  96.0 24.1 %collective-permute-start.10 = (bf16[256,1024]{1,0:T(8,128)(2,1)}, bf16[256,1024]{1,0:T(8,128)(2,1)S(1)}, u32[]{:S(2)}, u32[]{:S(2)}) collective-permute-start(bf16[256,1024]{1,0:T(8,128)(2,1)} %copy-done.17), channel_id=1, source_target_pairs={{0,511},{1,0},{2,1},{3,2},{4,3},{5,4},{6,5},{7,6},{8,7},{9,8},{10,... | collective-permute-start | bytes 1572872 | tf_op jit(solution)/shard_map/ppermute | solution.py:21
  102.5 24.9 %collective-permute-start.9 = (bf16[256,1024]{1,0:T(8,128)(2,1)}, bf16[256,1024]{1,0:T(8,128)(2,1)S(1)}, u32[]{:S(2)}, u32[]{:S(2)}) collective-permute-start(bf16[256,1024]{1,0:T(8,128)(2,1)} %copy-done.16), channel_id=1, source_target_pairs={{0,1},{1,2},{2,3},{3,4},{4,5},{5,6},{6,7},{7,8},{8,9},{9,10},{10,1... | collective-permute-start | bytes 1572872 | tf_op jit(solution)/shard_map/ppermute | solution.py:21
  104.4 1.5 copy-start.4
  106.7 1.2 copy-start.1
  109.7 30.6 %all-to-all-start.1 = ((bf16[16,16,256]{2,1,0:T(8,128)(2,1)}), bf16[16,16,256]{2,1,0:T(8,128)(2,1)S(1)}, u32[]{:S(2)}, u32[]{:S(2)}) async-start(bf16[16,16,256]{2,1,0:T(8,128)(2,1)} %broadcast_in_dim.10), calls=%async_computation.1 | async-start | bytes 262144 | tf_op jit(solution)/shard_map/all_to_all | solution.py:318
  127.4 1.5 copy-start.2
  140.3 46.6 %all-to-all-start.2 = ((bf16[8,32,1664]{2,1,0:T(8,128)(2,1)}), bf16[8,32,1664]{2,1,0:T(8,128)(2,1)S(1)}, u32[]{:S(2)}, u32[]{:S(2)}) async-start(bf16[8,32,1664]{2,1,0:T(8,128)(2,1)} %bitcast.6), calls=%async_computation.2 | async-start | bytes 1703936 | tf_op jit(solution)/shard_map/all_to_all | solution.py:323
  144.1 3.1 %collective-permute-start.11 = (bf16[16,256]{1,0:T(8,128)(2,1)S(1)}, bf16[16,256]{1,0:T(8,128)(2,1)S(1)}, u32[]{:S(2)}, u32[]{:S(2)}) collective-permute-start(bf16[16,256]{1,0:T(8,128)(2,1)S(1)} %multiply_convert_fusion), channel_id=1, source_target_pairs={{0,8},{8,0},{1,9},{9,1},{2,10},{10,2},{3,11},{11,3},{4,12},{12,4},... | collective-permute-start | bytes 24584 | tf_op jit(solution)/shard_map/ppermute | solution.py:29
  147.2 5.6 %collective-permute-start.12 = (bf16[32,256]{1,0:T(8,128)(2,1)S(1)}, bf16[32,256]{1,0:T(8,128)(2,1)S(1)}, u32[]{:S(2)}, u32[]{:S(2)}) collective-permute-start(bf16[32,256]{1,0:T(8,128)(2,1)S(1)} %pad_maximum_fusion.5), channel_id=1, source_target_pairs={{0,16},{16,0},{32,48},{48,32},{1,17},{17,1},{33,49},{49,33},{2,18}... | collective-permute-start | bytes 49160 | tf_op jit(solution)/shard_map/ppermute | solution.py:29
  152.9 7.3 %collective-permute-start.13 = (bf16[64,256]{1,0:T(8,128)(2,1)S(1)}, bf16[64,256]{1,0:T(8,128)(2,1)S(1)}, u32[]{:S(2)}, u32[]{:S(2)}) collective-permute-start(bf16[64,256]{1,0:T(8,128)(2,1)S(1)} %pad_maximum_fusion.4), channel_id=1, source_target_pairs={{0,32},{16,48},{32,0},{48,16},{1,33},{17,49},{33,1},{49,17},{2,34}... | collective-permute-start | bytes 98312 | tf_op jit(solution)/shard_map/ppermute | solution.py:29
  160.2 6.2 %collective-permute-start.14 = (bf16[128,256]{1,0:T(8,128)(2,1)S(1)}, bf16[128,256]{1,0:T(8,128)(2,1)S(1)}, u32[]{:S(2)}, u32[]{:S(2)}) collective-permute-start(bf16[128,256]{1,0:T(8,128)(2,1)S(1)} %pad_maximum_fusion.3), channel_id=1, source_target_pairs={{0,64},{64,0},{128,192},{192,128},{1,65},{65,1},{129,193},{193,129... | collective-permute-start | bytes 196616 | tf_op jit(solution)/shard_map/ppermute | solution.py:29
  166.4 8.4 %collective-permute-start.15 = (bf16[256,256]{1,0:T(8,128)(2,1)S(1)}, bf16[256,256]{1,0:T(8,128)(2,1)S(1)}, u32[]{:S(2)}, u32[]{:S(2)}) collective-permute-start(bf16[256,256]{1,0:T(8,128)(2,1)S(1)} %pad_maximum_fusion.2), channel_id=1, source_target_pairs={{0,128},{64,192},{128,0},{192,64},{1,129},{65,193},{129,1},{193,65... | collective-permute-start | bytes 393224 | tf_op jit(solution)/shard_map/ppermute | solution.py:29
  (5 other events, 3.4 us)

commit v11 on v10

--- a/solution.py
+++ b/solution.py
@@ -312,8 +312,8 @@
     from_prev = shifted(right, RING, 1)
     parts = lax.all_to_all(terms, PLANE, split_axis=0, concat_axis=0, tiled=True)
     partial = parts.reshape(plane, share, depth).sum(0).astype(jnp.bfloat16)
-    middle = after_step(lists, both, block_values)
-    partial, middle = lax.optimization_barrier((partial, middle))
+    partial, used = lax.optimization_barrier((partial, lists[0]))
+    middle = after_step([used, *lists[1:]], both, block_values)
     copies = jnp.broadcast_to(partial[None], (line, share, depth))
     copies = lax.all_to_all(copies, LINE, split_axis=0, concat_axis=0, tiled=True)
     factor = 1.0 / math.sqrt(rows_part * lax.axis_size(DOM))

time: 189 us -> 188 us (level)
  local copies, waits for them, and re-layouts: 16.6 us -> 14 us
    unnamed x38 -> x34, local copies, waits for them, and re-layouts: 14.9 us -> 12.4 us
  transfers between devices with their start and end apart: 19 -> 19, of which waited for: 11 -> 12; matrix products, arithmetic and copies ran while one was open for 4% -> 4% of each run, Pallas kernels for 2% -> 2%
where the time goes in v11:
time: 188 us; the launch traced here: 187 us
  starting transfers between devices  98.4 us (52%)
  waiting for transfers between devices  59.5 us (32%)
  local copies, waits for them, and re-layouts  14 us (7%)
  Pallas kernels  9.54 us (5%)
  other arithmetic  3.92 us (2%)
    ppermute x11, starting transfers between devices, shifted(): lax.ppermute(shard, axis, [(i, (i + by) % count) for i in range(count)])  58.7 us
    ppermute x11, waiting for transfers between devices, shifted(): lax.ppermute(shard, axis, [(i, (i + by) % count) for i in range(count)])  23.2 us
    ppermute x5, starting transfers between devices, collected(): other = lax.ppermute(rows, axis, [(i, i ^ apart) for i in range(count)])  16.3 us
    ppermute x5, waiting for transfers between devices, collected(): other = lax.ppermute(rows, axis, [(i, i ^ apart) for i in range(count)])  14.1 us
    unnamed x34, local copies, waits for them, and re-layouts  12.4 us
    all_to_all x1, starting transfers between devices, on_device(): lax.all_to_all(copies, LINE, split_axis=0, concat_axis=0, tiled=True)  11.4 us
    all_to_all x1, waiting for transfers between devices, on_device(): lax.all_to_all(total, 'feat', split_axis=0, concat_axis=1, tiled=True)  10.9 us
    all_to_all x1, waiting for transfers between devices, on_device(): lax.all_to_all(copies, LINE, split_axis=0, concat_axis=0, tiled=True)  10.7 us
  transfers between devices with their start and end apart: 19, of which 12 were waited for; matrix products, arithmetic and copies ran while one was open for 4% of the time, Pallas kernels for 2%

profile of v11, /device:TPU:6, one launch (start us, length us, event | category | flops | bytes accessed | tf_op | source)
XLA Modules:
  0.0 187.1 jit_solution(8569148871671644669)
XLA Ops:
  2.3 3.8 %collective-permute-start = (bf16[32,1664]{1,0:T(8,128)(2,1)S(1)}, bf16[32,1664]{1,0:T(8,128)(2,1)S(1)}, u32[]{:S(2)}, u32[]{:S(2)}) collective-permute-start(bf16[32,1664]{1,0:T(8,128)(2,1)S(1)} %get-tuple-element.31), channel_id=1, source_target_pairs={{0,1},{1,2},{2,3},{3,4},{4,5},{5,6},{6,7},{7,0},{8,9},{9,10},{10,1... | collective-permute-start | bytes 319496 | tf_op jit(solution)/shard_map/ppermute | solution.py:21
  6.2 5.2 %collective-permute-start.1 = (bf16[32,1664]{1,0:T(8,128)(2,1)S(1)}, bf16[32,1664]{1,0:T(8,128)(2,1)S(1)}, u32[]{:S(2)}, u32[]{:S(2)}) collective-permute-start(bf16[32,1664]{1,0:T(8,128)(2,1)S(1)} %get-tuple-element.32), channel_id=1, source_target_pairs={{0,2},{1,3},{2,4},{3,5},{4,6},{5,7},{6,0},{7,1},{8,10},{9,11},{10,... | collective-permute-start | bytes 319496 | tf_op jit(solution)/shard_map/ppermute | solution.py:21
  11.3 7.7 %collective-permute-start.2 = (bf16[32,1664]{1,0:T(8,128)(2,1)S(1)}, bf16[32,1664]{1,0:T(8,128)(2,1)S(1)}, u32[]{:S(2)}, u32[]{:S(2)}) collective-permute-start(bf16[32,1664]{1,0:T(8,128)(2,1)S(1)} %get-tuple-element.33), channel_id=1, source_target_pairs={{0,3},{1,4},{2,5},{3,6},{4,7},{5,0},{6,1},{7,2},{8,11},{9,12},{10,... | collective-permute-start | bytes 319496 | tf_op jit(solution)/shard_map/ppermute | solution.py:21
  19.1 3.3 %collective-permute-start.3 = (bf16[32,1664]{1,0:T(8,128)(2,1)S(1)}, bf16[32,1664]{1,0:T(8,128)(2,1)S(1)}, u32[]{:S(2)}, u32[]{:S(2)}) collective-permute-start(bf16[32,1664]{1,0:T(8,128)(2,1)S(1)} %get-tuple-element.34), channel_id=1, source_target_pairs={{0,4},{1,5},{2,6},{3,7},{4,0},{5,1},{6,2},{7,3},{8,12},{9,13},{10,... | collective-permute-start | bytes 319496 | tf_op jit(solution)/shard_map/ppermute | solution.py:21
  22.4 7.8 %collective-permute-start.4 = (bf16[32,1664]{1,0:T(8,128)(2,1)S(1)}, bf16[32,1664]{1,0:T(8,128)(2,1)S(1)}, u32[]{:S(2)}, u32[]{:S(2)}) collective-permute-start(bf16[32,1664]{1,0:T(8,128)(2,1)S(1)} %get-tuple-element.35), channel_id=1, source_target_pairs={{0,5},{1,6},{2,7},{3,0},{4,1},{5,2},{6,3},{7,4},{8,13},{9,14},{10,... | collective-permute-start | bytes 319496 | tf_op jit(solution)/shard_map/ppermute | solution.py:21
  30.2 4.6 %collective-permute-start.5 = (bf16[32,1664]{1,0:T(8,128)(2,1)S(1)}, bf16[32,1664]{1,0:T(8,128)(2,1)S(1)}, u32[]{:S(2)}, u32[]{:S(2)}) collective-permute-start(bf16[32,1664]{1,0:T(8,128)(2,1)S(1)} %get-tuple-element.36), channel_id=1, source_target_pairs={{0,6},{1,7},{2,0},{3,1},{4,2},{5,3},{6,4},{7,5},{8,14},{9,15},{10,... | collective-permute-start | bytes 319496 | tf_op jit(solution)/shard_map/ppermute | solution.py:21
  34.8 2.9 %collective-permute-start.6 = (bf16[32,1664]{1,0:T(8,128)(2,1)S(1)}, bf16[32,1664]{1,0:T(8,128)(2,1)S(1)}, u32[]{:S(2)}, u32[]{:S(2)}) collective-permute-start(bf16[32,1664]{1,0:T(8,128)(2,1)S(1)} %get-tuple-element.37), channel_id=1, source_target_pairs={{0,7},{1,0},{2,1},{3,2},{4,3},{5,4},{6,5},{7,6},{8,15},{9,8},{10,9... | collective-permute-start | bytes 319496 | tf_op jit(solution)/shard_map/ppermute | solution.py:21
  37.7 3.3 %collective-permute-done.2.refs_3_ = bf16[32,1664]{1,0:T(8,128)(2,1)S(1)} collective-permute-done((bf16[32,1664]{1,0:T(8,128)(2,1)S(1)}, bf16[32,1664]{1,0:T(8,128)(2,1)S(1)}, u32[]{:S(2)}, u32[]{:S(2)}) %collective-permute-start.2) | collective-permute-done | bytes 106528 | tf_op jit(solution)/shard_map/ppermute | solution.py:21
  41.1 4.8 %collective-permute-done.5.refs_6_ = bf16[32,1664]{1,0:T(8,128)(2,1)S(1)} collective-permute-done((bf16[32,1664]{1,0:T(8,128)(2,1)S(1)}, bf16[32,1664]{1,0:T(8,128)(2,1)S(1)}, u32[]{:S(2)}, u32[]{:S(2)}) %collective-permute-start.5) | collective-permute-done | bytes 106528 | tf_op jit(solution)/shard_map/ppermute | solution.py:21
  47.0 5.1 %collective-permute-start.7 = (bf16[256,1024]{1,0:T(8,128)(2,1)}, bf16[256,1024]{1,0:T(8,128)(2,1)S(1)}, u32[]{:S(2)}, u32[]{:S(2)}) collective-permute-start(bf16[256,1024]{1,0:T(8,128)(2,1)} %get-tuple-element.39), channel_id=1, source_target_pairs={{0,1},{1,2},{2,3},{3,4},{4,5},{5,6},{6,7},{7,8},{8,9},{9,10},{10,1... | collective-permute-start | bytes 1572872 | tf_op jit(solution)/shard_map/ppermute | solution.py:21
  52.1 9.4 %collective-permute-start.8 = (bf16[256,1024]{1,0:T(8,128)(2,1)}, bf16[256,1024]{1,0:T(8,128)(2,1)}, u32[]{:S(2)}, u32[]{:S(2)}) collective-permute-start(bf16[256,1024]{1,0:T(8,128)(2,1)} %get-tuple-element.40), channel_id=1, source_target_pairs={{0,511},{1,0},{2,1},{3,2},{4,3},{5,4},{6,5},{7,6},{8,7},{9,8},{10,... | collective-permute-start | bytes 1572872 | tf_op jit(solution)/shard_map/ppermute | solution.py:21
  62.2 1.7 copy.14
  63.8 1.7 copy.15
  72.4 8.0 %collective-permute-done.8.refs_7_ = bf16[256,1024]{1,0:T(8,128)(2,1)} collective-permute-done((bf16[256,1024]{1,0:T(8,128)(2,1)}, bf16[256,1024]{1,0:T(8,128)(2,1)}, u32[]{:S(2)}, u32[]{:S(2)}) %collective-permute-start.8) | collective-permute-done | bytes 524320 | tf_op jit(solution)/shard_map/ppermute | solution.py:21
  80.4 4.1 %shard_map.107 = (bf16[256,1024]{1,0:T(8,128)(2,1)S(1)}, bf16[256,1024]{1,0:T(8,128)(2,1)S(1)}, f32[512,256]{1,0:T(8,128)S(1)}, bf16[512,1664]{1,0:T(8,128)(2,1)S(1)}) custom-call(s32[3]{0:T(128)S(1)} %copy-done.13, s32[192]{0:T(256)S(1)} %copy-done.7, s32[192]{0:T(256)S(1)} %copy-done.9, s32[192]{0:T(256)S(1)} %copy-done.11, ...), custom_call_target="tpu_custom_call" | custom-call | flops 1308622848 | bytes 8388608 | tf_op jit(solution)/shard_map/pallas_call | solution.py:167
  88.2 8.4 %all-to-all-start = ((f32[32,16,256]{2,1,0:T(8,128)}), f32[32,16,256]{2,1,0:T(8,128)}, u32[]{:S(2)}, u32[]{:S(2)}) async-start(f32[32,16,256]{2,1,0:T(8,128)} %bitcast.10), calls=%async_computation | async-start | bytes 1048576 | tf_op jit(solution)/shard_map/all_to_all | solution.py:313
  96.6 7.0 %collective-permute-start.10 = (bf16[256,1024]{1,0:T(8,128)(2,1)}, bf16[256,1024]{1,0:T(8,128)(2,1)S(1)}, u32[]{:S(2)}, u32[]{:S(2)}) collective-permute-start(bf16[256,1024]{1,0:T(8,128)(2,1)} %copy-done.15), channel_id=1, source_target_pairs={{0,511},{1,0},{2,1},{3,2},{4,3},{5,4},{6,5},{7,6},{8,7},{9,8},{10,... | collective-permute-start | bytes 1572872 | tf_op jit(solution)/shard_map/ppermute | solution.py:21
  103.6 1.9 %collective-permute-start.9 = (bf16[256,1024]{1,0:T(8,128)(2,1)}, bf16[256,1024]{1,0:T(8,128)(2,1)S(1)}, u32[]{:S(2)}, u32[]{:S(2)}) collective-permute-start(bf16[256,1024]{1,0:T(8,128)(2,1)} %copy-done.14), channel_id=1, source_target_pairs={{0,1},{1,2},{2,3},{3,4},{4,5},{5,6},{6,7},{7,8},{8,9},{9,10},{10,1... | collective-permute-start | bytes 1572872 | tf_op jit(solution)/shard_map/ppermute | solution.py:21
  107.8 11.4 %all-to-all-start.1 = ((bf16[16,16,256]{2,1,0:T(8,128)(2,1)}), bf16[16,16,256]{2,1,0:T(8,128)(2,1)S(1)}, u32[]{:S(2)}, u32[]{:S(2)}) async-start(bf16[16,16,256]{2,1,0:T(8,128)(2,1)} %broadcast_in_dim.10), calls=%async_computation.1 | async-start | bytes 262144 | tf_op jit(solution)/shard_map/all_to_all | solution.py:318
  121.4 7.0 %collective-permute-done.9.prev_ref = bf16[256,1024]{1,0:T(8,128)(2,1)S(1)} collective-permute-done((bf16[256,1024]{1,0:T(8,128)(2,1)}, bf16[256,1024]{1,0:T(8,128)(2,1)S(1)}, u32[]{:S(2)}, u32[]{:S(2)}) %collective-permute-start.9) | collective-permute-done | bytes 524320 | tf_op jit(solution)/shard_map/ppermute | solution.py:21
  129.5 10.7 %all-to-all-done.1 = bf16[16,16,256]{2,1,0:T(8,128)(2,1)S(1)} async-done(((bf16[16,16,256]{2,1,0:T(8,128)(2,1)}), bf16[16,16,256]{2,1,0:T(8,128)(2,1)S(1)}, u32[]{:S(2)}, u32[]{:S(2)}) %all-to-all-start.1) | async-done | bytes 131104 | tf_op jit(solution)/shard_map/all_to_all | solution.py:318
  140.2 3.6 %all-to-all-start.2 = ((bf16[8,32,1664]{2,1,0:T(8,128)(2,1)}), bf16[8,32,1664]{2,1,0:T(8,128)(2,1)S(1)}, u32[]{:S(2)}, u32[]{:S(2)}) async-start(bf16[8,32,1664]{2,1,0:T(8,128)(2,1)} %bitcast.6), calls=%async_computation.2 | async-start | bytes 1703936 | tf_op jit(solution)/shard_map/all_to_all | solution.py:323
  143.8 1.9 %collective-permute-start.11 = (bf16[16,256]{1,0:T(8,128)(2,1)S(1)}, bf16[16,256]{1,0:T(8,128)(2,1)S(1)}, u32[]{:S(2)}, u32[]{:S(2)}) collective-permute-start(bf16[16,256]{1,0:T(8,128)(2,1)S(1)} %multiply_convert_fusion), channel_id=1, source_target_pairs={{0,8},{8,0},{1,9},{9,1},{2,10},{10,2},{3,11},{11,3},{4,12},{12,4},... | collective-permute-start | bytes 24584 | tf_op jit(solution)/shard_map/ppermute | solution.py:29
  146.9 2.8 %collective-permute-start.12 = (bf16[32,256]{1,0:T(8,128)(2,1)S(1)}, bf16[32,256]{1,0:T(8,128)(2,1)S(1)}, u32[]{:S(2)}, u32[]{:S(2)}) collective-permute-start(bf16[32,256]{1,0:T(8,128)(2,1)S(1)} %pad_maximum_fusion.5), channel_id=1, source_target_pairs={{0,16},{16,0},{32,48},{48,32},{1,17},{17,1},{33,49},{49,33},{2,18}... | collective-permute-start | bytes 49160 | tf_op jit(solution)/shard_map/ppermute | solution.py:29
  149.6 2.9 %collective-permute-done.12 = bf16[32,256]{1,0:T(8,128)(2,1)S(1)} collective-permute-done((bf16[32,256]{1,0:T(8,128)(2,1)S(1)}, bf16[32,256]{1,0:T(8,128)(2,1)S(1)}, u32[]{:S(2)}, u32[]{:S(2)}) %collective-permute-start.12) | collective-permute-done | bytes 16416 | tf_op jit(solution)/shard_map/ppermute | solution.py:29
  152.5 3.4 %collective-permute-start.13 = (bf16[64,256]{1,0:T(8,128)(2,1)S(1)}, bf16[64,256]{1,0:T(8,128)(2,1)S(1)}, u32[]{:S(2)}, u32[]{:S(2)}) collective-permute-start(bf16[64,256]{1,0:T(8,128)(2,1)S(1)} %pad_maximum_fusion.4), channel_id=1, source_target_pairs={{0,32},{16,48},{32,0},{48,16},{1,33},{17,49},{33,1},{49,17},{2,34}... | collective-permute-start | bytes 98312 | tf_op jit(solution)/shard_map/ppermute | solution.py:29
  155.9 3.9 %collective-permute-done.13 = bf16[64,256]{1,0:T(8,128)(2,1)S(1)} collective-permute-done((bf16[64,256]{1,0:T(8,128)(2,1)S(1)}, bf16[64,256]{1,0:T(8,128)(2,1)S(1)}, u32[]{:S(2)}, u32[]{:S(2)}) %collective-permute-start.13) | collective-permute-done | bytes 32800 | tf_op jit(solution)/shard_map/ppermute | solution.py:29
  159.9 3.4 %collective-permute-start.14 = (bf16[128,256]{1,0:T(8,128)(2,1)S(1)}, bf16[128,256]{1,0:T(8,128)(2,1)S(1)}, u32[]{:S(2)}, u32[]{:S(2)}) collective-permute-start(bf16[128,256]{1,0:T(8,128)(2,1)S(1)} %pad_maximum_fusion.3), channel_id=1, source_target_pairs={{0,64},{64,0},{128,192},{192,128},{1,65},{65,1},{129,193},{193,129... | collective-permute-start | bytes 196616 | tf_op jit(solution)/shard_map/ppermute | solution.py:29
  163.2 2.8 %collective-permute-done.14 = bf16[128,256]{1,0:T(8,128)(2,1)S(1)} collective-permute-done((bf16[128,256]{1,0:T(8,128)(2,1)S(1)}, bf16[128,256]{1,0:T(8,128)(2,1)S(1)}, u32[]{:S(2)}, u32[]{:S(2)}) %collective-permute-start.14) | collective-permute-done | bytes 65568 | tf_op jit(solution)/shard_map/ppermute | solution.py:29
  166.1 4.9 %collective-permute-start.15 = (bf16[256,256]{1,0:T(8,128)(2,1)S(1)}, bf16[256,256]{1,0:T(8,128)(2,1)S(1)}, u32[]{:S(2)}, u32[]{:S(2)}) collective-permute-start(bf16[256,256]{1,0:T(8,128)(2,1)S(1)} %pad_maximum_fusion.2), channel_id=1, source_target_pairs={{0,128},{64,192},{128,0},{192,64},{1,129},{65,193},{129,1},{193,65... | collective-permute-start | bytes 393224 | tf_op jit(solution)/shard_map/ppermute | solution.py:29
  171.0 3.4 %collective-permute-done.15 = bf16[256,256]{1,0:T(8,128)(2,1)S(1)} collective-permute-done((bf16[256,256]{1,0:T(8,128)(2,1)S(1)}, bf16[256,256]{1,0:T(8,128)(2,1)S(1)}, u32[]{:S(2)}, u32[]{:S(2)}) %collective-permute-start.15) | collective-permute-done | bytes 131104 | tf_op jit(solution)/shard_map/ppermute | solution.py:29
  175.2 10.9 %all-to-all-done.2 = bf16[8,32,1664]{2,1,0:T(8,128)(2,1)S(1)} async-done(((bf16[8,32,1664]{2,1,0:T(8,128)(2,1)}), bf16[8,32,1664]{2,1,0:T(8,128)(2,1)S(1)}, u32[]{:S(2)}, u32[]{:S(2)}) %all-to-all-start.2) | async-done | bytes 852000 | tf_op jit(solution)/shard_map/all_to_all | solution.py:323
  (63 shorter events, 21.7 us)
Async XLA Ops:
  0.6 68.3 %copy-start = (bf16[64,128,128]{2,1,0:T(8,128)(2,1)S(1)}, bf16[64,128,128]{2,1,0:T(8,128)(2,1)}, u32[]{:S(2)}) copy-start(bf16[64,128,128]{2,1,0:T(8,128)(2,1)} %refs_5_.3) | copy-start | bytes 6291460
  0.6 1.3 copy-start.3
  2.3 27.9 %collective-permute-start = (bf16[32,1664]{1,0:T(8,128)(2,1)S(1)}, bf16[32,1664]{1,0:T(8,128)(2,1)S(1)}, u32[]{:S(2)}, u32[]{:S(2)}) collective-permute-start(bf16[32,1664]{1,0:T(8,128)(2,1)S(1)} %get-tuple-element.31), channel_id=1, source_target_pairs={{0,1},{1,2},{2,3},{3,4},{4,5},{5,6},{6,7},{7,0},{8,9},{9,10},{10,1... | collective-permute-start | bytes 319496 | tf_op jit(solution)/shard_map/ppermute | solution.py:21
  6.2 28.6 %collective-permute-start.1 = (bf16[32,1664]{1,0:T(8,128)(2,1)S(1)}, bf16[32,1664]{1,0:T(8,128)(2,1)S(1)}, u32[]{:S(2)}, u32[]{:S(2)}) collective-permute-start(bf16[32,1664]{1,0:T(8,128)(2,1)S(1)} %get-tuple-element.32), channel_id=1, source_target_pairs={{0,2},{1,3},{2,4},{3,5},{4,6},{5,7},{6,0},{7,1},{8,10},{9,11},{10,... | collective-permute-start | bytes 319496 | tf_op jit(solution)/shard_map/ppermute | solution.py:21
  11.3 29.7 %collective-permute-start.2 = (bf16[32,1664]{1,0:T(8,128)(2,1)S(1)}, bf16[32,1664]{1,0:T(8,128)(2,1)S(1)}, u32[]{:S(2)}, u32[]{:S(2)}) collective-permute-start(bf16[32,1664]{1,0:T(8,128)(2,1)S(1)} %get-tuple-element.33), channel_id=1, source_target_pairs={{0,3},{1,4},{2,5},{3,6},{4,7},{5,0},{6,1},{7,2},{8,11},{9,12},{10,... | collective-permute-start | bytes 319496 | tf_op jit(solution)/shard_map/ppermute | solution.py:21
  19.1 22.0 %collective-permute-start.3 = (bf16[32,1664]{1,0:T(8,128)(2,1)S(1)}, bf16[32,1664]{1,0:T(8,128)(2,1)S(1)}, u32[]{:S(2)}, u32[]{:S(2)}) collective-permute-start(bf16[32,1664]{1,0:T(8,128)(2,1)S(1)} %get-tuple-element.34), channel_id=1, source_target_pairs={{0,4},{1,5},{2,6},{3,7},{4,0},{5,1},{6,2},{7,3},{8,12},{9,13},{10,... | collective-permute-start | bytes 319496 | tf_op jit(solution)/shard_map/ppermute | solution.py:21
  22.4 18.7 %collective-permute-start.4 = (bf16[32,1664]{1,0:T(8,128)(2,1)S(1)}, bf16[32,1664]{1,0:T(8,128)(2,1)S(1)}, u32[]{:S(2)}, u32[]{:S(2)}) collective-permute-start(bf16[32,1664]{1,0:T(8,128)(2,1)S(1)} %get-tuple-element.35), channel_id=1, source_target_pairs={{0,5},{1,6},{2,7},{3,0},{4,1},{5,2},{6,3},{7,4},{8,13},{9,14},{10,... | collective-permute-start | bytes 319496 | tf_op jit(solution)/shard_map/ppermute | solution.py:21
  30.2 15.6 %collective-permute-start.5 = (bf16[32,1664]{1,0:T(8,128)(2,1)S(1)}, bf16[32,1664]{1,0:T(8,128)(2,1)S(1)}, u32[]{:S(2)}, u32[]{:S(2)}) collective-permute-start(bf16[32,1664]{1,0:T(8,128)(2,1)S(1)} %get-tuple-element.36), channel_id=1, source_target_pairs={{0,6},{1,7},{2,0},{3,1},{4,2},{5,3},{6,4},{7,5},{8,14},{9,15},{10,... | collective-permute-start | bytes 319496 | tf_op jit(solution)/shard_map/ppermute | solution.py:21
  34.8 11.1 %collective-permute-start.6 = (bf16[32,1664]{1,0:T(8,128)(2,1)S(1)}, bf16[32,1664]{1,0:T(8,128)(2,1)S(1)}, u32[]{:S(2)}, u32[]{:S(2)}) collective-permute-start(bf16[32,1664]{1,0:T(8,128)(2,1)S(1)} %get-tuple-element.37), channel_id=1, source_target_pairs={{0,7},{1,0},{2,1},{3,2},{4,3},{5,4},{6,5},{7,6},{8,15},{9,8},{10,9... | collective-permute-start | bytes 319496 | tf_op jit(solution)/shard_map/ppermute | solution.py:21
  47.0 25.4 %collective-permute-start.7 = (bf16[256,1024]{1,0:T(8,128)(2,1)}, bf16[256,1024]{1,0:T(8,128)(2,1)S(1)}, u32[]{:S(2)}, u32[]{:S(2)}) collective-permute-start(bf16[256,1024]{1,0:T(8,128)(2,1)} %get-tuple-element.39), channel_id=1, source_target_pairs={{0,1},{1,2},{2,3},{3,4},{4,5},{5,6},{6,7},{7,8},{8,9},{9,10},{10,1... | collective-permute-start | bytes 1572872 | tf_op jit(solution)/shard_map/ppermute | solution.py:21
  52.1 28.3 %collective-permute-start.8 = (bf16[256,1024]{1,0:T(8,128)(2,1)}, bf16[256,1024]{1,0:T(8,128)(2,1)}, u32[]{:S(2)}, u32[]{:S(2)}) collective-permute-start(bf16[256,1024]{1,0:T(8,128)(2,1)} %get-tuple-element.40), channel_id=1, source_target_pairs={{0,511},{1,0},{2,1},{3,2},{4,3},{5,4},{6,5},{7,6},{8,7},{9,8},{10,... | collective-permute-start | bytes 1572872 | tf_op jit(solution)/shard_map/ppermute | solution.py:21
  70.9 0.7 copy-start.12
  71.6 8.8 %copy-start.4 = (bf16[256,1664]{1,0:T(8,128)(2,1)S(1)}, bf16[256,1664]{1,0:T(8,128)(2,1)}, u32[]{:S(2)}) copy-start(bf16[256,1664]{1,0:T(8,128)(2,1)} %refs_11_.1) | copy-start | bytes 2555908
  71.6 8.8 %copy-start.7 = (s32[192]{0:T(256)S(1)}, s32[192]{0:T(256)}, u32[]{:S(2)}) copy-start(s32[192]{0:T(256)} %get-tuple-element.27.refs_1_) | copy-start | bytes 2308
  71.6 8.8 %copy-start.9 = (s32[192]{0:T(256)S(1)}, s32[192]{0:T(256)}, u32[]{:S(2)}) copy-start(s32[192]{0:T(256)} %get-tuple-element.28.refs_2_) | copy-start | bytes 2308
  71.6 8.8 %copy-start.11 = (s32[192]{0:T(256)S(1)}, s32[192]{0:T(256)}, u32[]{:S(2)}) copy-start(s32[192]{0:T(256)} %get-tuple-element.29.refs_3_) | copy-start | bytes 2308
  71.6 8.8 %copy-start.13 = (s32[3]{0:T(128)S(1)}, s32[3]{0:T(128)}, u32[]{:S(2)}) copy-start(s32[3]{0:T(128)} %get-tuple-element.42.refs_0_) | copy-start | bytes 40
  84.5 1.2 copy-start.1
  85.8 0.8 copy-start.5
  86.6 0.8 copy-start.14
  87.4 0.8 copy-start.15
  88.2 17.9 %all-to-all-start = ((f32[32,16,256]{2,1,0:T(8,128)}), f32[32,16,256]{2,1,0:T(8,128)}, u32[]{:S(2)}, u32[]{:S(2)}) async-start(f32[32,16,256]{2,1,0:T(8,128)} %bitcast.10), calls=%async_computation | async-start | bytes 1048576 | tf_op jit(solution)/shard_map/all_to_all | solution.py:313
  96.6 24.7 %collective-permute-start.10 = (bf16[256,1024]{1,0:T(8,128)(2,1)}, bf16[256,1024]{1,0:T(8,128)(2,1)S(1)}, u32[]{:S(2)}, u32[]{:S(2)}) collective-permute-start(bf16[256,1024]{1,0:T(8,128)(2,1)} %copy-done.15), channel_id=1, source_target_pairs={{0,511},{1,0},{2,1},{3,2},{4,3},{5,4},{6,5},{7,6},{8,7},{9,8},{10,... | collective-permute-start | bytes 1572872 | tf_op jit(solution)/shard_map/ppermute | solution.py:21
  103.6 24.8 %collective-permute-start.9 = (bf16[256,1024]{1,0:T(8,128)(2,1)}, bf16[256,1024]{1,0:T(8,128)(2,1)S(1)}, u32[]{:S(2)}, u32[]{:S(2)}) collective-permute-start(bf16[256,1024]{1,0:T(8,128)(2,1)} %copy-done.14), channel_id=1, source_target_pairs={{0,1},{1,2},{2,3},{3,4},{4,5},{5,6},{6,7},{7,8},{8,9},{9,10},{10,1... | collective-permute-start | bytes 1572872 | tf_op jit(solution)/shard_map/ppermute | solution.py:21
  107.8 32.4 %all-to-all-start.1 = ((bf16[16,16,256]{2,1,0:T(8,128)(2,1)}), bf16[16,16,256]{2,1,0:T(8,128)(2,1)S(1)}, u32[]{:S(2)}, u32[]{:S(2)}) async-start(bf16[16,16,256]{2,1,0:T(8,128)(2,1)} %broadcast_in_dim.10), calls=%async_computation.1 | async-start | bytes 262144 | tf_op jit(solution)/shard_map/all_to_all | solution.py:318
  119.2 1.5 copy-start.2
  140.2 45.9 %all-to-all-start.2 = ((bf16[8,32,1664]{2,1,0:T(8,128)(2,1)}), bf16[8,32,1664]{2,1,0:T(8,128)(2,1)S(1)}, u32[]{:S(2)}, u32[]{:S(2)}) async-start(bf16[8,32,1664]{2,1,0:T(8,128)(2,1)} %bitcast.6), calls=%async_computation.2 | async-start | bytes 1703936 | tf_op jit(solution)/shard_map/all_to_all | solution.py:323
  143.8 3.1 %collective-permute-start.11 = (bf16[16,256]{1,0:T(8,128)(2,1)S(1)}, bf16[16,256]{1,0:T(8,128)(2,1)S(1)}, u32[]{:S(2)}, u32[]{:S(2)}) collective-permute-start(bf16[16,256]{1,0:T(8,128)(2,1)S(1)} %multiply_convert_fusion), channel_id=1, source_target_pairs={{0,8},{8,0},{1,9},{9,1},{2,10},{10,2},{3,11},{11,3},{4,12},{12,4},... | collective-permute-start | bytes 24584 | tf_op jit(solution)/shard_map/ppermute | solution.py:29
  146.9 5.6 %collective-permute-start.12 = (bf16[32,256]{1,0:T(8,128)(2,1)S(1)}, bf16[32,256]{1,0:T(8,128)(2,1)S(1)}, u32[]{:S(2)}, u32[]{:S(2)}) collective-permute-start(bf16[32,256]{1,0:T(8,128)(2,1)S(1)} %pad_maximum_fusion.5), channel_id=1, source_target_pairs={{0,16},{16,0},{32,48},{48,32},{1,17},{17,1},{33,49},{49,33},{2,18}... | collective-permute-start | bytes 49160 | tf_op jit(solution)/shard_map/ppermute | solution.py:29
  152.5 7.3 %collective-permute-start.13 = (bf16[64,256]{1,0:T(8,128)(2,1)S(1)}, bf16[64,256]{1,0:T(8,128)(2,1)S(1)}, u32[]{:S(2)}, u32[]{:S(2)}) collective-permute-start(bf16[64,256]{1,0:T(8,128)(2,1)S(1)} %pad_maximum_fusion.4), channel_id=1, source_target_pairs={{0,32},{16,48},{32,0},{48,16},{1,33},{17,49},{33,1},{49,17},{2,34}... | collective-permute-start | bytes 98312 | tf_op jit(solution)/shard_map/ppermute | solution.py:29
  159.9 6.2 %collective-permute-start.14 = (bf16[128,256]{1,0:T(8,128)(2,1)S(1)}, bf16[128,256]{1,0:T(8,128)(2,1)S(1)}, u32[]{:S(2)}, u32[]{:S(2)}) collective-permute-start(bf16[128,256]{1,0:T(8,128)(2,1)S(1)} %pad_maximum_fusion.3), channel_id=1, source_target_pairs={{0,64},{64,0},{128,192},{192,128},{1,65},{65,1},{129,193},{193,129... | collective-permute-start | bytes 196616 | tf_op jit(solution)/shard_map/ppermute | solution.py:29
  166.1 8.4 %collective-permute-start.15 = (bf16[256,256]{1,0:T(8,128)(2,1)S(1)}, bf16[256,256]{1,0:T(8,128)(2,1)S(1)}, u32[]{:S(2)}, u32[]{:S(2)}) collective-permute-start(bf16[256,256]{1,0:T(8,128)(2,1)S(1)} %pad_maximum_fusion.2), channel_id=1, source_target_pairs={{0,128},{64,192},{128,0},{192,64},{1,129},{65,193},{129,1},{193,65... | collective-permute-start | bytes 393224 | tf_op jit(solution)/shard_map/ppermute | solution.py:29
  (3 other events, 2.0 us)

commit v12 on v11

--- a/solution.py
+++ b/solution.py
@@ -297,7 +297,10 @@
     w_out = jnp.concatenate([w_self, w_neigh], axis=0)
     pieces = lax.axis_size("feat")
     received = list(cut_step(pos, features, pieces))
-    for step in sorted(range(1, pieces), key=lambda step: (abs(2 * step - pieces), step)):
+    far = sorted(range(1, pieces), key=lambda step: (abs(2 * step - pieces), step))
+    half = (pieces - 1) // 2 + 1
+    mixed = [step for pair in zip(far[:half], far[half:] + [0]) for step in pair if step]
+    for step in mixed:
         received[step] = shifted(received[step], "feat", step)
     own, head, tail = join_step(pos, received, rim)
     before = shifted(tail, RING, 1)

time: 188 us -> 188 us (level)
  no operation moved by 1% of the time
where the time goes in v12:
time: 188 us; the launch traced here: 187 us
  starting transfers between devices  98.2 us (52%)
  waiting for transfers between devices  59.4 us (32%)
  local copies, waits for them, and re-layouts  14 us (7%)
  Pallas kernels  10.2 us (5%)
  other arithmetic  3.92 us (2%)
    ppermute x11, starting transfers between devices, shifted(): lax.ppermute(shard, axis, [(i, (i + by) % count) for i in range(count)])  58.3 us
    ppermute x11, waiting for transfers between devices, shifted(): lax.ppermute(shard, axis, [(i, (i + by) % count) for i in range(count)])  21.6 us
    ppermute x5, starting transfers between devices, collected(): other = lax.ppermute(rows, axis, [(i, i ^ apart) for i in range(count)])  16.3 us
    ppermute x5, waiting for transfers between devices, collected(): other = lax.ppermute(rows, axis, [(i, i ^ apart) for i in range(count)])  14.1 us
    unnamed x34, local copies, waits for them, and re-layouts  12.4 us
    all_to_all x1, starting transfers between devices, on_device(): lax.all_to_all(copies, LINE, split_axis=0, concat_axis=0, tiled=True)  12.1 us
    all_to_all x1, waiting for transfers between devices, on_device(): lax.all_to_all(copies, LINE, split_axis=0, concat_axis=0, tiled=True)  11.7 us
    all_to_all x1, waiting for transfers between devices, on_device(): lax.all_to_all(total, 'feat', split_axis=0, concat_axis=1, tiled=True)  11 us
  transfers between devices with their start and end apart: 19, of which 12 were waited for; matrix products, arithmetic and copies ran while one was open for 4% of the time, Pallas kernels for 2%

profile of v12, /device:TPU:6, one launch (start us, length us, event | category | flops | bytes accessed | tf_op | source)
XLA Modules:
  0.0 187.4 jit_solution(8569148871671644669)
XLA Ops:
  2.3 3.8 %collective-permute-start = (bf16[32,1664]{1,0:T(8,128)(2,1)S(1)}, bf16[32,1664]{1,0:T(8,128)(2,1)S(1)}, u32[]{:S(2)}, u32[]{:S(2)}) collective-permute-start(bf16[32,1664]{1,0:T(8,128)(2,1)S(1)} %get-tuple-element.31), channel_id=1, source_target_pairs={{0,1},{1,2},{2,3},{3,4},{4,5},{5,6},{6,7},{7,0},{8,9},{9,10},{10,1... | collective-permute-start | bytes 319496 | tf_op jit(solution)/shard_map/ppermute | solution.py:21
  6.2 5.2 %collective-permute-start.1 = (bf16[32,1664]{1,0:T(8,128)(2,1)S(1)}, bf16[32,1664]{1,0:T(8,128)(2,1)S(1)}, u32[]{:S(2)}, u32[]{:S(2)}) collective-permute-start(bf16[32,1664]{1,0:T(8,128)(2,1)S(1)} %get-tuple-element.32), channel_id=1, source_target_pairs={{0,2},{1,3},{2,4},{3,5},{4,6},{5,7},{6,0},{7,1},{8,10},{9,11},{10,... | collective-permute-start | bytes 319496 | tf_op jit(solution)/shard_map/ppermute | solution.py:21
  11.3 7.7 %collective-permute-start.2 = (bf16[32,1664]{1,0:T(8,128)(2,1)S(1)}, bf16[32,1664]{1,0:T(8,128)(2,1)S(1)}, u32[]{:S(2)}, u32[]{:S(2)}) collective-permute-start(bf16[32,1664]{1,0:T(8,128)(2,1)S(1)} %get-tuple-element.33), channel_id=1, source_target_pairs={{0,3},{1,4},{2,5},{3,6},{4,7},{5,0},{6,1},{7,2},{8,11},{9,12},{10,... | collective-permute-start | bytes 319496 | tf_op jit(solution)/shard_map/ppermute | solution.py:21
  19.1 3.3 %collective-permute-start.3 = (bf16[32,1664]{1,0:T(8,128)(2,1)S(1)}, bf16[32,1664]{1,0:T(8,128)(2,1)S(1)}, u32[]{:S(2)}, u32[]{:S(2)}) collective-permute-start(bf16[32,1664]{1,0:T(8,128)(2,1)S(1)} %get-tuple-element.34), channel_id=1, source_target_pairs={{0,4},{1,5},{2,6},{3,7},{4,0},{5,1},{6,2},{7,3},{8,12},{9,13},{10,... | collective-permute-start | bytes 319496 | tf_op jit(solution)/shard_map/ppermute | solution.py:21
  22.4 7.8 %collective-permute-start.4 = (bf16[32,1664]{1,0:T(8,128)(2,1)S(1)}, bf16[32,1664]{1,0:T(8,128)(2,1)S(1)}, u32[]{:S(2)}, u32[]{:S(2)}) collective-permute-start(bf16[32,1664]{1,0:T(8,128)(2,1)S(1)} %get-tuple-element.35), channel_id=1, source_target_pairs={{0,5},{1,6},{2,7},{3,0},{4,1},{5,2},{6,3},{7,4},{8,13},{9,14},{10,... | collective-permute-start | bytes 319496 | tf_op jit(solution)/shard_map/ppermute | solution.py:21
  30.2 4.6 %collective-permute-start.5 = (bf16[32,1664]{1,0:T(8,128)(2,1)S(1)}, bf16[32,1664]{1,0:T(8,128)(2,1)S(1)}, u32[]{:S(2)}, u32[]{:S(2)}) collective-permute-start(bf16[32,1664]{1,0:T(8,128)(2,1)S(1)} %get-tuple-element.36), channel_id=1, source_target_pairs={{0,6},{1,7},{2,0},{3,1},{4,2},{5,3},{6,4},{7,5},{8,14},{9,15},{10,... | collective-permute-start | bytes 319496 | tf_op jit(solution)/shard_map/ppermute | solution.py:21
  34.8 2.9 %collective-permute-start.6 = (bf16[32,1664]{1,0:T(8,128)(2,1)S(1)}, bf16[32,1664]{1,0:T(8,128)(2,1)S(1)}, u32[]{:S(2)}, u32[]{:S(2)}) collective-permute-start(bf16[32,1664]{1,0:T(8,128)(2,1)S(1)} %get-tuple-element.37), channel_id=1, source_target_pairs={{0,7},{1,0},{2,1},{3,2},{4,3},{5,4},{6,5},{7,6},{8,15},{9,8},{10,9... | collective-permute-start | bytes 319496 | tf_op jit(solution)/shard_map/ppermute | solution.py:21
  37.7 3.3 %collective-permute-done.2.refs_3_ = bf16[32,1664]{1,0:T(8,128)(2,1)S(1)} collective-permute-done((bf16[32,1664]{1,0:T(8,128)(2,1)S(1)}, bf16[32,1664]{1,0:T(8,128)(2,1)S(1)}, u32[]{:S(2)}, u32[]{:S(2)}) %collective-permute-start.2) | collective-permute-done | bytes 106528 | tf_op jit(solution)/shard_map/ppermute | solution.py:21
  41.1 4.8 %collective-permute-done.5.refs_6_ = bf16[32,1664]{1,0:T(8,128)(2,1)S(1)} collective-permute-done((bf16[32,1664]{1,0:T(8,128)(2,1)S(1)}, bf16[32,1664]{1,0:T(8,128)(2,1)S(1)}, u32[]{:S(2)}, u32[]{:S(2)}) %collective-permute-start.5) | collective-permute-done | bytes 106528 | tf_op jit(solution)/shard_map/ppermute | solution.py:21
  47.0 5.1 %collective-permute-start.7 = (bf16[256,1024]{1,0:T(8,128)(2,1)}, bf16[256,1024]{1,0:T(8,128)(2,1)S(1)}, u32[]{:S(2)}, u32[]{:S(2)}) collective-permute-start(bf16[256,1024]{1,0:T(8,128)(2,1)} %get-tuple-element.39), channel_id=1, source_target_pairs={{0,1},{1,2},{2,3},{3,4},{4,5},{5,6},{6,7},{7,8},{8,9},{9,10},{10,1... | collective-permute-start | bytes 1572872 | tf_op jit(solution)/shard_map/ppermute | solution.py:21
  52.1 9.4 %collective-permute-start.8 = (bf16[256,1024]{1,0:T(8,128)(2,1)}, bf16[256,1024]{1,0:T(8,128)(2,1)}, u32[]{:S(2)}, u32[]{:S(2)}) collective-permute-start(bf16[256,1024]{1,0:T(8,128)(2,1)} %get-tuple-element.40), channel_id=1, source_target_pairs={{0,511},{1,0},{2,1},{3,2},{4,3},{5,4},{6,5},{7,6},{8,7},{9,8},{10,... | collective-permute-start | bytes 1572872 | tf_op jit(solution)/shard_map/ppermute | solution.py:21
  62.2 1.7 copy.14
  65.5 1.7 shard_map.103
  72.9 7.5 %collective-permute-done.8.refs_7_ = bf16[256,1024]{1,0:T(8,128)(2,1)} collective-permute-done((bf16[256,1024]{1,0:T(8,128)(2,1)}, bf16[256,1024]{1,0:T(8,128)(2,1)}, u32[]{:S(2)}, u32[]{:S(2)}) %collective-permute-start.8) | collective-permute-done | bytes 524320 | tf_op jit(solution)/shard_map/ppermute | solution.py:21
  80.4 4.1 %shard_map.107 = (bf16[256,1024]{1,0:T(8,128)(2,1)S(1)}, bf16[256,1024]{1,0:T(8,128)(2,1)S(1)}, f32[512,256]{1,0:T(8,128)S(1)}, bf16[512,1664]{1,0:T(8,128)(2,1)S(1)}) custom-call(s32[3]{0:T(128)S(1)} %copy-done.13, s32[192]{0:T(256)S(1)} %copy-done.7, s32[192]{0:T(256)S(1)} %copy-done.9, s32[192]{0:T(256)S(1)} %copy-done.11, ...), custom_call_target="tpu_custom_call" | custom-call | flops 1308622848 | bytes 8388608 | tf_op jit(solution)/shard_map/pallas_call | solution.py:167
  88.2 7.8 %all-to-all-start = ((f32[32,16,256]{2,1,0:T(8,128)}), f32[32,16,256]{2,1,0:T(8,128)}, u32[]{:S(2)}, u32[]{:S(2)}) async-start(f32[32,16,256]{2,1,0:T(8,128)} %bitcast.10), calls=%async_computation | async-start | bytes 1048576 | tf_op jit(solution)/shard_map/all_to_all | solution.py:316
  96.0 6.5 %collective-permute-start.10 = (bf16[256,1024]{1,0:T(8,128)(2,1)}, bf16[256,1024]{1,0:T(8,128)(2,1)S(1)}, u32[]{:S(2)}, u32[]{:S(2)}) collective-permute-start(bf16[256,1024]{1,0:T(8,128)(2,1)} %copy-done.15), channel_id=1, source_target_pairs={{0,511},{1,0},{2,1},{3,2},{4,3},{5,4},{6,5},{7,6},{8,7},{9,8},{10,... | collective-permute-start | bytes 1572872 | tf_op jit(solution)/shard_map/ppermute | solution.py:21
  102.5 1.9 %collective-permute-start.9 = (bf16[256,1024]{1,0:T(8,128)(2,1)}, bf16[256,1024]{1,0:T(8,128)(2,1)S(1)}, u32[]{:S(2)}, u32[]{:S(2)}) collective-permute-start(bf16[256,1024]{1,0:T(8,128)(2,1)} %copy-done.14), channel_id=1, source_target_pairs={{0,1},{1,2},{2,3},{3,4},{4,5},{5,6},{6,7},{7,8},{8,9},{9,10},{10,1... | collective-permute-start | bytes 1572872 | tf_op jit(solution)/shard_map/ppermute | solution.py:21
  107.1 12.1 %all-to-all-start.1 = ((bf16[16,16,256]{2,1,0:T(8,128)(2,1)}), bf16[16,16,256]{2,1,0:T(8,128)(2,1)S(1)}, u32[]{:S(2)}, u32[]{:S(2)}) async-start(bf16[16,16,256]{2,1,0:T(8,128)(2,1)} %broadcast_in_dim.10), calls=%async_computation.1 | async-start | bytes 262144 | tf_op jit(solution)/shard_map/all_to_all | solution.py:321
  121.6 5.9 %collective-permute-done.9.prev_ref = bf16[256,1024]{1,0:T(8,128)(2,1)S(1)} collective-permute-done((bf16[256,1024]{1,0:T(8,128)(2,1)}, bf16[256,1024]{1,0:T(8,128)(2,1)S(1)}, u32[]{:S(2)}, u32[]{:S(2)}) %collective-permute-start.9) | collective-permute-done | bytes 524320 | tf_op jit(solution)/shard_map/ppermute | solution.py:21
  128.6 11.7 %all-to-all-done.1 = bf16[16,16,256]{2,1,0:T(8,128)(2,1)S(1)} async-done(((bf16[16,16,256]{2,1,0:T(8,128)(2,1)}), bf16[16,16,256]{2,1,0:T(8,128)(2,1)S(1)}, u32[]{:S(2)}, u32[]{:S(2)}) %all-to-all-start.1) | async-done | bytes 131104 | tf_op jit(solution)/shard_map/all_to_all | solution.py:321
  140.3 3.7 %all-to-all-start.2 = ((bf16[8,32,1664]{2,1,0:T(8,128)(2,1)}), bf16[8,32,1664]{2,1,0:T(8,128)(2,1)S(1)}, u32[]{:S(2)}, u32[]{:S(2)}) async-start(bf16[8,32,1664]{2,1,0:T(8,128)(2,1)} %bitcast.6), calls=%async_computation.2 | async-start | bytes 1703936 | tf_op jit(solution)/shard_map/all_to_all | solution.py:326
  144.1 1.9 %collective-permute-start.11 = (bf16[16,256]{1,0:T(8,128)(2,1)S(1)}, bf16[16,256]{1,0:T(8,128)(2,1)S(1)}, u32[]{:S(2)}, u32[]{:S(2)}) collective-permute-start(bf16[16,256]{1,0:T(8,128)(2,1)S(1)} %multiply_convert_fusion), channel_id=1, source_target_pairs={{0,8},{8,0},{1,9},{9,1},{2,10},{10,2},{3,11},{11,3},{4,12},{12,4},... | collective-permute-start | bytes 24584 | tf_op jit(solution)/shard_map/ppermute | solution.py:29
  147.1 2.8 %collective-permute-start.12 = (bf16[32,256]{1,0:T(8,128)(2,1)S(1)}, bf16[32,256]{1,0:T(8,128)(2,1)S(1)}, u32[]{:S(2)}, u32[]{:S(2)}) collective-permute-start(bf16[32,256]{1,0:T(8,128)(2,1)S(1)} %pad_maximum_fusion.5), channel_id=1, source_target_pairs={{0,16},{16,0},{32,48},{48,32},{1,17},{17,1},{33,49},{49,33},{2,18}... | collective-permute-start | bytes 49160 | tf_op jit(solution)/shard_map/ppermute | solution.py:29
  149.9 2.9 %collective-permute-done.12 = bf16[32,256]{1,0:T(8,128)(2,1)S(1)} collective-permute-done((bf16[32,256]{1,0:T(8,128)(2,1)S(1)}, bf16[32,256]{1,0:T(8,128)(2,1)S(1)}, u32[]{:S(2)}, u32[]{:S(2)}) %collective-permute-start.12) | collective-permute-done | bytes 16416 | tf_op jit(solution)/shard_map/ppermute | solution.py:29
  152.8 3.4 %collective-permute-start.13 = (bf16[64,256]{1,0:T(8,128)(2,1)S(1)}, bf16[64,256]{1,0:T(8,128)(2,1)S(1)}, u32[]{:S(2)}, u32[]{:S(2)}) collective-permute-start(bf16[64,256]{1,0:T(8,128)(2,1)S(1)} %pad_maximum_fusion.4), channel_id=1, source_target_pairs={{0,32},{16,48},{32,0},{48,16},{1,33},{17,49},{33,1},{49,17},{2,34}... | collective-permute-start | bytes 98312 | tf_op jit(solution)/shard_map/ppermute | solution.py:29
  156.2 3.9 %collective-permute-done.13 = bf16[64,256]{1,0:T(8,128)(2,1)S(1)} collective-permute-done((bf16[64,256]{1,0:T(8,128)(2,1)S(1)}, bf16[64,256]{1,0:T(8,128)(2,1)S(1)}, u32[]{:S(2)}, u32[]{:S(2)}) %collective-permute-start.13) | collective-permute-done | bytes 32800 | tf_op jit(solution)/shard_map/ppermute | solution.py:29
  160.1 3.4 %collective-permute-start.14 = (bf16[128,256]{1,0:T(8,128)(2,1)S(1)}, bf16[128,256]{1,0:T(8,128)(2,1)S(1)}, u32[]{:S(2)}, u32[]{:S(2)}) collective-permute-start(bf16[128,256]{1,0:T(8,128)(2,1)S(1)} %pad_maximum_fusion.3), channel_id=1, source_target_pairs={{0,64},{64,0},{128,192},{192,128},{1,65},{65,1},{129,193},{193,129... | collective-permute-start | bytes 196616 | tf_op jit(solution)/shard_map/ppermute | solution.py:29
  163.5 2.8 %collective-permute-done.14 = bf16[128,256]{1,0:T(8,128)(2,1)S(1)} collective-permute-done((bf16[128,256]{1,0:T(8,128)(2,1)S(1)}, bf16[128,256]{1,0:T(8,128)(2,1)S(1)}, u32[]{:S(2)}, u32[]{:S(2)}) %collective-permute-start.14) | collective-permute-done | bytes 65568 | tf_op jit(solution)/shard_map/ppermute | solution.py:29
  166.3 4.9 %collective-permute-start.15 = (bf16[256,256]{1,0:T(8,128)(2,1)S(1)}, bf16[256,256]{1,0:T(8,128)(2,1)S(1)}, u32[]{:S(2)}, u32[]{:S(2)}) collective-permute-start(bf16[256,256]{1,0:T(8,128)(2,1)S(1)} %pad_maximum_fusion.2), channel_id=1, source_target_pairs={{0,128},{64,192},{128,0},{192,64},{1,129},{65,193},{129,1},{193,65... | collective-permute-start | bytes 393224 | tf_op jit(solution)/shard_map/ppermute | solution.py:29
  171.2 3.4 %collective-permute-done.15 = bf16[256,256]{1,0:T(8,128)(2,1)S(1)} collective-permute-done((bf16[256,256]{1,0:T(8,128)(2,1)S(1)}, bf16[256,256]{1,0:T(8,128)(2,1)S(1)}, u32[]{:S(2)}, u32[]{:S(2)}) %collective-permute-start.15) | collective-permute-done | bytes 131104 | tf_op jit(solution)/shard_map/ppermute | solution.py:29
  175.4 11.0 %all-to-all-done.2 = bf16[8,32,1664]{2,1,0:T(8,128)(2,1)S(1)} async-done(((bf16[8,32,1664]{2,1,0:T(8,128)(2,1)}), bf16[8,32,1664]{2,1,0:T(8,128)(2,1)S(1)}, u32[]{:S(2)}, u32[]{:S(2)}) %all-to-all-start.2) | async-done | bytes 852000 | tf_op jit(solution)/shard_map/all_to_all | solution.py:326
  (63 shorter events, 22.8 us)
Async XLA Ops:
  0.6 68.6 %copy-start = (bf16[64,128,128]{2,1,0:T(8,128)(2,1)S(1)}, bf16[64,128,128]{2,1,0:T(8,128)(2,1)}, u32[]{:S(2)}) copy-start(bf16[64,128,128]{2,1,0:T(8,128)(2,1)} %refs_5_.3) | copy-start | bytes 6291460
  0.6 1.3 copy-start.3
  2.3 27.9 %collective-permute-start = (bf16[32,1664]{1,0:T(8,128)(2,1)S(1)}, bf16[32,1664]{1,0:T(8,128)(2,1)S(1)}, u32[]{:S(2)}, u32[]{:S(2)}) collective-permute-start(bf16[32,1664]{1,0:T(8,128)(2,1)S(1)} %get-tuple-element.31), channel_id=1, source_target_pairs={{0,1},{1,2},{2,3},{3,4},{4,5},{5,6},{6,7},{7,0},{8,9},{9,10},{10,1... | collective-permute-start | bytes 319496 | tf_op jit(solution)/shard_map/ppermute | solution.py:21
  6.2 28.6 %collective-permute-start.1 = (bf16[32,1664]{1,0:T(8,128)(2,1)S(1)}, bf16[32,1664]{1,0:T(8,128)(2,1)S(1)}, u32[]{:S(2)}, u32[]{:S(2)}) collective-permute-start(bf16[32,1664]{1,0:T(8,128)(2,1)S(1)} %get-tuple-element.32), channel_id=1, source_target_pairs={{0,2},{1,3},{2,4},{3,5},{4,6},{5,7},{6,0},{7,1},{8,10},{9,11},{10,... | collective-permute-start | bytes 319496 | tf_op jit(solution)/shard_map/ppermute | solution.py:21
  11.3 29.7 %collective-permute-start.2 = (bf16[32,1664]{1,0:T(8,128)(2,1)S(1)}, bf16[32,1664]{1,0:T(8,128)(2,1)S(1)}, u32[]{:S(2)}, u32[]{:S(2)}) collective-permute-start(bf16[32,1664]{1,0:T(8,128)(2,1)S(1)} %get-tuple-element.33), channel_id=1, source_target_pairs={{0,3},{1,4},{2,5},{3,6},{4,7},{5,0},{6,1},{7,2},{8,11},{9,12},{10,... | collective-permute-start | bytes 319496 | tf_op jit(solution)/shard_map/ppermute | solution.py:21
  19.1 22.0 %collective-permute-start.3 = (bf16[32,1664]{1,0:T(8,128)(2,1)S(1)}, bf16[32,1664]{1,0:T(8,128)(2,1)S(1)}, u32[]{:S(2)}, u32[]{:S(2)}) collective-permute-start(bf16[32,1664]{1,0:T(8,128)(2,1)S(1)} %get-tuple-element.34), channel_id=1, source_target_pairs={{0,4},{1,5},{2,6},{3,7},{4,0},{5,1},{6,2},{7,3},{8,12},{9,13},{10,... | collective-permute-start | bytes 319496 | tf_op jit(solution)/shard_map/ppermute | solution.py:21
  22.4 18.7 %collective-permute-start.4 = (bf16[32,1664]{1,0:T(8,128)(2,1)S(1)}, bf16[32,1664]{1,0:T(8,128)(2,1)S(1)}, u32[]{:S(2)}, u32[]{:S(2)}) collective-permute-start(bf16[32,1664]{1,0:T(8,128)(2,1)S(1)} %get-tuple-element.35), channel_id=1, source_target_pairs={{0,5},{1,6},{2,7},{3,0},{4,1},{5,2},{6,3},{7,4},{8,13},{9,14},{10,... | collective-permute-start | bytes 319496 | tf_op jit(solution)/shard_map/ppermute | solution.py:21
  30.2 15.6 %collective-permute-start.5 = (bf16[32,1664]{1,0:T(8,128)(2,1)S(1)}, bf16[32,1664]{1,0:T(8,128)(2,1)S(1)}, u32[]{:S(2)}, u32[]{:S(2)}) collective-permute-start(bf16[32,1664]{1,0:T(8,128)(2,1)S(1)} %get-tuple-element.36), channel_id=1, source_target_pairs={{0,6},{1,7},{2,0},{3,1},{4,2},{5,3},{6,4},{7,5},{8,14},{9,15},{10,... | collective-permute-start | bytes 319496 | tf_op jit(solution)/shard_map/ppermute | solution.py:21
  34.8 11.1 %collective-permute-start.6 = (bf16[32,1664]{1,0:T(8,128)(2,1)S(1)}, bf16[32,1664]{1,0:T(8,128)(2,1)S(1)}, u32[]{:S(2)}, u32[]{:S(2)}) collective-permute-start(bf16[32,1664]{1,0:T(8,128)(2,1)S(1)} %get-tuple-element.37), channel_id=1, source_target_pairs={{0,7},{1,0},{2,1},{3,2},{4,3},{5,4},{6,5},{7,6},{8,15},{9,8},{10,9... | collective-permute-start | bytes 319496 | tf_op jit(solution)/shard_map/ppermute | solution.py:21
  47.0 25.9 %collective-permute-start.7 = (bf16[256,1024]{1,0:T(8,128)(2,1)}, bf16[256,1024]{1,0:T(8,128)(2,1)S(1)}, u32[]{:S(2)}, u32[]{:S(2)}) collective-permute-start(bf16[256,1024]{1,0:T(8,128)(2,1)} %get-tuple-element.39), channel_id=1, source_target_pairs={{0,1},{1,2},{2,3},{3,4},{4,5},{5,6},{6,7},{7,8},{8,9},{9,10},{10,1... | collective-permute-start | bytes 1572872 | tf_op jit(solution)/shard_map/ppermute | solution.py:21
  52.1 28.3 %collective-permute-start.8 = (bf16[256,1024]{1,0:T(8,128)(2,1)}, bf16[256,1024]{1,0:T(8,128)(2,1)}, u32[]{:S(2)}, u32[]{:S(2)}) collective-permute-start(bf16[256,1024]{1,0:T(8,128)(2,1)} %get-tuple-element.40), channel_id=1, source_target_pairs={{0,511},{1,0},{2,1},{3,2},{4,3},{5,4},{6,5},{7,6},{8,7},{9,8},{10,... | collective-permute-start | bytes 1572872 | tf_op jit(solution)/shard_map/ppermute | solution.py:21
  71.2 0.7 copy-start.12
  71.9 8.4 %copy-start.4 = (bf16[256,1664]{1,0:T(8,128)(2,1)S(1)}, bf16[256,1664]{1,0:T(8,128)(2,1)}, u32[]{:S(2)}) copy-start(bf16[256,1664]{1,0:T(8,128)(2,1)} %refs_11_.1) | copy-start | bytes 2555908
  71.9 8.4 %copy-start.7 = (s32[192]{0:T(256)S(1)}, s32[192]{0:T(256)}, u32[]{:S(2)}) copy-start(s32[192]{0:T(256)} %get-tuple-element.27.refs_1_) | copy-start | bytes 2308
  71.9 8.4 %copy-start.9 = (s32[192]{0:T(256)S(1)}, s32[192]{0:T(256)}, u32[]{:S(2)}) copy-start(s32[192]{0:T(256)} %get-tuple-element.28.refs_2_) | copy-start | bytes 2308
  71.9 8.5 %copy-start.11 = (s32[192]{0:T(256)S(1)}, s32[192]{0:T(256)}, u32[]{:S(2)}) copy-start(s32[192]{0:T(256)} %get-tuple-element.29.refs_3_) | copy-start | bytes 2308
  71.9 8.5 %copy-start.13 = (s32[3]{0:T(128)S(1)}, s32[3]{0:T(128)}, u32[]{:S(2)}) copy-start(s32[3]{0:T(128)} %get-tuple-element.42.refs_0_) | copy-start | bytes 40
  84.5 1.2 copy-start.1
  85.8 0.8 copy-start.5
  86.6 0.8 copy-start.14
  87.4 0.8 copy-start.15
  88.2 17.2 %all-to-all-start = ((f32[32,16,256]{2,1,0:T(8,128)}), f32[32,16,256]{2,1,0:T(8,128)}, u32[]{:S(2)}, u32[]{:S(2)}) async-start(f32[32,16,256]{2,1,0:T(8,128)} %bitcast.10), calls=%async_computation | async-start | bytes 1048576 | tf_op jit(solution)/shard_map/all_to_all | solution.py:316
  96.0 25.6 %collective-permute-start.10 = (bf16[256,1024]{1,0:T(8,128)(2,1)}, bf16[256,1024]{1,0:T(8,128)(2,1)S(1)}, u32[]{:S(2)}, u32[]{:S(2)}) collective-permute-start(bf16[256,1024]{1,0:T(8,128)(2,1)} %copy-done.15), channel_id=1, source_target_pairs={{0,511},{1,0},{2,1},{3,2},{4,3},{5,4},{6,5},{7,6},{8,7},{9,8},{10,... | collective-permute-start | bytes 1572872 | tf_op jit(solution)/shard_map/ppermute | solution.py:21
  102.5 25.0 %collective-permute-start.9 = (bf16[256,1024]{1,0:T(8,128)(2,1)}, bf16[256,1024]{1,0:T(8,128)(2,1)S(1)}, u32[]{:S(2)}, u32[]{:S(2)}) collective-permute-start(bf16[256,1024]{1,0:T(8,128)(2,1)} %copy-done.14), channel_id=1, source_target_pairs={{0,1},{1,2},{2,3},{3,4},{4,5},{5,6},{6,7},{7,8},{8,9},{9,10},{10,1... | collective-permute-start | bytes 1572872 | tf_op jit(solution)/shard_map/ppermute | solution.py:21
  107.1 33.1 %all-to-all-start.1 = ((bf16[16,16,256]{2,1,0:T(8,128)(2,1)}), bf16[16,16,256]{2,1,0:T(8,128)(2,1)S(1)}, u32[]{:S(2)}, u32[]{:S(2)}) async-start(bf16[16,16,256]{2,1,0:T(8,128)(2,1)} %broadcast_in_dim.10), calls=%async_computation.1 | async-start | bytes 262144 | tf_op jit(solution)/shard_map/all_to_all | solution.py:321
  119.2 1.5 copy-start.2
  140.3 46.2 %all-to-all-start.2 = ((bf16[8,32,1664]{2,1,0:T(8,128)(2,1)}), bf16[8,32,1664]{2,1,0:T(8,128)(2,1)S(1)}, u32[]{:S(2)}, u32[]{:S(2)}) async-start(bf16[8,32,1664]{2,1,0:T(8,128)(2,1)} %bitcast.6), calls=%async_computation.2 | async-start | bytes 1703936 | tf_op jit(solution)/shard_map/all_to_all | solution.py:326
  144.1 3.1 %collective-permute-start.11 = (bf16[16,256]{1,0:T(8,128)(2,1)S(1)}, bf16[16,256]{1,0:T(8,128)(2,1)S(1)}, u32[]{:S(2)}, u32[]{:S(2)}) collective-permute-start(bf16[16,256]{1,0:T(8,128)(2,1)S(1)} %multiply_convert_fusion), channel_id=1, source_target_pairs={{0,8},{8,0},{1,9},{9,1},{2,10},{10,2},{3,11},{11,3},{4,12},{12,4},... | collective-permute-start | bytes 24584 | tf_op jit(solution)/shard_map/ppermute | solution.py:29
  147.1 5.6 %collective-permute-start.12 = (bf16[32,256]{1,0:T(8,128)(2,1)S(1)}, bf16[32,256]{1,0:T(8,128)(2,1)S(1)}, u32[]{:S(2)}, u32[]{:S(2)}) collective-permute-start(bf16[32,256]{1,0:T(8,128)(2,1)S(1)} %pad_maximum_fusion.5), channel_id=1, source_target_pairs={{0,16},{16,0},{32,48},{48,32},{1,17},{17,1},{33,49},{49,33},{2,18}... | collective-permute-start | bytes 49160 | tf_op jit(solution)/shard_map/ppermute | solution.py:29
  152.8 7.3 %collective-permute-start.13 = (bf16[64,256]{1,0:T(8,128)(2,1)S(1)}, bf16[64,256]{1,0:T(8,128)(2,1)S(1)}, u32[]{:S(2)}, u32[]{:S(2)}) collective-permute-start(bf16[64,256]{1,0:T(8,128)(2,1)S(1)} %pad_maximum_fusion.4), channel_id=1, source_target_pairs={{0,32},{16,48},{32,0},{48,16},{1,33},{17,49},{33,1},{49,17},{2,34}... | collective-permute-start | bytes 98312 | tf_op jit(solution)/shard_map/ppermute | solution.py:29
  160.1 6.2 %collective-permute-start.14 = (bf16[128,256]{1,0:T(8,128)(2,1)S(1)}, bf16[128,256]{1,0:T(8,128)(2,1)S(1)}, u32[]{:S(2)}, u32[]{:S(2)}) collective-permute-start(bf16[128,256]{1,0:T(8,128)(2,1)S(1)} %pad_maximum_fusion.3), channel_id=1, source_target_pairs={{0,64},{64,0},{128,192},{192,128},{1,65},{65,1},{129,193},{193,129... | collective-permute-start | bytes 196616 | tf_op jit(solution)/shard_map/ppermute | solution.py:29
  166.3 8.4 %collective-permute-start.15 = (bf16[256,256]{1,0:T(8,128)(2,1)S(1)}, bf16[256,256]{1,0:T(8,128)(2,1)S(1)}, u32[]{:S(2)}, u32[]{:S(2)}) collective-permute-start(bf16[256,256]{1,0:T(8,128)(2,1)S(1)} %pad_maximum_fusion.2), channel_id=1, source_target_pairs={{0,128},{64,192},{128,0},{192,64},{1,129},{65,193},{129,1},{193,65... | collective-permute-start | bytes 393224 | tf_op jit(solution)/shard_map/ppermute | solution.py:29
  (3 other events, 2.0 us)

commit v13 on v11

--- a/solution.py
+++ b/solution.py
@@ -297,7 +297,8 @@
     w_out = jnp.concatenate([w_self, w_neigh], axis=0)
     pieces = lax.axis_size("feat")
     received = list(cut_step(pos, features, pieces))
-    for step in sorted(range(1, pieces), key=lambda step: (abs(2 * step - pieces), step)):
+    far = sorted(range(1, pieces), key=lambda step: (abs(2 * step - pieces), step))
+    for step in reversed(far):
         received[step] = shifted(received[step], "feat", step)
     own, head, tail = join_step(pos, received, rim)
     before = shifted(tail, RING, 1)

time: 188 us -> 189 us (level)
  no operation moved by 1% of the time
where the time goes in v13:
time: 189 us; the launch traced here: 188 us
  starting transfers between devices  98.3 us (52%)
  waiting for transfers between devices  59.9 us (32%)
  local copies, waits for them, and re-layouts  14 us (7%)
  Pallas kernels  10.4 us (6%)
  other arithmetic  3.92 us (2%)
    ppermute x11, starting transfers between devices, shifted(): lax.ppermute(shard, axis, [(i, (i + by) % count) for i in range(count)])  58.2 us
    ppermute x11, waiting for transfers between devices, shifted(): lax.ppermute(shard, axis, [(i, (i + by) % count) for i in range(count)])  21.5 us
    ppermute x5, starting transfers between devices, collected(): other = lax.ppermute(rows, axis, [(i, i ^ apart) for i in range(count)])  16.3 us
    ppermute x5, waiting for transfers between devices, collected(): other = lax.ppermute(rows, axis, [(i, i ^ apart) for i in range(count)])  14.1 us
    unnamed x34, local copies, waits for them, and re-layouts  12.4 us
    all_to_all x1, starting transfers between devices, on_device(): lax.all_to_all(copies, LINE, split_axis=0, concat_axis=0, tiled=True)  12.2 us
    all_to_all x1, waiting for transfers between devices, on_device(): lax.all_to_all(copies, LINE, split_axis=0, concat_axis=0, tiled=True)  12.1 us
    all_to_all x1, waiting for transfers between devices, on_device(): lax.all_to_all(total, 'feat', split_axis=0, concat_axis=1, tiled=True)  11.2 us
  transfers between devices with their start and end apart: 19, of which 12 were waited for; matrix products, arithmetic and copies ran while one was open for 4% of the time, Pallas kernels for 2%

profile of v13, /device:TPU:6, one launch (start us, length us, event | category | flops | bytes accessed | tf_op | source)
XLA Modules:
  0.0 188.2 jit_solution(8569148871671644669)
XLA Ops:
  2.3 3.8 %collective-permute-start = (bf16[32,1664]{1,0:T(8,128)(2,1)S(1)}, bf16[32,1664]{1,0:T(8,128)(2,1)S(1)}, u32[]{:S(2)}, u32[]{:S(2)}) collective-permute-start(bf16[32,1664]{1,0:T(8,128)(2,1)S(1)} %get-tuple-element.31), channel_id=1, source_target_pairs={{0,1},{1,2},{2,3},{3,4},{4,5},{5,6},{6,7},{7,0},{8,9},{9,10},{10,1... | collective-permute-start | bytes 319496 | tf_op jit(solution)/shard_map/ppermute | solution.py:21
  6.2 5.2 %collective-permute-start.1 = (bf16[32,1664]{1,0:T(8,128)(2,1)S(1)}, bf16[32,1664]{1,0:T(8,128)(2,1)S(1)}, u32[]{:S(2)}, u32[]{:S(2)}) collective-permute-start(bf16[32,1664]{1,0:T(8,128)(2,1)S(1)} %get-tuple-element.32), channel_id=1, source_target_pairs={{0,2},{1,3},{2,4},{3,5},{4,6},{5,7},{6,0},{7,1},{8,10},{9,11},{10,... | collective-permute-start | bytes 319496 | tf_op jit(solution)/shard_map/ppermute | solution.py:21
  11.3 7.7 %collective-permute-start.2 = (bf16[32,1664]{1,0:T(8,128)(2,1)S(1)}, bf16[32,1664]{1,0:T(8,128)(2,1)S(1)}, u32[]{:S(2)}, u32[]{:S(2)}) collective-permute-start(bf16[32,1664]{1,0:T(8,128)(2,1)S(1)} %get-tuple-element.33), channel_id=1, source_target_pairs={{0,3},{1,4},{2,5},{3,6},{4,7},{5,0},{6,1},{7,2},{8,11},{9,12},{10,... | collective-permute-start | bytes 319496 | tf_op jit(solution)/shard_map/ppermute | solution.py:21
  19.1 3.3 %collective-permute-start.3 = (bf16[32,1664]{1,0:T(8,128)(2,1)S(1)}, bf16[32,1664]{1,0:T(8,128)(2,1)S(1)}, u32[]{:S(2)}, u32[]{:S(2)}) collective-permute-start(bf16[32,1664]{1,0:T(8,128)(2,1)S(1)} %get-tuple-element.34), channel_id=1, source_target_pairs={{0,4},{1,5},{2,6},{3,7},{4,0},{5,1},{6,2},{7,3},{8,12},{9,13},{10,... | collective-permute-start | bytes 319496 | tf_op jit(solution)/shard_map/ppermute | solution.py:21
  22.4 7.8 %collective-permute-start.4 = (bf16[32,1664]{1,0:T(8,128)(2,1)S(1)}, bf16[32,1664]{1,0:T(8,128)(2,1)S(1)}, u32[]{:S(2)}, u32[]{:S(2)}) collective-permute-start(bf16[32,1664]{1,0:T(8,128)(2,1)S(1)} %get-tuple-element.35), channel_id=1, source_target_pairs={{0,5},{1,6},{2,7},{3,0},{4,1},{5,2},{6,3},{7,4},{8,13},{9,14},{10,... | collective-permute-start | bytes 319496 | tf_op jit(solution)/shard_map/ppermute | solution.py:21
  30.2 4.6 %collective-permute-start.5 = (bf16[32,1664]{1,0:T(8,128)(2,1)S(1)}, bf16[32,1664]{1,0:T(8,128)(2,1)S(1)}, u32[]{:S(2)}, u32[]{:S(2)}) collective-permute-start(bf16[32,1664]{1,0:T(8,128)(2,1)S(1)} %get-tuple-element.36), channel_id=1, source_target_pairs={{0,6},{1,7},{2,0},{3,1},{4,2},{5,3},{6,4},{7,5},{8,14},{9,15},{10,... | collective-permute-start | bytes 319496 | tf_op jit(solution)/shard_map/ppermute | solution.py:21
  34.8 2.9 %collective-permute-start.6 = (bf16[32,1664]{1,0:T(8,128)(2,1)S(1)}, bf16[32,1664]{1,0:T(8,128)(2,1)S(1)}, u32[]{:S(2)}, u32[]{:S(2)}) collective-permute-start(bf16[32,1664]{1,0:T(8,128)(2,1)S(1)} %get-tuple-element.37), channel_id=1, source_target_pairs={{0,7},{1,0},{2,1},{3,2},{4,3},{5,4},{6,5},{7,6},{8,15},{9,8},{10,9... | collective-permute-start | bytes 319496 | tf_op jit(solution)/shard_map/ppermute | solution.py:21
  37.7 3.3 %collective-permute-done.2.refs_3_ = bf16[32,1664]{1,0:T(8,128)(2,1)S(1)} collective-permute-done((bf16[32,1664]{1,0:T(8,128)(2,1)S(1)}, bf16[32,1664]{1,0:T(8,128)(2,1)S(1)}, u32[]{:S(2)}, u32[]{:S(2)}) %collective-permute-start.2) | collective-permute-done | bytes 106528 | tf_op jit(solution)/shard_map/ppermute | solution.py:21
  41.1 4.8 %collective-permute-done.5.refs_6_ = bf16[32,1664]{1,0:T(8,128)(2,1)S(1)} collective-permute-done((bf16[32,1664]{1,0:T(8,128)(2,1)S(1)}, bf16[32,1664]{1,0:T(8,128)(2,1)S(1)}, u32[]{:S(2)}, u32[]{:S(2)}) %collective-permute-start.5) | collective-permute-done | bytes 106528 | tf_op jit(solution)/shard_map/ppermute | solution.py:21
  47.0 5.1 %collective-permute-start.7 = (bf16[256,1024]{1,0:T(8,128)(2,1)}, bf16[256,1024]{1,0:T(8,128)(2,1)S(1)}, u32[]{:S(2)}, u32[]{:S(2)}) collective-permute-start(bf16[256,1024]{1,0:T(8,128)(2,1)} %get-tuple-element.39), channel_id=1, source_target_pairs={{0,1},{1,2},{2,3},{3,4},{4,5},{5,6},{6,7},{7,8},{8,9},{9,10},{10,1... | collective-permute-start | bytes 1572872 | tf_op jit(solution)/shard_map/ppermute | solution.py:21
  52.1 9.4 %collective-permute-start.8 = (bf16[256,1024]{1,0:T(8,128)(2,1)}, bf16[256,1024]{1,0:T(8,128)(2,1)}, u32[]{:S(2)}, u32[]{:S(2)}) collective-permute-start(bf16[256,1024]{1,0:T(8,128)(2,1)} %get-tuple-element.40), channel_id=1, source_target_pairs={{0,511},{1,0},{2,1},{3,2},{4,3},{5,4},{6,5},{7,6},{8,7},{9,8},{10,... | collective-permute-start | bytes 1572872 | tf_op jit(solution)/shard_map/ppermute | solution.py:21
  62.2 1.7 copy.14
  63.8 1.7 copy.15
  72.7 7.6 %collective-permute-done.8.refs_7_ = bf16[256,1024]{1,0:T(8,128)(2,1)} collective-permute-done((bf16[256,1024]{1,0:T(8,128)(2,1)}, bf16[256,1024]{1,0:T(8,128)(2,1)}, u32[]{:S(2)}, u32[]{:S(2)}) %collective-permute-start.8) | collective-permute-done | bytes 524320 | tf_op jit(solution)/shard_map/ppermute | solution.py:21
  80.4 4.5 %shard_map.107 = (bf16[256,1024]{1,0:T(8,128)(2,1)S(1)}, bf16[256,1024]{1,0:T(8,128)(2,1)S(1)}, f32[512,256]{1,0:T(8,128)S(1)}, bf16[512,1664]{1,0:T(8,128)(2,1)S(1)}) custom-call(s32[3]{0:T(128)S(1)} %copy-done.13, s32[192]{0:T(256)S(1)} %copy-done.7, s32[192]{0:T(256)S(1)} %copy-done.9, s32[192]{0:T(256)S(1)} %copy-done.11, ...), custom_call_target="tpu_custom_call" | custom-call | flops 1308622848 | bytes 8388608 | tf_op jit(solution)/shard_map/pallas_call | solution.py:167
  88.5 7.7 %all-to-all-start = ((f32[32,16,256]{2,1,0:T(8,128)}), f32[32,16,256]{2,1,0:T(8,128)}, u32[]{:S(2)}, u32[]{:S(2)}) async-start(f32[32,16,256]{2,1,0:T(8,128)} %bitcast.10), calls=%async_computation | async-start | bytes 1048576 | tf_op jit(solution)/shard_map/all_to_all | solution.py:314
  96.2 6.4 %collective-permute-start.10 = (bf16[256,1024]{1,0:T(8,128)(2,1)}, bf16[256,1024]{1,0:T(8,128)(2,1)S(1)}, u32[]{:S(2)}, u32[]{:S(2)}) collective-permute-start(bf16[256,1024]{1,0:T(8,128)(2,1)} %copy-done.15), channel_id=1, source_target_pairs={{0,511},{1,0},{2,1},{3,2},{4,3},{5,4},{6,5},{7,6},{8,7},{9,8},{10,... | collective-permute-start | bytes 1572872 | tf_op jit(solution)/shard_map/ppermute | solution.py:21
  102.7 1.9 %collective-permute-start.9 = (bf16[256,1024]{1,0:T(8,128)(2,1)}, bf16[256,1024]{1,0:T(8,128)(2,1)S(1)}, u32[]{:S(2)}, u32[]{:S(2)}) collective-permute-start(bf16[256,1024]{1,0:T(8,128)(2,1)} %copy-done.14), channel_id=1, source_target_pairs={{0,1},{1,2},{2,3},{3,4},{4,5},{5,6},{6,7},{7,8},{8,9},{9,10},{10,1... | collective-permute-start | bytes 1572872 | tf_op jit(solution)/shard_map/ppermute | solution.py:21
  107.4 12.2 %all-to-all-start.1 = ((bf16[16,16,256]{2,1,0:T(8,128)(2,1)}), bf16[16,16,256]{2,1,0:T(8,128)(2,1)S(1)}, u32[]{:S(2)}, u32[]{:S(2)}) async-start(bf16[16,16,256]{2,1,0:T(8,128)(2,1)} %broadcast_in_dim.10), calls=%async_computation.1 | async-start | bytes 262144 | tf_op jit(solution)/shard_map/all_to_all | solution.py:319
  121.9 5.7 %collective-permute-done.9.prev_ref = bf16[256,1024]{1,0:T(8,128)(2,1)S(1)} collective-permute-done((bf16[256,1024]{1,0:T(8,128)(2,1)}, bf16[256,1024]{1,0:T(8,128)(2,1)S(1)}, u32[]{:S(2)}, u32[]{:S(2)}) %collective-permute-start.9) | collective-permute-done | bytes 524320 | tf_op jit(solution)/shard_map/ppermute | solution.py:21
  128.7 12.1 %all-to-all-done.1 = bf16[16,16,256]{2,1,0:T(8,128)(2,1)S(1)} async-done(((bf16[16,16,256]{2,1,0:T(8,128)(2,1)}), bf16[16,16,256]{2,1,0:T(8,128)(2,1)S(1)}, u32[]{:S(2)}, u32[]{:S(2)}) %all-to-all-start.1) | async-done | bytes 131104 | tf_op jit(solution)/shard_map/all_to_all | solution.py:319
  140.8 3.8 %all-to-all-start.2 = ((bf16[8,32,1664]{2,1,0:T(8,128)(2,1)}), bf16[8,32,1664]{2,1,0:T(8,128)(2,1)S(1)}, u32[]{:S(2)}, u32[]{:S(2)}) async-start(bf16[8,32,1664]{2,1,0:T(8,128)(2,1)} %bitcast.6), calls=%async_computation.2 | async-start | bytes 1703936 | tf_op jit(solution)/shard_map/all_to_all | solution.py:324
  144.7 1.9 %collective-permute-start.11 = (bf16[16,256]{1,0:T(8,128)(2,1)S(1)}, bf16[16,256]{1,0:T(8,128)(2,1)S(1)}, u32[]{:S(2)}, u32[]{:S(2)}) collective-permute-start(bf16[16,256]{1,0:T(8,128)(2,1)S(1)} %multiply_convert_fusion), channel_id=1, source_target_pairs={{0,8},{8,0},{1,9},{9,1},{2,10},{10,2},{3,11},{11,3},{4,12},{12,4},... | collective-permute-start | bytes 24584 | tf_op jit(solution)/shard_map/ppermute | solution.py:29
  147.7 2.8 %collective-permute-start.12 = (bf16[32,256]{1,0:T(8,128)(2,1)S(1)}, bf16[32,256]{1,0:T(8,128)(2,1)S(1)}, u32[]{:S(2)}, u32[]{:S(2)}) collective-permute-start(bf16[32,256]{1,0:T(8,128)(2,1)S(1)} %pad_maximum_fusion.5), channel_id=1, source_target_pairs={{0,16},{16,0},{32,48},{48,32},{1,17},{17,1},{33,49},{49,33},{2,18}... | collective-permute-start | bytes 49160 | tf_op jit(solution)/shard_map/ppermute | solution.py:29
  150.5 2.9 %collective-permute-done.12 = bf16[32,256]{1,0:T(8,128)(2,1)S(1)} collective-permute-done((bf16[32,256]{1,0:T(8,128)(2,1)S(1)}, bf16[32,256]{1,0:T(8,128)(2,1)S(1)}, u32[]{:S(2)}, u32[]{:S(2)}) %collective-permute-start.12) | collective-permute-done | bytes 16416 | tf_op jit(solution)/shard_map/ppermute | solution.py:29
  153.4 3.4 %collective-permute-start.13 = (bf16[64,256]{1,0:T(8,128)(2,1)S(1)}, bf16[64,256]{1,0:T(8,128)(2,1)S(1)}, u32[]{:S(2)}, u32[]{:S(2)}) collective-permute-start(bf16[64,256]{1,0:T(8,128)(2,1)S(1)} %pad_maximum_fusion.4), channel_id=1, source_target_pairs={{0,32},{16,48},{32,0},{48,16},{1,33},{17,49},{33,1},{49,17},{2,34}... | collective-permute-start | bytes 98312 | tf_op jit(solution)/shard_map/ppermute | solution.py:29
  156.8 3.9 %collective-permute-done.13 = bf16[64,256]{1,0:T(8,128)(2,1)S(1)} collective-permute-done((bf16[64,256]{1,0:T(8,128)(2,1)S(1)}, bf16[64,256]{1,0:T(8,128)(2,1)S(1)}, u32[]{:S(2)}, u32[]{:S(2)}) %collective-permute-start.13) | collective-permute-done | bytes 32800 | tf_op jit(solution)/shard_map/ppermute | solution.py:29
  160.7 3.4 %collective-permute-start.14 = (bf16[128,256]{1,0:T(8,128)(2,1)S(1)}, bf16[128,256]{1,0:T(8,128)(2,1)S(1)}, u32[]{:S(2)}, u32[]{:S(2)}) collective-permute-start(bf16[128,256]{1,0:T(8,128)(2,1)S(1)} %pad_maximum_fusion.3), channel_id=1, source_target_pairs={{0,64},{64,0},{128,192},{192,128},{1,65},{65,1},{129,193},{193,129... | collective-permute-start | bytes 196616 | tf_op jit(solution)/shard_map/ppermute | solution.py:29
  164.1 2.8 %collective-permute-done.14 = bf16[128,256]{1,0:T(8,128)(2,1)S(1)} collective-permute-done((bf16[128,256]{1,0:T(8,128)(2,1)S(1)}, bf16[128,256]{1,0:T(8,128)(2,1)S(1)}, u32[]{:S(2)}, u32[]{:S(2)}) %collective-permute-start.14) | collective-permute-done | bytes 65568 | tf_op jit(solution)/shard_map/ppermute | solution.py:29
  166.9 4.9 %collective-permute-start.15 = (bf16[256,256]{1,0:T(8,128)(2,1)S(1)}, bf16[256,256]{1,0:T(8,128)(2,1)S(1)}, u32[]{:S(2)}, u32[]{:S(2)}) collective-permute-start(bf16[256,256]{1,0:T(8,128)(2,1)S(1)} %pad_maximum_fusion.2), channel_id=1, source_target_pairs={{0,128},{64,192},{128,0},{192,64},{1,129},{65,193},{129,1},{193,65... | collective-permute-start | bytes 393224 | tf_op jit(solution)/shard_map/ppermute | solution.py:29
  171.9 3.4 %collective-permute-done.15 = bf16[256,256]{1,0:T(8,128)(2,1)S(1)} collective-permute-done((bf16[256,256]{1,0:T(8,128)(2,1)S(1)}, bf16[256,256]{1,0:T(8,128)(2,1)S(1)}, u32[]{:S(2)}, u32[]{:S(2)}) %collective-permute-start.15) | collective-permute-done | bytes 131104 | tf_op jit(solution)/shard_map/ppermute | solution.py:29
  176.1 11.2 %all-to-all-done.2 = bf16[8,32,1664]{2,1,0:T(8,128)(2,1)S(1)} async-done(((bf16[8,32,1664]{2,1,0:T(8,128)(2,1)}), bf16[8,32,1664]{2,1,0:T(8,128)(2,1)S(1)}, u32[]{:S(2)}, u32[]{:S(2)}) %all-to-all-start.2) | async-done | bytes 852000 | tf_op jit(solution)/shard_map/all_to_all | solution.py:324
  (63 shorter events, 22.7 us)
Async XLA Ops:
  0.6 68.5 %copy-start = (bf16[64,128,128]{2,1,0:T(8,128)(2,1)S(1)}, bf16[64,128,128]{2,1,0:T(8,128)(2,1)}, u32[]{:S(2)}) copy-start(bf16[64,128,128]{2,1,0:T(8,128)(2,1)} %refs_5_.3) | copy-start | bytes 6291460
  0.6 1.3 copy-start.3
  2.3 27.9 %collective-permute-start = (bf16[32,1664]{1,0:T(8,128)(2,1)S(1)}, bf16[32,1664]{1,0:T(8,128)(2,1)S(1)}, u32[]{:S(2)}, u32[]{:S(2)}) collective-permute-start(bf16[32,1664]{1,0:T(8,128)(2,1)S(1)} %get-tuple-element.31), channel_id=1, source_target_pairs={{0,1},{1,2},{2,3},{3,4},{4,5},{5,6},{6,7},{7,0},{8,9},{9,10},{10,1... | collective-permute-start | bytes 319496 | tf_op jit(solution)/shard_map/ppermute | solution.py:21
  6.2 28.6 %collective-permute-start.1 = (bf16[32,1664]{1,0:T(8,128)(2,1)S(1)}, bf16[32,1664]{1,0:T(8,128)(2,1)S(1)}, u32[]{:S(2)}, u32[]{:S(2)}) collective-permute-start(bf16[32,1664]{1,0:T(8,128)(2,1)S(1)} %get-tuple-element.32), channel_id=1, source_target_pairs={{0,2},{1,3},{2,4},{3,5},{4,6},{5,7},{6,0},{7,1},{8,10},{9,11},{10,... | collective-permute-start | bytes 319496 | tf_op jit(solution)/shard_map/ppermute | solution.py:21
  11.3 29.7 %collective-permute-start.2 = (bf16[32,1664]{1,0:T(8,128)(2,1)S(1)}, bf16[32,1664]{1,0:T(8,128)(2,1)S(1)}, u32[]{:S(2)}, u32[]{:S(2)}) collective-permute-start(bf16[32,1664]{1,0:T(8,128)(2,1)S(1)} %get-tuple-element.33), channel_id=1, source_target_pairs={{0,3},{1,4},{2,5},{3,6},{4,7},{5,0},{6,1},{7,2},{8,11},{9,12},{10,... | collective-permute-start | bytes 319496 | tf_op jit(solution)/shard_map/ppermute | solution.py:21
  19.1 22.0 %collective-permute-start.3 = (bf16[32,1664]{1,0:T(8,128)(2,1)S(1)}, bf16[32,1664]{1,0:T(8,128)(2,1)S(1)}, u32[]{:S(2)}, u32[]{:S(2)}) collective-permute-start(bf16[32,1664]{1,0:T(8,128)(2,1)S(1)} %get-tuple-element.34), channel_id=1, source_target_pairs={{0,4},{1,5},{2,6},{3,7},{4,0},{5,1},{6,2},{7,3},{8,12},{9,13},{10,... | collective-permute-start | bytes 319496 | tf_op jit(solution)/shard_map/ppermute | solution.py:21
  22.4 18.7 %collective-permute-start.4 = (bf16[32,1664]{1,0:T(8,128)(2,1)S(1)}, bf16[32,1664]{1,0:T(8,128)(2,1)S(1)}, u32[]{:S(2)}, u32[]{:S(2)}) collective-permute-start(bf16[32,1664]{1,0:T(8,128)(2,1)S(1)} %get-tuple-element.35), channel_id=1, source_target_pairs={{0,5},{1,6},{2,7},{3,0},{4,1},{5,2},{6,3},{7,4},{8,13},{9,14},{10,... | collective-permute-start | bytes 319496 | tf_op jit(solution)/shard_map/ppermute | solution.py:21
  30.2 15.6 %collective-permute-start.5 = (bf16[32,1664]{1,0:T(8,128)(2,1)S(1)}, bf16[32,1664]{1,0:T(8,128)(2,1)S(1)}, u32[]{:S(2)}, u32[]{:S(2)}) collective-permute-start(bf16[32,1664]{1,0:T(8,128)(2,1)S(1)} %get-tuple-element.36), channel_id=1, source_target_pairs={{0,6},{1,7},{2,0},{3,1},{4,2},{5,3},{6,4},{7,5},{8,14},{9,15},{10,... | collective-permute-start | bytes 319496 | tf_op jit(solution)/shard_map/ppermute | solution.py:21
  34.8 11.1 %collective-permute-start.6 = (bf16[32,1664]{1,0:T(8,128)(2,1)S(1)}, bf16[32,1664]{1,0:T(8,128)(2,1)S(1)}, u32[]{:S(2)}, u32[]{:S(2)}) collective-permute-start(bf16[32,1664]{1,0:T(8,128)(2,1)S(1)} %get-tuple-element.37), channel_id=1, source_target_pairs={{0,7},{1,0},{2,1},{3,2},{4,3},{5,4},{6,5},{7,6},{8,15},{9,8},{10,9... | collective-permute-start | bytes 319496 | tf_op jit(solution)/shard_map/ppermute | solution.py:21
  47.0 25.7 %collective-permute-start.7 = (bf16[256,1024]{1,0:T(8,128)(2,1)}, bf16[256,1024]{1,0:T(8,128)(2,1)S(1)}, u32[]{:S(2)}, u32[]{:S(2)}) collective-permute-start(bf16[256,1024]{1,0:T(8,128)(2,1)} %get-tuple-element.39), channel_id=1, source_target_pairs={{0,1},{1,2},{2,3},{3,4},{4,5},{5,6},{6,7},{7,8},{8,9},{9,10},{10,1... | collective-permute-start | bytes 1572872 | tf_op jit(solution)/shard_map/ppermute | solution.py:21
  52.1 28.3 %collective-permute-start.8 = (bf16[256,1024]{1,0:T(8,128)(2,1)}, bf16[256,1024]{1,0:T(8,128)(2,1)}, u32[]{:S(2)}, u32[]{:S(2)}) collective-permute-start(bf16[256,1024]{1,0:T(8,128)(2,1)} %get-tuple-element.40), channel_id=1, source_target_pairs={{0,511},{1,0},{2,1},{3,2},{4,3},{5,4},{6,5},{7,6},{8,7},{9,8},{10,... | collective-permute-start | bytes 1572872 | tf_op jit(solution)/shard_map/ppermute | solution.py:21
  71.1 0.7 copy-start.12
  71.8 8.5 %copy-start.4 = (bf16[256,1664]{1,0:T(8,128)(2,1)S(1)}, bf16[256,1664]{1,0:T(8,128)(2,1)}, u32[]{:S(2)}) copy-start(bf16[256,1664]{1,0:T(8,128)(2,1)} %refs_11_.1) | copy-start | bytes 2555908
  71.8 8.5 %copy-start.7 = (s32[192]{0:T(256)S(1)}, s32[192]{0:T(256)}, u32[]{:S(2)}) copy-start(s32[192]{0:T(256)} %get-tuple-element.27.refs_1_) | copy-start | bytes 2308
  71.8 8.6 %copy-start.9 = (s32[192]{0:T(256)S(1)}, s32[192]{0:T(256)}, u32[]{:S(2)}) copy-start(s32[192]{0:T(256)} %get-tuple-element.28.refs_2_) | copy-start | bytes 2308
  71.8 8.6 %copy-start.11 = (s32[192]{0:T(256)S(1)}, s32[192]{0:T(256)}, u32[]{:S(2)}) copy-start(s32[192]{0:T(256)} %get-tuple-element.29.refs_3_) | copy-start | bytes 2308
  71.8 8.6 %copy-start.13 = (s32[3]{0:T(128)S(1)}, s32[3]{0:T(128)}, u32[]{:S(2)}) copy-start(s32[3]{0:T(128)} %get-tuple-element.42.refs_0_) | copy-start | bytes 40
  84.9 1.2 copy-start.1
  86.1 0.8 copy-start.5
  86.9 0.8 copy-start.14
  87.7 0.8 copy-start.15
  88.5 17.2 %all-to-all-start = ((f32[32,16,256]{2,1,0:T(8,128)}), f32[32,16,256]{2,1,0:T(8,128)}, u32[]{:S(2)}, u32[]{:S(2)}) async-start(f32[32,16,256]{2,1,0:T(8,128)} %bitcast.10), calls=%async_computation | async-start | bytes 1048576 | tf_op jit(solution)/shard_map/all_to_all | solution.py:314
  96.2 25.7 %collective-permute-start.10 = (bf16[256,1024]{1,0:T(8,128)(2,1)}, bf16[256,1024]{1,0:T(8,128)(2,1)S(1)}, u32[]{:S(2)}, u32[]{:S(2)}) collective-permute-start(bf16[256,1024]{1,0:T(8,128)(2,1)} %copy-done.15), channel_id=1, source_target_pairs={{0,511},{1,0},{2,1},{3,2},{4,3},{5,4},{6,5},{7,6},{8,7},{9,8},{10,... | collective-permute-start | bytes 1572872 | tf_op jit(solution)/shard_map/ppermute | solution.py:21
  102.7 24.9 %collective-permute-start.9 = (bf16[256,1024]{1,0:T(8,128)(2,1)}, bf16[256,1024]{1,0:T(8,128)(2,1)S(1)}, u32[]{:S(2)}, u32[]{:S(2)}) collective-permute-start(bf16[256,1024]{1,0:T(8,128)(2,1)} %copy-done.14), channel_id=1, source_target_pairs={{0,1},{1,2},{2,3},{3,4},{4,5},{5,6},{6,7},{7,8},{8,9},{9,10},{10,1... | collective-permute-start | bytes 1572872 | tf_op jit(solution)/shard_map/ppermute | solution.py:21
  107.4 33.4 %all-to-all-start.1 = ((bf16[16,16,256]{2,1,0:T(8,128)(2,1)}), bf16[16,16,256]{2,1,0:T(8,128)(2,1)S(1)}, u32[]{:S(2)}, u32[]{:S(2)}) async-start(bf16[16,16,256]{2,1,0:T(8,128)(2,1)} %broadcast_in_dim.10), calls=%async_computation.1 | async-start | bytes 262144 | tf_op jit(solution)/shard_map/all_to_all | solution.py:319
  119.6 1.5 copy-start.2
  140.8 46.4 %all-to-all-start.2 = ((bf16[8,32,1664]{2,1,0:T(8,128)(2,1)}), bf16[8,32,1664]{2,1,0:T(8,128)(2,1)S(1)}, u32[]{:S(2)}, u32[]{:S(2)}) async-start(bf16[8,32,1664]{2,1,0:T(8,128)(2,1)} %bitcast.6), calls=%async_computation.2 | async-start | bytes 1703936 | tf_op jit(solution)/shard_map/all_to_all | solution.py:324
  144.7 3.1 %collective-permute-start.11 = (bf16[16,256]{1,0:T(8,128)(2,1)S(1)}, bf16[16,256]{1,0:T(8,128)(2,1)S(1)}, u32[]{:S(2)}, u32[]{:S(2)}) collective-permute-start(bf16[16,256]{1,0:T(8,128)(2,1)S(1)} %multiply_convert_fusion), channel_id=1, source_target_pairs={{0,8},{8,0},{1,9},{9,1},{2,10},{10,2},{3,11},{11,3},{4,12},{12,4},... | collective-permute-start | bytes 24584 | tf_op jit(solution)/shard_map/ppermute | solution.py:29
  147.7 5.6 %collective-permute-start.12 = (bf16[32,256]{1,0:T(8,128)(2,1)S(1)}, bf16[32,256]{1,0:T(8,128)(2,1)S(1)}, u32[]{:S(2)}, u32[]{:S(2)}) collective-permute-start(bf16[32,256]{1,0:T(8,128)(2,1)S(1)} %pad_maximum_fusion.5), channel_id=1, source_target_pairs={{0,16},{16,0},{32,48},{48,32},{1,17},{17,1},{33,49},{49,33},{2,18}... | collective-permute-start | bytes 49160 | tf_op jit(solution)/shard_map/ppermute | solution.py:29
  153.4 7.3 %collective-permute-start.13 = (bf16[64,256]{1,0:T(8,128)(2,1)S(1)}, bf16[64,256]{1,0:T(8,128)(2,1)S(1)}, u32[]{:S(2)}, u32[]{:S(2)}) collective-permute-start(bf16[64,256]{1,0:T(8,128)(2,1)S(1)} %pad_maximum_fusion.4), channel_id=1, source_target_pairs={{0,32},{16,48},{32,0},{48,16},{1,33},{17,49},{33,1},{49,17},{2,34}... | collective-permute-start | bytes 98312 | tf_op jit(solution)/shard_map/ppermute | solution.py:29
  160.7 6.2 %collective-permute-start.14 = (bf16[128,256]{1,0:T(8,128)(2,1)S(1)}, bf16[128,256]{1,0:T(8,128)(2,1)S(1)}, u32[]{:S(2)}, u32[]{:S(2)}) collective-permute-start(bf16[128,256]{1,0:T(8,128)(2,1)S(1)} %pad_maximum_fusion.3), channel_id=1, source_target_pairs={{0,64},{64,0},{128,192},{192,128},{1,65},{65,1},{129,193},{193,129... | collective-permute-start | bytes 196616 | tf_op jit(solution)/shard_map/ppermute | solution.py:29
  166.9 8.4 %collective-permute-start.15 = (bf16[256,256]{1,0:T(8,128)(2,1)S(1)}, bf16[256,256]{1,0:T(8,128)(2,1)S(1)}, u32[]{:S(2)}, u32[]{:S(2)}) collective-permute-start(bf16[256,256]{1,0:T(8,128)(2,1)S(1)} %pad_maximum_fusion.2), channel_id=1, source_target_pairs={{0,128},{64,192},{128,0},{192,64},{1,129},{65,193},{129,1},{193,65... | collective-permute-start | bytes 393224 | tf_op jit(solution)/shard_map/ppermute | solution.py:29
  (3 other events, 2.0 us)
